TPU v7x, 32 devices: a whole 2x2x4 slice. The times are simulated.
32 devices in a mesh: lon: 8 (over z, x), lat: 4 (over y, core).
Axes of the slice: x: 2, y: 2, z: 4, core: 2. Of those that a mesh axis runs over, the one named last changes fastest.
Arguments:
- state: float32 [25, 512, 1024], P(None, 'lat', 'lon'), may hold values from -6 to 6
- adjoint_in: float32 [25, 512, 1024], P(None, 'lat', 'lon'), may hold values from -6 to 6
- land_mask: int32 [512, 1024], P('lat', 'lon'), may hold values 0 or 1
- east_coef: float32 [512, 1024], P('lat', 'lon'), may hold values from 0.03 to 0.25
- north_coef: float32 [512, 1024], P('lat', 'lon'), may hold values from 0.03 to 0.25
- zonal_flow: float32 [512, 1024], P('lat', 'lon'), may hold values from -0.2 to 0.2
- vertical_coef: float32 [512, 1024], P('lat', 'lon'), may hold values from 0.05 to 0.3
- slot_cell: int32 [32, 2048], P(('lon', 'lat')), may hold values from -1 to 16383, as said below
- slot_weight: float32 [32, 2048], P(('lon', 'lat')), may hold values from 0.1 to 1
- arrive_obs: int32 [32, 2048], P(('lon', 'lat')), may hold values from -1 to 511, as said below
- obs_value: float32 [25, 16384], P(None, ('lon', 'lat')), may hold values from -6 to 6
- obs_invvar: float32 [25, 16384], P(None, ('lon', 'lat')), may hold values from 0.5 to 4
Outputs:
- adjoint_state: float32 [25, 512, 1024], P(None, 'lat', 'lon')
- misfit: float32 [25, 16384], P(None, ('lon', 'lat'))
Inputs may be any that keep to these rules, and one draw needn't show every extreme that they name: slot_cell[s, t * 64 + p] is the index, row-major over the 128 x 128 block of device s, of the cell that slot p from device s to device t reads, or -1 where that slot is empty; from each device to each device the live slots are those with p below a count of 1 to 64, and some device receives 64 live slots from every device. arrive_obs[t, s * 64 + p] is the observation of device t fed by slot p from device s, and is -1 exactly where slot_cell[s, t * 64 + p] is -1.
All inputs are finite; a program needn't handle non-finite values. No bound on the sum of `land_mask` on one device may be relied on, other than what follows from the above.
Results may differ from a plain program's by a relative error of at most 0.00002.
Values sent between devices are 32-bit elements; how exact they have to be, the bound alone decides.
No kernel may reach another device: no remote copies, remote signals or barrier semaphores. Data moves between devices by JAX's collectives and lax.ppermute only.
A program may use at most 64 MiB of HBM per device.

v0:
```python
import jax
import jax.numpy as jnp
from jax import lax
from jax.sharding import PartitionSpec as P

STEPS = 2


def from_behind(value, axis, steps):
    count = lax.axis_size(axis)
    pairs = [(source, (source + steps) % count) for source in range(count)]
    return lax.ppermute(value, axis, pairs)


def from_behind_2(block, axis, distance):
    devices = range(lax.axis_size(axis))
    route = [(i - distance, i) for i in devices if i - distance in devices]
    return lax.ppermute(block, axis, route)


def padded(cells, sides, width, closed):
    for axis, dim in sides:
        count = lax.axis_size(axis)
        ends = count if closed else count - 1
        head = lax.slice_in_dim(cells, 0, width, axis=dim)
        tail = lax.slice_in_dim(cells, cells.shape[dim] - width, cells.shape[dim], axis=dim)
        cells = jnp.concatenate(
            [
                lax.ppermute(tail, axis, [(i, (i + 1) % count) for i in range(ends)]),
                cells,
                lax.ppermute(head, axis, [((i + 1) % count, i) for i in range(ends)]),
            ],
            axis=dim,
        )
    return cells


def from_partner(value, axis, bit):
    return lax.ppermute(value, axis, [(i, i ^ 1 << bit) for i in range(lax.axis_size(axis))])


def on_device(
    state,
    adjoint_in,
    land_mask,
    east_coef,
    north_coef,
    zonal_flow,
    vertical_coef,
    slot_cell,
    slot_weight,
    arrive_obs,
    obs_value,
    obs_invvar,
):
    levels_n, rows_n, cols_n = state.shape
    flat_state = state.reshape(levels_n, rows_n * cols_n)
    slot_row = slot_cell[0]
    live_slot = slot_row >= 0
    cell_index = jnp.where(live_slot, slot_row, 0)
    weights = jnp.where(live_slot, slot_weight[0], 0.0)
    partial_vals = flat_state[:, cell_index] * weights[None, :]
    arrived = lax.all_to_all(partial_vals, ("lon", "lat"), split_axis=1, concat_axis=1, tiled=True)
    target_row = arrive_obs[0]
    live_target = target_row >= 0
    target_index = jnp.where(live_target, target_row, 0)
    incoming = jnp.where(live_target[None, :], arrived, 0.0)
    interp = jnp.zeros(obs_value.shape, jnp.float32).at[:, target_index].add(incoming)
    misfit = obs_invvar * (interp - obs_value)
    outgoing = jnp.where(live_target[None, :], misfit[:, target_index], 0.0)
    returned = lax.all_to_all(outgoing, ("lon", "lat"), split_axis=1, concat_axis=1, tiled=True)
    forcing = (
        jnp.zeros((levels_n, rows_n * cols_n), jnp.float32)
        .at[:, cell_index]
        .add(returned * weights[None, :])
    )
    adjoint_state = adjoint_in + forcing.reshape(state.shape)
    ocean = land_mask.astype(jnp.float32)
    east_weight = east_coef - 0.5 * zonal_flow
    own_east = east_coef + 0.5 * zonal_flow
    west_column = from_behind(east_weight[:, -1:], "lon", 1)
    west_weight = jnp.concatenate([west_column, east_weight[:, :-1]], axis=1)
    south_row = from_behind_2(north_coef[-1:, :], "lat", 1)
    south_weight = jnp.concatenate([south_row, north_coef[:-1, :]], axis=0)
    lat_last = lax.axis_index("lat") == lax.axis_size("lat") - 1
    zero_level = jnp.zeros((1, rows_n, cols_n), jnp.float32)
    for repeat in range(STEPS):
        masked = ocean * adjoint_state
        zonal_pad = padded(masked, (("lon", 2),), 1, True)
        merid_pad = padded(masked, (("lat", 1),), 1, False)
        east_vals = zonal_pad[:, :, 2:]
        west_vals = zonal_pad[:, :, :-2]
        north_vals = merid_pad[:, 2:, :]
        south_vals = merid_pad[:, :-2, :]
        east_diff = masked - east_vals
        north_diff = masked - north_vals
        updated = adjoint_state - own_east * east_diff + west_weight * (west_vals - masked)
        updated = updated - north_coef * north_diff + south_weight * (south_vals - masked)
        fold_top = north_coef[-1][None, :] * masked[:, -1, :]
        for bit_index in range(lax.axis_size("lon").bit_length() - 1):
            fold_top = from_partner(fold_top, "lon", bit_index)
        mirrored = fold_top[:, ::-1]
        updated = updated.at[:, -1, :].add(jnp.where(lat_last, mirrored, 0.0))
        vertical_term = vertical_coef[None] * (masked[:-1] - masked[1:])
        updated = updated - jnp.concatenate([vertical_term, zero_level], axis=0)
        updated = updated + jnp.concatenate([zero_level, vertical_term], axis=0)
        adjoint_state = updated
    return (adjoint_state, misfit)


def solution(mesh):
    in_specs = (
        P(None, "lat", "lon"),
        P(None, "lat", "lon"),
        P("lat", "lon"),
        P("lat", "lon"),
        P("lat", "lon"),
        P("lat", "lon"),
        P("lat", "lon"),
        P(("lon", "lat"), None),
        P(("lon", "lat"), None),
        P(("lon", "lat"), None),
        P(None, ("lon", "lat")),
        P(None, ("lon", "lat")),
    )
    out_specs = (P(None, "lat", "lon"), P(None, ("lon", "lat")))
    return jax.shard_map(
        on_device, mesh=mesh, in_specs=in_specs, out_specs=out_specs, check_vma=False
    )
```

profile of v0, /device:TPU:7, one launch (start us, length us, event | category | flops | bytes accessed | tf_op | source)
XLA Modules:
  0.0 171.9 jit_solution(3077808672154394988)
XLA Ops:
  1.4 6.2 %copy.77 = f32[25,128,128]{0,2,1:T(8,128)} copy(f32[25,128,128]{2,1,0:T(8,128)} %param.16) | data formatting | bytes 3276800 | tf_op args[0]
  7.6 8.9 %gather_fusion = f32[2048,25]{1,0:T(8,128)S(1)} fusion(f32[25,16384]{0,1:T(8,128)} %bitcast.38, s32[2048]{0:T(1024)S(1)} %broadcast_clamp_fusion.1), kind=kCustom, calls=%fused_computation | custom fusion | bytes 417792 | tf_op jit(solution)/shard_map/gather | solution.py:62
  18.2 1.0 reshape.200
  19.2 6.4 %all-to-all-start = ((f32[32,1,1600]{2,1,0:T(1,128)}), f32[32,1,1600]{2,1,0:T(1,128)S(1)}, u32[]{:S(2)}, u32[]{:S(2)}) async-start(f32[32,1,1600]{2,1,0:T(1,128)} %reshape.200), calls=%async_computation | async-start | bytes 425984 | tf_op jit(solution)/shard_map/all_to_all | solution.py:63
  25.7 1.2 collective-permute-start.1
  27.4 6.1 %all-to-all-done = f32[32,1,1600]{2,1,0:T(1,128)S(1)} async-done(((f32[32,1,1600]{2,1,0:T(1,128)}), f32[32,1,1600]{2,1,0:T(1,128)S(1)}, u32[]{:S(2)}, u32[]{:S(2)}) %all-to-all-start) | async-done | bytes 204832 | tf_op jit(solution)/shard_map/all_to_all | solution.py:63
  34.1 1.2 reduce.12
  36.2 12.6 %scatter_custom_fusion = f32[25,512]{0,1:T(8,128)S(1)} fusion(s32[2048]{0:T(1024)S(1)} %bitcast.49, f32[2048,25]{1,0:T(8,128)S(1)} %copy.80, f32[]{:T(128)} %constant.60.clone.1), kind=kCustom, calls=%fused_computation.52 | custom fusion | flops 51200 | bytes 51204 | tf_op jit(solution)/shard_map/scatter-add | solution.py:68
  48.9 5.5 %gather_fusion.1 = f32[2048,25]{1,0:T(8,128)S(1)} fusion(f32[25,512]{0,1:T(8,128)S(1)} %subtract_multiply_fusion, s32[2048]{0:T(1024)S(1)} %broadcast_clamp_fusion), kind=kCustom, calls=%fused_computation.1 | custom fusion | bytes 417792 | tf_op jit(solution)/shard_map/gather | solution.py:70
  54.9 1.0 reshape.202
  55.8 4.3 %all-to-all-start.1 = ((f32[32,1,1600]{2,1,0:T(1,128)}), f32[32,1,1600]{2,1,0:T(1,128)S(1)}, u32[]{:S(2)}, u32[]{:S(2)}) async-start(f32[32,1,1600]{2,1,0:T(1,128)} %reshape.202), calls=%async_computation.1 | async-start | bytes 425984 | tf_op jit(solution)/shard_map/all_to_all | solution.py:71
  60.2 1.3 collective-permute-start.4
  61.6 1.6 collective-permute-done.4
  63.2 0.8 copy.97
  64.0 3.8 %all-to-all-done.1 = f32[32,1,1600]{2,1,0:T(1,128)S(1)} async-done(((f32[32,1,1600]{2,1,0:T(1,128)}), f32[32,1,1600]{2,1,0:T(1,128)S(1)}, u32[]{:S(2)}, u32[]{:S(2)}) %all-to-all-start.1) | async-done | bytes 204832 | tf_op jit(solution)/shard_map/all_to_all | solution.py:71
  67.8 1.2 reduce.13
  70.0 16.2 %scatter_custom_fusion.1 = f32[25,16384]{0,1:T(8,128)} fusion(s32[2048]{0:T(1024)S(1)} %bitcast.47, f32[2048,25]{1,0:T(8,128)S(1)} %copy.85, f32[]{:T(128)} %constant.60.clone.1), kind=kCustom, calls=%fused_computation.4 | custom fusion | flops 51200 | bytes 1638404 | tf_op jit(solution)/shard_map/scatter-add | solution.py:75
  86.2 6.4 %copy.87 = f32[25,128,128]{2,0,1:T(8,128)} copy(f32[25,128,128]{0,2,1:T(8,128)} %bitcast.37) | data formatting | bytes 3276800 | tf_op jit(solution)/shard_map/reshape | solution.py:77
  92.6 3.1 %broadcast_multiply_fusion.1 = f32[25,128,128]{2,0,1:T(8,128)S(1)} fusion(f32[128,128]{1,0:T(8,128)S(1)} %convert_element_type.3, f32[25,128,128]{2,0,1:T(8,128)} %copy.87, f32[25,128,128]{2,1,0:T(8,128)} %param.17), kind=kLoop, calls=%fused_computation.46 | loop fusion | flops 819200 | bytes 4980736 | tf_op jit(solution)/shard_map/mul | solution.py:88
  95.7 2.7 %fusion.35 = (f32[25,128,1]{2,0,1:T(8,128)}, f32[25,128,1]{2,0,1:T(8,128)}) fusion(f32[25,128,128]{2,0,1:T(8,128)S(1)} %broadcast_multiply_fusion.1), kind=kLoop, calls=%fused_computation.76 | loop fusion | bytes 51200 | tf_op jit(solution)/shard_map/slice | solution.py:25
  98.5 1.1 collective-permute-start.6
  99.6 2.5 %copy.88 = f32[25,128,1]{1,2,0:T(1,128)S(1)} copy(f32[25,128,1]{2,0,1:T(8,128)} %get-tuple-element.42) | data formatting | bytes 25600 | tf_op jit(solution)/shard_map/slice | solution.py:25
  102.4 2.5 %copy.90 = f32[25,128,1]{1,2,0:T(1,128)S(1)} copy(f32[25,128,1]{2,0,1:T(8,128)} %get-tuple-element.43) | data formatting | bytes 25600 | tf_op jit(solution)/shard_map/slice | solution.py:26
  104.9 2.0 %collective-permute-start.2 = (f32[25,128,1]{1,2,0:T(1,128)S(1)}, f32[25,128,1]{1,2,0:T(1,128)S(1)}, u32[]{:S(2)}, u32[]{:S(2)}) collective-permute-start(f32[25,128,1]{1,2,0:T(1,128)S(1)} %copy.90), channel_id=1, source_target_pairs={{0,4},{4,8},{8,12},{12,16},{16,20},{20,24},{24,28},{28,0},{1,5},{5... | collective-permute-start | bytes 38408 | tf_op jit(solution)/shard_map/ppermute | solution.py:29
  106.9 2.8 %collective-permute-start.3 = (f32[25,1,128]{2,0,1:T(8,128)S(1)}, f32[25,1,128]{2,0,1:T(8,128)S(1)}, u32[]{:S(2)}, u32[]{:S(2)}) collective-permute-start(f32[25,1,128]{2,0,1:T(8,128)S(1)} %get-tuple-element.44), channel_id=1, source_target_pairs={{1,0},{2,1},{3,2},{5,4},{6,5},{7,6},{9,8},{10,9},{11,10},{13,12},{... | collective-permute-start | bytes 38408 | tf_op jit(solution)/shard_map/ppermute | solution.py:31
  109.7 1.3 collective-permute-start.5
  111.1 1.5 fusion.27
  112.6 2.9 %copy.89 = f32[25,128,1]{2,0,1:T(8,128)} copy(f32[25,128,1]{1,2,0:T(1,128)S(1)} %collective-permute-done) | data formatting | bytes 25600 | tf_op jit(solution)/shard_map/ppermute | solution.py:31
  115.5 2.9 %copy.91 = f32[25,128,1]{2,0,1:T(8,128)} copy(f32[25,128,1]{1,2,0:T(1,128)S(1)} %collective-permute-done.2) | data formatting | bytes 25600 | tf_op jit(solution)/shard_map/ppermute | solution.py:29
  118.4 3.2 %collective-permute-start.8 = (f32[25,128]{1,0:T(8,128)S(1)}, f32[25,128]{1,0:T(8,128)S(1)}, u32[]{:S(2)}, u32[]{:S(2)}) collective-permute-start(f32[25,128]{1,0:T(8,128)S(1)} %collective-permute-done.7), channel_id=1, source_target_pairs={{0,16},{4,20},{8,24},{12,28},{16,0},{20,4},{24,8},{28,12},{1,17},{... | collective-permute-start | bytes 38408 | tf_op jit(solution)/shard_map/ppermute | solution.py:39
  121.6 6.1 %fusion.16 = f32[25,128,128]{2,0,1:T(8,128)} fusion(f32[25,128,128]{2,0,1:T(8,128)S(1)} %broadcast_multiply_fusion.1, f32[25,1,128]{2,0,1:T(8,128)S(1)} %collective-permute-done.5, f32[25,1,128]{2,0,1:T(8,128)S(1)} %collective-permute-done.3, f32[25,128,1]{2,0,1:T(8,128)} %copy.91, f32[25,128,1]{2,0,1:T(8,128)} %copy.89, ...), kind=kLoop, calls=%fused_computation.25 | loop fusion | flops 6963200 | bytes 6866944 | tf_op jit(solution)/shard_map/add | solution.py:98
  127.8 1.3 fusion.31
  129.2 3.1 %broadcast_multiply_fusion = f32[25,128,128]{2,0,1:T(8,128)S(1)} fusion(f32[128,128]{1,0:T(8,128)S(1)} %convert_element_type.3, f32[24,128,128]{2,0,1:T(8,128)} %fusion.27, f32[25,128,128]{2,0,1:T(8,128)} %fusion.31), kind=kLoop, calls=%fused_computation.45 | loop fusion | flops 1228800 | bytes 4915200 | tf_op jit(solution)/shard_map/mul | solution.py:88
  132.3 2.8 %fusion.33 = (f32[25,128,1]{2,0,1:T(8,128)}, f32[25,128,1]{2,0,1:T(8,128)}) fusion(f32[25,128,128]{2,0,1:T(8,128)S(1)} %broadcast_multiply_fusion), kind=kLoop, calls=%fused_computation.74 | loop fusion | bytes 51200 | tf_op jit(solution)/shard_map/slice | solution.py:25
  135.1 2.5 %copy.92 = f32[25,128,1]{1,2,0:T(1,128)S(1)} copy(f32[25,128,1]{2,0,1:T(8,128)} %get-tuple-element.38) | data formatting | bytes 25600 | tf_op jit(solution)/shard_map/slice | solution.py:25
  137.6 1.7 collective-permute-start.9
  139.3 2.5 %copy.94 = f32[25,128,1]{1,2,0:T(1,128)S(1)} copy(f32[25,128,1]{2,0,1:T(8,128)} %get-tuple-element.39) | data formatting | bytes 25600 | tf_op jit(solution)/shard_map/slice | solution.py:26
  141.7 0.9 collective-permute-start.10
  142.6 4.1 %collective-permute-start.11 = (f32[25,1,128]{2,0,1:T(8,128)S(1)}, f32[25,1,128]{2,0,1:T(8,128)S(1)}, u32[]{:S(2)}, u32[]{:S(2)}) collective-permute-start(f32[25,1,128]{2,0,1:T(8,128)S(1)} %get-tuple-element.40), channel_id=1, source_target_pairs={{1,0},{2,1},{3,2},{5,4},{6,5},{7,6},{9,8},{10,9},{11,10},{13,12},{... | collective-permute-start | bytes 38408 | tf_op jit(solution)/shard_map/ppermute | solution.py:31
  146.8 1.3 collective-permute-start.12
  148.2 1.6 fusion.26
  149.8 2.9 %copy.93 = f32[25,128,1]{2,0,1:T(8,128)} copy(f32[25,128,1]{1,2,0:T(1,128)S(1)} %collective-permute-done.9) | data formatting | bytes 25600 | tf_op jit(solution)/shard_map/ppermute | solution.py:31
  152.7 2.9 %copy.95 = f32[25,128,1]{2,0,1:T(8,128)} copy(f32[25,128,1]{1,2,0:T(1,128)S(1)} %collective-permute-done.10) | data formatting | bytes 25600 | tf_op jit(solution)/shard_map/ppermute | solution.py:29
  155.6 2.7 %collective-permute-start.15 = (f32[25,128]{1,0:T(8,128)S(1)}, f32[25,128]{1,0:T(8,128)S(1)}, u32[]{:S(2)}, u32[]{:S(2)}) collective-permute-start(f32[25,128]{1,0:T(8,128)S(1)} %collective-permute-done.14), channel_id=1, source_target_pairs={{0,16},{4,20},{8,24},{12,28},{16,0},{20,4},{24,8},{28,12},{1,17},{... | collective-permute-start | bytes 38408 | tf_op jit(solution)/shard_map/ppermute | solution.py:39
  158.2 7.0 %fusion.4 = f32[25,128,128]{2,0,1:T(8,128)} fusion(f32[25,128,128]{2,0,1:T(8,128)S(1)} %broadcast_multiply_fusion, f32[25,1,128]{2,0,1:T(8,128)S(1)} %collective-permute-done.12, f32[25,1,128]{2,0,1:T(8,128)S(1)} %collective-permute-done.11, f32[25,128,1]{2,0,1:T(8,128)} %copy.95, f32[25,128,1]{2,0,1:T(8,128)} %copy.93, f32[128,128]{1,0:T(8,128)S(1)} %pad_maximum_fusion.9, ...), kind=kLoop, calls=%fused_computation.9 | loop fusion | flops 7372800 | bytes 6801408 | tf_op jit(solution)/shard_map/add | solution.py:98
  165.3 1.3 fusion.30
  166.6 3.1 %pad_add_fusion = f32[25,128,128]{2,0,1:T(8,128)S(1)} fusion(f32[24,128,128]{2,0,1:T(8,128)} %fusion.26, f32[25,128,128]{2,0,1:T(8,128)} %fusion.30), kind=kLoop, calls=%fused_computation.39 | loop fusion | flops 819200 | bytes 4849664 | tf_op jit(solution)/shard_map/add | solution.py:106
  169.8 2.1 %copy.96 = f32[25,128,128]{2,1,0:T(8,128)} copy(f32[25,128,128]{2,0,1:T(8,128)S(1)} %pad_add_fusion) | data formatting | bytes 3276800
  (78 shorter events, 6.7 us)
Async XLA Ops:
  7.6 9.9 %copy-start.8 = (s32[1,2048]{1,0:T(1,128)S(1)}, s32[1,2048]{1,0:T(1,128)}, u32[]{:S(2)}) copy-start(s32[1,2048]{1,0:T(1,128)} %param.23) | copy-start | bytes 24580
  7.6 9.9 %copy-start.9 = (f32[1,2048]{1,0:T(1,128)S(1)}, f32[1,2048]{1,0:T(1,128)}, u32[]{:S(2)}) copy-start(f32[1,2048]{1,0:T(1,128)} %param.24) | copy-start | bytes 24580
  16.4 9.1 %copy-start.5 = (f32[128,128]{1,0:T(8,128)S(1)}, f32[128,128]{1,0:T(8,128)}, u32[]{:S(2)}) copy-start(f32[128,128]{1,0:T(8,128)} %param.19) | copy-start | bytes 196612
  16.4 9.1 %copy-start.6 = (f32[128,128]{1,0:T(8,128)S(1)}, f32[128,128]{1,0:T(8,128)}, u32[]{:S(2)}) copy-start(f32[128,128]{1,0:T(8,128)} %param.21) | copy-start | bytes 196612
  16.5 10.5 %copy-start.7 = (s32[1,2048]{1,0:T(1,128)S(1)}, s32[1,2048]{1,0:T(1,128)}, u32[]{:S(2)}) copy-start(s32[1,2048]{1,0:T(1,128)} %param.25) | copy-start | bytes 24580
  16.5 10.5 %copy-start.2 = (f32[25,512]{1,0:T(8,128)S(1)}, f32[25,512]{1,0:T(8,128)}, u32[]{:S(2)}) copy-start(f32[25,512]{1,0:T(8,128)} %param.26) | copy-start | bytes 153604
  16.5 10.6 %copy-start.3 = (f32[25,512]{1,0:T(8,128)S(1)}, f32[25,512]{1,0:T(8,128)}, u32[]{:S(2)}) copy-start(f32[25,512]{1,0:T(8,128)} %param.27) | copy-start | bytes 153604
  19.2 14.3 %all-to-all-start = ((f32[32,1,1600]{2,1,0:T(1,128)}), f32[32,1,1600]{2,1,0:T(1,128)S(1)}, u32[]{:S(2)}, u32[]{:S(2)}) async-start(f32[32,1,1600]{2,1,0:T(1,128)} %reshape.200), calls=%async_computation | async-start | bytes 425984 | tf_op jit(solution)/shard_map/all_to_all | solution.py:63
  25.7 35.8 %collective-permute-start.1 = (f32[128,1]{1,0:T(8,128)S(1)}, f32[128,1]{1,0:T(8,128)S(1)}, u32[]{:S(2)}, u32[]{:S(2)}) collective-permute-start(f32[128,1]{1,0:T(8,128)S(1)} %slice.159), channel_id=1, source_target_pairs={{0,4},{4,8},{8,12},{12,16},{16,20},{20,24},{24,28},{28,0},{1,5},{5... | collective-permute-start | bytes 1544 | tf_op jit(solution)/shard_map/ppermute | solution.py:12
  54.4 5.8 %copy-start = (f32[128,128]{1,0:T(8,128)S(1)}, f32[128,128]{1,0:T(8,128)}, u32[]{:S(2)}) copy-start(f32[128,128]{1,0:T(8,128)} %param.20) | copy-start | bytes 196612
  54.4 7.1 %copy-start.4 = (s32[128,128]{1,0:T(8,128)S(1)}, s32[128,128]{1,0:T(8,128)}, u32[]{:S(2)}) copy-start(s32[128,128]{1,0:T(8,128)} %param.18) | copy-start | bytes 196612
  55.8 12.0 %all-to-all-start.1 = ((f32[32,1,1600]{2,1,0:T(1,128)}), f32[32,1,1600]{2,1,0:T(1,128)S(1)}, u32[]{:S(2)}, u32[]{:S(2)}) async-start(f32[32,1,1600]{2,1,0:T(1,128)} %reshape.202), calls=%async_computation.1 | async-start | bytes 425984 | tf_op jit(solution)/shard_map/all_to_all | solution.py:71
  60.2 3.0 %collective-permute-start.4 = (f32[1,128]{1,0:T(1,128)S(1)}, f32[1,128]{1,0:T(1,128)S(1)}, u32[]{:S(2)}, u32[]{:S(2)}) collective-permute-start(f32[1,128]{1,0:T(1,128)S(1)} %get-tuple-element.49), channel_id=1, source_target_pairs={{0,1},{1,2},{2,3},{4,5},{5,6},{6,7},{8,9},{9,10},{10,11},{12,13},{... | collective-permute-start | bytes 1544 | tf_op jit(solution)/shard_map/ppermute | solution.py:18
  98.5 12.5 %collective-permute-start.6 = (f32[25,128]{1,0:T(8,128)S(1)}, f32[25,128]{1,0:T(8,128)S(1)}, u32[]{:S(2)}, u32[]{:S(2)}) collective-permute-start(f32[25,128]{1,0:T(8,128)S(1)} %bitcast_multiply_fusion.1), channel_id=1, source_target_pairs={{0,4},{4,0},{8,12},{12,8},{16,20},{20,16},{24,28},{28,24},{1,5},{5... | collective-permute-start | bytes 38408 | tf_op jit(solution)/shard_map/ppermute | solution.py:39
  99.6 11.5 %copy-start.1 = (f32[128,128]{1,0:T(8,128)S(1)}, f32[128,128]{1,0:T(8,128)}, u32[]{:S(2)}) copy-start(f32[128,128]{1,0:T(8,128)} %param.22) | copy-start | bytes 196612
  102.1 10.5 %collective-permute-start = (f32[25,128,1]{1,2,0:T(1,128)S(1)}, f32[25,128,1]{1,2,0:T(1,128)S(1)}, u32[]{:S(2)}, u32[]{:S(2)}) collective-permute-start(f32[25,128,1]{1,2,0:T(1,128)S(1)} %copy.88), channel_id=1, source_target_pairs={{4,0},{8,4},{12,8},{16,12},{20,16},{24,20},{28,24},{0,28},{5,1},{9... | collective-permute-start | bytes 38408 | tf_op jit(solution)/shard_map/ppermute | solution.py:31
  104.9 10.6 %collective-permute-start.2 = (f32[25,128,1]{1,2,0:T(1,128)S(1)}, f32[25,128,1]{1,2,0:T(1,128)S(1)}, u32[]{:S(2)}, u32[]{:S(2)}) collective-permute-start(f32[25,128,1]{1,2,0:T(1,128)S(1)} %copy.90), channel_id=1, source_target_pairs={{0,4},{4,8},{8,12},{12,16},{16,20},{20,24},{24,28},{28,0},{1,5},{5... | collective-permute-start | bytes 38408 | tf_op jit(solution)/shard_map/ppermute | solution.py:29
  106.9 14.7 %collective-permute-start.3 = (f32[25,1,128]{2,0,1:T(8,128)S(1)}, f32[25,1,128]{2,0,1:T(8,128)S(1)}, u32[]{:S(2)}, u32[]{:S(2)}) collective-permute-start(f32[25,1,128]{2,0,1:T(8,128)S(1)} %get-tuple-element.44), channel_id=1, source_target_pairs={{1,0},{2,1},{3,2},{5,4},{6,5},{7,6},{9,8},{10,9},{11,10},{13,12},{... | collective-permute-start | bytes 38408 | tf_op jit(solution)/shard_map/ppermute | solution.py:31
  109.7 11.9 %collective-permute-start.5 = (f32[25,1,128]{2,0,1:T(8,128)S(1)}, f32[25,1,128]{2,0,1:T(8,128)S(1)}, u32[]{:S(2)}, u32[]{:S(2)}) collective-permute-start(f32[25,1,128]{2,0,1:T(8,128)S(1)} %get-tuple-element.45), channel_id=1, source_target_pairs={{0,1},{1,2},{2,3},{4,5},{5,6},{6,7},{8,9},{9,10},{10,11},{12,13},{... | collective-permute-start | bytes 38408 | tf_op jit(solution)/shard_map/ppermute | solution.py:29
  111.0 7.4 %collective-permute-start.7 = (f32[25,128]{1,0:T(8,128)S(1)}, f32[25,128]{1,0:T(8,128)S(1)}, u32[]{:S(2)}, u32[]{:S(2)}) collective-permute-start(f32[25,128]{1,0:T(8,128)S(1)} %collective-permute-done.6), channel_id=1, source_target_pairs={{0,8},{4,12},{8,0},{12,4},{16,24},{20,28},{24,16},{28,20},{1,9},{5... | collective-permute-start | bytes 38408 | tf_op jit(solution)/shard_map/ppermute | solution.py:39
  118.4 9.4 %collective-permute-start.8 = (f32[25,128]{1,0:T(8,128)S(1)}, f32[25,128]{1,0:T(8,128)S(1)}, u32[]{:S(2)}, u32[]{:S(2)}) collective-permute-start(f32[25,128]{1,0:T(8,128)S(1)} %collective-permute-done.7), channel_id=1, source_target_pairs={{0,16},{4,20},{8,24},{12,28},{16,0},{20,4},{24,8},{28,12},{1,17},{... | collective-permute-start | bytes 38408 | tf_op jit(solution)/shard_map/ppermute | solution.py:39
  135.1 13.0 %collective-permute-start.13 = (f32[25,128]{1,0:T(8,128)S(1)}, f32[25,128]{1,0:T(8,128)S(1)}, u32[]{:S(2)}, u32[]{:S(2)}) collective-permute-start(f32[25,128]{1,0:T(8,128)S(1)} %bitcast_multiply_fusion), channel_id=1, source_target_pairs={{0,4},{4,0},{8,12},{12,8},{16,20},{20,16},{24,28},{28,24},{1,5},{5... | collective-permute-start | bytes 38408 | tf_op jit(solution)/shard_map/ppermute | solution.py:39
  137.6 12.2 %collective-permute-start.9 = (f32[25,128,1]{1,2,0:T(1,128)S(1)}, f32[25,128,1]{1,2,0:T(1,128)S(1)}, u32[]{:S(2)}, u32[]{:S(2)}) collective-permute-start(f32[25,128,1]{1,2,0:T(1,128)S(1)} %copy.92), channel_id=1, source_target_pairs={{4,0},{8,4},{12,8},{16,12},{20,16},{24,20},{28,24},{0,28},{5,1},{9... | collective-permute-start | bytes 38408 | tf_op jit(solution)/shard_map/ppermute | solution.py:31
  141.7 10.9 %collective-permute-start.10 = (f32[25,128,1]{1,2,0:T(1,128)S(1)}, f32[25,128,1]{1,2,0:T(1,128)S(1)}, u32[]{:S(2)}, u32[]{:S(2)}) collective-permute-start(f32[25,128,1]{1,2,0:T(1,128)S(1)} %copy.94), channel_id=1, source_target_pairs={{0,4},{4,8},{8,12},{12,16},{16,20},{20,24},{24,28},{28,0},{1,5},{5... | collective-permute-start | bytes 38408 | tf_op jit(solution)/shard_map/ppermute | solution.py:29
  142.6 15.6 %collective-permute-start.11 = (f32[25,1,128]{2,0,1:T(8,128)S(1)}, f32[25,1,128]{2,0,1:T(8,128)S(1)}, u32[]{:S(2)}, u32[]{:S(2)}) collective-permute-start(f32[25,1,128]{2,0,1:T(8,128)S(1)} %get-tuple-element.40), channel_id=1, source_target_pairs={{1,0},{2,1},{3,2},{5,4},{6,5},{7,6},{9,8},{10,9},{11,10},{13,12},{... | collective-permute-start | bytes 38408 | tf_op jit(solution)/shard_map/ppermute | solution.py:31
  146.8 11.4 %collective-permute-start.12 = (f32[25,1,128]{2,0,1:T(8,128)S(1)}, f32[25,1,128]{2,0,1:T(8,128)S(1)}, u32[]{:S(2)}, u32[]{:S(2)}) collective-permute-start(f32[25,1,128]{2,0,1:T(8,128)S(1)} %get-tuple-element.41), channel_id=1, source_target_pairs={{0,1},{1,2},{2,3},{4,5},{5,6},{6,7},{8,9},{9,10},{10,11},{12,13},{... | collective-permute-start | bytes 38408 | tf_op jit(solution)/shard_map/ppermute | solution.py:29
  148.1 7.5 %collective-permute-start.14 = (f32[25,128]{1,0:T(8,128)S(1)}, f32[25,128]{1,0:T(8,128)S(1)}, u32[]{:S(2)}, u32[]{:S(2)}) collective-permute-start(f32[25,128]{1,0:T(8,128)S(1)} %collective-permute-done.13), channel_id=1, source_target_pairs={{0,8},{4,12},{8,0},{12,4},{16,24},{20,28},{24,16},{28,20},{1,9},{5... | collective-permute-start | bytes 38408 | tf_op jit(solution)/shard_map/ppermute | solution.py:39
  155.6 9.6 %collective-permute-start.15 = (f32[25,128]{1,0:T(8,128)S(1)}, f32[25,128]{1,0:T(8,128)S(1)}, u32[]{:S(2)}, u32[]{:S(2)}) collective-permute-start(f32[25,128]{1,0:T(8,128)S(1)} %collective-permute-done.14), channel_id=1, source_target_pairs={{0,16},{4,20},{8,24},{12,28},{16,0},{20,4},{24,8},{28,12},{1,17},{... | collective-permute-start | bytes 38408 | tf_op jit(solution)/shard_map/ppermute | solution.py:39
where the time goes:
time: 175 us; the launch traced here: 172 us
  local copies, waits for them, and re-layouts  63.1 us (36%)
  other arithmetic  61.3 us (35%)
  starting transfers between devices  34.9 us (20%)
  waiting for transfers between devices  11.6 us (7%)
    scatter-add x1, other arithmetic, on_device(): forcing = jnp.zeros((levels_n, rows_n * cols_n), jnp.float32).at[:, cell_...  16.2 us
    add x2, other arithmetic, on_device(): updated - north_coef * north_diff + south_weight * (south_vals - masked)  13.1 us
    scatter-add x1, other arithmetic, on_device(): jnp.zeros(obs_value.shape, jnp.float32).at[:, target_index].add(incoming)  12.6 us
    unnamed x29, local copies, waits for them, and re-layouts  11.7 us
    slice x6, local copies, waits for them, and re-layouts, padded(): head = lax.slice_in_dim(cells, 0, width, axis=dim)  10.5 us
    gather x2, local copies, waits for them, and re-layouts, on_device(): partial_vals = flat_state[:, cell_index] * weights[None, :]  9.25 us
    ppermute x4, starting transfers between devices, padded(): lax.ppermute(head, axis, [((i + 1) % count, i) for i in range(ends)])  8.91 us
    ppermute x6, starting transfers between devices, from_partner(): lax.ppermute(value, axis, [(i, i ^ 1 << bit) for i in range(lax.axis_size...  7.16 us
  transfers between devices with their start and end apart: 18, of which 3 were waited for; matrix products, arithmetic and copies ran while one was open for 36% of the time, Pallas kernels for 0%

commit v1 on v0

--- a/solution.py
+++ b/solution.py
@@ -1,9 +1,191 @@
+import functools
+
 import jax
 import jax.numpy as jnp
 from jax import lax
+from jax.experimental import pallas as pl
+from jax.experimental.pallas import tpu as pltpu
 from jax.sharding import PartitionSpec as P
 
 STEPS = 2
+LANES = 128
+GROUP = 32
+VMEM_BYTES = 48 * 1024 * 1024
+BOTH = ("lon", "lat")
+
+
+def pieces(value):
+    high = value.astype(jnp.bfloat16)
+    rest = value - high.astype(jnp.float32)
+    middle = rest.astype(jnp.bfloat16)
+    low = (rest - middle.astype(jnp.float32)).astype(jnp.bfloat16)
+    return high, middle, low
+
+
+def log2(size):
+    assert size & (size - 1) == 0
+    return size.bit_length() - 1
+
+
+def cell_parts(cell, rows_n, cols_n):
+    cell = jnp.maximum(cell, 0)
+    row = jnp.right_shift(cell, log2(cols_n))
+    group = jnp.right_shift(row, log2(GROUP))
+    place = jnp.bitwise_and(cell, cols_n - 1) + group * cols_n
+    return place, jnp.bitwise_and(row, GROUP - 1)
+
+
+def one_hot(index, size):
+    rows = lax.broadcasted_iota(jnp.int32, (size, index.shape[1]), 0)
+    return jnp.where(rows == index, 1.0, 0.0).astype(jnp.bfloat16)
+
+
+def packed_pair(values):
+    half = values.shape[0] // 2
+    first = lax.broadcasted_iota(jnp.int32, (half, LANES), 1) < LANES // 2
+    top, bottom = values[:half], values[half:]
+    left = jnp.where(first, top, pltpu.roll(bottom, LANES // 2, 1))
+    right = jnp.where(first, pltpu.roll(top, LANES // 2, 1), bottom)
+    return left, right
+
+
+def unpacked_pair(left, right):
+    half = left.shape[0]
+    first = lax.broadcasted_iota(jnp.int32, (half, LANES), 1) < LANES // 2
+    top = jnp.where(first, left, pltpu.roll(right, LANES // 2, 1))
+    bottom = jnp.where(first, pltpu.roll(left, LANES // 2, 1), right)
+    return jnp.concatenate([top, bottom], axis=0)
+
+
+def padded_levels(values, levels):
+    return jnp.concatenate(
+        [values, jnp.zeros((levels - values.shape[0], values.shape[1]), values.dtype)], axis=0
+    )
+
+
+def gather_kernel(cell_ref, weight_ref, state_ref, out_ref, field_ref):
+    levels_n, rows_n, cols_n = state_ref.shape
+    groups = rows_n // GROUP
+    width = groups * cols_n
+    for group in range(groups):
+        block = state_ref[:, group * GROUP : (group + 1) * GROUP, :]
+        for part, piece in enumerate(pieces(block.reshape(levels_n * GROUP, cols_n))):
+            at = part * width + group * cols_n
+            field_ref[:, at : at + cols_n] = piece
+    tile = 2 * LANES
+
+    def body(step, carry):
+        at = pl.ds(pl.multiple_of(step * tile, tile), tile)
+        cell = cell_ref[:, at]
+        weight = jnp.where(cell >= 0, weight_ref[:, at], 0.0)
+        place, row = cell_parts(cell, rows_n, cols_n)
+        hot = one_hot(place, width)
+        found = jnp.dot(
+            field_ref[...],
+            jnp.concatenate([hot, hot, hot], axis=0),
+            preferred_element_type=jnp.float32,
+        ).reshape(levels_n, GROUP, tile)
+        mine = lax.broadcasted_iota(jnp.int32, (GROUP, tile), 0) == row
+        values = jnp.sum(jnp.where(mine[None], found, 0.0), axis=1) * weight
+        values = padded_levels(values, 2 * out_ref.shape[1])
+        for pair in range(tile // LANES):
+            left, right = packed_pair(values[:, pair * LANES : (pair + 1) * LANES])
+            out_ref[step * (2 * tile // LANES) + 2 * pair] = left
+            out_ref[step * (2 * tile // LANES) + 2 * pair + 1] = right
+        return carry
+
+    lax.fori_loop(0, cell_ref.shape[1] // tile, body, 0)
+
+
+def observe_kernel(arrived_ref, target_ref, value_ref, invvar_ref, misfit_ref, out_ref, hot_ref, in_ref):
+    devices, half, _ = arrived_ref.shape
+    levels_n, obs_n = value_ref.shape
+    levels = 2 * half
+
+    def load(pair, carry):
+        at = pl.ds(pl.multiple_of(pair * LANES, LANES), LANES)
+        values = unpacked_pair(arrived_ref[2 * pair], arrived_ref[2 * pair + 1])
+        for part, piece in enumerate(pieces(values)):
+            in_ref[part * levels : (part + 1) * levels, at] = piece
+        hot_ref[:, at] = one_hot(target_ref[:, at], obs_n)
+        return carry
+
+    lax.fori_loop(0, devices // 2, load, 0)
+    sums = lax.dot_general(
+        in_ref[...], hot_ref[...], (((1,), (1,)), ((), ())), preferred_element_type=jnp.float32
+    )
+    interp = sums[:levels] + sums[levels : 2 * levels] + sums[2 * levels :]
+    misfit = invvar_ref[...] * (interp[:levels_n] - value_ref[...])
+    misfit_ref[...] = misfit
+    back = jnp.concatenate(pieces(padded_levels(misfit, levels)), axis=0)
+    tile = 4 * LANES
+
+    def store(step, carry):
+        at = pl.ds(pl.multiple_of(step * tile, tile), tile)
+        found = jnp.dot(back, hot_ref[:, at], preferred_element_type=jnp.float32)
+        values = found[:levels] + found[levels : 2 * levels] + found[2 * levels :]
+        for pair in range(tile // LANES):
+            left, right = packed_pair(values[:, pair * LANES : (pair + 1) * LANES])
+            out_ref[step * (2 * tile // LANES) + 2 * pair] = left
+            out_ref[step * (2 * tile // LANES) + 2 * pair + 1] = right
+        return carry
+
+    lax.fori_loop(0, target_ref.shape[1] // tile, store, 0)
+
+
+def scatter_kernel(returned_ref, cell_ref, weight_ref, adjoint_ref, out_ref, rows_ref, hot_ref, sum_ref):
+    levels_n, rows_n, cols_n = out_ref.shape
+    groups = rows_n // GROUP
+    width = groups * cols_n
+    tile = hot_ref.shape[1] // 3
+
+    sum_ref[...] = jnp.zeros_like(sum_ref)
+
+    def body(step, carry):
+        at = pl.ds(pl.multiple_of(step * tile, tile), tile)
+        cell = cell_ref[:, at]
+        weight = jnp.where(cell >= 0, weight_ref[:, at], 0.0)
+        place, row = cell_parts(cell, rows_n, cols_n)
+        base = step * (2 * tile // LANES)
+        values = jnp.concatenate(
+            [
+                unpacked_pair(returned_ref[base + 2 * pair], returned_ref[base + 2 * pair + 1])
+                for pair in range(tile // LANES)
+            ],
+            axis=1,
+        )
+        values = pieces(values * weight)
+        hot = one_hot(place, width)
+        mine = one_hot(row, GROUP)
+        for part in range(3):
+            hot_ref[:, part * tile : (part + 1) * tile] = hot
+            for level in range(levels_n):
+                rows_ref[level * GROUP : (level + 1) * GROUP, part * tile : (part + 1) * tile] = (
+                    mine * values[part][level : level + 1, :]
+                )
+        sum_ref[...] += lax.dot_general(
+            rows_ref[...], hot_ref[...], (((1,), (1,)), ((), ())), preferred_element_type=jnp.float32
+        )
+        return carry
+
+    lax.fori_loop(0, cell_ref.shape[1] // tile, body, 0)
+    for group in range(groups):
+        at = slice(group * GROUP, (group + 1) * GROUP)
+        forcing = sum_ref[:, group * cols_n : (group + 1) * cols_n]
+        out_ref[:, at, :] = adjoint_ref[:, at, :] + forcing.reshape(levels_n, GROUP, cols_n)
+
+
+def kernel_call(body, out_shape, scratch):
+    return pl.pallas_call(
+        body,
+        out_shape=out_shape,
+        scratch_shapes=scratch,
+        compiler_params=pltpu.CompilerParams(vmem_limit_bytes=VMEM_BYTES),
+    )
+
+
+def f32(*shape):
+    return jax.ShapeDtypeStruct(shape, jnp.float32)
 
 
 def from_behind(value, axis, steps):
@@ -54,27 +236,34 @@
     obs_invvar,
 ):
     levels_n, rows_n, cols_n = state.shape
-    flat_state = state.reshape(levels_n, rows_n * cols_n)
-    slot_row = slot_cell[0]
-    live_slot = slot_row >= 0
-    cell_index = jnp.where(live_slot, slot_row, 0)
-    weights = jnp.where(live_slot, slot_weight[0], 0.0)
-    partial_vals = flat_state[:, cell_index] * weights[None, :]
-    arrived = lax.all_to_all(partial_vals, ("lon", "lat"), split_axis=1, concat_axis=1, tiled=True)
-    target_row = arrive_obs[0]
-    live_target = target_row >= 0
-    target_index = jnp.where(live_target, target_row, 0)
-    incoming = jnp.where(live_target[None, :], arrived, 0.0)
-    interp = jnp.zeros(obs_value.shape, jnp.float32).at[:, target_index].add(incoming)
-    misfit = obs_invvar * (interp - obs_value)
-    outgoing = jnp.where(live_target[None, :], misfit[:, target_index], 0.0)
-    returned = lax.all_to_all(outgoing, ("lon", "lat"), split_axis=1, concat_axis=1, tiled=True)
-    forcing = (
-        jnp.zeros((levels_n, rows_n * cols_n), jnp.float32)
-        .at[:, cell_index]
-        .add(returned * weights[None, :])
-    )
-    adjoint_state = adjoint_in + forcing.reshape(state.shape)
+    devices = lax.axis_size(BOTH)
+    slots = slot_cell.shape[1]
+    obs_n = obs_value.shape[1]
+    assert 2 * (slots // devices) == LANES
+    half = (levels_n + 15) // 16 * 8
+    width = rows_n // GROUP * cols_n
+    bf16 = jnp.bfloat16
+
+    partial_vals = kernel_call(
+        gather_kernel, f32(devices, half, LANES), [pltpu.VMEM((levels_n * GROUP, 3 * width), bf16)]
+    )(slot_cell, slot_weight, state)
+    arrived = lax.all_to_all(partial_vals, BOTH, split_axis=0, concat_axis=0, tiled=True)
+    misfit, outgoing = kernel_call(
+        observe_kernel,
+        (f32(levels_n, obs_n), f32(devices, half, LANES)),
+        [pltpu.VMEM((obs_n, slots), bf16), pltpu.VMEM((6 * half, slots), bf16)],
+    )(arrived, arrive_obs, obs_value, obs_invvar)
+    returned = lax.all_to_all(outgoing, BOTH, split_axis=0, concat_axis=0, tiled=True)
+    tile = 4 * LANES
+    adjoint_state = kernel_call(
+        scatter_kernel,
+        f32(levels_n, rows_n, cols_n),
+        [
+            pltpu.VMEM((levels_n * GROUP, 3 * tile), bf16),
+            pltpu.VMEM((width, 3 * tile), bf16),
+            pltpu.VMEM((levels_n * GROUP, width), jnp.float32),
+        ],
+    )(returned, slot_cell, slot_weight, adjoint_in)
     ocean = land_mask.astype(jnp.float32)
     east_weight = east_coef - 0.5 * zonal_flow
     own_east = east_coef + 0.5 * zonal_flow

time: 175 us -> 127 us (0.73)
  other arithmetic: 61.3 us -> 21 us
  local copies, waits for them, and re-layouts: 63.1 us -> 34.4 us
  Pallas kernels: 0 us -> 18.1 us
  blocking collectives: 0 us -> 14.9 us
  waiting for transfers between devices: 11.6 us -> 3.31 us
  starting transfers between devices: 34.9 us -> 32.6 us
    scatter-add x4 -> x0, other arithmetic: 31.5 us -> none  [the longest x1 16.2 us: on_device(): forcing = jnp.zeros((levels_n, rows_n * cols_n), jnp.float32).at[:, cell_...]
    pallas_call x0 -> x3, Pallas kernels: none -> 18.1 us  [the longest x1 7.75 us: on_device(): kernel_call(gather_kernel, f32(devices, half, LANES), [pltpu.VMEM((levels...]
    gather x4 -> x0, local copies, waits for them, and re-layouts: 15.1 us -> none  [the longest x2 9.25 us: on_device(): partial_vals = flat_state[:, cell_index] * weights[None, :]]
    all_to_all x0 -> x1, blocking collectives: none -> 14.9 us  [on_device(): lax.all_to_all(partial_vals, BOTH, split_axis=0, concat_axis=0, tiled=True)]
    all_to_all x2 -> x1, waiting for transfers between devices: 9.94 us -> 1.97 us  [on_device(): lax.all_to_all(outgoing, BOTH, split_axis=0, concat_axis=0, tiled=True)]
    unnamed x29 -> x49, local copies, waits for them, and re-layouts: 11.7 us -> 5.21 us
    reshape x1 -> x0, local copies, waits for them, and re-layouts: 6.38 us -> none  [on_device(): adjoint_state = adjoint_in + forcing.reshape(state.shape)]
    all_to_all x2 -> x1, starting transfers between devices: 10.7 us -> 4.39 us  [on_device(): lax.all_to_all(outgoing, BOTH, split_axis=0, concat_axis=0, tiled=True)]
  transfers between devices with their start and end apart: 18 -> 17, of which waited for: 3 -> 2; matrix products, arithmetic and copies ran while one was open for 36% -> 30% of each run, Pallas kernels for 0% -> 0%
where the time goes in v1:
time: 127 us; the launch traced here: 125 us
  local copies, waits for them, and re-layouts  34.4 us (27%)
  starting transfers between devices  32.6 us (26%)
  other arithmetic  21 us (17%)
  Pallas kernels  18.1 us (14%)
  blocking collectives  14.9 us (12%)
  waiting for transfers between devices  3.31 us (3%)
    all_to_all x1, blocking collectives, on_device(): lax.all_to_all(partial_vals, BOTH, split_axis=0, concat_axis=0, tiled=True)  14.9 us
    ppermute x4, starting transfers between devices, padded(): lax.ppermute(head, axis, [((i + 1) % count, i) for i in range(ends)])  10.9 us
    slice x6, local copies, waits for them, and re-layouts, padded(): head = lax.slice_in_dim(cells, 0, width, axis=dim)  10.4 us
    ppermute x6, starting transfers between devices, from_partner(): lax.ppermute(value, axis, [(i, i ^ 1 << bit) for i in range(lax.axis_size...  8.9 us
    pallas_call x1, Pallas kernels, on_device(): kernel_call(gather_kernel, f32(devices, half, LANES), [pltpu.VMEM((levels...  7.75 us
    add x2, other arithmetic, on_device(): updated - north_coef * north_diff + south_weight * (south_vals - masked)  7.21 us
    pallas_call x1, Pallas kernels, on_device(): kernel_call(scatter_kernel, f32(levels_n, rows_n, cols_n), [pltpu.VMEM((l...  6.25 us
    ppermute x4, starting transfers between devices, padded(): lax.ppermute(tail, axis, [(i, (i + 1) % count) for i in range(ends)])  5.81 us
  transfers between devices with their start and end apart: 17, of which 2 were waited for; matrix products, arithmetic and copies ran while one was open for 30% of the time, Pallas kernels for 0%

profile of v1, /device:TPU:7, one launch (start us, length us, event | category | flops | bytes accessed | tf_op | source)
XLA Modules:
  0.0 125.2 jit_solution(4050029422504078829)
XLA Ops:
  0.6 1.4 %copy-done.1 = f32[25,128,128]{2,1,0:T(8,128)S(1)} copy-done((f32[25,128,128]{2,1,0:T(8,128)S(1)}, f32[25,128,128]{2,1,0:T(8,128)}, u32[]{:S(2)}) %copy-start.1) | copy-done | bytes 1638424
  2.1 0.7 copy-done.4
  2.8 0.7 copy-done.6
  3.5 7.8 %shard_map.131 = f32[32,16,128]{2,1,0:T(8,128)S(1)} custom-call(s32[1,2048]{1,0:T(1,128)S(1)} %copy-done.4, f32[1,2048]{1,0:T(1,128)S(1)} %copy-done.6, f32[25,128,128]{2,1,0:T(8,128)S(1)} %copy-done.1), custom_call_target="tpu_custom_call" | custom-call | tf_op jit(solution)/shard_map/pallas_call | solution.py:247
  11.3 14.9 %all_to_all.10.arrived_ref = f32[32,16,128]{2,1,0:T(8,128)S(1)} all-to-all(f32[32,16,128]{2,1,0:T(8,128)S(1)} %shard_map.131), channel_id=1, replica_groups=mesh['lon'=8,'lat'=4] {'lon','lat'}, dimensions={0} | all-to-all | bytes 524288 | tf_op jit(solution)/shard_map/all_to_all | solution.py:250
  26.2 4.1 %shard_map.132 = (f32[25,512]{1,0:T(8,128)}, f32[32,16,128]{2,1,0:T(8,128)}) custom-call(f32[32,16,128]{2,1,0:T(8,128)S(1)} %all_to_all.10.arrived_ref, s32[1,2048]{1,0:T(1,128)S(1)} %copy-done.8, f32[25,512]{1,0:T(8,128)S(1)} %copy-done.2, f32[25,512]{1,0:T(8,128)S(1)} %copy-done.3), custom_call_target="tpu_custom_call" | custom-call | tf_op jit(solution)/shard_map/pallas_call | solution.py:251
  30.3 4.4 %all-to-all-start.1 = ((f32[32,16,128]{2,1,0:T(8,128)}), f32[32,16,128]{2,1,0:T(8,128)S(1)}, u32[]{:S(2)}, u32[]{:S(2)}) async-start(f32[32,16,128]{2,1,0:T(8,128)} %get-tuple-element.28), calls=%async_computation.1 | async-start | bytes 524288 | tf_op jit(solution)/shard_map/all_to_all | solution.py:256
  34.7 0.6 multiply_add_fusion
  35.4 1.3 %collective-permute-start.1 = (f32[128,1]{1,0:T(8,128)S(1)}, f32[128,1]{1,0:T(8,128)S(1)}, u32[]{:S(2)}, u32[]{:S(2)}) collective-permute-start(f32[128,1]{1,0:T(8,128)S(1)} %slice.155), channel_id=1, source_target_pairs={{0,4},{4,8},{8,12},{12,16},{16,20},{20,24},{24,28},{28,0},{1,5},{5... | collective-permute-start | bytes 1544 | tf_op jit(solution)/shard_map/ppermute | solution.py:194
  37.2 1.3 %collective-permute-start.4 = (f32[1,128]{1,0:T(1,128)S(1)}, f32[1,128]{1,0:T(1,128)S(1)}, u32[]{:S(2)}, u32[]{:S(2)}) collective-permute-start(f32[1,128]{1,0:T(1,128)S(1)} %get-tuple-element.41), channel_id=1, source_target_pairs={{0,1},{1,2},{2,3},{4,5},{5,6},{6,7},{8,9},{9,10},{10,11},{12,13},{... | collective-permute-start | bytes 1544 | tf_op jit(solution)/shard_map/ppermute | solution.py:200
  38.5 0.6 convert_element_type.3
  39.1 1.3 %collective-permute-done.1 = f32[128,1]{1,0:T(8,128)S(1)} collective-permute-done((f32[128,1]{1,0:T(8,128)S(1)}, f32[128,1]{1,0:T(8,128)S(1)}, u32[]{:S(2)}, u32[]{:S(2)}) %collective-permute-start.1) | collective-permute-done | bytes 544 | tf_op jit(solution)/shard_map/ppermute | solution.py:194
  40.4 0.7 pad_maximum_fusion.8
  41.1 0.6 pad_maximum_fusion.9
  41.8 2.0 %all-to-all-done.1.returned_ref = f32[32,16,128]{2,1,0:T(8,128)S(1)} async-done(((f32[32,16,128]{2,1,0:T(8,128)}), f32[32,16,128]{2,1,0:T(8,128)S(1)}, u32[]{:S(2)}, u32[]{:S(2)}) %all-to-all-start.1) | async-done | bytes 262176 | tf_op jit(solution)/shard_map/all_to_all | solution.py:256
  43.8 6.3 %shard_map.133 = f32[25,128,128]{2,1,0:T(8,128)S(1)} custom-call(f32[32,16,128]{2,1,0:T(8,128)S(1)} %all-to-all-done.1.returned_ref, s32[1,2048]{1,0:T(1,128)S(1)} %copy-done.5, f32[1,2048]{1,0:T(1,128)S(1)} %copy-done.7, f32[25,128,128]{2,1,0:T(8,128)S(1)} %copy-done), custom_call_target="tpu_custom_call" | custom-call | tf_op jit(solution)/shard_map/pallas_call | solution.py:258
  50.8 1.3 %collective-permute-start.5 = (f32[25,1,128]{2,1,0:T(1,128)S(1)}, f32[25,1,128]{2,1,0:T(1,128)}, u32[]{:S(2)}, u32[]{:S(2)}) collective-permute-start(f32[25,1,128]{2,1,0:T(1,128)S(1)} %get-tuple-element.37), channel_id=1, source_target_pairs={{0,1},{1,2},{2,3},{4,5},{5,6},{6,7},{8,9},{9,10},{10,11},{12,13},{... | collective-permute-start | bytes 38408 | tf_op jit(solution)/shard_map/ppermute | solution.py:211
  52.1 3.2 %collective-permute-start.6 = (f32[25,128]{1,0:T(8,128)S(1)}, f32[25,128]{1,0:T(8,128)}, u32[]{:S(2)}, u32[]{:S(2)}) collective-permute-start(f32[25,128]{1,0:T(8,128)S(1)} %bitcast_multiply_fusion), channel_id=1, source_target_pairs={{0,4},{4,0},{8,12},{12,8},{16,20},{20,16},{24,28},{28,24},{1,5},{5... | collective-permute-start | bytes 38408 | tf_op jit(solution)/shard_map/ppermute | solution.py:221
  55.3 2.3 %fusion.28 = (f32[25,128,1]{2,1,0:T(8,128)}, f32[25,128,1]{2,1,0:T(8,128)}) fusion(f32[25,128,128]{2,1,0:T(8,128)S(1)} %broadcast_multiply_fusion.1), kind=kLoop, calls=%fused_computation.51 | loop fusion | bytes 51200 | tf_op jit(solution)/shard_map/slice | solution.py:207
  57.6 2.6 %copy.20 = f32[25,128,1]{1,2,0:T(1,128)} copy(f32[25,128,1]{2,1,0:T(8,128)} %get-tuple-element.34) | data formatting | bytes 25600 | tf_op jit(solution)/shard_map/slice | solution.py:207
  60.2 2.5 %copy.22 = f32[25,128,1]{1,2,0:T(1,128)} copy(f32[25,128,1]{2,1,0:T(8,128)} %get-tuple-element.35) | data formatting | bytes 25600 | tf_op jit(solution)/shard_map/slice | solution.py:208
  62.7 2.3 %collective-permute-start.2 = (f32[25,128,1]{1,2,0:T(1,128)}, f32[25,128,1]{1,2,0:T(1,128)}, u32[]{:S(2)}, u32[]{:S(2)}) collective-permute-start(f32[25,128,1]{1,2,0:T(1,128)} %copy.22), channel_id=1, source_target_pairs={{0,4},{4,8},{8,12},{12,16},{16,20},{20,24},{24,28},{28,0},{1,5},{5... | collective-permute-start | bytes 38408 | tf_op jit(solution)/shard_map/ppermute | solution.py:211
  65.1 4.8 %collective-permute-start.3 = (f32[25,1,128]{2,1,0:T(1,128)}, f32[25,1,128]{2,1,0:T(1,128)}, u32[]{:S(2)}, u32[]{:S(2)}) collective-permute-start(f32[25,1,128]{2,1,0:T(1,128)} %get-tuple-element.36), channel_id=1, source_target_pairs={{1,0},{2,1},{3,2},{5,4},{6,5},{7,6},{9,8},{10,9},{11,10},{13,12},{... | collective-permute-start | bytes 38408 | tf_op jit(solution)/shard_map/ppermute | solution.py:213
  69.9 1.4 %fusion.25 = f32[24,128,128]{2,1,0:T(8,128)} fusion(f32[25,128,128]{2,1,0:T(8,128)S(1)} %broadcast_multiply_fusion.1, f32[128,128]{1,0:T(8,128)S(1)} %copy-done.18), kind=kLoop, calls=%fused_computation.37 | loop fusion | flops 786432 | bytes 4784128 | tf_op jit(solution)/shard_map/mul | solution.py:293
  71.3 2.5 %copy.21 = f32[25,128,1]{2,1,0:T(8,128)} copy(f32[25,128,1]{1,2,0:T(1,128)} %collective-permute-done) | data formatting | bytes 25600 | tf_op jit(solution)/shard_map/ppermute | solution.py:213
  73.8 2.4 %copy.23 = f32[25,128,1]{2,1,0:T(8,128)} copy(f32[25,128,1]{1,2,0:T(1,128)} %collective-permute-done.2) | data formatting | bytes 25600 | tf_op jit(solution)/shard_map/ppermute | solution.py:211
  76.2 2.2 %collective-permute-start.8 = (f32[25,128]{1,0:T(8,128)}, f32[25,128]{1,0:T(8,128)}, u32[]{:S(2)}, u32[]{:S(2)}) collective-permute-start(f32[25,128]{1,0:T(8,128)} %collective-permute-done.7), channel_id=1, source_target_pairs={{0,16},{4,20},{8,24},{12,28},{16,0},{20,4},{24,8},{28,12},{1,17},{... | collective-permute-start | bytes 38408 | tf_op jit(solution)/shard_map/ppermute | solution.py:221
  78.4 3.3 %fusion.14 = f32[25,128,128]{2,1,0:T(8,128)S(1)} fusion(f32[25,128,128]{2,1,0:T(8,128)S(1)} %broadcast_multiply_fusion.1, f32[25,1,128]{2,1,0:T(1,128)} %collective-permute-done.5, f32[25,1,128]{2,1,0:T(1,128)} %collective-permute-done.3, f32[25,128,1]{2,1,0:T(8,128)} %copy.23, f32[25,128,128]{2,1,0:T(8,128)S(1)} %shard_map.133, f32[25,128,1]{2,1,0:T(8,128)} %copy.21, ...), kind=kLoop, calls=%fused_computation.19 | loop fusion | flops 6553600 | bytes 5228544 | tf_op jit(solution)/shard_map/add | solution.py:287
  81.7 1.2 copy-done.9
  82.9 0.8 rev.6
  83.7 1.6 %scatter-add.6 = f32[25,128,128]{2,1,0:T(8,128)} dynamic-update-slice(f32[25,128,128]{2,1,0:T(8,128)} %copy-done.9, f32[25,1,128]{2,1,0:T(1,128)S(1)} %copy.25, s32[]{:T(128)} %constant.58.clone.1, s32[]{:T(128)} %constant.59.clone.1, s32[]{:T(128)} %constant.58.clone.1) | dynamic-update-slice | bytes 25604 | tf_op jit(solution)/shard_map/scatter-add | solution.py:292
  85.3 2.8 %broadcast_multiply_fusion = f32[25,128,128]{2,1,0:T(8,128)S(1)} fusion(f32[128,128]{1,0:T(8,128)} %convert_element_type.3, f32[24,128,128]{2,1,0:T(8,128)} %fusion.25, f32[25,128,128]{2,1,0:T(8,128)} %scatter-add.6), kind=kLoop, calls=%fused_computation.38 | loop fusion | flops 1228800 | bytes 4915200 | tf_op jit(solution)/shard_map/mul | solution.py:277
  89.3 1.8 %fusion.26 = (f32[25,128,1]{2,1,0:T(8,128)}, f32[25,128,1]{2,1,0:T(8,128)S(1)}) fusion(f32[25,128,128]{2,1,0:T(8,128)S(1)} %broadcast_multiply_fusion), kind=kLoop, calls=%fused_computation.49 | loop fusion | bytes 51200 | tf_op jit(solution)/shard_map/slice | solution.py:207
  91.1 2.5 %copy.26 = f32[25,128,1]{1,2,0:T(1,128)} copy(f32[25,128,1]{2,1,0:T(8,128)} %get-tuple-element.30) | data formatting | bytes 25600 | tf_op jit(solution)/shard_map/slice | solution.py:207
  93.6 1.5 %collective-permute-start.9 = (f32[25,128,1]{1,2,0:T(1,128)}, f32[25,128,1]{1,2,0:T(1,128)}, u32[]{:S(2)}, u32[]{:S(2)}) collective-permute-start(f32[25,128,1]{1,2,0:T(1,128)} %copy.26), channel_id=1, source_target_pairs={{4,0},{8,4},{12,8},{16,12},{20,16},{24,20},{28,24},{0,28},{5,1},{9... | collective-permute-start | bytes 38408 | tf_op jit(solution)/shard_map/ppermute | solution.py:213
  95.1 1.1 copy.28
  96.2 0.9 collective-permute-start.10
  97.1 1.3 %collective-permute-start.12 = (f32[25,1,128]{2,0,1:T(8,128)S(1)}, f32[25,1,128]{2,0,1:T(8,128)}, u32[]{:S(2)}, u32[]{:S(2)}) collective-permute-start(f32[25,1,128]{2,0,1:T(8,128)S(1)} %copy.36), channel_id=1, source_target_pairs={{0,1},{1,2},{2,3},{4,5},{5,6},{6,7},{8,9},{9,10},{10,11},{12,13},{... | collective-permute-start | bytes 38408 | tf_op jit(solution)/shard_map/ppermute | solution.py:211
  98.4 4.6 %collective-permute-start.11 = (f32[25,1,128]{2,1,0:T(1,128)}, f32[25,1,128]{2,1,0:T(1,128)}, u32[]{:S(2)}, u32[]{:S(2)}) collective-permute-start(f32[25,1,128]{2,1,0:T(1,128)} %get-tuple-element.32), channel_id=1, source_target_pairs={{1,0},{2,1},{3,2},{5,4},{6,5},{7,6},{9,8},{10,9},{11,10},{13,12},{... | collective-permute-start | bytes 38408 | tf_op jit(solution)/shard_map/ppermute | solution.py:213
  103.0 2.2 %fusion.24 = f32[24,128,128]{2,1,0:T(8,128)} fusion(f32[25,128,128]{2,1,0:T(8,128)S(1)} %broadcast_multiply_fusion, f32[128,128]{1,0:T(8,128)} %param.22), kind=kLoop, calls=%fused_computation.35 | loop fusion | flops 786432 | bytes 4784128 | tf_op jit(solution)/shard_map/mul | solution.py:293
  105.2 2.5 %copy.27 = f32[25,128,1]{2,1,0:T(8,128)} copy(f32[25,128,1]{1,2,0:T(1,128)} %collective-permute-done.9) | data formatting | bytes 25600 | tf_op jit(solution)/shard_map/ppermute | solution.py:213
  107.8 2.4 %copy.29 = f32[25,128,1]{2,1,0:T(8,128)} copy(f32[25,128,1]{1,2,0:T(1,128)} %collective-permute-done.10) | data formatting | bytes 25600 | tf_op jit(solution)/shard_map/ppermute | solution.py:211
  110.2 0.7 copy.31
  110.9 3.5 %collective-permute-start.15 = (f32[25,128]{1,0:T(8,128)}, f32[25,128]{1,0:T(8,128)S(1)}, u32[]{:S(2)}, u32[]{:S(2)}) collective-permute-start(f32[25,128]{1,0:T(8,128)} %collective-permute-done.14), channel_id=1, source_target_pairs={{0,16},{4,20},{8,24},{12,28},{16,0},{20,4},{24,8},{28,12},{1,17},{... | collective-permute-start | bytes 38408 | tf_op jit(solution)/shard_map/ppermute | solution.py:221
  114.5 3.9 %fusion.2 = f32[25,128,128]{2,1,0:T(8,128)S(1)} fusion(f32[25,128,128]{2,1,0:T(8,128)S(1)} %broadcast_multiply_fusion, f32[25,1,128]{2,1,0:T(1,128)S(1)} %copy.31, f32[25,1,128]{2,1,0:T(1,128)} %collective-permute-done.11, f32[25,128,1]{2,1,0:T(8,128)} %copy.29, f32[25,128,1]{2,1,0:T(8,128)} %copy.27, f32[128,128]{1,0:T(8,128)S(1)} %copy-done.15, ...), kind=kLoop, calls=%fused_computation.3 | loop fusion | flops 7372800 | bytes 6801408 | tf_op jit(solution)/shard_map/add | solution.py:287
  118.4 1.2 copy-done.11
  119.7 1.6 %scatter-add.9 = f32[25,128,128]{2,1,0:T(8,128)} dynamic-update-slice(f32[25,128,128]{2,1,0:T(8,128)} %copy-done.11, f32[25,1,128]{2,1,0:T(1,128)S(1)} %copy.33, s32[]{:T(128)} %constant.58.clone.1, s32[]{:T(128)} %constant.59.clone.1, s32[]{:T(128)} %constant.58.clone.1) | dynamic-update-slice | bytes 25604 | tf_op jit(solution)/shard_map/scatter-add | solution.py:292
  121.3 4.0 %pad_add_fusion = f32[25,128,128]{2,1,0:T(8,128)} fusion(f32[24,128,128]{2,1,0:T(8,128)} %fusion.24, f32[25,128,128]{2,1,0:T(8,128)} %scatter-add.9), kind=kLoop, calls=%fused_computation.32 | loop fusion | flops 819200 | bytes 4849664 | tf_op jit(solution)/shard_map/add | solution.py:295
  (77 shorter events, 2.9 us)
Async XLA Ops:
  0.6 1.4 %copy-start.1 = (f32[25,128,128]{2,1,0:T(8,128)S(1)}, f32[25,128,128]{2,1,0:T(8,128)}, u32[]{:S(2)}) copy-start(f32[25,128,128]{2,1,0:T(8,128)} %state_ref.1) | copy-start | bytes 4915204
  2.1 0.7 copy-start.4
  2.8 0.7 copy-start.6
  3.5 22.7 %copy-start.2 = (f32[25,512]{1,0:T(8,128)S(1)}, f32[25,512]{1,0:T(8,128)}, u32[]{:S(2)}) copy-start(f32[25,512]{1,0:T(8,128)} %value_ref.1) | copy-start | bytes 153604
  3.5 22.7 %copy-start.3 = (f32[25,512]{1,0:T(8,128)S(1)}, f32[25,512]{1,0:T(8,128)}, u32[]{:S(2)}) copy-start(f32[25,512]{1,0:T(8,128)} %invvar_ref.1) | copy-start | bytes 153604
  3.5 22.7 %copy-start.8 = (s32[1,2048]{1,0:T(1,128)S(1)}, s32[1,2048]{1,0:T(1,128)}, u32[]{:S(2)}) copy-start(s32[1,2048]{1,0:T(1,128)} %target_ref.1) | copy-start | bytes 24580
  3.5 31.2 %copy-start.20 = (f32[128,128]{1,0:T(8,128)S(1)}, f32[128,128]{1,0:T(8,128)}, u32[]{:S(2)}) copy-start(f32[128,128]{1,0:T(8,128)} %param.19) | copy-start | bytes 196612
  3.5 31.2 %copy-start.21 = (f32[128,128]{1,0:T(8,128)S(1)}, f32[128,128]{1,0:T(8,128)}, u32[]{:S(2)}) copy-start(f32[128,128]{1,0:T(8,128)} %param.21) | copy-start | bytes 196612
  3.5 33.2 %copy-start.13 = (f32[128,128]{1,0:T(8,128)S(1)}, f32[128,128]{1,0:T(8,128)}, u32[]{:S(2)}) copy-start(f32[128,128]{1,0:T(8,128)} %param.20) | copy-start | bytes 196612
  3.5 35.0 %copy-start.19 = (s32[128,128]{1,0:T(8,128)S(1)}, s32[128,128]{1,0:T(8,128)}, u32[]{:S(2)}) copy-start(s32[128,128]{1,0:T(8,128)} %param.18) | copy-start | bytes 196612
  11.3 32.5 %copy-start = (f32[25,128,128]{2,1,0:T(8,128)S(1)}, f32[25,128,128]{2,1,0:T(8,128)}, u32[]{:S(2)}) copy-start(f32[25,128,128]{2,1,0:T(8,128)} %adjoint_ref.1) | copy-start | bytes 4915204
  11.3 32.5 %copy-start.5 = (s32[1,2048]{1,0:T(1,128)S(1)}, s32[1,2048]{1,0:T(1,128)}, u32[]{:S(2)}) copy-start(s32[1,2048]{1,0:T(1,128)} %cell_ref.3) | copy-start | bytes 24580
  11.3 32.5 %copy-start.7 = (f32[1,2048]{1,0:T(1,128)S(1)}, f32[1,2048]{1,0:T(1,128)}, u32[]{:S(2)}) copy-start(f32[1,2048]{1,0:T(1,128)} %weight_ref.3) | copy-start | bytes 24580
  30.3 13.5 %all-to-all-start.1 = ((f32[32,16,128]{2,1,0:T(8,128)}), f32[32,16,128]{2,1,0:T(8,128)S(1)}, u32[]{:S(2)}, u32[]{:S(2)}) async-start(f32[32,16,128]{2,1,0:T(8,128)} %get-tuple-element.28), calls=%async_computation.1 | async-start | bytes 524288 | tf_op jit(solution)/shard_map/all_to_all | solution.py:256
  35.4 5.0 %collective-permute-start.1 = (f32[128,1]{1,0:T(8,128)S(1)}, f32[128,1]{1,0:T(8,128)S(1)}, u32[]{:S(2)}, u32[]{:S(2)}) collective-permute-start(f32[128,1]{1,0:T(8,128)S(1)} %slice.155), channel_id=1, source_target_pairs={{0,4},{4,8},{8,12},{12,16},{16,20},{20,24},{24,28},{28,0},{1,5},{5... | collective-permute-start | bytes 1544 | tf_op jit(solution)/shard_map/ppermute | solution.py:194
  37.2 4.0 %collective-permute-start.4 = (f32[1,128]{1,0:T(1,128)S(1)}, f32[1,128]{1,0:T(1,128)S(1)}, u32[]{:S(2)}, u32[]{:S(2)}) collective-permute-start(f32[1,128]{1,0:T(1,128)S(1)} %get-tuple-element.41), channel_id=1, source_target_pairs={{0,1},{1,2},{2,3},{4,5},{5,6},{6,7},{8,9},{9,10},{10,11},{12,13},{... | collective-permute-start | bytes 1544 | tf_op jit(solution)/shard_map/ppermute | solution.py:200
  43.7 6.3 %copy-start.17 = (f32[128,128]{1,0:T(8,128)S(1)}, f32[128,128]{1,0:T(8,128)}, u32[]{:S(2)}) copy-start(f32[128,128]{1,0:T(8,128)} %convert_element_type.3) | copy-start | bytes 196612
  50.0 2.1 %copy-start.22 = (f32[128]{0:T(128)S(1)}, f32[128]{0:T(128)}, u32[]{:S(2)}) copy-start(f32[128]{0:T(128)} %get-tuple-element.40) | copy-start | bytes 1540
  50.8 27.5 %collective-permute-start.5 = (f32[25,1,128]{2,1,0:T(1,128)S(1)}, f32[25,1,128]{2,1,0:T(1,128)}, u32[]{:S(2)}, u32[]{:S(2)}) collective-permute-start(f32[25,1,128]{2,1,0:T(1,128)S(1)} %get-tuple-element.37), channel_id=1, source_target_pairs={{0,1},{1,2},{2,3},{4,5},{5,6},{6,7},{8,9},{9,10},{10,11},{12,13},{... | collective-permute-start | bytes 38408 | tf_op jit(solution)/shard_map/ppermute | solution.py:211
  52.1 17.8 %collective-permute-start.6 = (f32[25,128]{1,0:T(8,128)S(1)}, f32[25,128]{1,0:T(8,128)}, u32[]{:S(2)}, u32[]{:S(2)}) collective-permute-start(f32[25,128]{1,0:T(8,128)S(1)} %bitcast_multiply_fusion), channel_id=1, source_target_pairs={{0,4},{4,0},{8,12},{12,8},{16,20},{20,16},{24,28},{28,24},{1,5},{5... | collective-permute-start | bytes 38408 | tf_op jit(solution)/shard_map/ppermute | solution.py:221
  57.6 12.3 %copy-start.18 = (f32[128,128]{1,0:T(8,128)S(1)}, f32[128,128]{1,0:T(8,128)}, u32[]{:S(2)}) copy-start(f32[128,128]{1,0:T(8,128)} %param.22) | copy-start | bytes 196612
  60.2 11.1 %collective-permute-start = (f32[25,128,1]{1,2,0:T(1,128)}, f32[25,128,1]{1,2,0:T(1,128)}, u32[]{:S(2)}, u32[]{:S(2)}) collective-permute-start(f32[25,128,1]{1,2,0:T(1,128)} %copy.20), channel_id=1, source_target_pairs={{4,0},{8,4},{12,8},{16,12},{20,16},{24,20},{28,24},{0,28},{5,1},{9... | collective-permute-start | bytes 38408 | tf_op jit(solution)/shard_map/ppermute | solution.py:213
  62.7 11.1 %collective-permute-start.2 = (f32[25,128,1]{1,2,0:T(1,128)}, f32[25,128,1]{1,2,0:T(1,128)}, u32[]{:S(2)}, u32[]{:S(2)}) collective-permute-start(f32[25,128,1]{1,2,0:T(1,128)} %copy.22), channel_id=1, source_target_pairs={{0,4},{4,8},{8,12},{12,16},{16,20},{20,24},{24,28},{28,0},{1,5},{5... | collective-permute-start | bytes 38408 | tf_op jit(solution)/shard_map/ppermute | solution.py:211
  65.1 13.3 %collective-permute-start.3 = (f32[25,1,128]{2,1,0:T(1,128)}, f32[25,1,128]{2,1,0:T(1,128)}, u32[]{:S(2)}, u32[]{:S(2)}) collective-permute-start(f32[25,1,128]{2,1,0:T(1,128)} %get-tuple-element.36), channel_id=1, source_target_pairs={{1,0},{2,1},{3,2},{5,4},{6,5},{7,6},{9,8},{10,9},{11,10},{13,12},{... | collective-permute-start | bytes 38408 | tf_op jit(solution)/shard_map/ppermute | solution.py:213
  69.9 6.3 %collective-permute-start.7 = (f32[25,128]{1,0:T(8,128)}, f32[25,128]{1,0:T(8,128)}, u32[]{:S(2)}, u32[]{:S(2)}) collective-permute-start(f32[25,128]{1,0:T(8,128)} %collective-permute-done.6), channel_id=1, source_target_pairs={{0,8},{4,12},{8,0},{12,4},{16,24},{20,28},{24,16},{28,20},{1,9},{5... | collective-permute-start | bytes 38408 | tf_op jit(solution)/shard_map/ppermute | solution.py:221
  71.3 7.1 %copy-start.12 = (f32[128,128]{1,0:T(8,128)S(1)}, f32[128,128]{1,0:T(8,128)}, u32[]{:S(2)}) copy-start(f32[128,128]{1,0:T(8,128)} %pad_maximum_fusion.8) | copy-start | bytes 196612
  71.3 7.1 %copy-start.14 = (f32[128,128]{1,0:T(8,128)S(1)}, f32[128,128]{1,0:T(8,128)}, u32[]{:S(2)}) copy-start(f32[128,128]{1,0:T(8,128)} %param.20) | copy-start | bytes 196612
  71.3 7.1 %copy-start.15 = (f32[128,128]{1,0:T(8,128)S(1)}, f32[128,128]{1,0:T(8,128)}, u32[]{:S(2)}) copy-start(f32[128,128]{1,0:T(8,128)} %pad_maximum_fusion.9) | copy-start | bytes 196612
  71.3 7.1 %copy-start.16 = (f32[128,128]{1,0:T(8,128)S(1)}, f32[128,128]{1,0:T(8,128)}, u32[]{:S(2)}) copy-start(f32[128,128]{1,0:T(8,128)} %get-tuple-element.38) | copy-start | bytes 196612
  76.2 6.7 %collective-permute-start.8 = (f32[25,128]{1,0:T(8,128)}, f32[25,128]{1,0:T(8,128)}, u32[]{:S(2)}, u32[]{:S(2)}) collective-permute-start(f32[25,128]{1,0:T(8,128)} %collective-permute-done.7), channel_id=1, source_target_pairs={{0,16},{4,20},{8,24},{12,28},{16,0},{20,4},{24,8},{28,12},{1,17},{... | collective-permute-start | bytes 38408 | tf_op jit(solution)/shard_map/ppermute | solution.py:221
  81.7 1.2 copy-start.9
  85.3 3.4 %copy-start.23 = (f32[128]{0:T(128)S(1)}, f32[128]{0:T(128)}, u32[]{:S(2)}) copy-start(f32[128]{0:T(128)} %get-tuple-element.40) | copy-start | bytes 1540
  89.3 13.7 %collective-permute-start.13 = (f32[25,128]{1,0:T(8,128)}, f32[25,128]{1,0:T(8,128)}, u32[]{:S(2)}, u32[]{:S(2)}) collective-permute-start(f32[25,128]{1,0:T(8,128)} %bitcast_multiply_fusion.1), channel_id=1, source_target_pairs={{0,4},{4,0},{8,12},{12,8},{16,20},{20,16},{24,28},{28,24},{1,5},{5... | collective-permute-start | bytes 38408 | tf_op jit(solution)/shard_map/ppermute | solution.py:221
  93.6 11.6 %collective-permute-start.9 = (f32[25,128,1]{1,2,0:T(1,128)}, f32[25,128,1]{1,2,0:T(1,128)}, u32[]{:S(2)}, u32[]{:S(2)}) collective-permute-start(f32[25,128,1]{1,2,0:T(1,128)} %copy.26), channel_id=1, source_target_pairs={{4,0},{8,4},{12,8},{16,12},{20,16},{24,20},{28,24},{0,28},{5,1},{9... | collective-permute-start | bytes 38408 | tf_op jit(solution)/shard_map/ppermute | solution.py:213
  96.2 11.6 %collective-permute-start.10 = (f32[25,128,1]{1,2,0:T(1,128)}, f32[25,128,1]{1,2,0:T(1,128)}, u32[]{:S(2)}, u32[]{:S(2)}) collective-permute-start(f32[25,128,1]{1,2,0:T(1,128)} %copy.28), channel_id=1, source_target_pairs={{0,4},{4,8},{8,12},{12,16},{16,20},{20,24},{24,28},{28,0},{1,5},{5... | collective-permute-start | bytes 38408 | tf_op jit(solution)/shard_map/ppermute | solution.py:211
  97.1 13.1 %collective-permute-start.12 = (f32[25,1,128]{2,0,1:T(8,128)S(1)}, f32[25,1,128]{2,0,1:T(8,128)}, u32[]{:S(2)}, u32[]{:S(2)}) collective-permute-start(f32[25,1,128]{2,0,1:T(8,128)S(1)} %copy.36), channel_id=1, source_target_pairs={{0,1},{1,2},{2,3},{4,5},{5,6},{6,7},{8,9},{9,10},{10,11},{12,13},{... | collective-permute-start | bytes 38408 | tf_op jit(solution)/shard_map/ppermute | solution.py:211
  98.4 16.1 %collective-permute-start.11 = (f32[25,1,128]{2,1,0:T(1,128)}, f32[25,1,128]{2,1,0:T(1,128)}, u32[]{:S(2)}, u32[]{:S(2)}) collective-permute-start(f32[25,1,128]{2,1,0:T(1,128)} %get-tuple-element.32), channel_id=1, source_target_pairs={{1,0},{2,1},{3,2},{5,4},{6,5},{7,6},{9,8},{10,9},{11,10},{13,12},{... | collective-permute-start | bytes 38408 | tf_op jit(solution)/shard_map/ppermute | solution.py:213
  103.0 7.9 %collective-permute-start.14 = (f32[25,128]{1,0:T(8,128)}, f32[25,128]{1,0:T(8,128)}, u32[]{:S(2)}, u32[]{:S(2)}) collective-permute-start(f32[25,128]{1,0:T(8,128)} %collective-permute-done.13), channel_id=1, source_target_pairs={{0,8},{4,12},{8,0},{12,4},{16,24},{20,28},{24,16},{28,20},{1,9},{5... | collective-permute-start | bytes 38408 | tf_op jit(solution)/shard_map/ppermute | solution.py:221
  105.2 9.2 %copy-start.10 = (f32[25,128,128]{2,1,0:T(8,128)S(1)}, f32[25,128,128]{2,1,0:T(8,128)}, u32[]{:S(2)}) copy-start(f32[25,128,128]{2,1,0:T(8,128)} %scatter-add.6) | copy-start | bytes 4915204
  110.9 8.6 %collective-permute-start.15 = (f32[25,128]{1,0:T(8,128)}, f32[25,128]{1,0:T(8,128)S(1)}, u32[]{:S(2)}, u32[]{:S(2)}) collective-permute-start(f32[25,128]{1,0:T(8,128)} %collective-permute-done.14), channel_id=1, source_target_pairs={{0,16},{4,20},{8,24},{12,28},{16,0},{20,4},{24,8},{28,12},{1,17},{... | collective-permute-start | bytes 38408 | tf_op jit(solution)/shard_map/ppermute | solution.py:221
  118.4 1.2 copy-start.11

commit v2 on v1

--- a/solution.py
+++ b/solution.py
@@ -10,6 +10,7 @@
 STEPS = 2
 LANES = 128
 GROUP = 32
+SUB = 8
 VMEM_BYTES = 48 * 1024 * 1024
 BOTH = ("lon", "lat")
 
@@ -133,7 +134,11 @@
     lax.fori_loop(0, target_ref.shape[1] // tile, store, 0)
 
 
-def scatter_kernel(returned_ref, cell_ref, weight_ref, adjoint_ref, out_ref, rows_ref, hot_ref, sum_ref):
+def scatter_kernel(
+    returned_ref, cell_ref, weight_ref, adjoint_ref, mask_ref,
+    out_ref, columns_ref, edges_ref,
+    rows_ref, hot_ref, sum_ref,
+):
     levels_n, rows_n, cols_n = out_ref.shape
     groups = rows_n // GROUP
     width = groups * cols_n
@@ -174,13 +179,324 @@
         forcing = sum_ref[:, group * cols_n : (group + 1) * cols_n]
         out_ref[:, at, :] = adjoint_ref[:, at, :] + forcing.reshape(levels_n, GROUP, cols_n)
 
-
-def kernel_call(body, out_shape, scratch):
+    level_at = jnp.right_shift(lax.broadcasted_iota(jnp.int32, (SUB, cols_n), 1), 2)
+    for top in range(0, rows_n, SUB):
+        ocean = mask_ref[top : top + SUB, :].astype(jnp.float32)
+        found = jnp.zeros((SUB, cols_n), jnp.float32)
+        for level in range(levels_n):
+            block = pltpu.roll(out_ref[level, top : top + SUB, :], 4 * level + 2, 1)
+            found = jnp.where(level_at == level, block, found)
+        sides = pltpu.roll(ocean, 2, 1)
+        spread = jnp.where(level_at == 0, sides, 0.0)
+        shift = 4
+        while shift < cols_n:
+            spread = spread + pltpu.roll(spread, shift, 1)
+            shift *= 2
+        columns_ref[top : top + SUB, :] = found * spread
+    for place, row in enumerate((0, 1, rows_n - 2, rows_n - 1)):
+        ocean = mask_ref[row : row + 1, :].astype(jnp.float32)
+        for level in range(levels_n):
+            edges_ref[place, level : level + 1, :] = out_ref[level, row : row + 1, :] * ocean
+
+
+def lane(shape):
+    return lax.broadcasted_iota(jnp.int32, shape, 1)
+
+
+def sublane(shape):
+    return lax.broadcasted_iota(jnp.int32, shape, 0)
+
+
+def shifted(block, steps, axis, edge):
+    size = block.shape[axis]
+    at = lax.broadcasted_iota(jnp.int32, block.shape, axis)
+    moved = pltpu.roll(block, steps % size, axis)
+    return jnp.where(at == (0 if steps > 0 else size - 1), edge, moved)
+
+
+def reversed_lanes(block):
+    at = block.shape[1] - 1 - lane(block.shape)
+    return jnp.take_along_axis(block, at, axis=1, mode="promise_in_bounds")
+
+
+def lon_neighbours(flag_ref, first, second):
+    even = flag_ref[0] == 1
+    return jnp.where(even, first, second), jnp.where(even, second, first)
+
+
+def lat_neighbours(flag_ref, first, second):
+    even = flag_ref[1] == 1
+    return jnp.where(even, first, second), jnp.where(even, second, first)
+
+
+def coefficient_columns_kernel(mask_ref, east_ref, north_ref, flow_ref, vertical_ref, out_ref):
+    rows_n, cols_n = mask_ref.shape
+    ocean = mask_ref[...].astype(jnp.float32)
+    here = east_ref[...] + 0.5 * flow_ref[...]
+    behind = east_ref[...] - 0.5 * flow_ref[...]
+    north, vertical = north_ref[...], vertical_ref[...]
+    last = cols_n - 1
+    wanted = (
+        (ocean, 0), (here, 0), (north, 0), (vertical, 0),
+        (ocean, last), (here, last), (behind, last), (behind, last - 1), (north, last), (vertical, last),
+    )
+    found = jnp.zeros((rows_n, cols_n), jnp.float32)
+    for place, (field, column) in enumerate(wanted):
+        found = jnp.where(
+            lane(found.shape) == place, pltpu.roll(field, (place - column) % cols_n, 1), found
+        )
+    out_ref[...] = found
+
+
+def coefficient_rows_kernel(
+    flag_ref, mask_ref, east_ref, north_ref, flow_ref, vertical_ref, first_ref, second_ref, out_ref
+):
+    rows_n, cols_n = mask_ref.shape
+    east, west = lon_neighbours(flag_ref, first_ref[...], second_ref[...])
+    top, last = slice(0, 1), slice(rows_n - 1, rows_n)
+    found = []
+    for at in (top, last):
+        behind = east_ref[at, :] - 0.5 * flow_ref[at, :]
+        found.append(mask_ref[at, :].astype(jnp.float32))
+        found.append(east_ref[at, :] + 0.5 * flow_ref[at, :])
+        found.append(shifted(behind, 1, 1, west[at, 6:7]))
+        found.append(north_ref[at, :])
+        if at is last:
+            found.append(north_ref[rows_n - 2 : rows_n - 1, :])
+        found.append(vertical_ref[at, :])
+    found += [east[top], east[last], west[top], west[last]]
+    for place, row in enumerate(found):
+        out_ref[place : place + 1, :] = row
+    out_ref[len(found) :, :] = jnp.zeros((out_ref.shape[0] - len(found), cols_n), jnp.float32)
+
+
+def coefficients_kernel(
+    flag_ref, mask_ref, east_ref, north_ref, flow_ref, vertical_ref,
+    lon_first_ref, lon_second_ref, lat_first_ref, lat_second_ref,
+    field_ref, side_ref, edge_ref,
+):
+    rows_n, cols_n = mask_ref.shape
+    fold = flag_ref[2] == 1
+    east, west = lon_neighbours(flag_ref, lon_first_ref[...], lon_second_ref[...])
+    up, down = lat_neighbours(flag_ref, lat_first_ref[...], lat_second_ref[...])
+    mirrored = reversed_lanes(up)
+    ocean = mask_ref[...].astype(jnp.float32)
+    here = east_ref[...] + 0.5 * flow_ref[...]
+    behind = east_ref[...] - 0.5 * flow_ref[...]
+    north = north_ref[...]
+    back = shifted(behind, 1, 1, west[:, 6:7])
+    south = shifted(north, 1, 0, down[8:9])
+    top = sublane((rows_n, cols_n)) == rows_n - 1
+    onto = jnp.where(jnp.logical_and(top, fold), mirrored[8:9], north)
+    parts = (ocean, here + back + north + south, here, back, onto, south, vertical_ref[...])
+    for place, part in enumerate(parts):
+        field_ref[place] = part
+
+    def side(ocean, here, back, north, vertical, below, fold_top):
+        south = shifted(north, 1, 0, below)
+        top = sublane(north.shape) == rows_n - 1
+        onto = jnp.where(jnp.logical_and(top, fold), fold_top, north)
+        return ocean, here + back + north + south, here, back, onto, south, vertical
+
+    def spread(columns, place):
+        return jnp.broadcast_to(columns[:, place : place + 1], (columns.shape[0], cols_n))
+
+    eastern = side(
+        spread(east, 0), spread(east, 1), spread(behind, cols_n - 1), spread(east, 2), spread(east, 3),
+        spread(down[12:13], 2), spread(up[14:15], 8),
+    )
+    western = side(
+        spread(west, 4), spread(west, 5), spread(west, 7), spread(west, 8), spread(west, 9),
+        spread(down[14:15], 8), spread(up[12:13], 2),
+    )
+    found = jnp.zeros((rows_n, cols_n), jnp.float32)
+    for place, part in enumerate(eastern + western):
+        found = jnp.where(lane(found.shape) == place, part, found)
+    side_ref[...] = found
+
+    into = north[rows_n - 1 :, :]
+    plain = (up[0:1], up[1:2] + up[2:3] + up[3:4] + into, up[1:2], up[2:3], into, up[3:4], up[4:5])
+    turned = mirrored
+    folded = (
+        turned[5:6], turned[6:7] + turned[7:8] + turned[8:9] + turned[9:10],
+        turned[7:8], turned[6:7], into, turned[9:10], turned[10:11],
+    )
+    low = (
+        down[5:6], down[6:7] + down[7:8] + down[8:9] + down[9:10],
+        down[6:7], down[7:8], down[8:9], down[9:10], down[10:11],
+    )
+    for place in range(len(plain)):
+        edge_ref[place : place + 1, :] = jnp.where(fold, folded[place], plain[place])
+        edge_ref[SUB + place : SUB + place + 1, :] = low[place]
+    for place in (len(plain), SUB + len(plain)):
+        edge_ref[place : place + 1, :] = jnp.zeros((1, cols_n), jnp.float32)
+
+
+def edge_message_kernel(flag_ref, edges_ref, first_ref, second_ref, out_ref):
+    places, levels, cols_n = edges_ref.shape
+    last = first_ref.shape[0] - 1
+    for place in range(places):
+        out_ref[place * levels : (place + 1) * levels, :] = edges_ref[place]
+    ends = []
+    for row in (0, last):
+        ends.append(lon_neighbours(flag_ref, first_ref[row : row + 1, :], second_ref[row : row + 1, :]))
+    found = (ends[0][0], ends[1][0], ends[0][1], ends[1][1])
+    for place, row in enumerate(found):
+        out_ref[places * levels + place : places * levels + place + 1, :] = row
+
+
+def steps_kernel(
+    flag_ref, seed_ref, field_ref, side_ref, edge_ref,
+    columns_ref, edges_ref, lon_first_ref, lon_second_ref, lat_first_ref, lat_second_ref,
+    out_ref,
+    masked_ref, next_ref, half_ref, turn_ref,
+):
+    levels_n, rows_n, cols_n = seed_ref.shape
+    levels = edges_ref.shape[1]
+    fold = flag_ref[2] == 1
+    east, west = lon_neighbours(flag_ref, lon_first_ref[...], lon_second_ref[...])
+    up, down = lat_neighbours(flag_ref, lat_first_ref[...], lat_second_ref[...])
+    own = columns_ref[...]
+
+    ends = edges_ref.shape[0] * levels
+    east_up = jnp.where(fold, pltpu.roll(up[ends + 3 : ends + 4], 1, 1), up[ends : ends + 1])
+    west_up = jnp.where(fold, pltpu.roll(up[ends + 1 : ends + 2], cols_n - 1, 1), up[ends + 2 : ends + 3])
+    east_down, west_down = down[ends + 1 : ends + 2], down[ends + 3 : ends + 4]
+
+    level_at = jnp.right_shift(lane((rows_n, cols_n)), 2)
+
+    def side_step(block, eastern, western, above, below, base):
+        def coefficient(place):
+            return side_ref[:, base + place : base + place + 1]
+
+        higher = jnp.where(level_at > 0, pltpu.roll(block, 4, 1) - block, 0.0)
+        lower = jnp.where(level_at < levels_n - 1, pltpu.roll(block, cols_n - 4, 1) - block, 0.0)
+        change = (
+            coefficient(2) * eastern
+            + coefficient(3) * western
+            + coefficient(4) * shifted(block, -1, 0, above)
+            + coefficient(5) * shifted(block, 1, 0, below)
+            - coefficient(1) * block
+            + coefficient(6) * (higher + lower)
+        )
+        return block + coefficient(0) * change
+
+    east_next = side_step(
+        east, pltpu.roll(east, cols_n - 1, 1), pltpu.roll(own, 1, 1), east_up, east_down, 0
+    )
+    west_next = side_step(
+        west, pltpu.roll(own, cols_n - 1, 1), pltpu.roll(west, 1, 1), west_up, west_down, 7
+    )
+    slot = jnp.bitwise_and(lane((rows_n, cols_n)), 3)
+    for step, (eastern, western) in enumerate(((east, west), (east_next, west_next))):
+        turn_ref[step] = jnp.where(
+            slot == 1, pltpu.roll(eastern, cols_n - 1, 1), pltpu.roll(western, 1, 1)
+        )
+
+    plane = (levels, cols_n)
+    corner_at = 4 * sublane(plane)
+
+    def corner(row, place):
+        found = jnp.where(lane(plane) == corner_at + place, jnp.broadcast_to(row, plane), 0.0)
+        return jnp.sum(found, axis=1, keepdims=True)
+
+    def edge(block, place):
+        return block[place * levels : (place + 1) * levels]
+
+    def edge_step(block, outer, inner, eastern, western, base):
+        def coefficient(place):
+            return edge_ref[base + place : base + place + 1, :]
+
+        level = sublane(plane)
+        higher = jnp.where(level > 0, pltpu.roll(block, 1, 0) - block, 0.0)
+        lower = jnp.where(level < levels_n - 1, pltpu.roll(block, levels - 1, 0) - block, 0.0)
+        change = (
+            coefficient(2) * shifted(block, -1, 1, eastern)
+            + coefficient(3) * shifted(block, 1, 1, western)
+            + coefficient(4) * inner
+            + coefficient(5) * outer
+            - coefficient(1) * block
+            + coefficient(6) * (higher + lower)
+        )
+        return block + coefficient(0) * change
+
+    above = jnp.where(fold, reversed_lanes(edge(up, 3)), edge(up, 0))
+    above_outer = jnp.where(fold, reversed_lanes(edge(up, 2)), edge(up, 1))
+    below, below_outer = edge(down, 3), edge(down, 2)
+    above_next = edge_step(
+        above, above_outer, edges_ref[3], corner(east_up, 2), corner(west_up, 1), 0
+    )
+    below_next = edge_step(
+        below, below_outer, edges_ref[0], corner(east_down, 2), corner(west_down, 1), SUB
+    )
+    for level in range(levels_n):
+        for ref, high, low in ((masked_ref, above, below), (next_ref, above_next, below_next)):
+            ref[level, SUB + rows_n : SUB + rows_n + 1, :] = high[level : level + 1, :]
+            ref[level, SUB - 1 : SUB, :] = low[level : level + 1, :]
+
+    def mask(level, carry):
+        masked_ref[level, SUB : SUB + rows_n, :] = field_ref[0] * seed_ref[level]
+        return carry
+
+    lax.fori_loop(0, levels_n, mask, 0)
+    first = lane((SUB, cols_n)) == 0
+    last = lane((SUB, cols_n)) == cols_n - 1
+
+    def advance(step, level, source_ref, from_ref, store):
+        higher, lower = jnp.maximum(level - 1, 0), jnp.minimum(level + 1, levels_n - 1)
+        turn = lax.rem(2 * cols_n - 2 - 4 * level, cols_n)
+        for top in range(0, rows_n, SUB):
+            at = slice(top, top + SUB)
+            inner = slice(SUB + top, 2 * SUB + top)
+            block = from_ref[level, inner, :]
+            sides = pltpu.roll(turn_ref[step, at, :], turn, 1)
+            eastern = jnp.where(last, sides, pltpu.roll(block, cols_n - 1, 1))
+            western = jnp.where(first, sides, pltpu.roll(block, 1, 1))
+            north = from_ref[level, SUB + top + 1 : 2 * SUB + top + 1, :]
+            south = from_ref[level, SUB + top - 1 : 2 * SUB + top - 1, :]
+            vertical = (from_ref[higher, inner, :] - block) + (from_ref[lower, inner, :] - block)
+            found = (
+                source_ref[level, at, :]
+                - field_ref[1, at, :] * block
+                + field_ref[2, at, :] * eastern
+                + field_ref[3, at, :] * western
+                + field_ref[4, at, :] * north
+                + field_ref[5, at, :] * south
+                + field_ref[6, at, :] * vertical
+            )
+            store(level, top, found)
+
+    def keep(level, top, found):
+        half_ref[level, top : top + SUB, :] = found
+        next_ref[level, SUB + top : 2 * SUB + top, :] = field_ref[0, top : top + SUB, :] * found
+
+    def finish(level, top, found):
+        out_ref[level, top : top + SUB, :] = found
+
+    def first_step(level, carry):
+        advance(0, level, seed_ref, masked_ref, keep)
+        return carry
+
+    def second_step(level, carry):
+        advance(1, level, half_ref, next_ref, finish)
+        return carry
+
+    lax.fori_loop(0, levels_n, first_step, 0)
+    lax.fori_loop(0, levels_n, second_step, 0)
+
+
+def kernel_call(body, out_shape, scratch=(), flagged=False, inputs=0):
+    memory = {}
+    if flagged:
+        memory["in_specs"] = [pl.BlockSpec(memory_space=pltpu.SMEM)] + [
+            pl.BlockSpec(memory_space=pltpu.VMEM)
+        ] * (inputs - 1)
     return pl.pallas_call(
         body,
         out_shape=out_shape,
-        scratch_shapes=scratch,
+        scratch_shapes=list(scratch),
         compiler_params=pltpu.CompilerParams(vmem_limit_bytes=VMEM_BYTES),
+        **memory,
     )
 
 
@@ -188,37 +504,28 @@
     return jax.ShapeDtypeStruct(shape, jnp.float32)
 
 
-def from_behind(value, axis, steps):
-    count = lax.axis_size(axis)
-    pairs = [(source, (source + steps) % count) for source in range(count)]
-    return lax.ppermute(value, axis, pairs)
-
-
-def from_behind_2(block, axis, distance):
-    devices = range(lax.axis_size(axis))
-    route = [(i - distance, i) for i in devices if i - distance in devices]
-    return lax.ppermute(block, axis, route)
-
-
-def padded(cells, sides, width, closed):
-    for axis, dim in sides:
-        count = lax.axis_size(axis)
-        ends = count if closed else count - 1
-        head = lax.slice_in_dim(cells, 0, width, axis=dim)
-        tail = lax.slice_in_dim(cells, cells.shape[dim] - width, cells.shape[dim], axis=dim)
-        cells = jnp.concatenate(
-            [
-                lax.ppermute(tail, axis, [(i, (i + 1) % count) for i in range(ends)]),
-                cells,
-                lax.ppermute(head, axis, [((i + 1) % count, i) for i in range(ends)]),
-            ],
-            axis=dim,
-        )
-    return cells
-
-
-def from_partner(value, axis, bit):
-    return lax.ppermute(value, axis, [(i, i ^ 1 << bit) for i in range(lax.axis_size(axis))])
+def lon_swaps(value):
+    count = lax.axis_size("lon")
+    assert count % 2 == 0
+    first = [(i, i ^ 1) for i in range(count)]
+    second = [(i, (i + 1 if i % 2 else i - 1) % count) for i in range(count)]
+    return lax.ppermute(value, "lon", first), lax.ppermute(value, "lon", second)
+
+
+def lat_swaps(value):
+    lons, lats = lax.axis_size("lon"), lax.axis_size("lat")
+    found = []
+    for parity in (0, 1):
+        pairs = []
+        for i in range(lons):
+            for j in range(lats):
+                other = j + 1 if j % 2 == parity else j - 1
+                if other == lats:
+                    pairs.append((i * lats + j, (lons - 1 - i) * lats + j))
+                elif other >= 0:
+                    pairs.append((i * lats + j, i * lats + other))
+        found.append(lax.ppermute(value, BOTH, pairs))
+    return tuple(found)
 
 
 def on_device(
@@ -239,15 +546,30 @@
     devices = lax.axis_size(BOTH)
     slots = slot_cell.shape[1]
     obs_n = obs_value.shape[1]
-    assert 2 * (slots // devices) == LANES
+    assert 2 * (slots // devices) == LANES and cols_n == LANES and 4 * levels_n <= LANES
     half = (levels_n + 15) // 16 * 8
     width = rows_n // GROUP * cols_n
     bf16 = jnp.bfloat16
+    raw = (land_mask, east_coef, north_coef, zonal_flow, vertical_coef)
+    lon, lat = lax.axis_index("lon"), lax.axis_index("lat")
+    flags = jnp.stack([1 - lon % 2, 1 - lat % 2, lat == lax.axis_size("lat") - 1]).astype(jnp.int32)
 
     partial_vals = kernel_call(
         gather_kernel, f32(devices, half, LANES), [pltpu.VMEM((levels_n * GROUP, 3 * width), bf16)]
     )(slot_cell, slot_weight, state)
     arrived = lax.all_to_all(partial_vals, BOTH, split_axis=0, concat_axis=0, tiled=True)
+
+    side_coefs = lon_swaps(kernel_call(coefficient_columns_kernel, f32(rows_n, cols_n))(*raw))
+    row_coefs = kernel_call(coefficient_rows_kernel, f32(2 * SUB, cols_n), (), True, 8)(
+        flags, *raw, *side_coefs
+    )
+    edge_coefs = lat_swaps(row_coefs)
+    fields, sides, edges = kernel_call(
+        coefficients_kernel,
+        (f32(7, rows_n, cols_n), f32(rows_n, cols_n), f32(2 * SUB, cols_n)),
+        (), True, 10,
+    )(flags, *raw, *side_coefs, *edge_coefs)
+
     misfit, outgoing = kernel_call(
         observe_kernel,
         (f32(levels_n, obs_n), f32(devices, half, LANES)),
@@ -255,45 +577,32 @@
     )(arrived, arrive_obs, obs_value, obs_invvar)
     returned = lax.all_to_all(outgoing, BOTH, split_axis=0, concat_axis=0, tiled=True)
     tile = 4 * LANES
-    adjoint_state = kernel_call(
+    seed, own_columns, own_edges = kernel_call(
         scatter_kernel,
-        f32(levels_n, rows_n, cols_n),
+        (f32(levels_n, rows_n, cols_n), f32(rows_n, cols_n), f32(4, 2 * half, cols_n)),
         [
             pltpu.VMEM((levels_n * GROUP, 3 * tile), bf16),
             pltpu.VMEM((width, 3 * tile), bf16),
             pltpu.VMEM((levels_n * GROUP, width), jnp.float32),
         ],
-    )(returned, slot_cell, slot_weight, adjoint_in)
-    ocean = land_mask.astype(jnp.float32)
-    east_weight = east_coef - 0.5 * zonal_flow
-    own_east = east_coef + 0.5 * zonal_flow
-    west_column = from_behind(east_weight[:, -1:], "lon", 1)
-    west_weight = jnp.concatenate([west_column, east_weight[:, :-1]], axis=1)
-    south_row = from_behind_2(north_coef[-1:, :], "lat", 1)
-    south_weight = jnp.concatenate([south_row, north_coef[:-1, :]], axis=0)
-    lat_last = lax.axis_index("lat") == lax.axis_size("lat") - 1
-    zero_level = jnp.zeros((1, rows_n, cols_n), jnp.float32)
-    for repeat in range(STEPS):
-        masked = ocean * adjoint_state
-        zonal_pad = padded(masked, (("lon", 2),), 1, True)
-        merid_pad = padded(masked, (("lat", 1),), 1, False)
-        east_vals = zonal_pad[:, :, 2:]
-        west_vals = zonal_pad[:, :, :-2]
-        north_vals = merid_pad[:, 2:, :]
-        south_vals = merid_pad[:, :-2, :]
-        east_diff = masked - east_vals
-        north_diff = masked - north_vals
-        updated = adjoint_state - own_east * east_diff + west_weight * (west_vals - masked)
-        updated = updated - north_coef * north_diff + south_weight * (south_vals - masked)
-        fold_top = north_coef[-1][None, :] * masked[:, -1, :]
-        for bit_index in range(lax.axis_size("lon").bit_length() - 1):
-            fold_top = from_partner(fold_top, "lon", bit_index)
-        mirrored = fold_top[:, ::-1]
-        updated = updated.at[:, -1, :].add(jnp.where(lat_last, mirrored, 0.0))
-        vertical_term = vertical_coef[None] * (masked[:-1] - masked[1:])
-        updated = updated - jnp.concatenate([vertical_term, zero_level], axis=0)
-        updated = updated + jnp.concatenate([zero_level, vertical_term], axis=0)
-        adjoint_state = updated
+    )(returned, slot_cell, slot_weight, adjoint_in, land_mask)
+    side_columns = lon_swaps(own_columns)
+    message = kernel_call(edge_message_kernel, f32(8 * half + SUB, cols_n), (), True, 4)(
+        flags, own_edges, *side_columns
+    )
+    side_edges = lat_swaps(message)
+    extended = (levels_n, rows_n + 2 * SUB, cols_n)
+    adjoint_state = kernel_call(
+        steps_kernel,
+        f32(levels_n, rows_n, cols_n),
+        [
+            pltpu.VMEM(extended, jnp.float32),
+            pltpu.VMEM(extended, jnp.float32),
+            pltpu.VMEM((levels_n, rows_n, cols_n), jnp.float32),
+            pltpu.VMEM((STEPS, rows_n, cols_n), jnp.float32),
+        ],
+        True, 11,
+    )(flags, seed, fields, sides, edges, own_columns, own_edges, *side_columns, *side_edges)
     return (adjoint_state, misfit)
 
 

time: 127 us -> 85.1 us (0.67)
  the two profiles are of different devices: /device:TPU:7 before, /device:TPU:5 now
where the time goes in v2:
time: 85.1 us; the launch traced here: 84.7 us
  Pallas kernels  32.5 us (38%)
  starting transfers between devices  17.4 us (20%)
  blocking collectives  15.7 us (18%)
  waiting for transfers between devices  15.3 us (18%)
  local copies, waits for them, and re-layouts  2.86 us (3%)
    all_to_all x1, blocking collectives, on_device(): lax.all_to_all(partial_vals, BOTH, split_axis=0, concat_axis=0, tiled=True)  15.7 us
    pallas_call x1, Pallas kernels, on_device(): kernel_call(steps_kernel, f32(levels_n, rows_n, cols_n), [pltpu.VMEM(exte...  9.82 us
    pallas_call x1, Pallas kernels, on_device(): kernel_call(scatter_kernel, (f32(levels_n, rows_n, cols_n), f32(rows_n, c...  8.55 us
    ppermute x4, starting transfers between devices, lat_swaps(): found.append(lax.ppermute(value, BOTH, pairs))  8.11 us
    pallas_call x1, Pallas kernels, on_device(): kernel_call(gather_kernel, f32(devices, half, LANES), [pltpu.VMEM((levels...  7.75 us
    all_to_all x1, waiting for transfers between devices, on_device(): lax.all_to_all(outgoing, BOTH, split_axis=0, concat_axis=0, tiled=True)  6.61 us
    ppermute x2, starting transfers between devices, lon_swaps(): lax.ppermute(value, 'lon', second)  5.39 us
    ppermute x2, waiting for transfers between devices, lon_swaps(): lax.ppermute(value, 'lon', second)  4.46 us
  transfers between devices with their start and end apart: 9, of which 3 were waited for; matrix products, arithmetic and copies ran while one was open for 0% of the time, Pallas kernels for 13%

profile of v2, /device:TPU:5, one launch (start us, length us, event | category | flops | bytes accessed | tf_op | source)
XLA Modules:
  0.0 84.7 jit_solution(8125578261592826101)
XLA Ops:
  0.6 0.0 copy-start
  0.6 1.4 %copy-done = f32[25,128,128]{2,1,0:T(8,128)S(1)} copy-done((f32[25,128,128]{2,1,0:T(8,128)S(1)}, f32[25,128,128]{2,1,0:T(8,128)}, u32[]{:S(2)}) %copy-start) | copy-done | bytes 1638424
  2.1 0.7 copy-done.9
  2.8 0.7 copy-done.11
  3.5 0.0 copy-start.3
  3.5 0.0 copy-start.4
  3.5 0.0 copy-start.5
  3.5 0.0 copy-start.6
  3.5 0.0 copy-start.1
  3.5 0.0 copy-start.10
  3.5 0.0 copy-start.12
  3.5 7.7 %shard_map.131 = f32[32,16,128]{2,1,0:T(8,128)S(1)} custom-call(s32[1,2048]{1,0:T(1,128)S(1)} %copy-done.9, f32[1,2048]{1,0:T(1,128)S(1)} %copy-done.11, f32[25,128,128]{2,1,0:T(8,128)S(1)} %copy-done), custom_call_target="tpu_custom_call" | custom-call | tf_op jit(solution)/shard_map/pallas_call | solution.py:557
  11.3 15.7 %all_to_all.10.arrived_ref = f32[32,16,128]{2,1,0:T(8,128)S(1)} all-to-all(f32[32,16,128]{2,1,0:T(8,128)S(1)} %shard_map.131), channel_id=1, replica_groups=mesh['lon'=8,'lat'=4] {'lon','lat'}, dimensions={0} | all-to-all | bytes 524288 | tf_op jit(solution)/shard_map/all_to_all | solution.py:560
  27.0 0.0 copy-done.7
  27.0 0.0 copy-done.8
  27.0 0.0 copy-done.13
  27.0 4.1 %shard_map.132 = (f32[25,512]{1,0:T(8,128)}, f32[32,16,128]{2,1,0:T(8,128)}) custom-call(f32[32,16,128]{2,1,0:T(8,128)S(1)} %all_to_all.10.arrived_ref, s32[1,2048]{1,0:T(1,128)S(1)} %copy-done.13, f32[25,512]{1,0:T(8,128)S(1)} %copy-done.7, f32[25,512]{1,0:T(8,128)S(1)} %copy-done.8), custom_call_target="tpu_custom_call" | custom-call | tf_op jit(solution)/shard_map/pallas_call | solution.py:573
  31.1 3.6 %all-to-all-start.1 = ((f32[32,16,128]{2,1,0:T(8,128)}), f32[32,16,128]{2,1,0:T(8,128)S(1)}, u32[]{:S(2)}, u32[]{:S(2)}) async-start(f32[32,16,128]{2,1,0:T(8,128)} %get-tuple-element.10), calls=%async_computation.1 | async-start | bytes 524288 | tf_op jit(solution)/shard_map/all_to_all | solution.py:578
  34.7 0.0 copy-done.2
  34.7 0.0 copy-done.3
  34.7 0.0 copy-done.4
  34.7 0.0 copy-done.5
  34.7 0.0 copy-done.6
  34.7 0.2 shard_map.134
  35.0 4.2 %collective-permute-start.1 = (f32[128,128]{1,0:T(8,128)S(1)}, f32[128,128]{1,0:T(8,128)S(1)}, u32[]{:S(2)}, u32[]{:S(2)}) collective-permute-start(f32[128,128]{1,0:T(8,128)S(1)} %shard_map.134), channel_id=1, source_target_pairs={{0,28},{4,8},{8,4},{12,16},{16,12},{20,24},{24,20},{28,0},{1,29},{... | collective-permute-start | bytes 196616 | tf_op jit(solution)/shard_map/ppermute | solution.py:512
  39.1 0.0 collective-permute-start
  39.1 6.6 %all-to-all-done.1.returned_ref = f32[32,16,128]{2,1,0:T(8,128)S(1)} async-done(((f32[32,16,128]{2,1,0:T(8,128)}), f32[32,16,128]{2,1,0:T(8,128)S(1)}, u32[]{:S(2)}, u32[]{:S(2)}) %all-to-all-start.1) | async-done | bytes 262176 | tf_op jit(solution)/shard_map/all_to_all | solution.py:578
  45.8 0.0 copy-done.1
  45.8 8.5 %shard_map.133 = (f32[25,128,128]{2,1,0:T(8,128)S(1)}, f32[128,128]{1,0:T(8,128)S(1)}, f32[4,32,128]{2,1,0:T(8,128)S(1)}) custom-call(f32[32,16,128]{2,1,0:T(8,128)S(1)} %all-to-all-done.1.returned_ref, s32[1,2048]{1,0:T(1,128)S(1)} %copy-done.10, f32[1,2048]{1,0:T(1,128)S(1)} %copy-done.12, f32[25,128,128]{2,1,0:T(8,128)S(1)} %copy-done.1, ...), custom_call_target="tpu_custom_call" | custom-call | tf_op jit(solution)/shard_map/pallas_call | solution.py:580
  54.3 1.2 %collective-permute-start.5 = (f32[128,128]{1,0:T(8,128)S(1)}, f32[128,128]{1,0:T(8,128)S(1)}, u32[]{:S(2)}, u32[]{:S(2)}) collective-permute-start(f32[128,128]{1,0:T(8,128)S(1)} %get-tuple-element.15.columns_ref), channel_id=1, source_target_pairs={{0,28},{4,8},{8,4},{12,16},{16,12},{20,24},{24,20},{28,0},{1,29},{... | collective-permute-start | bytes 196616 | tf_op jit(solution)/shard_map/ppermute | solution.py:512
  55.5 0.4 collective-permute-start.4
  55.9 0.1 pad_add_fusion.flag_ref
  56.0 4.5 %collective-permute-done.5.second_ref.lon_second_ref = f32[128,128]{1,0:T(8,128)S(1)} collective-permute-done((f32[128,128]{1,0:T(8,128)S(1)}, f32[128,128]{1,0:T(8,128)S(1)}, u32[]{:S(2)}, u32[]{:S(2)}) %collective-permute-start.5) | collective-permute-done | bytes 65568 | tf_op jit(solution)/shard_map/ppermute | solution.py:512
  60.4 0.0 collective-permute-done.4.first_ref.lon_first_ref
  60.4 0.5 shard_map.137
  61.0 5.2 %collective-permute-start.7 = (f32[136,128]{1,0:T(8,128)S(1)}, f32[136,128]{1,0:T(8,128)S(1)}, u32[]{:S(2)}, u32[]{:S(2)}) collective-permute-start(f32[136,128]{1,0:T(8,128)S(1)} %shard_map.137), channel_id=1, source_target_pairs={{1,2},{2,1},{3,31},{5,6},{6,5},{7,27},{9,10},{10,9},{11,23},{13,14... | collective-permute-start | bytes 208904 | tf_op jit(solution)/shard_map/ppermute | solution.py:527
  66.2 0.1 collective-permute-start.6
  66.3 0.0 collective-permute-done.1.second_ref.lon_second_ref
  66.3 0.0 collective-permute-done.first_ref.lon_first_ref
  66.3 0.6 shard_map.135
  66.9 2.8 %collective-permute-start.3 = (f32[16,128]{1,0:T(8,128)S(1)}, f32[16,128]{1,0:T(8,128)S(1)}, u32[]{:S(2)}, u32[]{:S(2)}) collective-permute-start(f32[16,128]{1,0:T(8,128)S(1)} %shard_map.135), channel_id=1, source_target_pairs={{1,2},{2,1},{3,31},{5,6},{6,5},{7,27},{9,10},{10,9},{11,23},{13,14... | collective-permute-start | bytes 24584 | tf_op jit(solution)/shard_map/ppermute | solution.py:527
  69.7 0.1 collective-permute-start.2
  69.8 4.2 %collective-permute-done.3.lat_second_ref = f32[16,128]{1,0:T(8,128)S(1)} collective-permute-done((f32[16,128]{1,0:T(8,128)S(1)}, f32[16,128]{1,0:T(8,128)S(1)}, u32[]{:S(2)}, u32[]{:S(2)}) %collective-permute-start.3) | collective-permute-done | bytes 8224 | tf_op jit(solution)/shard_map/ppermute | solution.py:527
  74.0 0.0 collective-permute-done.2.lat_first_ref
  74.0 0.9 %shard_map.136 = (f32[7,128,128]{2,1,0:T(8,128)S(1)}, f32[128,128]{1,0:T(8,128)S(1)}, f32[16,128]{1,0:T(8,128)S(1)}) custom-call(s32[3]{0:T(128)S(1)} %pad_add_fusion.flag_ref, s32[128,128]{1,0:T(8,128)S(1)} %copy-done.2, f32[128,128]{1,0:T(8,128)S(1)} %copy-done.3, f32[128,128]{1,0:T(8,128)S(1)} %copy-done.4, f32[128,128]{1,0:T(8,128)S(1)} %copy-done.5, ...), custom_call_target="tpu_custom_call" | custom-call | tf_op jit(solution)/shard_map/pallas_call | solution.py:567
  74.9 0.0 collective-permute-done.7.lat_second_ref
  74.9 0.0 collective-permute-done.6.lat_first_ref
  74.9 9.8 %shard_map.138 = f32[25,128,128]{2,1,0:T(8,128)} custom-call(s32[3]{0:T(128)S(1)} %pad_add_fusion.flag_ref, f32[25,128,128]{2,1,0:T(8,128)S(1)} %get-tuple-element.11.seed_ref, f32[7,128,128]{2,1,0:T(8,128)S(1)} %get-tuple-element.12.field_ref, f32[128,128]{1,0:T(8,128)S(1)} %get-tuple-element.13.side_ref, f32[16,128]{1,0:T(8,128)S(1)} %get-tuple-element.14.edge_ref, ...), custom_call_target="tpu_custom_call" | custom-call | tf_op jit(solution)/shard_map/pallas_call | solution.py:595
  (8 shorter events, 0.0 us)
Async XLA Ops:
  0.6 1.4 %copy-start = (f32[25,128,128]{2,1,0:T(8,128)S(1)}, f32[25,128,128]{2,1,0:T(8,128)}, u32[]{:S(2)}) copy-start(f32[25,128,128]{2,1,0:T(8,128)} %state_ref.1) | copy-start | bytes 4915204
  2.1 0.7 copy-start.9
  2.8 0.7 copy-start.11
  3.5 23.6 %copy-start.7 = (f32[25,512]{1,0:T(8,128)S(1)}, f32[25,512]{1,0:T(8,128)}, u32[]{:S(2)}) copy-start(f32[25,512]{1,0:T(8,128)} %value_ref.1) | copy-start | bytes 153604
  3.5 23.6 %copy-start.8 = (f32[25,512]{1,0:T(8,128)S(1)}, f32[25,512]{1,0:T(8,128)}, u32[]{:S(2)}) copy-start(f32[25,512]{1,0:T(8,128)} %invvar_ref.1) | copy-start | bytes 153604
  3.5 23.6 %copy-start.13 = (s32[1,2048]{1,0:T(1,128)S(1)}, s32[1,2048]{1,0:T(1,128)}, u32[]{:S(2)}) copy-start(s32[1,2048]{1,0:T(1,128)} %target_ref.1) | copy-start | bytes 24580
  3.5 31.2 %copy-start.2 = (s32[128,128]{1,0:T(8,128)S(1)}, s32[128,128]{1,0:T(8,128)}, u32[]{:S(2)}) copy-start(s32[128,128]{1,0:T(8,128)} %mask_ref.7) | copy-start | bytes 196612
  3.5 31.2 %copy-start.3 = (f32[128,128]{1,0:T(8,128)S(1)}, f32[128,128]{1,0:T(8,128)}, u32[]{:S(2)}) copy-start(f32[128,128]{1,0:T(8,128)} %east_ref.5) | copy-start | bytes 196612
  3.5 31.2 %copy-start.4 = (f32[128,128]{1,0:T(8,128)S(1)}, f32[128,128]{1,0:T(8,128)}, u32[]{:S(2)}) copy-start(f32[128,128]{1,0:T(8,128)} %north_ref.5) | copy-start | bytes 196612
  3.5 31.2 %copy-start.5 = (f32[128,128]{1,0:T(8,128)S(1)}, f32[128,128]{1,0:T(8,128)}, u32[]{:S(2)}) copy-start(f32[128,128]{1,0:T(8,128)} %flow_ref.5) | copy-start | bytes 196612
  3.5 31.2 %copy-start.6 = (f32[128,128]{1,0:T(8,128)S(1)}, f32[128,128]{1,0:T(8,128)}, u32[]{:S(2)}) copy-start(f32[128,128]{1,0:T(8,128)} %vertical_ref.5) | copy-start | bytes 196612
  3.5 42.2 %copy-start.1 = (f32[25,128,128]{2,1,0:T(8,128)S(1)}, f32[25,128,128]{2,1,0:T(8,128)}, u32[]{:S(2)}) copy-start(f32[25,128,128]{2,1,0:T(8,128)} %adjoint_ref.1) | copy-start | bytes 4915204
  3.5 42.2 %copy-start.10 = (s32[1,2048]{1,0:T(1,128)S(1)}, s32[1,2048]{1,0:T(1,128)}, u32[]{:S(2)}) copy-start(s32[1,2048]{1,0:T(1,128)} %cell_ref.3) | copy-start | bytes 24580
  3.5 42.2 %copy-start.12 = (f32[1,2048]{1,0:T(1,128)S(1)}, f32[1,2048]{1,0:T(1,128)}, u32[]{:S(2)}) copy-start(f32[1,2048]{1,0:T(1,128)} %weight_ref.3) | copy-start | bytes 24580
  31.1 14.6 %all-to-all-start.1 = ((f32[32,16,128]{2,1,0:T(8,128)}), f32[32,16,128]{2,1,0:T(8,128)S(1)}, u32[]{:S(2)}, u32[]{:S(2)}) async-start(f32[32,16,128]{2,1,0:T(8,128)} %get-tuple-element.10), calls=%async_computation.1 | async-start | bytes 524288 | tf_op jit(solution)/shard_map/all_to_all | solution.py:578
  35.0 31.3 %collective-permute-start.1 = (f32[128,128]{1,0:T(8,128)S(1)}, f32[128,128]{1,0:T(8,128)S(1)}, u32[]{:S(2)}, u32[]{:S(2)}) collective-permute-start(f32[128,128]{1,0:T(8,128)S(1)} %shard_map.134), channel_id=1, source_target_pairs={{0,28},{4,8},{8,4},{12,16},{16,12},{20,24},{24,20},{28,0},{1,29},{... | collective-permute-start | bytes 196616 | tf_op jit(solution)/shard_map/ppermute | solution.py:512
  39.1 27.2 %collective-permute-start = (f32[128,128]{1,0:T(8,128)S(1)}, f32[128,128]{1,0:T(8,128)S(1)}, u32[]{:S(2)}, u32[]{:S(2)}) collective-permute-start(f32[128,128]{1,0:T(8,128)S(1)} %shard_map.134), channel_id=1, source_target_pairs={{0,4},{4,0},{8,12},{12,8},{16,20},{20,16},{24,28},{28,24},{1,5},{5... | collective-permute-start | bytes 196616 | tf_op jit(solution)/shard_map/ppermute | solution.py:512
  54.3 6.1 %collective-permute-start.5 = (f32[128,128]{1,0:T(8,128)S(1)}, f32[128,128]{1,0:T(8,128)S(1)}, u32[]{:S(2)}, u32[]{:S(2)}) collective-permute-start(f32[128,128]{1,0:T(8,128)S(1)} %get-tuple-element.15.columns_ref), channel_id=1, source_target_pairs={{0,28},{4,8},{8,4},{12,16},{16,12},{20,24},{24,20},{28,0},{1,29},{... | collective-permute-start | bytes 196616 | tf_op jit(solution)/shard_map/ppermute | solution.py:512
  55.5 4.9 %collective-permute-start.4 = (f32[128,128]{1,0:T(8,128)S(1)}, f32[128,128]{1,0:T(8,128)S(1)}, u32[]{:S(2)}, u32[]{:S(2)}) collective-permute-start(f32[128,128]{1,0:T(8,128)S(1)} %get-tuple-element.15.columns_ref), channel_id=1, source_target_pairs={{0,4},{4,0},{8,12},{12,8},{16,20},{20,16},{24,28},{28,24},{1,5},{5... | collective-permute-start | bytes 196616 | tf_op jit(solution)/shard_map/ppermute | solution.py:512
  61.0 13.9 %collective-permute-start.7 = (f32[136,128]{1,0:T(8,128)S(1)}, f32[136,128]{1,0:T(8,128)S(1)}, u32[]{:S(2)}, u32[]{:S(2)}) collective-permute-start(f32[136,128]{1,0:T(8,128)S(1)} %shard_map.137), channel_id=1, source_target_pairs={{1,2},{2,1},{3,31},{5,6},{6,5},{7,27},{9,10},{10,9},{11,23},{13,14... | collective-permute-start | bytes 208904 | tf_op jit(solution)/shard_map/ppermute | solution.py:527
  66.2 8.7 %collective-permute-start.6 = (f32[136,128]{1,0:T(8,128)S(1)}, f32[136,128]{1,0:T(8,128)S(1)}, u32[]{:S(2)}, u32[]{:S(2)}) collective-permute-start(f32[136,128]{1,0:T(8,128)S(1)} %shard_map.137), channel_id=1, source_target_pairs={{0,1},{1,0},{2,3},{3,2},{4,5},{5,4},{6,7},{7,6},{8,9},{9,8},{10,11... | collective-permute-start | bytes 208904 | tf_op jit(solution)/shard_map/ppermute | solution.py:527
  66.9 7.1 %collective-permute-start.3 = (f32[16,128]{1,0:T(8,128)S(1)}, f32[16,128]{1,0:T(8,128)S(1)}, u32[]{:S(2)}, u32[]{:S(2)}) collective-permute-start(f32[16,128]{1,0:T(8,128)S(1)} %shard_map.135), channel_id=1, source_target_pairs={{1,2},{2,1},{3,31},{5,6},{6,5},{7,27},{9,10},{10,9},{11,23},{13,14... | collective-permute-start | bytes 24584 | tf_op jit(solution)/shard_map/ppermute | solution.py:527
  69.7 4.3 %collective-permute-start.2 = (f32[16,128]{1,0:T(8,128)S(1)}, f32[16,128]{1,0:T(8,128)S(1)}, u32[]{:S(2)}, u32[]{:S(2)}) collective-permute-start(f32[16,128]{1,0:T(8,128)S(1)} %shard_map.135), channel_id=1, source_target_pairs={{0,1},{1,0},{2,3},{3,2},{4,5},{5,4},{6,7},{7,6},{8,9},{9,8},{10,11... | collective-permute-start | bytes 24584 | tf_op jit(solution)/shard_map/ppermute | solution.py:527

commit v3 on v2

--- a/solution.py
+++ b/solution.py
@@ -134,32 +134,109 @@
     lax.fori_loop(0, target_ref.shape[1] // tile, store, 0)
 
 
+def returned_values(returned_ref, cell_ref, weight_ref, start, tile):
+    at = pl.ds(pl.multiple_of(start, tile), tile)
+    weight = jnp.where(cell_ref[:, at] >= 0, weight_ref[:, at], 0.0)
+    base = start // (LANES // 2)
+    values = jnp.concatenate(
+        [
+            unpacked_pair(returned_ref[base + 2 * pair], returned_ref[base + 2 * pair + 1])
+            for pair in range(tile // LANES)
+        ],
+        axis=1,
+    )
+    return pieces(values * weight)
+
+
+def across(left, right):
+    return lax.dot_general(
+        left, right, (((1,), (1,)), ((), ())), preferred_element_type=jnp.float32
+    )
+
+
+def seed_strips_kernel(adjoint_ref, mask_ref, columns_ref, ocean_ref, edges_ref):
+    levels_n, rows_n, cols_n = adjoint_ref.shape
+    level_at = jnp.right_shift(lane((SUB, cols_n)), 2)
+    for top in range(0, rows_n, SUB):
+        at = slice(top, top + SUB)
+        found = jnp.zeros((SUB, cols_n), jnp.float32)
+        for level in range(levels_n):
+            block = pltpu.roll(adjoint_ref[level, at, :], (4 * level + 2) % cols_n, 1)
+            found = jnp.where(level_at == level, block, found)
+        columns_ref[at, :] = found
+        spread = jnp.where(level_at == 0, pltpu.roll(mask_ref[at, :].astype(jnp.float32), 2, 1), 0.0)
+        shift = 4
+        while shift < cols_n:
+            spread = spread + pltpu.roll(spread, shift, 1)
+            shift *= 2
+        ocean_ref[at, :] = spread
+    places, levels, _ = edges_ref.shape
+    for place, row in enumerate((0, 1, rows_n - 2, rows_n - 1)):
+        for level in range(levels_n):
+            edges_ref[place, level : level + 1, :] = adjoint_ref[level, row : row + 1, :]
+        edges_ref[place, levels_n:, :] = jnp.zeros((levels - levels_n, cols_n), jnp.float32)
+
+
+def strips_kernel(
+    returned_ref, cell_ref, weight_ref, mask_ref, seed_columns_ref, ocean_ref, seed_edges_ref,
+    columns_ref, edges_ref,
+    left_ref, right_ref,
+):
+    rows_n, cols_n = mask_ref.shape
+    places, levels, _ = edges_ref.shape
+    slots = cell_ref.shape[1]
+    tile = left_ref.shape[1] // 3
+    column_sum = jnp.zeros((rows_n, LANES), jnp.float32)
+    edge_sum = jnp.zeros((places * levels, cols_n), jnp.float32)
+    for start in range(0, slots, tile):
+        cell = jnp.maximum(cell_ref[:, start : start + tile], 0)
+        row, column = jnp.right_shift(cell, log2(cols_n)), jnp.bitwise_and(cell, cols_n - 1)
+        values = returned_values(returned_ref, cell_ref, weight_ref, start, tile)
+
+        def chosen(index, wanted):
+            for place, number in enumerate(wanted):
+                here = jnp.where(index == number, 1.0, 0.0).astype(jnp.bfloat16)
+                for part in range(3):
+                    right_ref[place * levels : (place + 1) * levels, part * tile : (part + 1) * tile] = (
+                        values[part] * here
+                    )
+
+        def repeated(hot):
+            for part in range(3):
+                left_ref[:, part * tile : (part + 1) * tile] = hot
+
+        repeated(one_hot(row, rows_n))
+        chosen(column, (cols_n - 2, cols_n - 1, 0, 1))
+        column_sum += across(left_ref[...], right_ref[...])
+        repeated(one_hot(column, cols_n))
+        chosen(row, (0, 1, rows_n - 2, rows_n - 1))
+        edge_sum += across(right_ref[...], left_ref[...])
+    source, target = sublane((LANES, LANES)), lane((LANES, LANES))
+    turn = jnp.bitwise_and(target, 3) * levels + jnp.right_shift(target, 2)
+    turn = jnp.where(source == turn, 1.0, 0.0).astype(jnp.bfloat16)
+    column_sum = sum(
+        jnp.dot(piece, turn, preferred_element_type=jnp.float32) for piece in pieces(column_sum)
+    )
+    columns_ref[...] = (seed_columns_ref[...] + column_sum) * ocean_ref[...]
+    for place, row in enumerate((0, 1, rows_n - 2, rows_n - 1)):
+        ocean = mask_ref[row : row + 1, :].astype(jnp.float32)
+        forcing = edge_sum[place * levels : (place + 1) * levels]
+        edges_ref[place] = (seed_edges_ref[place] + forcing) * ocean
+
+
 def scatter_kernel(
-    returned_ref, cell_ref, weight_ref, adjoint_ref, mask_ref,
-    out_ref, columns_ref, edges_ref,
-    rows_ref, hot_ref, sum_ref,
+    returned_ref, cell_ref, weight_ref, adjoint_ref, field_ref,
+    out_ref,
+    rows_ref, hot_ref, seed_ref, masked_ref,
 ):
     levels_n, rows_n, cols_n = out_ref.shape
     groups = rows_n // GROUP
     width = groups * cols_n
     tile = hot_ref.shape[1] // 3
-
-    sum_ref[...] = jnp.zeros_like(sum_ref)
-
-    def body(step, carry):
-        at = pl.ds(pl.multiple_of(step * tile, tile), tile)
-        cell = cell_ref[:, at]
-        weight = jnp.where(cell >= 0, weight_ref[:, at], 0.0)
-        place, row = cell_parts(cell, rows_n, cols_n)
-        base = step * (2 * tile // LANES)
-        values = jnp.concatenate(
-            [
-                unpacked_pair(returned_ref[base + 2 * pair], returned_ref[base + 2 * pair + 1])
-                for pair in range(tile // LANES)
-            ],
-            axis=1,
-        )
-        values = pieces(values * weight)
+    total = None
+    for start in range(0, cell_ref.shape[1], tile):
+        place, row = cell_parts(cell_ref[:, start : start + tile], rows_n, cols_n)
+        values = returned_values(returned_ref, cell_ref, weight_ref, start, tile)
         hot = one_hot(place, width)
         mine = one_hot(row, GROUP)
         for part in range(3):
@@ -168,35 +245,58 @@
                 rows_ref[level * GROUP : (level + 1) * GROUP, part * tile : (part + 1) * tile] = (
                     mine * values[part][level : level + 1, :]
                 )
-        sum_ref[...] += lax.dot_general(
-            rows_ref[...], hot_ref[...], (((1,), (1,)), ((), ())), preferred_element_type=jnp.float32
-        )
-        return carry
-
-    lax.fori_loop(0, cell_ref.shape[1] // tile, body, 0)
+        found = across(rows_ref[...], hot_ref[...])
+        total = found if total is None else total + found
+    zero = jnp.zeros((1, cols_n), jnp.float32)
+    for level in range(levels_n):
+        masked_ref[level, SUB - 1 : SUB, :] = zero
+        masked_ref[level, SUB + rows_n : SUB + rows_n + 1, :] = zero
     for group in range(groups):
         at = slice(group * GROUP, (group + 1) * GROUP)
-        forcing = sum_ref[:, group * cols_n : (group + 1) * cols_n]
-        out_ref[:, at, :] = adjoint_ref[:, at, :] + forcing.reshape(levels_n, GROUP, cols_n)
-
-    level_at = jnp.right_shift(lax.broadcasted_iota(jnp.int32, (SUB, cols_n), 1), 2)
+        forcing = total[:, group * cols_n : (group + 1) * cols_n].reshape(levels_n, GROUP, cols_n)
+        seed = adjoint_ref[:, at, :] + forcing
+        seed_ref[:, at, :] = seed
+        masked_ref[:, SUB + group * GROUP : SUB + (group + 1) * GROUP, :] = seed * field_ref[0, at, :]
+
+    def store(level, top, ocean, found):
+        out_ref[level, top : top + SUB, :] = found
+
+    advance(seed_ref, masked_ref, field_ref, None, store)
+
+
+def advance(source_ref, from_ref, field_ref, turn_ref, store):
+    levels_n, rows_n, cols_n = source_ref.shape
+    first = lane((SUB, cols_n)) == 0
+    last = lane((SUB, cols_n)) == cols_n - 1
     for top in range(0, rows_n, SUB):
-        ocean = mask_ref[top : top + SUB, :].astype(jnp.float32)
-        found = jnp.zeros((SUB, cols_n), jnp.float32)
+        at, inner = slice(top, top + SUB), slice(top + SUB, top + 2 * SUB)
+        ocean, own, here, back, onto, south_at, mixing = (
+            field_ref[place, at, :] for place in range(7)
+        )
+        if turn_ref is None:
+            here_in, back_in = jnp.where(last, 0.0, here), jnp.where(first, 0.0, back)
+        else:
+            turned = turn_ref[at, :]
+        higher = block = from_ref[0, inner, :]
         for level in range(levels_n):
-            block = pltpu.roll(out_ref[level, top : top + SUB, :], 4 * level + 2, 1)
-            found = jnp.where(level_at == level, block, found)
-        sides = pltpu.roll(ocean, 2, 1)
-        spread = jnp.where(level_at == 0, sides, 0.0)
-        shift = 4
-        while shift < cols_n:
-            spread = spread + pltpu.roll(spread, shift, 1)
-            shift *= 2
-        columns_ref[top : top + SUB, :] = found * spread
-    for place, row in enumerate((0, 1, rows_n - 2, rows_n - 1)):
-        ocean = mask_ref[row : row + 1, :].astype(jnp.float32)
-        for level in range(levels_n):
-            edges_ref[place, level : level + 1, :] = out_ref[level, row : row + 1, :] * ocean
+            lower = from_ref[level + 1, inner, :] if level + 1 < levels_n else block
+            eastern, western = pltpu.roll(block, cols_n - 1, 1), pltpu.roll(block, 1, 1)
+            if turn_ref is None:
+                sides = here_in * eastern + back_in * western
+            else:
+                beyond = pltpu.roll(turned, (2 * cols_n - 2 - 4 * level) % cols_n, 1)
+                sides = here * jnp.where(last, beyond, eastern) + back * jnp.where(first, beyond, western)
+            north = from_ref[level, top + SUB + 1 : top + 2 * SUB + 1, :]
+            south = from_ref[level, top + SUB - 1 : top + 2 * SUB - 1, :]
+            vertical = (higher - block) + (lower - block)
+            found = (
+                (source_ref[level, at, :] - own * block)
+                + sides
+                + (onto * north + south_at * south)
+                + mixing * vertical
+            )
+            store(level, top, ocean, found)
+            higher, block = block, lower
 
 
 def lane(shape):
@@ -346,12 +446,12 @@
 
 
 def steps_kernel(
-    flag_ref, seed_ref, field_ref, side_ref, edge_ref,
+    flag_ref, inner_ref, field_ref, side_ref, edge_ref,
     columns_ref, edges_ref, lon_first_ref, lon_second_ref, lat_first_ref, lat_second_ref,
     out_ref,
-    masked_ref, next_ref, half_ref, turn_ref,
+    masked_ref, half_ref, turn_ref,
 ):
-    levels_n, rows_n, cols_n = seed_ref.shape
+    levels_n, rows_n, cols_n = inner_ref.shape
     levels = edges_ref.shape[1]
     fold = flag_ref[2] == 1
     east, west = lon_neighbours(flag_ref, lon_first_ref[...], lon_second_ref[...])
@@ -430,59 +530,32 @@
         below, below_outer, edges_ref[0], corner(east_down, 2), corner(west_down, 1), SUB
     )
     for level in range(levels_n):
-        for ref, high, low in ((masked_ref, above, below), (next_ref, above_next, below_next)):
-            ref[level, SUB + rows_n : SUB + rows_n + 1, :] = high[level : level + 1, :]
-            ref[level, SUB - 1 : SUB, :] = low[level : level + 1, :]
-
-    def mask(level, carry):
-        masked_ref[level, SUB : SUB + rows_n, :] = field_ref[0] * seed_ref[level]
-        return carry
-
-    lax.fori_loop(0, levels_n, mask, 0)
+        masked_ref[level, SUB + rows_n : SUB + rows_n + 1, :] = above_next[level : level + 1, :]
+        masked_ref[level, SUB - 1 : SUB, :] = below_next[level : level + 1, :]
     first = lane((SUB, cols_n)) == 0
     last = lane((SUB, cols_n)) == cols_n - 1
-
-    def advance(step, level, source_ref, from_ref, store):
-        higher, lower = jnp.maximum(level - 1, 0), jnp.minimum(level + 1, levels_n - 1)
-        turn = lax.rem(2 * cols_n - 2 - 4 * level, cols_n)
-        for top in range(0, rows_n, SUB):
-            at = slice(top, top + SUB)
-            inner = slice(SUB + top, 2 * SUB + top)
-            block = from_ref[level, inner, :]
-            sides = pltpu.roll(turn_ref[step, at, :], turn, 1)
-            eastern = jnp.where(last, sides, pltpu.roll(block, cols_n - 1, 1))
-            western = jnp.where(first, sides, pltpu.roll(block, 1, 1))
-            north = from_ref[level, SUB + top + 1 : 2 * SUB + top + 1, :]
-            south = from_ref[level, SUB + top - 1 : 2 * SUB + top - 1, :]
-            vertical = (from_ref[higher, inner, :] - block) + (from_ref[lower, inner, :] - block)
-            found = (
-                source_ref[level, at, :]
-                - field_ref[1, at, :] * block
-                + field_ref[2, at, :] * eastern
-                + field_ref[3, at, :] * western
-                + field_ref[4, at, :] * north
-                + field_ref[5, at, :] * south
-                + field_ref[6, at, :] * vertical
-            )
-            store(level, top, found)
-
-    def keep(level, top, found):
-        half_ref[level, top : top + SUB, :] = found
-        next_ref[level, SUB + top : 2 * SUB + top, :] = field_ref[0, top : top + SUB, :] * found
-
-    def finish(level, top, found):
+    for top in range(0, rows_n, SUB):
+        at, inner = slice(top, top + SUB), slice(top + SUB, top + 2 * SUB)
+        ocean = field_ref[0, at, :]
+        side = jnp.where(last, field_ref[2, at, :], jnp.where(first, field_ref[3, at, :], 0.0))
+        turned = turn_ref[0, at, :]
+        place = sublane((SUB, cols_n))
+        for level in range(levels_n):
+            beyond = pltpu.roll(turned, (2 * cols_n - 2 - 4 * level) % cols_n, 1)
+            found = inner_ref[level, at, :] + side * beyond
+            if top == 0:
+                below_row = field_ref[5, 0:1, :] * below[level : level + 1, :]
+                found = found + jnp.where(place == 0, below_row, 0.0)
+            if top == rows_n - SUB:
+                above_row = field_ref[4, rows_n - 1 : rows_n, :] * above[level : level + 1, :]
+                found = found + jnp.where(place == SUB - 1, above_row, 0.0)
+            half_ref[level, at, :] = found
+            masked_ref[level, inner, :] = ocean * found
+
+    def store(level, top, ocean, found):
         out_ref[level, top : top + SUB, :] = found
 
-    def first_step(level, carry):
-        advance(0, level, seed_ref, masked_ref, keep)
-        return carry
-
-    def second_step(level, carry):
-        advance(1, level, half_ref, next_ref, finish)
-        return carry
-
-    lax.fori_loop(0, levels_n, first_step, 0)
-    lax.fori_loop(0, levels_n, second_step, 0)
+    advance(half_ref, masked_ref, field_ref, turn_ref.at[1], store)
 
 
 def kernel_call(body, out_shape, scratch=(), flagged=False, inputs=0):
@@ -557,52 +630,68 @@
     partial_vals = kernel_call(
         gather_kernel, f32(devices, half, LANES), [pltpu.VMEM((levels_n * GROUP, 3 * width), bf16)]
     )(slot_cell, slot_weight, state)
+    columns = kernel_call(coefficient_columns_kernel, f32(rows_n, cols_n))(*raw)
+    partial_vals, columns = lax.optimization_barrier((partial_vals, columns))
     arrived = lax.all_to_all(partial_vals, BOTH, split_axis=0, concat_axis=0, tiled=True)
-
-    side_coefs = lon_swaps(kernel_call(coefficient_columns_kernel, f32(rows_n, cols_n))(*raw))
+    arrived, side_coefs = lax.optimization_barrier((arrived, lon_swaps(columns)))
     row_coefs = kernel_call(coefficient_rows_kernel, f32(2 * SUB, cols_n), (), True, 8)(
         flags, *raw, *side_coefs
     )
-    edge_coefs = lat_swaps(row_coefs)
-    fields, sides, edges = kernel_call(
-        coefficients_kernel,
-        (f32(7, rows_n, cols_n), f32(rows_n, cols_n), f32(2 * SUB, cols_n)),
-        (), True, 10,
-    )(flags, *raw, *side_coefs, *edge_coefs)
-
     misfit, outgoing = kernel_call(
         observe_kernel,
         (f32(levels_n, obs_n), f32(devices, half, LANES)),
         [pltpu.VMEM((obs_n, slots), bf16), pltpu.VMEM((6 * half, slots), bf16)],
     )(arrived, arrive_obs, obs_value, obs_invvar)
+    outgoing, row_coefs, adjoint_in, land_mask = lax.optimization_barrier(
+        (outgoing, row_coefs, adjoint_in, land_mask)
+    )
     returned = lax.all_to_all(outgoing, BOTH, split_axis=0, concat_axis=0, tiled=True)
-    tile = 4 * LANES
-    seed, own_columns, own_edges = kernel_call(
+    levels = 2 * half
+    fields, sides, edges = kernel_call(
+        coefficients_kernel,
+        (f32(7, rows_n, cols_n), f32(rows_n, cols_n), f32(2 * SUB, cols_n)),
+        (), True, 10,
+    )(flags, *raw, *side_coefs, *lat_swaps(row_coefs))
+    strips = kernel_call(
+        seed_strips_kernel,
+        (f32(rows_n, cols_n), f32(rows_n, cols_n), f32(4, levels, cols_n)),
+    )(adjoint_in, land_mask)
+    returned, fields, sides, edges, strips = lax.optimization_barrier(
+        (returned, fields, sides, edges, strips)
+    )
+    tile = min(slots, 16 * LANES)
+    own_columns, own_edges = kernel_call(
+        strips_kernel,
+        (f32(rows_n, cols_n), f32(4, levels, cols_n)),
+        [pltpu.VMEM((rows_n, 3 * tile), bf16), pltpu.VMEM((4 * levels, 3 * tile), bf16)],
+    )(returned, slot_cell, slot_weight, land_mask, *strips)
+    side_columns = lon_swaps(own_columns)
+    extended = (levels_n, rows_n + 2 * SUB, cols_n)
+    inner = kernel_call(
         scatter_kernel,
-        (f32(levels_n, rows_n, cols_n), f32(rows_n, cols_n), f32(4, 2 * half, cols_n)),
+        f32(levels_n, rows_n, cols_n),
         [
             pltpu.VMEM((levels_n * GROUP, 3 * tile), bf16),
             pltpu.VMEM((width, 3 * tile), bf16),
-            pltpu.VMEM((levels_n * GROUP, width), jnp.float32),
+            pltpu.VMEM((levels_n, rows_n, cols_n), jnp.float32),
+            pltpu.VMEM(extended, jnp.float32),
         ],
-    )(returned, slot_cell, slot_weight, adjoint_in, land_mask)
-    side_columns = lon_swaps(own_columns)
+    )(returned, slot_cell, slot_weight, adjoint_in, fields)
+    inner, side_columns = lax.optimization_barrier((inner, side_columns))
     message = kernel_call(edge_message_kernel, f32(8 * half + SUB, cols_n), (), True, 4)(
         flags, own_edges, *side_columns
     )
     side_edges = lat_swaps(message)
-    extended = (levels_n, rows_n + 2 * SUB, cols_n)
     adjoint_state = kernel_call(
         steps_kernel,
         f32(levels_n, rows_n, cols_n),
         [
             pltpu.VMEM(extended, jnp.float32),
-            pltpu.VMEM(extended, jnp.float32),
             pltpu.VMEM((levels_n, rows_n, cols_n), jnp.float32),
             pltpu.VMEM((STEPS, rows_n, cols_n), jnp.float32),
         ],
         True, 11,
-    )(flags, seed, fields, sides, edges, own_columns, own_edges, *side_columns, *side_edges)
+    )(flags, inner, fields, sides, edges, own_columns, own_edges, *side_columns, *side_edges)
     return (adjoint_state, misfit)
 
 

time: 85.1 us -> 70.1 us (0.82)
  the two profiles are of different devices: /device:TPU:5 before, /device:TPU:7 now
where the time goes in v3:
time: 70.1 us; the launch traced here: 69.7 us
  Pallas kernels  28.9 us (41%)
  starting transfers between devices  28.1 us (40%)
  waiting for transfers between devices  8.88 us (13%)
  local copies, waits for them, and re-layouts  2.87 us (4%)
  between operations  0.87 us (1%)
    ppermute x4, starting transfers between devices, lat_swaps(): found.append(lax.ppermute(value, BOTH, pairs))  9.06 us
    pallas_call x1, Pallas kernels, on_device(): kernel_call(gather_kernel, f32(devices, half, LANES), [pltpu.VMEM((levels...  8.46 us
    pallas_call x1, Pallas kernels, on_device(): kernel_call(scatter_kernel, f32(levels_n, rows_n, cols_n), [pltpu.VMEM((l...  6.39 us
    all_to_all x1, starting transfers between devices, on_device(): lax.all_to_all(partial_vals, BOTH, split_axis=0, concat_axis=0, tiled=True)  6.39 us
    all_to_all x1, starting transfers between devices, on_device(): lax.all_to_all(outgoing, BOTH, split_axis=0, concat_axis=0, tiled=True)  4.88 us
    ppermute x2, starting transfers between devices, lon_swaps(): lax.ppermute(value, 'lon', first)  4.69 us
    ppermute x4, waiting for transfers between devices, lat_swaps(): found.append(lax.ppermute(value, BOTH, pairs))  4.22 us
    pallas_call x1, Pallas kernels, on_device(): kernel_call(observe_kernel, (f32(levels_n, obs_n), f32(devices, half, LAN...  4.09 us
  transfers between devices with their start and end apart: 10, of which 5 were waited for; matrix products, arithmetic and copies ran while one was open for 0% of the time, Pallas kernels for 14%

profile of v3, /device:TPU:7, one launch (start us, length us, event | category | flops | bytes accessed | tf_op | source)
XLA Modules:
  0.0 69.7 jit_solution(16750255030656035508)
XLA Ops:
  0.6 0.0 copy-start.1
  0.6 1.4 %copy-done.1 = f32[25,128,128]{2,1,0:T(8,128)S(1)} copy-done((f32[25,128,128]{2,1,0:T(8,128)S(1)}, f32[25,128,128]{2,1,0:T(8,128)}, u32[]{:S(2)}) %copy-start.1) | copy-done | bytes 1638424
  2.1 0.7 copy-done.7
  2.8 0.7 copy-done.9
  3.5 0.0 copy-start.6
  3.5 0.0 copy-start.11
  3.5 0.0 copy-start.12
  3.5 0.0 copy-start.13
  3.5 8.5 %shard_map.131 = f32[32,16,128]{2,1,0:T(8,128)} custom-call(s32[1,2048]{1,0:T(1,128)S(1)} %copy-done.7, f32[1,2048]{1,0:T(1,128)S(1)} %copy-done.9, f32[25,128,128]{2,1,0:T(8,128)S(1)} %copy-done.1), custom_call_target="tpu_custom_call" | custom-call | tf_op jit(solution)/shard_map/pallas_call | solution.py:630
  12.0 0.0 copy-done.2
  12.0 0.0 copy-done.3
  12.0 0.0 copy-done.4
  12.0 0.0 copy-done.5
  12.0 0.0 copy-start
  12.0 0.2 shard_map.132
  12.2 6.4 %all-to-all-start = ((f32[32,16,128]{2,1,0:T(8,128)}), f32[32,16,128]{2,1,0:T(8,128)S(1)}, u32[]{:S(2)}, u32[]{:S(2)}) async-start(f32[32,16,128]{2,1,0:T(8,128)} %shard_map.131), calls=%async_computation | async-start | bytes 524288 | tf_op jit(solution)/shard_map/all_to_all | solution.py:635
  18.6 1.3 %collective-permute-start.1 = (f32[128,128]{1,0:T(8,128)S(1)}, f32[128,128]{1,0:T(8,128)S(1)}, u32[]{:S(2)}, u32[]{:S(2)}) collective-permute-start(f32[128,128]{1,0:T(8,128)S(1)} %shard_map.132), channel_id=1, source_target_pairs={{0,28},{4,8},{8,4},{12,16},{16,12},{20,24},{24,20},{28,0},{1,29},{... | collective-permute-start | bytes 196616 | tf_op jit(solution)/shard_map/ppermute | solution.py:585
  19.9 3.1 %collective-permute-start = (f32[128,128]{1,0:T(8,128)S(1)}, f32[128,128]{1,0:T(8,128)S(1)}, u32[]{:S(2)}, u32[]{:S(2)}) collective-permute-start(f32[128,128]{1,0:T(8,128)S(1)} %shard_map.132), channel_id=1, source_target_pairs={{0,4},{4,0},{8,12},{12,8},{16,20},{20,16},{24,28},{28,24},{1,5},{5... | collective-permute-start | bytes 196616 | tf_op jit(solution)/shard_map/ppermute | solution.py:585
  23.0 0.1 pad_add_fusion.flag_ref
  23.0 2.1 %collective-permute-done.1.second_ref.lon_second_ref = f32[128,128]{1,0:T(8,128)S(1)} collective-permute-done((f32[128,128]{1,0:T(8,128)S(1)}, f32[128,128]{1,0:T(8,128)S(1)}, u32[]{:S(2)}, u32[]{:S(2)}) %collective-permute-start.1) | collective-permute-done | bytes 65568 | tf_op jit(solution)/shard_map/ppermute | solution.py:585
  25.1 1.6 %collective-permute-done.first_ref.lon_first_ref = f32[128,128]{1,0:T(8,128)S(1)} collective-permute-done((f32[128,128]{1,0:T(8,128)S(1)}, f32[128,128]{1,0:T(8,128)S(1)}, u32[]{:S(2)}, u32[]{:S(2)}) %collective-permute-start) | collective-permute-done | bytes 65568 | tf_op jit(solution)/shard_map/ppermute | solution.py:585
  26.7 1.0 %all-to-all-done.arrived_ref = f32[32,16,128]{2,1,0:T(8,128)S(1)} async-done(((f32[32,16,128]{2,1,0:T(8,128)}), f32[32,16,128]{2,1,0:T(8,128)S(1)}, u32[]{:S(2)}, u32[]{:S(2)}) %all-to-all-start) | async-done | bytes 262176 | tf_op jit(solution)/shard_map/all_to_all | solution.py:635
  27.7 0.6 shard_map.134
  28.3 0.0 copy-done.11
  28.3 0.0 copy-start.8
  28.3 0.0 copy-start.10
  28.3 4.1 %shard_map.133 = (f32[25,512]{1,0:T(8,128)}, f32[32,16,128]{2,1,0:T(8,128)}) custom-call(f32[32,16,128]{2,1,0:T(8,128)S(1)} %all-to-all-done.arrived_ref, s32[1,2048]{1,0:T(1,128)S(1)} %copy-done.13, f32[25,512]{1,0:T(8,128)S(1)} %copy-done.11, f32[25,512]{1,0:T(8,128)S(1)} %copy-done.12), custom_call_target="tpu_custom_call" | custom-call | tf_op jit(solution)/shard_map/pallas_call | solution.py:640
  32.4 4.9 %all-to-all-start.1 = ((f32[32,16,128]{2,1,0:T(8,128)}), f32[32,16,128]{2,1,0:T(8,128)S(1)}, u32[]{:S(2)}, u32[]{:S(2)}) async-start(f32[32,16,128]{2,1,0:T(8,128)} %get-tuple-element.37), calls=%async_computation.1 | async-start | bytes 524288 | tf_op jit(solution)/shard_map/all_to_all | solution.py:648
  37.3 5.0 %collective-permute-start.3 = (f32[16,128]{1,0:T(8,128)S(1)}, f32[16,128]{1,0:T(8,128)S(1)}, u32[]{:S(2)}, u32[]{:S(2)}) collective-permute-start(f32[16,128]{1,0:T(8,128)S(1)} %shard_map.134), channel_id=1, source_target_pairs={{1,2},{2,1},{3,31},{5,6},{6,5},{7,27},{9,10},{10,9},{11,23},{13,14... | collective-permute-start | bytes 24584 | tf_op jit(solution)/shard_map/ppermute | solution.py:600
  42.3 0.1 collective-permute-start.2
  42.4 0.0 copy-done
  42.4 2.5 %shard_map.136 = (f32[128,128]{1,0:T(8,128)S(1)}, f32[128,128]{1,0:T(8,128)S(1)}, f32[4,32,128]{2,1,0:T(8,128)S(1)}) custom-call(f32[25,128,128]{2,1,0:T(8,128)S(1)} %copy-done, s32[128,128]{1,0:T(8,128)S(1)} %copy-done.2), custom_call_target="tpu_custom_call" | custom-call | tf_op jit(solution)/shard_map/pallas_call | solution.py:655
  44.9 0.5 collective-permute-done.3.lat_second_ref
  45.4 0.0 collective-permute-done.2.lat_first_ref
  45.4 0.9 %shard_map.135 = (f32[7,128,128]{2,1,0:T(8,128)S(1)}, f32[128,128]{1,0:T(8,128)S(1)}, f32[16,128]{1,0:T(8,128)S(1)}) custom-call(s32[3]{0:T(128)S(1)} %pad_add_fusion.flag_ref, s32[128,128]{1,0:T(8,128)S(1)} %copy-done.2, f32[128,128]{1,0:T(8,128)S(1)} %copy-done.3, f32[128,128]{1,0:T(8,128)S(1)} %copy-done.4, f32[128,128]{1,0:T(8,128)S(1)} %copy-done.5, ...), custom_call_target="tpu_custom_call" | custom-call | tf_op jit(solution)/shard_map/pallas_call | solution.py:650
  46.2 0.0 all-to-all-done.1.returned_ref
  46.3 1.2 %shard_map.138 = (f32[128,128]{1,0:T(8,128)S(1)}, f32[4,32,128]{2,1,0:T(8,128)S(1)}) custom-call(f32[32,16,128]{2,1,0:T(8,128)S(1)} %all-to-all-done.1.returned_ref, s32[1,2048]{1,0:T(1,128)S(1)} %copy-done.8, f32[1,2048]{1,0:T(1,128)S(1)} %copy-done.10, s32[128,128]{1,0:T(8,128)S(1)} %copy-done.2, f32[128,128]{1,0:T(8,128)S(1)} %get-tuple-element.49.seed_columns_ref, ...), custom_call_target="tpu_custom_call" | custom-call | tf_op jit(solution)/shard_map/pallas_call | solution.py:663
  47.5 1.8 %collective-permute-start.5 = (f32[128,128]{1,0:T(8,128)S(1)}, f32[128,128]{1,0:T(8,128)S(1)}, u32[]{:S(2)}, u32[]{:S(2)}) collective-permute-start(f32[128,128]{1,0:T(8,128)S(1)} %get-tuple-element.52.columns_ref), channel_id=1, source_target_pairs={{0,28},{4,8},{8,4},{12,16},{16,12},{20,24},{24,20},{28,0},{1,29},{... | collective-permute-start | bytes 196616 | tf_op jit(solution)/shard_map/ppermute | solution.py:585
  49.3 1.6 %collective-permute-start.4 = (f32[128,128]{1,0:T(8,128)S(1)}, f32[128,128]{1,0:T(8,128)S(1)}, u32[]{:S(2)}, u32[]{:S(2)}) collective-permute-start(f32[128,128]{1,0:T(8,128)S(1)} %get-tuple-element.52.columns_ref), channel_id=1, source_target_pairs={{0,4},{4,0},{8,12},{12,8},{16,20},{20,16},{24,28},{28,24},{1,5},{5... | collective-permute-start | bytes 196616 | tf_op jit(solution)/shard_map/ppermute | solution.py:585
  50.9 6.4 %shard_map.137.inner_ref = f32[25,128,128]{2,1,0:T(8,128)S(1)} custom-call(f32[32,16,128]{2,1,0:T(8,128)S(1)} %all-to-all-done.1.returned_ref, s32[1,2048]{1,0:T(1,128)S(1)} %copy-done.8, f32[1,2048]{1,0:T(1,128)S(1)} %copy-done.10, f32[25,128,128]{2,1,0:T(8,128)S(1)} %copy-done, f32[7,128,128]{2,1,0:T(8,128)S(1)} %get-tuple-element.48.field_ref), custom_call_target="tpu_custom_call" | custom-call | tf_op jit(solution)/shard_map/pallas_call | solution.py:670
  57.3 0.0 collective-permute-done.5.second_ref.lon_second_ref
  57.3 0.0 collective-permute-done.4.first_ref.lon_first_ref
  57.3 0.6 shard_map.139
  57.9 3.9 %collective-permute-start.7 = (f32[136,128]{1,0:T(8,128)S(1)}, f32[136,128]{1,0:T(8,128)S(1)}, u32[]{:S(2)}, u32[]{:S(2)}) collective-permute-start(f32[136,128]{1,0:T(8,128)S(1)} %shard_map.139), channel_id=1, source_target_pairs={{1,2},{2,1},{3,31},{5,6},{6,5},{7,27},{9,10},{10,9},{11,23},{13,14... | collective-permute-start | bytes 208904 | tf_op jit(solution)/shard_map/ppermute | solution.py:600
  61.8 0.1 collective-permute-start.6
  61.9 3.7 %collective-permute-done.7.lat_second_ref = f32[136,128]{1,0:T(8,128)S(1)} collective-permute-done((f32[136,128]{1,0:T(8,128)S(1)}, f32[136,128]{1,0:T(8,128)S(1)}, u32[]{:S(2)}, u32[]{:S(2)}) %collective-permute-start.7) | collective-permute-done | bytes 69664 | tf_op jit(solution)/shard_map/ppermute | solution.py:600
  65.6 0.0 collective-permute-done.6.lat_first_ref
  65.6 4.1 %shard_map.140 = f32[25,128,128]{2,1,0:T(8,128)} custom-call(s32[3]{0:T(128)S(1)} %pad_add_fusion.flag_ref, f32[25,128,128]{2,1,0:T(8,128)S(1)} %shard_map.137.inner_ref, f32[7,128,128]{2,1,0:T(8,128)S(1)} %get-tuple-element.48.field_ref, f32[128,128]{1,0:T(8,128)S(1)} %get-tuple-element.54.side_ref, f32[16,128]{1,0:T(8,128)S(1)} %get-tuple-element.55.edge_ref, ...), custom_call_target="tpu_custom_call" | custom-call | tf_op jit(solution)/shard_map/pallas_call | solution.py:685
  (11 shorter events, 0.0 us)
Async XLA Ops:
  0.6 1.4 %copy-start.1 = (f32[25,128,128]{2,1,0:T(8,128)S(1)}, f32[25,128,128]{2,1,0:T(8,128)}, u32[]{:S(2)}) copy-start(f32[25,128,128]{2,1,0:T(8,128)} %state_ref.1) | copy-start | bytes 4915204
  2.1 0.7 copy-start.7
  2.8 0.7 copy-start.9
  3.5 8.5 %copy-start.2 = (s32[128,128]{1,0:T(8,128)S(1)}, s32[128,128]{1,0:T(8,128)}, u32[]{:S(2)}) copy-start(s32[128,128]{1,0:T(8,128)} %mask_ref.7) | copy-start | bytes 196612
  3.5 8.5 %copy-start.3 = (f32[128,128]{1,0:T(8,128)S(1)}, f32[128,128]{1,0:T(8,128)}, u32[]{:S(2)}) copy-start(f32[128,128]{1,0:T(8,128)} %east_ref.5) | copy-start | bytes 196612
  3.5 8.5 %copy-start.4 = (f32[128,128]{1,0:T(8,128)S(1)}, f32[128,128]{1,0:T(8,128)}, u32[]{:S(2)}) copy-start(f32[128,128]{1,0:T(8,128)} %north_ref.5) | copy-start | bytes 196612
  3.5 8.5 %copy-start.5 = (f32[128,128]{1,0:T(8,128)S(1)}, f32[128,128]{1,0:T(8,128)}, u32[]{:S(2)}) copy-start(f32[128,128]{1,0:T(8,128)} %flow_ref.5) | copy-start | bytes 196612
  3.5 8.5 %copy-start.6 = (f32[128,128]{1,0:T(8,128)S(1)}, f32[128,128]{1,0:T(8,128)}, u32[]{:S(2)}) copy-start(f32[128,128]{1,0:T(8,128)} %vertical_ref.5) | copy-start | bytes 196612
  3.5 24.8 %copy-start.11 = (f32[25,512]{1,0:T(8,128)S(1)}, f32[25,512]{1,0:T(8,128)}, u32[]{:S(2)}) copy-start(f32[25,512]{1,0:T(8,128)} %value_ref.1) | copy-start | bytes 153604
  3.5 24.8 %copy-start.12 = (f32[25,512]{1,0:T(8,128)S(1)}, f32[25,512]{1,0:T(8,128)}, u32[]{:S(2)}) copy-start(f32[25,512]{1,0:T(8,128)} %invvar_ref.1) | copy-start | bytes 153604
  3.5 24.8 %copy-start.13 = (s32[1,2048]{1,0:T(1,128)S(1)}, s32[1,2048]{1,0:T(1,128)}, u32[]{:S(2)}) copy-start(s32[1,2048]{1,0:T(1,128)} %target_ref.1) | copy-start | bytes 24580
  12.0 30.4 %copy-start = (f32[25,128,128]{2,1,0:T(8,128)S(1)}, f32[25,128,128]{2,1,0:T(8,128)}, u32[]{:S(2)}) copy-start(f32[25,128,128]{2,1,0:T(8,128)} %adjoint_ref.1) | copy-start | bytes 4915204
  12.2 15.5 %all-to-all-start = ((f32[32,16,128]{2,1,0:T(8,128)}), f32[32,16,128]{2,1,0:T(8,128)S(1)}, u32[]{:S(2)}, u32[]{:S(2)}) async-start(f32[32,16,128]{2,1,0:T(8,128)} %shard_map.131), calls=%async_computation | async-start | bytes 524288 | tf_op jit(solution)/shard_map/all_to_all | solution.py:635
  18.6 6.5 %collective-permute-start.1 = (f32[128,128]{1,0:T(8,128)S(1)}, f32[128,128]{1,0:T(8,128)S(1)}, u32[]{:S(2)}, u32[]{:S(2)}) collective-permute-start(f32[128,128]{1,0:T(8,128)S(1)} %shard_map.132), channel_id=1, source_target_pairs={{0,28},{4,8},{8,4},{12,16},{16,12},{20,24},{24,20},{28,0},{1,29},{... | collective-permute-start | bytes 196616 | tf_op jit(solution)/shard_map/ppermute | solution.py:585
  19.9 6.8 %collective-permute-start = (f32[128,128]{1,0:T(8,128)S(1)}, f32[128,128]{1,0:T(8,128)S(1)}, u32[]{:S(2)}, u32[]{:S(2)}) collective-permute-start(f32[128,128]{1,0:T(8,128)S(1)} %shard_map.132), channel_id=1, source_target_pairs={{0,4},{4,0},{8,12},{12,8},{16,20},{20,16},{24,28},{28,24},{1,5},{5... | collective-permute-start | bytes 196616 | tf_op jit(solution)/shard_map/ppermute | solution.py:585
  28.3 17.9 %copy-start.8 = (s32[1,2048]{1,0:T(1,128)S(1)}, s32[1,2048]{1,0:T(1,128)}, u32[]{:S(2)}) copy-start(s32[1,2048]{1,0:T(1,128)} %cell_ref.5) | copy-start | bytes 24580
  28.3 17.9 %copy-start.10 = (f32[1,2048]{1,0:T(1,128)S(1)}, f32[1,2048]{1,0:T(1,128)}, u32[]{:S(2)}) copy-start(f32[1,2048]{1,0:T(1,128)} %weight_ref.5) | copy-start | bytes 24580
  32.4 13.8 %all-to-all-start.1 = ((f32[32,16,128]{2,1,0:T(8,128)}), f32[32,16,128]{2,1,0:T(8,128)S(1)}, u32[]{:S(2)}, u32[]{:S(2)}) async-start(f32[32,16,128]{2,1,0:T(8,128)} %get-tuple-element.37), calls=%async_computation.1 | async-start | bytes 524288 | tf_op jit(solution)/shard_map/all_to_all | solution.py:648
  37.3 8.0 %collective-permute-start.3 = (f32[16,128]{1,0:T(8,128)S(1)}, f32[16,128]{1,0:T(8,128)S(1)}, u32[]{:S(2)}, u32[]{:S(2)}) collective-permute-start(f32[16,128]{1,0:T(8,128)S(1)} %shard_map.134), channel_id=1, source_target_pairs={{1,2},{2,1},{3,31},{5,6},{6,5},{7,27},{9,10},{10,9},{11,23},{13,14... | collective-permute-start | bytes 24584 | tf_op jit(solution)/shard_map/ppermute | solution.py:600
  42.3 3.0 %collective-permute-start.2 = (f32[16,128]{1,0:T(8,128)S(1)}, f32[16,128]{1,0:T(8,128)S(1)}, u32[]{:S(2)}, u32[]{:S(2)}) collective-permute-start(f32[16,128]{1,0:T(8,128)S(1)} %shard_map.134), channel_id=1, source_target_pairs={{0,1},{1,0},{2,3},{3,2},{4,5},{5,4},{6,7},{7,6},{8,9},{9,8},{10,11... | collective-permute-start | bytes 24584 | tf_op jit(solution)/shard_map/ppermute | solution.py:600
  47.5 9.8 %collective-permute-start.5 = (f32[128,128]{1,0:T(8,128)S(1)}, f32[128,128]{1,0:T(8,128)S(1)}, u32[]{:S(2)}, u32[]{:S(2)}) collective-permute-start(f32[128,128]{1,0:T(8,128)S(1)} %get-tuple-element.52.columns_ref), channel_id=1, source_target_pairs={{0,28},{4,8},{8,4},{12,16},{16,12},{20,24},{24,20},{28,0},{1,29},{... | collective-permute-start | bytes 196616 | tf_op jit(solution)/shard_map/ppermute | solution.py:585
  49.3 8.0 %collective-permute-start.4 = (f32[128,128]{1,0:T(8,128)S(1)}, f32[128,128]{1,0:T(8,128)S(1)}, u32[]{:S(2)}, u32[]{:S(2)}) collective-permute-start(f32[128,128]{1,0:T(8,128)S(1)} %get-tuple-element.52.columns_ref), channel_id=1, source_target_pairs={{0,4},{4,0},{8,12},{12,8},{16,20},{20,16},{24,28},{28,24},{1,5},{5... | collective-permute-start | bytes 196616 | tf_op jit(solution)/shard_map/ppermute | solution.py:585
  57.9 7.8 %collective-permute-start.7 = (f32[136,128]{1,0:T(8,128)S(1)}, f32[136,128]{1,0:T(8,128)S(1)}, u32[]{:S(2)}, u32[]{:S(2)}) collective-permute-start(f32[136,128]{1,0:T(8,128)S(1)} %shard_map.139), channel_id=1, source_target_pairs={{1,2},{2,1},{3,31},{5,6},{6,5},{7,27},{9,10},{10,9},{11,23},{13,14... | collective-permute-start | bytes 208904 | tf_op jit(solution)/shard_map/ppermute | solution.py:600
  61.8 3.8 %collective-permute-start.6 = (f32[136,128]{1,0:T(8,128)S(1)}, f32[136,128]{1,0:T(8,128)S(1)}, u32[]{:S(2)}, u32[]{:S(2)}) collective-permute-start(f32[136,128]{1,0:T(8,128)S(1)} %shard_map.139), channel_id=1, source_target_pairs={{0,1},{1,0},{2,3},{3,2},{4,5},{5,4},{6,7},{7,6},{8,9},{9,8},{10,11... | collective-permute-start | bytes 208904 | tf_op jit(solution)/shard_map/ppermute | solution.py:600

commit v4 on v3

--- a/solution.py
+++ b/solution.py
@@ -11,7 +11,8 @@
 LANES = 128
 GROUP = 32
 SUB = 8
-VMEM_BYTES = 48 * 1024 * 1024
+SLOT_TILE = 16 * LANES
+MIB = 1024 * 1024
 BOTH = ("lon", "lat")
 
 
@@ -41,109 +42,119 @@
     return jnp.where(rows == index, 1.0, 0.0).astype(jnp.bfloat16)
 
 
-def packed_pair(values):
+def first_half(rows):
+    return lane((rows, LANES)) < LANES // 2
+
+
+def pack(values, out_ref, first_pair):
     half = values.shape[0] // 2
-    first = lax.broadcasted_iota(jnp.int32, (half, LANES), 1) < LANES // 2
-    top, bottom = values[:half], values[half:]
-    left = jnp.where(first, top, pltpu.roll(bottom, LANES // 2, 1))
-    right = jnp.where(first, pltpu.roll(top, LANES // 2, 1), bottom)
-    return left, right
-
-
-def unpacked_pair(left, right):
-    half = left.shape[0]
-    first = lax.broadcasted_iota(jnp.int32, (half, LANES), 1) < LANES // 2
-    top = jnp.where(first, left, pltpu.roll(right, LANES // 2, 1))
-    bottom = jnp.where(first, pltpu.roll(left, LANES // 2, 1), right)
-    return jnp.concatenate([top, bottom], axis=0)
-
-
-def padded_levels(values, levels):
-    return jnp.concatenate(
-        [values, jnp.zeros((levels - values.shape[0], values.shape[1]), values.dtype)], axis=0
-    )
-
-
-def gather_kernel(cell_ref, weight_ref, state_ref, out_ref, field_ref):
+    for pair in range(values.shape[1] // LANES):
+        block = values[:, pair * LANES : (pair + 1) * LANES]
+        top, bottom = block[:half], block[half:]
+        at = 2 * (first_pair + pair) * half
+        out_ref[at : at + half, :] = jnp.where(
+            first_half(half), top, pltpu.roll(bottom, LANES // 2, 1)
+        )
+        out_ref[at + half : at + 2 * half, :] = jnp.where(
+            first_half(half), pltpu.roll(top, LANES // 2, 1), bottom
+        )
+
+
+def unpack(in_ref, half, first_pair, pairs, levels):
+    found = []
+    for pair in range(first_pair, first_pair + pairs):
+        at = 2 * pair * half
+        left, right = in_ref[at : at + half, :], in_ref[at + half : at + 2 * half, :]
+        top = jnp.where(first_half(half), left, pltpu.roll(right, LANES // 2, 1))
+        bottom = jnp.where(first_half(half), pltpu.roll(left, LANES // 2, 1), right)
+        filler = jnp.zeros((levels - 2 * half, LANES), jnp.float32)
+        found.append(jnp.concatenate([top, bottom, filler], axis=0))
+    return jnp.concatenate(found, axis=1)
+
+
+def gather_kernel(
+    cell_in, weight_in, state_in, out_ref, cell_ref, weight_ref, state_ref, field_ref, sems
+):
     levels_n, rows_n, cols_n = state_ref.shape
     groups = rows_n // GROUP
     width = groups * cols_n
-    for group in range(groups):
-        block = state_ref[:, group * GROUP : (group + 1) * GROUP, :]
-        for part, piece in enumerate(pieces(block.reshape(levels_n * GROUP, cols_n))):
-            at = part * width + group * cols_n
-            field_ref[:, at : at + cols_n] = piece
-    tile = 2 * LANES
-
-    def body(step, carry):
-        at = pl.ds(pl.multiple_of(step * tile, tile), tile)
-        cell = cell_ref[:, at]
-        weight = jnp.where(cell >= 0, weight_ref[:, at], 0.0)
+    slots = cell_ref.shape[1]
+    tile = min(slots, SLOT_TILE)
+    chunk = max(n for n in range(1, 9) if levels_n % n == 0)
+    copies = [
+        pltpu.make_async_copy(cell_in, cell_ref, sems.at[0]),
+        pltpu.make_async_copy(weight_in, weight_ref, sems.at[1]),
+    ]
+    for place, level in enumerate(range(0, levels_n, chunk)):
+        at = slice(level, level + chunk)
+        copies.append(pltpu.make_async_copy(state_in.at[at], state_ref.at[at], sems.at[2 + place]))
+    for copy in copies:
+        copy.start()
+    copies[0].wait()
+    for start in range(0, slots, tile):
+        cell = cell_ref[:, start : start + tile]
         place, row = cell_parts(cell, rows_n, cols_n)
         hot = one_hot(place, width)
-        found = jnp.dot(
-            field_ref[...],
-            jnp.concatenate([hot, hot, hot], axis=0),
-            preferred_element_type=jnp.float32,
-        ).reshape(levels_n, GROUP, tile)
-        mine = lax.broadcasted_iota(jnp.int32, (GROUP, tile), 0) == row
-        values = jnp.sum(jnp.where(mine[None], found, 0.0), axis=1) * weight
-        values = padded_levels(values, 2 * out_ref.shape[1])
-        for pair in range(tile // LANES):
-            left, right = packed_pair(values[:, pair * LANES : (pair + 1) * LANES])
-            out_ref[step * (2 * tile // LANES) + 2 * pair] = left
-            out_ref[step * (2 * tile // LANES) + 2 * pair + 1] = right
-        return carry
-
-    lax.fori_loop(0, cell_ref.shape[1] // tile, body, 0)
-
-
-def observe_kernel(arrived_ref, target_ref, value_ref, invvar_ref, misfit_ref, out_ref, hot_ref, in_ref):
-    devices, half, _ = arrived_ref.shape
+        hot = jnp.concatenate([hot, hot, hot], axis=0)
+        mine = sublane((GROUP, tile)) == row
+        values = []
+        for index, level in enumerate(range(0, levels_n, chunk)):
+            at = slice(level * GROUP, (level + chunk) * GROUP)
+            if start == 0:
+                copies[2 + index].wait()
+                for group in range(groups):
+                    block = state_ref[
+                        level : level + chunk, group * GROUP : (group + 1) * GROUP, :
+                    ].reshape(chunk * GROUP, cols_n)
+                    for part, piece in enumerate(pieces(block)):
+                        begin = part * width + group * cols_n
+                        field_ref[at, begin : begin + cols_n] = piece
+            found = jnp.dot(field_ref[at, :], hot, preferred_element_type=jnp.float32)
+            found = found.reshape(chunk, GROUP, tile)
+            values.append(jnp.sum(jnp.where(mine[None], found, 0.0), axis=1))
+        if start == 0:
+            copies[1].wait()
+        weight = jnp.where(cell >= 0, weight_ref[:, start : start + tile], 0.0)
+        if levels_n % 2:
+            values.append(jnp.zeros((1, tile), jnp.float32))
+        pack(jnp.concatenate(values, axis=0) * weight, out_ref, start // LANES)
+
+
+def observe_kernel(arrived_ref, target_ref, value_ref, invvar_ref, misfit_ref, out_ref, hot_ref):
     levels_n, obs_n = value_ref.shape
-    levels = 2 * half
-
-    def load(pair, carry):
-        at = pl.ds(pl.multiple_of(pair * LANES, LANES), LANES)
-        values = unpacked_pair(arrived_ref[2 * pair], arrived_ref[2 * pair + 1])
-        for part, piece in enumerate(pieces(values)):
-            in_ref[part * levels : (part + 1) * levels, at] = piece
-        hot_ref[:, at] = one_hot(target_ref[:, at], obs_n)
-        return carry
-
-    lax.fori_loop(0, devices // 2, load, 0)
-    sums = lax.dot_general(
-        in_ref[...], hot_ref[...], (((1,), (1,)), ((), ())), preferred_element_type=jnp.float32
-    )
+    half = (levels_n + 1) // 2
+    levels = padded_levels(levels_n)
+    slots = target_ref.shape[1]
+    tile = min(slots, SLOT_TILE)
+    sums = None
+    for start in range(0, slots, tile):
+        hot = one_hot(target_ref[:, start : start + tile], obs_n)
+        hot_ref[:, start : start + tile] = hot
+        values = unpack(arrived_ref, half, start // LANES, tile // LANES, levels)
+        found = across(jnp.concatenate(pieces(values), axis=0), hot)
+        sums = found if sums is None else sums + found
     interp = sums[:levels] + sums[levels : 2 * levels] + sums[2 * levels :]
     misfit = invvar_ref[...] * (interp[:levels_n] - value_ref[...])
     misfit_ref[...] = misfit
-    back = jnp.concatenate(pieces(padded_levels(misfit, levels)), axis=0)
-    tile = 4 * LANES
-
-    def store(step, carry):
-        at = pl.ds(pl.multiple_of(step * tile, tile), tile)
-        found = jnp.dot(back, hot_ref[:, at], preferred_element_type=jnp.float32)
+    filler = jnp.zeros((levels - levels_n, obs_n), jnp.float32)
+    back = jnp.concatenate(pieces(jnp.concatenate([misfit, filler], axis=0)), axis=0)
+    for start in range(0, slots, tile):
+        found = jnp.dot(
+            back, hot_ref[:, start : start + tile], preferred_element_type=jnp.float32
+        )
         values = found[:levels] + found[levels : 2 * levels] + found[2 * levels :]
-        for pair in range(tile // LANES):
-            left, right = packed_pair(values[:, pair * LANES : (pair + 1) * LANES])
-            out_ref[step * (2 * tile // LANES) + 2 * pair] = left
-            out_ref[step * (2 * tile // LANES) + 2 * pair + 1] = right
-        return carry
-
-    lax.fori_loop(0, target_ref.shape[1] // tile, store, 0)
-
-
-def returned_values(returned_ref, cell_ref, weight_ref, start, tile):
-    at = pl.ds(pl.multiple_of(start, tile), tile)
+        pack(values[: 2 * half], out_ref, start // LANES)
+
+
+def padded_levels(levels_n):
+    return (levels_n + 15) // 16 * 16
+
+
+def returned_values(returned_ref, cell_ref, weight_ref, levels_n, start, tile):
+    at = slice(start, start + tile)
     weight = jnp.where(cell_ref[:, at] >= 0, weight_ref[:, at], 0.0)
-    base = start // (LANES // 2)
-    values = jnp.concatenate(
-        [
-            unpacked_pair(returned_ref[base + 2 * pair], returned_ref[base + 2 * pair + 1])
-            for pair in range(tile // LANES)
-        ],
-        axis=1,
+    values = unpack(
+        returned_ref, (levels_n + 1) // 2, start // LANES, tile // LANES, padded_levels(levels_n)
     )
     return pieces(values * weight)
 
@@ -178,7 +189,7 @@
 
 
 def strips_kernel(
-    returned_ref, cell_ref, weight_ref, mask_ref, seed_columns_ref, ocean_ref, seed_edges_ref,
+    levels_n, returned_ref, cell_ref, weight_ref, mask_ref, seed_columns_ref, ocean_ref, seed_edges_ref,
     columns_ref, edges_ref,
     left_ref, right_ref,
 ):
@@ -191,7 +202,7 @@
     for start in range(0, slots, tile):
         cell = jnp.maximum(cell_ref[:, start : start + tile], 0)
         row, column = jnp.right_shift(cell, log2(cols_n)), jnp.bitwise_and(cell, cols_n - 1)
-        values = returned_values(returned_ref, cell_ref, weight_ref, start, tile)
+        values = returned_values(returned_ref, cell_ref, weight_ref, levels_n, start, tile)
 
         def chosen(index, wanted):
             for place, number in enumerate(wanted):
@@ -236,7 +247,7 @@
     total = None
     for start in range(0, cell_ref.shape[1], tile):
         place, row = cell_parts(cell_ref[:, start : start + tile], rows_n, cols_n)
-        values = returned_values(returned_ref, cell_ref, weight_ref, start, tile)
+        values = returned_values(returned_ref, cell_ref, weight_ref, levels_n, start, tile)
         hot = one_hot(place, width)
         mine = one_hot(row, GROUP)
         for part in range(3):
@@ -449,7 +460,7 @@
     flag_ref, inner_ref, field_ref, side_ref, edge_ref,
     columns_ref, edges_ref, lon_first_ref, lon_second_ref, lat_first_ref, lat_second_ref,
     out_ref,
-    masked_ref, half_ref, turn_ref,
+    masked_ref, half_ref, turn_ref, sems,
 ):
     levels_n, rows_n, cols_n = inner_ref.shape
     levels = edges_ref.shape[1]
@@ -552,25 +563,45 @@
             half_ref[level, at, :] = found
             masked_ref[level, inner, :] = ocean * found
 
+    copies = []
+
     def store(level, top, ocean, found):
-        out_ref[level, top : top + SUB, :] = found
+        half_ref[level, top : top + SUB, :] = found
+        if level == levels_n - 1 and (top + SUB) % (rows_n // sems.shape[0]) == 0:
+            rows = slice(top + SUB - rows_n // sems.shape[0], top + SUB)
+            copy = pltpu.make_async_copy(
+                half_ref.at[:, rows, :], out_ref.at[:, rows, :], sems.at[len(copies)]
+            )
+            copy.start()
+            copies.append(copy)
 
     advance(half_ref, masked_ref, field_ref, turn_ref.at[1], store)
-
-
-def kernel_call(body, out_shape, scratch=(), flagged=False, inputs=0):
+    for copy in copies:
+        copy.wait()
+
+
+def kernel_call(mebibytes, body, out_shape, scratch=(), ins=None, outs=None):
     memory = {}
-    if flagged:
-        memory["in_specs"] = [pl.BlockSpec(memory_space=pltpu.SMEM)] + [
-            pl.BlockSpec(memory_space=pltpu.VMEM)
-        ] * (inputs - 1)
+    if ins is not None:
+        memory["in_specs"] = [pl.BlockSpec(memory_space=space) for space in ins]
+    if outs is not None:
+        memory["out_specs"] = pl.BlockSpec(memory_space=outs)
     return pl.pallas_call(
         body,
         out_shape=out_shape,
         scratch_shapes=list(scratch),
-        compiler_params=pltpu.CompilerParams(vmem_limit_bytes=VMEM_BYTES),
+        compiler_params=pltpu.CompilerParams(vmem_limit_bytes=mebibytes * MIB),
         **memory,
     )
+
+
+def flagged(inputs):
+    return [pltpu.SMEM] + [pltpu.VMEM] * (inputs - 1)
+
+
+def exchanged(value, devices):
+    rows = value.reshape(devices, 1, value.size // devices)
+    return lax.all_to_all(rows, BOTH, split_axis=0, concat_axis=0, tiled=True).reshape(value.shape)
 
 
 def f32(*shape):
@@ -620,7 +651,7 @@
     slots = slot_cell.shape[1]
     obs_n = obs_value.shape[1]
     assert 2 * (slots // devices) == LANES and cols_n == LANES and 4 * levels_n <= LANES
-    half = (levels_n + 15) // 16 * 8
+    half = (levels_n + 1) // 2
     width = rows_n // GROUP * cols_n
     bf16 = jnp.bfloat16
     raw = (land_mask, east_coef, north_coef, zonal_flow, vertical_coef)
@@ -628,46 +659,61 @@
     flags = jnp.stack([1 - lon % 2, 1 - lat % 2, lat == lax.axis_size("lat") - 1]).astype(jnp.int32)
 
     partial_vals = kernel_call(
-        gather_kernel, f32(devices, half, LANES), [pltpu.VMEM((levels_n * GROUP, 3 * width), bf16)]
+        60,
+        gather_kernel,
+        f32(devices * half, LANES),
+        [
+            pltpu.VMEM((1, slots), jnp.int32),
+            pltpu.VMEM((1, slots), jnp.float32),
+            pltpu.VMEM((levels_n, rows_n, cols_n), jnp.float32),
+            pltpu.VMEM((levels_n * GROUP, 3 * width), bf16),
+            pltpu.SemaphoreType.DMA((2 + levels_n,)),
+        ],
+        [pltpu.HBM] * 3,
     )(slot_cell, slot_weight, state)
-    columns = kernel_call(coefficient_columns_kernel, f32(rows_n, cols_n))(*raw)
+    columns = kernel_call(8, coefficient_columns_kernel, f32(rows_n, cols_n))(*raw)
     partial_vals, columns = lax.optimization_barrier((partial_vals, columns))
-    arrived = lax.all_to_all(partial_vals, BOTH, split_axis=0, concat_axis=0, tiled=True)
+    arrived = exchanged(partial_vals, devices)
     arrived, side_coefs = lax.optimization_barrier((arrived, lon_swaps(columns)))
-    row_coefs = kernel_call(coefficient_rows_kernel, f32(2 * SUB, cols_n), (), True, 8)(
+    row_coefs = kernel_call(8, coefficient_rows_kernel, f32(2 * SUB, cols_n), (), flagged(8))(
         flags, *raw, *side_coefs
     )
     misfit, outgoing = kernel_call(
+        32,
         observe_kernel,
-        (f32(levels_n, obs_n), f32(devices, half, LANES)),
-        [pltpu.VMEM((obs_n, slots), bf16), pltpu.VMEM((6 * half, slots), bf16)],
+        (f32(levels_n, obs_n), f32(devices * half, LANES)),
+        [pltpu.VMEM((obs_n, slots), bf16)],
     )(arrived, arrive_obs, obs_value, obs_invvar)
     outgoing, row_coefs, adjoint_in, land_mask = lax.optimization_barrier(
         (outgoing, row_coefs, adjoint_in, land_mask)
     )
-    returned = lax.all_to_all(outgoing, BOTH, split_axis=0, concat_axis=0, tiled=True)
-    levels = 2 * half
+    returned = exchanged(outgoing, devices)
+    levels = padded_levels(levels_n)
     fields, sides, edges = kernel_call(
+        8,
         coefficients_kernel,
         (f32(7, rows_n, cols_n), f32(rows_n, cols_n), f32(2 * SUB, cols_n)),
-        (), True, 10,
+        (), flagged(10),
     )(flags, *raw, *side_coefs, *lat_swaps(row_coefs))
     strips = kernel_call(
+        8,
         seed_strips_kernel,
         (f32(rows_n, cols_n), f32(rows_n, cols_n), f32(4, levels, cols_n)),
     )(adjoint_in, land_mask)
     returned, fields, sides, edges, strips = lax.optimization_barrier(
         (returned, fields, sides, edges, strips)
     )
-    tile = min(slots, 16 * LANES)
+    tile = min(slots, SLOT_TILE)
     own_columns, own_edges = kernel_call(
-        strips_kernel,
+        32,
+        functools.partial(strips_kernel, levels_n),
         (f32(rows_n, cols_n), f32(4, levels, cols_n)),
         [pltpu.VMEM((rows_n, 3 * tile), bf16), pltpu.VMEM((4 * levels, 3 * tile), bf16)],
     )(returned, slot_cell, slot_weight, land_mask, *strips)
     side_columns = lon_swaps(own_columns)
     extended = (levels_n, rows_n + 2 * SUB, cols_n)
     inner = kernel_call(
+        40,
         scatter_kernel,
         f32(levels_n, rows_n, cols_n),
         [
@@ -678,19 +724,21 @@
         ],
     )(returned, slot_cell, slot_weight, adjoint_in, fields)
     inner, side_columns = lax.optimization_barrier((inner, side_columns))
-    message = kernel_call(edge_message_kernel, f32(8 * half + SUB, cols_n), (), True, 4)(
+    message = kernel_call(8, edge_message_kernel, f32(4 * levels + SUB, cols_n), (), flagged(4))(
         flags, own_edges, *side_columns
     )
     side_edges = lat_swaps(message)
     adjoint_state = kernel_call(
+        16,
         steps_kernel,
         f32(levels_n, rows_n, cols_n),
         [
             pltpu.VMEM(extended, jnp.float32),
             pltpu.VMEM((levels_n, rows_n, cols_n), jnp.float32),
             pltpu.VMEM((STEPS, rows_n, cols_n), jnp.float32),
+            pltpu.SemaphoreType.DMA((4,)),
         ],
-        True, 11,
+        flagged(11), pltpu.HBM,
     )(flags, inner, fields, sides, edges, own_columns, own_edges, *side_columns, *side_edges)
     return (adjoint_state, misfit)
 

time: 70.1 us -> 64.6 us (0.922)
  local copies, waits for them, and re-layouts: 2.87 us -> 0.05 us
  Pallas kernels: 28.9 us -> 26.9 us
  waiting for transfers between devices: 8.88 us -> 7.67 us
    unnamed x28 -> x22, local copies, waits for them, and re-layouts: 2.87 us -> 0.05 us
    pallas_call x10, Pallas kernels: 28.9 us -> 26.9 us  [the longest x1 8.56 us: on_device(): kernel_call(60, gather_kernel, f32(devices * half, LANES), [pltpu.VMEM((1...]
    ppermute x2, starting transfers between devices: 4.69 us -> 6.06 us  [lon_swaps(): lax.ppermute(value, 'lon', first)]
    ppermute x2, starting transfers between devices: 3.04 us -> 1.96 us  [lon_swaps(): lax.ppermute(value, 'lon', second)]
    all_to_all x2, waiting for transfers between devices: 0.99 us -> 0.19 us  [exchanged(): lax.all_to_all(rows, BOTH, split_axis=0, concat_axis=0, tiled=True)]
  transfers between devices with their start and end apart: 10 -> 10, of which waited for: 5 -> 4; matrix products, arithmetic and copies ran while one was open for 0% -> 0% of each run, Pallas kernels for 14% -> 16%
where the time goes in v4:
time: 64.6 us; the launch traced here: 64.2 us
  starting transfers between devices  28.4 us (44%)
  Pallas kernels  26.9 us (42%)
  waiting for transfers between devices  7.67 us (12%)
  between operations  1.08 us (2%)
    all_to_all x2, starting transfers between devices, exchanged(): lax.all_to_all(rows, BOTH, split_axis=0, concat_axis=0, tiled=True)  11.4 us
    ppermute x4, starting transfers between devices, lat_swaps(): found.append(lax.ppermute(value, BOTH, pairs))  9.04 us
    pallas_call x1, Pallas kernels, on_device(): kernel_call(60, gather_kernel, f32(devices * half, LANES), [pltpu.VMEM((1...  8.56 us
    pallas_call x1, Pallas kernels, on_device(): kernel_call(40, scatter_kernel, f32(levels_n, rows_n, cols_n), [pltpu.VME...  6.66 us
    ppermute x2, starting transfers between devices, lon_swaps(): lax.ppermute(value, 'lon', first)  6.06 us
    ppermute x4, waiting for transfers between devices, lat_swaps(): found.append(lax.ppermute(value, BOTH, pairs))  4.03 us
    pallas_call x1, Pallas kernels, on_device(): kernel_call(16, steps_kernel, f32(levels_n, rows_n, cols_n), [pltpu.VMEM(...  3.71 us
    pallas_call x1, Pallas kernels, on_device(): kernel_call(8, seed_strips_kernel, (f32(rows_n, cols_n), f32(rows_n, cols...  2.46 us
  transfers between devices with their start and end apart: 10, of which 4 were waited for; matrix products, arithmetic and copies ran while one was open for 0% of the time, Pallas kernels for 16%

profile of v4, /device:TPU:7, one launch (start us, length us, event | category | flops | bytes accessed | tf_op | source)
XLA Modules:
  0.0 64.2 jit_solution(3562200808603423295)
XLA Ops:
  0.6 0.0 copy-start.1
  0.6 0.0 copy-start.5
  0.7 0.0 copy-start.4
  0.7 0.0 copy-start.3
  0.7 0.0 copy-start.2
  0.7 0.0 copy-start.9
  0.7 0.0 copy-start.8
  0.7 0.0 copy-start.10
  0.7 0.0 copy-start
  0.7 8.6 %shard_map.131 = f32[416,128]{1,0:T(8,128)} custom-call(s32[1,2048]{1,0:T(1,128)} %cell_ref.3, f32[1,2048]{1,0:T(1,128)} %weight_ref.3, f32[25,128,128]{2,1,0:T(8,128)} %state_in.1), custom_call_target="tpu_custom_call" | custom-call | tf_op jit(solution)/shard_map/pallas_call | solution.py:661
  9.3 0.0 copy-done.1
  9.3 0.0 copy-done.5
  9.3 0.0 copy-done.4
  9.3 0.0 copy-done.3
  9.3 0.0 copy-done.2
  9.3 0.2 shard_map.132
  9.6 6.4 %all-to-all-start = ((f32[32,1,1664]{2,1,0:T(1,128)}), f32[32,1,1664]{2,1,0:T(1,128)S(1)}, u32[]{:S(2)}, u32[]{:S(2)}) async-start(f32[32,1,1664]{2,1,0:T(1,128)} %bitcast.10), calls=%async_computation | async-start | bytes 425984 | tf_op jit(solution)/shard_map/all_to_all | solution.py:604
  16.0 1.3 %collective-permute-start.1 = (f32[128,128]{1,0:T(8,128)S(1)}, f32[128,128]{1,0:T(8,128)S(1)}, u32[]{:S(2)}, u32[]{:S(2)}) collective-permute-start(f32[128,128]{1,0:T(8,128)S(1)} %shard_map.132), channel_id=1, source_target_pairs={{0,28},{4,8},{8,4},{12,16},{16,12},{20,24},{24,20},{28,0},{1,29},{... | collective-permute-start | bytes 196616 | tf_op jit(solution)/shard_map/ppermute | solution.py:616
  17.2 3.1 %collective-permute-start = (f32[128,128]{1,0:T(8,128)S(1)}, f32[128,128]{1,0:T(8,128)S(1)}, u32[]{:S(2)}, u32[]{:S(2)}) collective-permute-start(f32[128,128]{1,0:T(8,128)S(1)} %shard_map.132), channel_id=1, source_target_pairs={{0,4},{4,0},{8,12},{12,8},{16,20},{20,16},{24,28},{28,24},{1,5},{5... | collective-permute-start | bytes 196616 | tf_op jit(solution)/shard_map/ppermute | solution.py:616
  20.3 0.1 pad_add_fusion.flag_ref
  20.4 1.6 %collective-permute-done.1.second_ref.lon_second_ref = f32[128,128]{1,0:T(8,128)S(1)} collective-permute-done((f32[128,128]{1,0:T(8,128)S(1)}, f32[128,128]{1,0:T(8,128)S(1)}, u32[]{:S(2)}, u32[]{:S(2)}) %collective-permute-start.1) | collective-permute-done | bytes 65568 | tf_op jit(solution)/shard_map/ppermute | solution.py:616
  22.0 1.8 %collective-permute-done.first_ref.lon_first_ref = f32[128,128]{1,0:T(8,128)S(1)} collective-permute-done((f32[128,128]{1,0:T(8,128)S(1)}, f32[128,128]{1,0:T(8,128)S(1)}, u32[]{:S(2)}, u32[]{:S(2)}) %collective-permute-start) | collective-permute-done | bytes 65568 | tf_op jit(solution)/shard_map/ppermute | solution.py:616
  23.8 0.2 all-to-all-done
  24.0 0.6 shard_map.134
  24.6 0.0 copy-done.9
  24.6 0.0 copy-done.8
  24.6 0.0 copy-done.10
  24.6 2.1 %shard_map.133 = (f32[25,512]{1,0:T(8,128)}, f32[416,128]{1,0:T(8,128)}) custom-call(f32[416,128]{1,0:T(8,128)S(1)} %bitcast.9, s32[1,2048]{1,0:T(1,128)S(1)} %copy-done.10, f32[25,512]{1,0:T(8,128)S(1)} %copy-done.8, f32[25,512]{1,0:T(8,128)S(1)} %copy-done.9), custom_call_target="tpu_custom_call" | custom-call | tf_op jit(solution)/shard_map/pallas_call | solution.py:681
  26.7 5.0 %all-to-all-start.1 = ((f32[32,1,1664]{2,1,0:T(1,128)}), f32[32,1,1664]{2,1,0:T(1,128)S(1)}, u32[]{:S(2)}, u32[]{:S(2)}) async-start(f32[32,1,1664]{2,1,0:T(1,128)} %bitcast.5), calls=%async_computation.1 | async-start | bytes 425984 | tf_op jit(solution)/shard_map/all_to_all | solution.py:604
  31.7 5.3 %collective-permute-start.3 = (f32[16,128]{1,0:T(8,128)S(1)}, f32[16,128]{1,0:T(8,128)S(1)}, u32[]{:S(2)}, u32[]{:S(2)}) collective-permute-start(f32[16,128]{1,0:T(8,128)S(1)} %shard_map.134), channel_id=1, source_target_pairs={{1,2},{2,1},{3,31},{5,6},{6,5},{7,27},{9,10},{10,9},{11,23},{13,14... | collective-permute-start | bytes 24584 | tf_op jit(solution)/shard_map/ppermute | solution.py:631
  36.9 0.1 collective-permute-start.2
  37.0 2.5 %shard_map.136 = (f32[128,128]{1,0:T(8,128)S(1)}, f32[128,128]{1,0:T(8,128)S(1)}, f32[4,32,128]{2,1,0:T(8,128)S(1)}) custom-call(f32[25,128,128]{2,1,0:T(8,128)S(1)} %copy-done, s32[128,128]{1,0:T(8,128)S(1)} %copy-done.1), custom_call_target="tpu_custom_call" | custom-call | tf_op jit(solution)/shard_map/pallas_call | solution.py:698
  39.5 0.0 collective-permute-done.3.lat_second_ref
  39.5 0.0 collective-permute-done.2.lat_first_ref
  39.5 0.9 %shard_map.135 = (f32[7,128,128]{2,1,0:T(8,128)S(1)}, f32[128,128]{1,0:T(8,128)S(1)}, f32[16,128]{1,0:T(8,128)S(1)}) custom-call(s32[3]{0:T(128)S(1)} %pad_add_fusion.flag_ref, s32[128,128]{1,0:T(8,128)S(1)} %copy-done.1, f32[128,128]{1,0:T(8,128)S(1)} %copy-done.2, f32[128,128]{1,0:T(8,128)S(1)} %copy-done.3, f32[128,128]{1,0:T(8,128)S(1)} %copy-done.4, ...), custom_call_target="tpu_custom_call" | custom-call | tf_op jit(solution)/shard_map/pallas_call | solution.py:692
  40.4 0.0 all-to-all-done.1
  40.4 1.2 %shard_map.138 = (f32[128,128]{1,0:T(8,128)S(1)}, f32[4,32,128]{2,1,0:T(8,128)S(1)}) custom-call(f32[416,128]{1,0:T(8,128)S(1)} %bitcast.7, s32[1,2048]{1,0:T(1,128)S(1)} %copy-done.6, f32[1,2048]{1,0:T(1,128)S(1)} %copy-done.7, s32[128,128]{1,0:T(8,128)S(1)} %copy-done.1, f32[128,128]{1,0:T(8,128)S(1)} %get-tuple-element.49.seed_columns_ref, ...), custom_call_target="tpu_custom_call" | custom-call | tf_op jit(solution)/shard_map/pallas_call | solution.py:707
  41.7 0.7 %collective-permute-start.5 = (f32[128,128]{1,0:T(8,128)S(1)}, f32[128,128]{1,0:T(8,128)S(1)}, u32[]{:S(2)}, u32[]{:S(2)}) collective-permute-start(f32[128,128]{1,0:T(8,128)S(1)} %get-tuple-element.52.columns_ref), channel_id=1, source_target_pairs={{0,28},{4,8},{8,4},{12,16},{16,12},{20,24},{24,20},{28,0},{1,29},{... | collective-permute-start | bytes 196616 | tf_op jit(solution)/shard_map/ppermute | solution.py:616
  42.4 3.0 %collective-permute-start.4 = (f32[128,128]{1,0:T(8,128)S(1)}, f32[128,128]{1,0:T(8,128)S(1)}, u32[]{:S(2)}, u32[]{:S(2)}) collective-permute-start(f32[128,128]{1,0:T(8,128)S(1)} %get-tuple-element.52.columns_ref), channel_id=1, source_target_pairs={{0,4},{4,0},{8,12},{12,8},{16,20},{20,16},{24,28},{28,24},{1,5},{5... | collective-permute-start | bytes 196616 | tf_op jit(solution)/shard_map/ppermute | solution.py:616
  45.4 6.7 %shard_map.137.inner_ref = f32[25,128,128]{2,1,0:T(8,128)S(1)} custom-call(f32[416,128]{1,0:T(8,128)S(1)} %bitcast.8, s32[1,2048]{1,0:T(1,128)S(1)} %copy-done.6, f32[1,2048]{1,0:T(1,128)S(1)} %copy-done.7, f32[25,128,128]{2,1,0:T(8,128)S(1)} %copy-done, f32[7,128,128]{2,1,0:T(8,128)S(1)} %get-tuple-element.48.field_ref), custom_call_target="tpu_custom_call" | custom-call | tf_op jit(solution)/shard_map/pallas_call | solution.py:715
  52.0 0.0 collective-permute-done.5.second_ref.lon_second_ref
  52.0 0.0 collective-permute-done.4.first_ref.lon_first_ref
  52.0 0.6 shard_map.139
  52.6 3.6 %collective-permute-start.7 = (f32[136,128]{1,0:T(8,128)S(1)}, f32[136,128]{1,0:T(8,128)S(1)}, u32[]{:S(2)}, u32[]{:S(2)}) collective-permute-start(f32[136,128]{1,0:T(8,128)S(1)} %shard_map.139), channel_id=1, source_target_pairs={{1,2},{2,1},{3,31},{5,6},{6,5},{7,27},{9,10},{10,9},{11,23},{13,14... | collective-permute-start | bytes 208904 | tf_op jit(solution)/shard_map/ppermute | solution.py:631
  56.3 0.1 collective-permute-start.6
  56.3 4.0 %collective-permute-done.7.lat_second_ref = f32[136,128]{1,0:T(8,128)S(1)} collective-permute-done((f32[136,128]{1,0:T(8,128)S(1)}, f32[136,128]{1,0:T(8,128)S(1)}, u32[]{:S(2)}, u32[]{:S(2)}) %collective-permute-start.7) | collective-permute-done | bytes 69664 | tf_op jit(solution)/shard_map/ppermute | solution.py:631
  60.4 0.0 collective-permute-done.6.lat_first_ref
  60.4 3.7 %shard_map.140 = f32[25,128,128]{2,1,0:T(8,128)} custom-call(s32[3]{0:T(128)S(1)} %pad_add_fusion.flag_ref, f32[25,128,128]{2,1,0:T(8,128)S(1)} %shard_map.137.inner_ref, f32[7,128,128]{2,1,0:T(8,128)S(1)} %get-tuple-element.48.field_ref, f32[128,128]{1,0:T(8,128)S(1)} %get-tuple-element.54.side_ref, f32[16,128]{1,0:T(8,128)S(1)} %get-tuple-element.55.edge_ref, ...), custom_call_target="tpu_custom_call" | custom-call | tf_op jit(solution)/shard_map/pallas_call | solution.py:731
  (5 shorter events, 0.0 us)
Async XLA Ops:
  0.6 8.7 %copy-start.1 = (s32[128,128]{1,0:T(8,128)S(1)}, s32[128,128]{1,0:T(8,128)}, u32[]{:S(2)}) copy-start(s32[128,128]{1,0:T(8,128)} %mask_ref.7) | copy-start | bytes 196612
  0.6 8.7 %copy-start.5 = (f32[128,128]{1,0:T(8,128)S(1)}, f32[128,128]{1,0:T(8,128)}, u32[]{:S(2)}) copy-start(f32[128,128]{1,0:T(8,128)} %vertical_ref.5) | copy-start | bytes 196612
  0.7 8.7 %copy-start.4 = (f32[128,128]{1,0:T(8,128)S(1)}, f32[128,128]{1,0:T(8,128)}, u32[]{:S(2)}) copy-start(f32[128,128]{1,0:T(8,128)} %flow_ref.5) | copy-start | bytes 196612
  0.7 8.7 %copy-start.3 = (f32[128,128]{1,0:T(8,128)S(1)}, f32[128,128]{1,0:T(8,128)}, u32[]{:S(2)}) copy-start(f32[128,128]{1,0:T(8,128)} %north_ref.5) | copy-start | bytes 196612
  0.7 8.7 %copy-start.2 = (f32[128,128]{1,0:T(8,128)S(1)}, f32[128,128]{1,0:T(8,128)}, u32[]{:S(2)}) copy-start(f32[128,128]{1,0:T(8,128)} %east_ref.5) | copy-start | bytes 196612
  0.7 23.9 %copy-start.9 = (f32[25,512]{1,0:T(8,128)S(1)}, f32[25,512]{1,0:T(8,128)}, u32[]{:S(2)}) copy-start(f32[25,512]{1,0:T(8,128)} %invvar_ref.1) | copy-start | bytes 153604
  0.7 23.9 %copy-start.8 = (f32[25,512]{1,0:T(8,128)S(1)}, f32[25,512]{1,0:T(8,128)}, u32[]{:S(2)}) copy-start(f32[25,512]{1,0:T(8,128)} %value_ref.1) | copy-start | bytes 153604
  0.7 23.9 %copy-start.10 = (s32[1,2048]{1,0:T(1,128)S(1)}, s32[1,2048]{1,0:T(1,128)}, u32[]{:S(2)}) copy-start(s32[1,2048]{1,0:T(1,128)} %target_ref.1) | copy-start | bytes 24580
  0.7 36.3 %copy-start = (f32[25,128,128]{2,1,0:T(8,128)S(1)}, f32[25,128,128]{2,1,0:T(8,128)}, u32[]{:S(2)}) copy-start(f32[25,128,128]{2,1,0:T(8,128)} %adjoint_ref.1) | copy-start | bytes 4915204
  9.6 14.4 %all-to-all-start = ((f32[32,1,1664]{2,1,0:T(1,128)}), f32[32,1,1664]{2,1,0:T(1,128)S(1)}, u32[]{:S(2)}, u32[]{:S(2)}) async-start(f32[32,1,1664]{2,1,0:T(1,128)} %bitcast.10), calls=%async_computation | async-start | bytes 425984 | tf_op jit(solution)/shard_map/all_to_all | solution.py:604
  16.0 6.0 %collective-permute-start.1 = (f32[128,128]{1,0:T(8,128)S(1)}, f32[128,128]{1,0:T(8,128)S(1)}, u32[]{:S(2)}, u32[]{:S(2)}) collective-permute-start(f32[128,128]{1,0:T(8,128)S(1)} %shard_map.132), channel_id=1, source_target_pairs={{0,28},{4,8},{8,4},{12,16},{16,12},{20,24},{24,20},{28,0},{1,29},{... | collective-permute-start | bytes 196616 | tf_op jit(solution)/shard_map/ppermute | solution.py:616
  17.2 6.6 %collective-permute-start = (f32[128,128]{1,0:T(8,128)S(1)}, f32[128,128]{1,0:T(8,128)S(1)}, u32[]{:S(2)}, u32[]{:S(2)}) collective-permute-start(f32[128,128]{1,0:T(8,128)S(1)} %shard_map.132), channel_id=1, source_target_pairs={{0,4},{4,0},{8,12},{12,8},{16,20},{20,16},{24,28},{28,24},{1,5},{5... | collective-permute-start | bytes 196616 | tf_op jit(solution)/shard_map/ppermute | solution.py:616
  24.0 16.4 %copy-start.6 = (s32[1,2048]{1,0:T(1,128)S(1)}, s32[1,2048]{1,0:T(1,128)}, u32[]{:S(2)}) copy-start(s32[1,2048]{1,0:T(1,128)} %cell_ref.3) | copy-start | bytes 24580
  24.0 16.4 %copy-start.7 = (f32[1,2048]{1,0:T(1,128)S(1)}, f32[1,2048]{1,0:T(1,128)}, u32[]{:S(2)}) copy-start(f32[1,2048]{1,0:T(1,128)} %weight_ref.3) | copy-start | bytes 24580
  26.7 13.7 %all-to-all-start.1 = ((f32[32,1,1664]{2,1,0:T(1,128)}), f32[32,1,1664]{2,1,0:T(1,128)S(1)}, u32[]{:S(2)}, u32[]{:S(2)}) async-start(f32[32,1,1664]{2,1,0:T(1,128)} %bitcast.5), calls=%async_computation.1 | async-start | bytes 425984 | tf_op jit(solution)/shard_map/all_to_all | solution.py:604
  31.7 7.8 %collective-permute-start.3 = (f32[16,128]{1,0:T(8,128)S(1)}, f32[16,128]{1,0:T(8,128)S(1)}, u32[]{:S(2)}, u32[]{:S(2)}) collective-permute-start(f32[16,128]{1,0:T(8,128)S(1)} %shard_map.134), channel_id=1, source_target_pairs={{1,2},{2,1},{3,31},{5,6},{6,5},{7,27},{9,10},{10,9},{11,23},{13,14... | collective-permute-start | bytes 24584 | tf_op jit(solution)/shard_map/ppermute | solution.py:631
  36.9 2.6 %collective-permute-start.2 = (f32[16,128]{1,0:T(8,128)S(1)}, f32[16,128]{1,0:T(8,128)S(1)}, u32[]{:S(2)}, u32[]{:S(2)}) collective-permute-start(f32[16,128]{1,0:T(8,128)S(1)} %shard_map.134), channel_id=1, source_target_pairs={{0,1},{1,0},{2,3},{3,2},{4,5},{5,4},{6,7},{7,6},{8,9},{9,8},{10,11... | collective-permute-start | bytes 24584 | tf_op jit(solution)/shard_map/ppermute | solution.py:631
  41.7 10.4 %collective-permute-start.5 = (f32[128,128]{1,0:T(8,128)S(1)}, f32[128,128]{1,0:T(8,128)S(1)}, u32[]{:S(2)}, u32[]{:S(2)}) collective-permute-start(f32[128,128]{1,0:T(8,128)S(1)} %get-tuple-element.52.columns_ref), channel_id=1, source_target_pairs={{0,28},{4,8},{8,4},{12,16},{16,12},{20,24},{24,20},{28,0},{1,29},{... | collective-permute-start | bytes 196616 | tf_op jit(solution)/shard_map/ppermute | solution.py:616
  42.4 9.7 %collective-permute-start.4 = (f32[128,128]{1,0:T(8,128)S(1)}, f32[128,128]{1,0:T(8,128)S(1)}, u32[]{:S(2)}, u32[]{:S(2)}) collective-permute-start(f32[128,128]{1,0:T(8,128)S(1)} %get-tuple-element.52.columns_ref), channel_id=1, source_target_pairs={{0,4},{4,0},{8,12},{12,8},{16,20},{20,16},{24,28},{28,24},{1,5},{5... | collective-permute-start | bytes 196616 | tf_op jit(solution)/shard_map/ppermute | solution.py:616
  52.6 7.8 %collective-permute-start.7 = (f32[136,128]{1,0:T(8,128)S(1)}, f32[136,128]{1,0:T(8,128)S(1)}, u32[]{:S(2)}, u32[]{:S(2)}) collective-permute-start(f32[136,128]{1,0:T(8,128)S(1)} %shard_map.139), channel_id=1, source_target_pairs={{1,2},{2,1},{3,31},{5,6},{6,5},{7,27},{9,10},{10,9},{11,23},{13,14... | collective-permute-start | bytes 208904 | tf_op jit(solution)/shard_map/ppermute | solution.py:631
  56.3 4.1 %collective-permute-start.6 = (f32[136,128]{1,0:T(8,128)S(1)}, f32[136,128]{1,0:T(8,128)S(1)}, u32[]{:S(2)}, u32[]{:S(2)}) collective-permute-start(f32[136,128]{1,0:T(8,128)S(1)} %shard_map.139), channel_id=1, source_target_pairs={{0,1},{1,0},{2,3},{3,2},{4,5},{5,4},{6,7},{7,6},{8,9},{9,8},{10,11... | collective-permute-start | bytes 208904 | tf_op jit(solution)/shard_map/ppermute | solution.py:631

commit v5 on v4

--- a/solution.py
+++ b/solution.py
@@ -235,11 +235,7 @@
         edges_ref[place] = (seed_edges_ref[place] + forcing) * ocean
 
 
-def scatter_kernel(
-    returned_ref, cell_ref, weight_ref, adjoint_ref, field_ref,
-    out_ref,
-    rows_ref, hot_ref, seed_ref, masked_ref,
-):
+def scatter_kernel(returned_ref, cell_ref, weight_ref, adjoint_ref, out_ref, rows_ref, hot_ref):
     levels_n, rows_n, cols_n = out_ref.shape
     groups = rows_n // GROUP
     width = groups * cols_n
@@ -258,16 +254,22 @@
                 )
         found = across(rows_ref[...], hot_ref[...])
         total = found if total is None else total + found
+    for group in range(groups):
+        at = slice(group * GROUP, (group + 1) * GROUP)
+        forcing = total[:, group * cols_n : (group + 1) * cols_n].reshape(levels_n, GROUP, cols_n)
+        out_ref[:, at, :] = adjoint_ref[:, at, :] + forcing
+
+
+def inner_step_kernel(seed_ref, field_ref, out_ref, masked_ref):
+    levels_n, rows_n, cols_n = out_ref.shape
     zero = jnp.zeros((1, cols_n), jnp.float32)
     for level in range(levels_n):
         masked_ref[level, SUB - 1 : SUB, :] = zero
         masked_ref[level, SUB + rows_n : SUB + rows_n + 1, :] = zero
-    for group in range(groups):
-        at = slice(group * GROUP, (group + 1) * GROUP)
-        forcing = total[:, group * cols_n : (group + 1) * cols_n].reshape(levels_n, GROUP, cols_n)
-        seed = adjoint_ref[:, at, :] + forcing
-        seed_ref[:, at, :] = seed
-        masked_ref[:, SUB + group * GROUP : SUB + (group + 1) * GROUP, :] = seed * field_ref[0, at, :]
+    for top in range(0, rows_n, SUB):
+        ocean = field_ref[0, top : top + SUB, :]
+        for level in range(levels_n):
+            masked_ref[level, SUB + top : 2 * SUB + top, :] = ocean * seed_ref[level, top : top + SUB, :]
 
     def store(level, top, ocean, found):
         out_ref[level, top : top + SUB, :] = found
@@ -340,6 +342,12 @@
     return jnp.where(even, first, second), jnp.where(even, second, first)
 
 
+def side_columns(flag_ref, first_ref, second_ref):
+    filler = jnp.zeros((first_ref.shape[1] - first_ref.shape[0], first_ref.shape[1]), jnp.float32)
+    east, west = lon_neighbours(flag_ref, first_ref[...], second_ref[...])
+    return tuple(jnp.concatenate([block, filler], axis=0).T for block in (east, west))
+
+
 def coefficient_columns_kernel(mask_ref, east_ref, north_ref, flow_ref, vertical_ref, out_ref):
     rows_n, cols_n = mask_ref.shape
     ocean = mask_ref[...].astype(jnp.float32)
@@ -356,14 +364,14 @@
         found = jnp.where(
             lane(found.shape) == place, pltpu.roll(field, (place - column) % cols_n, 1), found
         )
-    out_ref[...] = found
+    out_ref[...] = found.T[: out_ref.shape[0]]
 
 
 def coefficient_rows_kernel(
     flag_ref, mask_ref, east_ref, north_ref, flow_ref, vertical_ref, first_ref, second_ref, out_ref
 ):
     rows_n, cols_n = mask_ref.shape
-    east, west = lon_neighbours(flag_ref, first_ref[...], second_ref[...])
+    east, west = side_columns(flag_ref, first_ref, second_ref)
     top, last = slice(0, 1), slice(rows_n - 1, rows_n)
     found = []
     for at in (top, last):
@@ -388,7 +396,7 @@
 ):
     rows_n, cols_n = mask_ref.shape
     fold = flag_ref[2] == 1
-    east, west = lon_neighbours(flag_ref, lon_first_ref[...], lon_second_ref[...])
+    east, west = side_columns(flag_ref, lon_first_ref, lon_second_ref)
     up, down = lat_neighbours(flag_ref, lat_first_ref[...], lat_second_ref[...])
     mirrored = reversed_lanes(up)
     ocean = mask_ref[...].astype(jnp.float32)
@@ -443,17 +451,23 @@
         edge_ref[place : place + 1, :] = jnp.zeros((1, cols_n), jnp.float32)
 
 
-def edge_message_kernel(flag_ref, edges_ref, first_ref, second_ref, out_ref):
+def edge_message_kernel(flag_ref, edges_ref, lon_first_ref, lon_second_ref, first_ref, second_ref):
     places, levels, cols_n = edges_ref.shape
-    last = first_ref.shape[0] - 1
-    for place in range(places):
-        out_ref[place * levels : (place + 1) * levels, :] = edges_ref[place]
-    ends = []
-    for row in (0, last):
-        ends.append(lon_neighbours(flag_ref, first_ref[row : row + 1, :], second_ref[row : row + 1, :]))
-    found = (ends[0][0], ends[1][0], ends[0][1], ends[1][1])
-    for place, row in enumerate(found):
-        out_ref[places * levels + place : places * levels + place + 1, :] = row
+    last = lon_first_ref.shape[0] - 1
+    even = flag_ref[1] == 1
+    first_ref[2 * levels :, :] = jnp.zeros((SUB, cols_n), jnp.float32)
+    second_ref[2 * levels :, :] = jnp.zeros((SUB, cols_n), jnp.float32)
+    for place, (north, south) in enumerate(((places - 1, 0), (places - 2, 1))):
+        at = slice(place * levels, (place + 1) * levels)
+        northern, southern = edges_ref[north], edges_ref[south]
+        first_ref[at, :] = jnp.where(even, northern, southern)
+        second_ref[at, :] = jnp.where(even, southern, northern)
+    northern = lon_neighbours(flag_ref, lon_first_ref[last:, :], lon_second_ref[last:, :])
+    southern = lon_neighbours(flag_ref, lon_first_ref[0:1, :], lon_second_ref[0:1, :])
+    for place in range(2):
+        at = slice(2 * levels + place, 2 * levels + place + 1)
+        first_ref[at, :] = jnp.where(even, northern[place], southern[place])
+        second_ref[at, :] = jnp.where(even, southern[place], northern[place])
 
 
 def steps_kernel(
@@ -469,10 +483,10 @@
     up, down = lat_neighbours(flag_ref, lat_first_ref[...], lat_second_ref[...])
     own = columns_ref[...]
 
-    ends = edges_ref.shape[0] * levels
-    east_up = jnp.where(fold, pltpu.roll(up[ends + 3 : ends + 4], 1, 1), up[ends : ends + 1])
-    west_up = jnp.where(fold, pltpu.roll(up[ends + 1 : ends + 2], cols_n - 1, 1), up[ends + 2 : ends + 3])
-    east_down, west_down = down[ends + 1 : ends + 2], down[ends + 3 : ends + 4]
+    ends = 2 * levels
+    east_up = jnp.where(fold, pltpu.roll(up[ends + 1 : ends + 2], 1, 1), up[ends : ends + 1])
+    west_up = jnp.where(fold, pltpu.roll(up[ends : ends + 1], cols_n - 1, 1), up[ends + 1 : ends + 2])
+    east_down, west_down = down[ends : ends + 1], down[ends + 1 : ends + 2]
 
     level_at = jnp.right_shift(lane((rows_n, cols_n)), 2)
 
@@ -531,9 +545,9 @@
         )
         return block + coefficient(0) * change
 
-    above = jnp.where(fold, reversed_lanes(edge(up, 3)), edge(up, 0))
-    above_outer = jnp.where(fold, reversed_lanes(edge(up, 2)), edge(up, 1))
-    below, below_outer = edge(down, 3), edge(down, 2)
+    above = jnp.where(fold, reversed_lanes(edge(up, 0)), edge(up, 0))
+    above_outer = jnp.where(fold, reversed_lanes(edge(up, 1)), edge(up, 1))
+    below, below_outer = edge(down, 0), edge(down, 1)
     above_next = edge_step(
         above, above_outer, edges_ref[3], corner(east_up, 2), corner(west_up, 1), 0
     )
@@ -616,7 +630,7 @@
     return lax.ppermute(value, "lon", first), lax.ppermute(value, "lon", second)
 
 
-def lat_swaps(value):
+def lat_swaps(*values):
     lons, lats = lax.axis_size("lon"), lax.axis_size("lat")
     found = []
     for parity in (0, 1):
@@ -628,7 +642,7 @@
                     pairs.append((i * lats + j, (lons - 1 - i) * lats + j))
                 elif other >= 0:
                     pairs.append((i * lats + j, i * lats + other))
-        found.append(lax.ppermute(value, BOTH, pairs))
+        found.append(lax.ppermute(values[parity], BOTH, pairs))
     return tuple(found)
 
 
@@ -671,7 +685,7 @@
         ],
         [pltpu.HBM] * 3,
     )(slot_cell, slot_weight, state)
-    columns = kernel_call(8, coefficient_columns_kernel, f32(rows_n, cols_n))(*raw)
+    columns = kernel_call(8, coefficient_columns_kernel, f32(2 * SUB, rows_n))(*raw)
     partial_vals, columns = lax.optimization_barrier((partial_vals, columns))
     arrived = exchanged(partial_vals, devices)
     arrived, side_coefs = lax.optimization_barrier((arrived, lon_swaps(columns)))
@@ -694,7 +708,7 @@
         coefficients_kernel,
         (f32(7, rows_n, cols_n), f32(rows_n, cols_n), f32(2 * SUB, cols_n)),
         (), flagged(10),
-    )(flags, *raw, *side_coefs, *lat_swaps(row_coefs))
+    )(flags, *raw, *side_coefs, *lat_swaps(row_coefs, row_coefs))
     strips = kernel_call(
         8,
         seed_strips_kernel,
@@ -710,24 +724,28 @@
         (f32(rows_n, cols_n), f32(4, levels, cols_n)),
         [pltpu.VMEM((rows_n, 3 * tile), bf16), pltpu.VMEM((4 * levels, 3 * tile), bf16)],
     )(returned, slot_cell, slot_weight, land_mask, *strips)
-    side_columns = lon_swaps(own_columns)
+    columns_beside = lon_swaps(own_columns)
     extended = (levels_n, rows_n + 2 * SUB, cols_n)
-    inner = kernel_call(
+    seed = kernel_call(
         40,
         scatter_kernel,
         f32(levels_n, rows_n, cols_n),
-        [
-            pltpu.VMEM((levels_n * GROUP, 3 * tile), bf16),
-            pltpu.VMEM((width, 3 * tile), bf16),
-            pltpu.VMEM((levels_n, rows_n, cols_n), jnp.float32),
-            pltpu.VMEM(extended, jnp.float32),
-        ],
-    )(returned, slot_cell, slot_weight, adjoint_in, fields)
-    inner, side_columns = lax.optimization_barrier((inner, side_columns))
-    message = kernel_call(8, edge_message_kernel, f32(4 * levels + SUB, cols_n), (), flagged(4))(
-        flags, own_edges, *side_columns
-    )
-    side_edges = lat_swaps(message)
+        [pltpu.VMEM((levels_n * GROUP, 3 * tile), bf16), pltpu.VMEM((width, 3 * tile), bf16)],
+    )(returned, slot_cell, slot_weight, adjoint_in)
+    seed, columns_beside = lax.optimization_barrier((seed, columns_beside))
+    message = f32(2 * levels + SUB, cols_n)
+    messages = kernel_call(8, edge_message_kernel, (message, message), (), flagged(4))(
+        flags, own_edges, *columns_beside
+    )
+    rows_beside = lat_swaps(*messages)
+    seed, messages = lax.optimization_barrier((seed, messages))
+    inner = kernel_call(
+        16,
+        inner_step_kernel,
+        f32(levels_n, rows_n, cols_n),
+        [pltpu.VMEM(extended, jnp.float32)],
+    )(seed, fields)
+    inner, rows_beside = lax.optimization_barrier((inner, rows_beside))
     adjoint_state = kernel_call(
         16,
         steps_kernel,
@@ -739,7 +757,7 @@
             pltpu.SemaphoreType.DMA((4,)),
         ],
         flagged(11), pltpu.HBM,
-    )(flags, inner, fields, sides, edges, own_columns, own_edges, *side_columns, *side_edges)
+    )(flags, inner, fields, sides, edges, own_columns, own_edges, *columns_beside, *rows_beside)
     return (adjoint_state, misfit)
 
 

time: 64.6 us -> 62.2 us (0.963)
  waiting for transfers between devices: 7.67 us -> 5.09 us
    ppermute x4, waiting for transfers between devices: 4.03 us -> 1.77 us  [lat_swaps(): found.append(lax.ppermute(values[parity], BOTH, pairs))]
    all_to_all x2, waiting for transfers between devices: 0.19 us -> 2.06 us  [exchanged(): lax.all_to_all(rows, BOTH, split_axis=0, concat_axis=0, tiled=True)]
    ppermute x2, waiting for transfers between devices: 1.63 us -> 0.01 us  [lon_swaps(): lax.ppermute(value, 'lon', second)]
    pallas_call x1, Pallas kernels: 6.66 us -> 5.29 us  [on_device(): kernel_call(40, scatter_kernel, f32(levels_n, rows_n, cols_n), [pltpu.VME...]
    pallas_call x2 -> x3, Pallas kernels: 0.77 us -> 1.76 us  [the longest x1 0.95 us: on_device(): kernel_call(16, inner_step_kernel, f32(levels_n, rows_n, cols_n), [pltpu....]
    ppermute x4, starting transfers between devices: 9.04 us -> 9.96 us  [lat_swaps(): found.append(lax.ppermute(values[parity], BOTH, pairs))]
  transfers between devices with their start and end apart: 10 -> 10, of which waited for: 4 -> 3; matrix products, arithmetic and copies ran while one was open for 0% -> 0% of each run, Pallas kernels for 16% -> 16%
where the time goes in v5:
time: 62.2 us; the launch traced here: 61.9 us
  starting transfers between devices  28.9 us (46%)
  Pallas kernels  26.7 us (43%)
  waiting for transfers between devices  5.09 us (8%)
  between operations  1.09 us (2%)
    all_to_all x2, starting transfers between devices, exchanged(): lax.all_to_all(rows, BOTH, split_axis=0, concat_axis=0, tiled=True)  10.9 us
    ppermute x4, starting transfers between devices, lat_swaps(): found.append(lax.ppermute(values[parity], BOTH, pairs))  9.96 us
    pallas_call x1, Pallas kernels, on_device(): kernel_call(60, gather_kernel, f32(devices * half, LANES), [pltpu.VMEM((1...  8.56 us
    ppermute x2, starting transfers between devices, lon_swaps(): lax.ppermute(value, 'lon', first)  6.06 us
    pallas_call x1, Pallas kernels, on_device(): kernel_call(40, scatter_kernel, f32(levels_n, rows_n, cols_n), [pltpu.VME...  5.29 us
    pallas_call x1, Pallas kernels, on_device(): kernel_call(16, steps_kernel, f32(levels_n, rows_n, cols_n), [pltpu.VMEM(...  3.71 us
    pallas_call x1, Pallas kernels, on_device(): kernel_call(8, seed_strips_kernel, (f32(rows_n, cols_n), f32(rows_n, cols...  2.46 us
    all_to_all x2, waiting for transfers between devices, exchanged(): lax.all_to_all(rows, BOTH, split_axis=0, concat_axis=0, tiled=True)  2.06 us
  transfers between devices with their start and end apart: 10, of which 3 were waited for; matrix products, arithmetic and copies ran while one was open for 0% of the time, Pallas kernels for 16%

profile of v5, /device:TPU:7, one launch (start us, length us, event | category | flops | bytes accessed | tf_op | source)
XLA Modules:
  0.0 61.9 jit_solution(13239166837009054187)
XLA Ops:
  0.6 0.0 copy-start.1
  0.6 0.0 copy-start.5
  0.7 0.0 copy-start.4
  0.7 0.0 copy-start.3
  0.7 0.0 copy-start.2
  0.7 0.0 copy-start.9
  0.7 0.0 copy-start.8
  0.7 8.6 %shard_map.131 = f32[416,128]{1,0:T(8,128)} custom-call(s32[1,2048]{1,0:T(1,128)} %cell_ref.3, f32[1,2048]{1,0:T(1,128)} %weight_ref.3, f32[25,128,128]{2,1,0:T(8,128)} %state_in.1), custom_call_target="tpu_custom_call" | custom-call | tf_op jit(solution)/shard_map/pallas_call | solution.py:675
  9.3 0.0 copy-done.1
  9.3 0.0 copy-done.5
  9.3 0.0 copy-done.4
  9.3 0.0 copy-done.3
  9.3 0.0 copy-done.2
  9.3 0.3 shard_map.132
  9.6 6.4 %all-to-all-start = ((f32[32,1,1664]{2,1,0:T(1,128)}), f32[32,1,1664]{2,1,0:T(1,128)S(1)}, u32[]{:S(2)}, u32[]{:S(2)}) async-start(f32[32,1,1664]{2,1,0:T(1,128)} %bitcast.10), calls=%async_computation | async-start | bytes 425984 | tf_op jit(solution)/shard_map/all_to_all | solution.py:618
  16.0 1.3 %collective-permute-start.1 = (f32[16,128]{1,0:T(8,128)S(1)}, f32[16,128]{1,0:T(8,128)S(1)}, u32[]{:S(2)}, u32[]{:S(2)}) collective-permute-start(f32[16,128]{1,0:T(8,128)S(1)} %shard_map.132), channel_id=1, source_target_pairs={{0,28},{4,8},{8,4},{12,16},{16,12},{20,24},{24,20},{28,0},{1,29},{... | collective-permute-start | bytes 24584 | tf_op jit(solution)/shard_map/ppermute | solution.py:630
  17.2 3.1 %collective-permute-start = (f32[16,128]{1,0:T(8,128)S(1)}, f32[16,128]{1,0:T(8,128)S(1)}, u32[]{:S(2)}, u32[]{:S(2)}) collective-permute-start(f32[16,128]{1,0:T(8,128)S(1)} %shard_map.132), channel_id=1, source_target_pairs={{0,4},{4,0},{8,12},{12,8},{16,20},{20,16},{24,28},{28,24},{1,5},{5... | collective-permute-start | bytes 24584 | tf_op jit(solution)/shard_map/ppermute | solution.py:630
  20.3 0.1 pad_add_fusion.flag_ref
  20.4 0.0 collective-permute-done.1.second_ref.lon_second_ref
  20.4 1.2 %collective-permute-done.first_ref.lon_first_ref = f32[16,128]{1,0:T(8,128)S(1)} collective-permute-done((f32[16,128]{1,0:T(8,128)S(1)}, f32[16,128]{1,0:T(8,128)S(1)}, u32[]{:S(2)}, u32[]{:S(2)}) %collective-permute-start) | collective-permute-done | bytes 8224 | tf_op jit(solution)/shard_map/ppermute | solution.py:630
  21.7 2.1 %all-to-all-done = f32[32,1,1664]{2,1,0:T(1,128)S(1)} async-done(((f32[32,1,1664]{2,1,0:T(1,128)}), f32[32,1,1664]{2,1,0:T(1,128)S(1)}, u32[]{:S(2)}, u32[]{:S(2)}) %all-to-all-start) | async-done | bytes 213024 | tf_op jit(solution)/shard_map/all_to_all | solution.py:618
  23.7 0.7 %shard_map.134 = f32[16,128]{1,0:T(8,128)S(1)} custom-call(s32[3]{0:T(128)S(1)} %pad_add_fusion.flag_ref, s32[128,128]{1,0:T(8,128)S(1)} %copy-done.1, f32[128,128]{1,0:T(8,128)S(1)} %copy-done.2, f32[128,128]{1,0:T(8,128)S(1)} %copy-done.3, f32[128,128]{1,0:T(8,128)S(1)} %copy-done.4, f32[128,128]{1,0:T(8,128)S(1)} %copy-done.5, ...), custom_call_target="tpu_custom_call" | custom-call | tf_op jit(solution)/shard_map/pallas_call | solution.py:692
  24.4 0.0 copy-done.8
  24.4 0.0 copy-done.10
  24.4 2.1 %shard_map.133 = (f32[25,512]{1,0:T(8,128)}, f32[416,128]{1,0:T(8,128)}) custom-call(f32[416,128]{1,0:T(8,128)S(1)} %bitcast.9, s32[1,2048]{1,0:T(1,128)S(1)} %copy-done.10, f32[25,512]{1,0:T(8,128)S(1)} %copy-done.8, f32[25,512]{1,0:T(8,128)S(1)} %copy-done.9), custom_call_target="tpu_custom_call" | custom-call | tf_op jit(solution)/shard_map/pallas_call | solution.py:695
  26.5 4.5 %all-to-all-start.1 = ((f32[32,1,1664]{2,1,0:T(1,128)}), f32[32,1,1664]{2,1,0:T(1,128)S(1)}, u32[]{:S(2)}, u32[]{:S(2)}) async-start(f32[32,1,1664]{2,1,0:T(1,128)} %bitcast.5), calls=%async_computation.1 | async-start | bytes 425984 | tf_op jit(solution)/shard_map/all_to_all | solution.py:618
  31.0 5.2 %collective-permute-start.3 = (f32[16,128]{1,0:T(8,128)S(1)}, f32[16,128]{1,0:T(8,128)S(1)}, u32[]{:S(2)}, u32[]{:S(2)}) collective-permute-start(f32[16,128]{1,0:T(8,128)S(1)} %shard_map.134), channel_id=1, source_target_pairs={{1,2},{2,1},{3,31},{5,6},{6,5},{7,27},{9,10},{10,9},{11,23},{13,14... | collective-permute-start | bytes 24584 | tf_op jit(solution)/shard_map/ppermute | solution.py:645
  36.2 0.1 collective-permute-start.2
  36.3 2.5 %shard_map.136 = (f32[128,128]{1,0:T(8,128)S(1)}, f32[128,128]{1,0:T(8,128)S(1)}, f32[4,32,128]{2,1,0:T(8,128)S(1)}) custom-call(f32[25,128,128]{2,1,0:T(8,128)S(1)} %copy-done, s32[128,128]{1,0:T(8,128)S(1)} %copy-done.1), custom_call_target="tpu_custom_call" | custom-call | tf_op jit(solution)/shard_map/pallas_call | solution.py:712
  38.8 0.0 collective-permute-done.3.lat_second_ref
  38.8 0.0 collective-permute-done.2.lat_first_ref
  38.8 0.9 %shard_map.135 = (f32[7,128,128]{2,1,0:T(8,128)S(1)}, f32[128,128]{1,0:T(8,128)S(1)}, f32[16,128]{1,0:T(8,128)S(1)}) custom-call(s32[3]{0:T(128)S(1)} %pad_add_fusion.flag_ref, s32[128,128]{1,0:T(8,128)S(1)} %copy-done.1, f32[128,128]{1,0:T(8,128)S(1)} %copy-done.2, f32[128,128]{1,0:T(8,128)S(1)} %copy-done.3, f32[128,128]{1,0:T(8,128)S(1)} %copy-done.4, ...), custom_call_target="tpu_custom_call" | custom-call | tf_op jit(solution)/shard_map/pallas_call | solution.py:706
  39.7 0.0 all-to-all-done.1
  39.7 0.0 copy-done.6
  39.7 0.0 copy-done.7
  39.7 1.2 %shard_map.138 = (f32[128,128]{1,0:T(8,128)S(1)}, f32[4,32,128]{2,1,0:T(8,128)S(1)}) custom-call(f32[416,128]{1,0:T(8,128)S(1)} %bitcast.7, s32[1,2048]{1,0:T(1,128)S(1)} %copy-done.6, f32[1,2048]{1,0:T(1,128)S(1)} %copy-done.7, s32[128,128]{1,0:T(8,128)S(1)} %copy-done.1, f32[128,128]{1,0:T(8,128)S(1)} %get-tuple-element.54.seed_columns_ref, ...), custom_call_target="tpu_custom_call" | custom-call | tf_op jit(solution)/shard_map/pallas_call | solution.py:721
  41.0 0.7 %collective-permute-start.5 = (f32[128,128]{1,0:T(8,128)S(1)}, f32[128,128]{1,0:T(8,128)S(1)}, u32[]{:S(2)}, u32[]{:S(2)}) collective-permute-start(f32[128,128]{1,0:T(8,128)S(1)} %get-tuple-element.57.columns_ref), channel_id=1, source_target_pairs={{0,28},{4,8},{8,4},{12,16},{16,12},{20,24},{24,20},{28,0},{1,29},{... | collective-permute-start | bytes 196616 | tf_op jit(solution)/shard_map/ppermute | solution.py:630
  41.7 3.0 %collective-permute-start.4 = (f32[128,128]{1,0:T(8,128)S(1)}, f32[128,128]{1,0:T(8,128)S(1)}, u32[]{:S(2)}, u32[]{:S(2)}) collective-permute-start(f32[128,128]{1,0:T(8,128)S(1)} %get-tuple-element.57.columns_ref), channel_id=1, source_target_pairs={{0,4},{4,0},{8,12},{12,8},{16,20},{20,16},{24,28},{28,24},{1,5},{5... | collective-permute-start | bytes 196616 | tf_op jit(solution)/shard_map/ppermute | solution.py:630
  44.7 5.3 %shard_map.137.seed_ref = f32[25,128,128]{2,1,0:T(8,128)S(1)} custom-call(f32[416,128]{1,0:T(8,128)S(1)} %bitcast.8, s32[1,2048]{1,0:T(1,128)S(1)} %copy-done.6, f32[1,2048]{1,0:T(1,128)S(1)} %copy-done.7, f32[25,128,128]{2,1,0:T(8,128)S(1)} %copy-done), custom_call_target="tpu_custom_call" | custom-call | tf_op jit(solution)/shard_map/pallas_call | solution.py:729
  50.0 0.0 collective-permute-done.5.lon_second_ref
  50.0 0.0 collective-permute-done.4.lon_first_ref
  50.0 0.6 shard_map.139
  50.6 0.1 collective-permute-start.6
  50.7 4.7 %collective-permute-start.7 = (f32[72,128]{1,0:T(8,128)S(1)}, f32[72,128]{1,0:T(8,128)S(1)}, u32[]{:S(2)}, u32[]{:S(2)}) collective-permute-start(f32[72,128]{1,0:T(8,128)S(1)} %get-tuple-element.63), channel_id=1, source_target_pairs={{1,2},{2,1},{3,31},{5,6},{6,5},{7,27},{9,10},{10,9},{11,23},{13,14... | collective-permute-start | bytes 110600 | tf_op jit(solution)/shard_map/ppermute | solution.py:645
  55.3 0.9 %shard_map.140.inner_ref = f32[25,128,128]{2,1,0:T(8,128)S(1)} custom-call(f32[25,128,128]{2,1,0:T(8,128)S(1)} %shard_map.137.seed_ref, f32[7,128,128]{2,1,0:T(8,128)S(1)} %get-tuple-element.65.field_ref), custom_call_target="tpu_custom_call" | custom-call | tf_op jit(solution)/shard_map/pallas_call | solution.py:742
  56.3 0.0 collective-permute-done.6.lat_first_ref
  56.3 1.8 %collective-permute-done.7.lat_second_ref = f32[72,128]{1,0:T(8,128)S(1)} collective-permute-done((f32[72,128]{1,0:T(8,128)S(1)}, f32[72,128]{1,0:T(8,128)S(1)}, u32[]{:S(2)}, u32[]{:S(2)}) %collective-permute-start.7) | collective-permute-done | bytes 36896 | tf_op jit(solution)/shard_map/ppermute | solution.py:645
  58.1 3.7 %shard_map.141 = f32[25,128,128]{2,1,0:T(8,128)} custom-call(s32[3]{0:T(128)S(1)} %pad_add_fusion.flag_ref, f32[25,128,128]{2,1,0:T(8,128)S(1)} %shard_map.140.inner_ref, f32[7,128,128]{2,1,0:T(8,128)S(1)} %get-tuple-element.65.field_ref, f32[128,128]{1,0:T(8,128)S(1)} %get-tuple-element.67.side_ref, f32[16,128]{1,0:T(8,128)S(1)} %get-tuple-element.68.edge_ref, ...), custom_call_target="tpu_custom_call" | custom-call | tf_op jit(solution)/shard_map/pallas_call | solution.py:749
  (6 shorter events, 0.0 us)
Async XLA Ops:
  0.6 8.7 %copy-start.1 = (s32[128,128]{1,0:T(8,128)S(1)}, s32[128,128]{1,0:T(8,128)}, u32[]{:S(2)}) copy-start(s32[128,128]{1,0:T(8,128)} %mask_ref.7) | copy-start | bytes 196612
  0.6 8.7 %copy-start.5 = (f32[128,128]{1,0:T(8,128)S(1)}, f32[128,128]{1,0:T(8,128)}, u32[]{:S(2)}) copy-start(f32[128,128]{1,0:T(8,128)} %vertical_ref.5) | copy-start | bytes 196612
  0.7 8.7 %copy-start.4 = (f32[128,128]{1,0:T(8,128)S(1)}, f32[128,128]{1,0:T(8,128)}, u32[]{:S(2)}) copy-start(f32[128,128]{1,0:T(8,128)} %flow_ref.5) | copy-start | bytes 196612
  0.7 8.7 %copy-start.3 = (f32[128,128]{1,0:T(8,128)S(1)}, f32[128,128]{1,0:T(8,128)}, u32[]{:S(2)}) copy-start(f32[128,128]{1,0:T(8,128)} %north_ref.5) | copy-start | bytes 196612
  0.7 8.7 %copy-start.2 = (f32[128,128]{1,0:T(8,128)S(1)}, f32[128,128]{1,0:T(8,128)}, u32[]{:S(2)}) copy-start(f32[128,128]{1,0:T(8,128)} %east_ref.5) | copy-start | bytes 196612
  0.7 23.7 %copy-start.9 = (f32[25,512]{1,0:T(8,128)S(1)}, f32[25,512]{1,0:T(8,128)}, u32[]{:S(2)}) copy-start(f32[25,512]{1,0:T(8,128)} %invvar_ref.1) | copy-start | bytes 153604
  0.7 23.7 %copy-start.8 = (f32[25,512]{1,0:T(8,128)S(1)}, f32[25,512]{1,0:T(8,128)}, u32[]{:S(2)}) copy-start(f32[25,512]{1,0:T(8,128)} %value_ref.1) | copy-start | bytes 153604
  0.7 23.7 %copy-start.10 = (s32[1,2048]{1,0:T(1,128)S(1)}, s32[1,2048]{1,0:T(1,128)}, u32[]{:S(2)}) copy-start(s32[1,2048]{1,0:T(1,128)} %target_ref.1) | copy-start | bytes 24580
  0.7 35.6 %copy-start = (f32[25,128,128]{2,1,0:T(8,128)S(1)}, f32[25,128,128]{2,1,0:T(8,128)}, u32[]{:S(2)}) copy-start(f32[25,128,128]{2,1,0:T(8,128)} %adjoint_ref.1) | copy-start | bytes 4915204
  9.6 14.1 %all-to-all-start = ((f32[32,1,1664]{2,1,0:T(1,128)}), f32[32,1,1664]{2,1,0:T(1,128)S(1)}, u32[]{:S(2)}, u32[]{:S(2)}) async-start(f32[32,1,1664]{2,1,0:T(1,128)} %bitcast.10), calls=%async_computation | async-start | bytes 425984 | tf_op jit(solution)/shard_map/all_to_all | solution.py:618
  16.0 4.4 %collective-permute-start.1 = (f32[16,128]{1,0:T(8,128)S(1)}, f32[16,128]{1,0:T(8,128)S(1)}, u32[]{:S(2)}, u32[]{:S(2)}) collective-permute-start(f32[16,128]{1,0:T(8,128)S(1)} %shard_map.132), channel_id=1, source_target_pairs={{0,28},{4,8},{8,4},{12,16},{16,12},{20,24},{24,20},{28,0},{1,29},{... | collective-permute-start | bytes 24584 | tf_op jit(solution)/shard_map/ppermute | solution.py:630
  17.2 4.4 %collective-permute-start = (f32[16,128]{1,0:T(8,128)S(1)}, f32[16,128]{1,0:T(8,128)S(1)}, u32[]{:S(2)}, u32[]{:S(2)}) collective-permute-start(f32[16,128]{1,0:T(8,128)S(1)} %shard_map.132), channel_id=1, source_target_pairs={{0,4},{4,0},{8,12},{12,8},{16,20},{20,16},{24,28},{28,24},{1,5},{5... | collective-permute-start | bytes 24584 | tf_op jit(solution)/shard_map/ppermute | solution.py:630
  20.3 19.4 %copy-start.6 = (s32[1,2048]{1,0:T(1,128)S(1)}, s32[1,2048]{1,0:T(1,128)}, u32[]{:S(2)}) copy-start(s32[1,2048]{1,0:T(1,128)} %cell_ref.3) | copy-start | bytes 24580
  20.3 19.4 %copy-start.7 = (f32[1,2048]{1,0:T(1,128)S(1)}, f32[1,2048]{1,0:T(1,128)}, u32[]{:S(2)}) copy-start(f32[1,2048]{1,0:T(1,128)} %weight_ref.3) | copy-start | bytes 24580
  26.5 13.2 %all-to-all-start.1 = ((f32[32,1,1664]{2,1,0:T(1,128)}), f32[32,1,1664]{2,1,0:T(1,128)S(1)}, u32[]{:S(2)}, u32[]{:S(2)}) async-start(f32[32,1,1664]{2,1,0:T(1,128)} %bitcast.5), calls=%async_computation.1 | async-start | bytes 425984 | tf_op jit(solution)/shard_map/all_to_all | solution.py:618
  31.0 7.7 %collective-permute-start.3 = (f32[16,128]{1,0:T(8,128)S(1)}, f32[16,128]{1,0:T(8,128)S(1)}, u32[]{:S(2)}, u32[]{:S(2)}) collective-permute-start(f32[16,128]{1,0:T(8,128)S(1)} %shard_map.134), channel_id=1, source_target_pairs={{1,2},{2,1},{3,31},{5,6},{6,5},{7,27},{9,10},{10,9},{11,23},{13,14... | collective-permute-start | bytes 24584 | tf_op jit(solution)/shard_map/ppermute | solution.py:645
  36.2 2.6 %collective-permute-start.2 = (f32[16,128]{1,0:T(8,128)S(1)}, f32[16,128]{1,0:T(8,128)S(1)}, u32[]{:S(2)}, u32[]{:S(2)}) collective-permute-start(f32[16,128]{1,0:T(8,128)S(1)} %shard_map.134), channel_id=1, source_target_pairs={{0,1},{1,0},{2,3},{3,2},{4,5},{5,4},{6,7},{7,6},{8,9},{9,8},{10,11... | collective-permute-start | bytes 24584 | tf_op jit(solution)/shard_map/ppermute | solution.py:645
  41.0 9.0 %collective-permute-start.5 = (f32[128,128]{1,0:T(8,128)S(1)}, f32[128,128]{1,0:T(8,128)S(1)}, u32[]{:S(2)}, u32[]{:S(2)}) collective-permute-start(f32[128,128]{1,0:T(8,128)S(1)} %get-tuple-element.57.columns_ref), channel_id=1, source_target_pairs={{0,28},{4,8},{8,4},{12,16},{16,12},{20,24},{24,20},{28,0},{1,29},{... | collective-permute-start | bytes 196616 | tf_op jit(solution)/shard_map/ppermute | solution.py:630
  41.7 8.3 %collective-permute-start.4 = (f32[128,128]{1,0:T(8,128)S(1)}, f32[128,128]{1,0:T(8,128)S(1)}, u32[]{:S(2)}, u32[]{:S(2)}) collective-permute-start(f32[128,128]{1,0:T(8,128)S(1)} %get-tuple-element.57.columns_ref), channel_id=1, source_target_pairs={{0,4},{4,0},{8,12},{12,8},{16,20},{20,16},{24,28},{28,24},{1,5},{5... | collective-permute-start | bytes 196616 | tf_op jit(solution)/shard_map/ppermute | solution.py:630
  50.6 5.7 %collective-permute-start.6 = (f32[72,128]{1,0:T(8,128)S(1)}, f32[72,128]{1,0:T(8,128)S(1)}, u32[]{:S(2)}, u32[]{:S(2)}) collective-permute-start(f32[72,128]{1,0:T(8,128)S(1)} %get-tuple-element.62), channel_id=1, source_target_pairs={{0,1},{1,0},{2,3},{3,2},{4,5},{5,4},{6,7},{7,6},{8,9},{9,8},{10,11... | collective-permute-start | bytes 110600 | tf_op jit(solution)/shard_map/ppermute | solution.py:645
  50.7 7.4 %collective-permute-start.7 = (f32[72,128]{1,0:T(8,128)S(1)}, f32[72,128]{1,0:T(8,128)S(1)}, u32[]{:S(2)}, u32[]{:S(2)}) collective-permute-start(f32[72,128]{1,0:T(8,128)S(1)} %get-tuple-element.63), channel_id=1, source_target_pairs={{1,2},{2,1},{3,31},{5,6},{6,5},{7,27},{9,10},{10,9},{11,23},{13,14... | collective-permute-start | bytes 110600 | tf_op jit(solution)/shard_map/ppermute | solution.py:645

commit v6 on v5

--- a/solution.py
+++ b/solution.py
@@ -277,7 +277,7 @@
     advance(seed_ref, masked_ref, field_ref, None, store)
 
 
-def advance(source_ref, from_ref, field_ref, turn_ref, store):
+def advance(source_ref, from_ref, field_ref, turn_ref, store, south_row=None, north_row=None):
     levels_n, rows_n, cols_n = source_ref.shape
     first = lane((SUB, cols_n)) == 0
     last = lane((SUB, cols_n)) == cols_n - 1
@@ -286,6 +286,11 @@
         ocean, own, here, back, onto, south_at, mixing = (
             field_ref[place, at, :] for place in range(7)
         )
+        if south_row is not None and top == 0:
+            south_at = jnp.where(sublane(own.shape) == 0, south_row, south_at)
+            own = jnp.where(sublane(own.shape) == 0, own + south_row, own)
+        if north_row is not None and top == rows_n - SUB:
+            onto = jnp.where(sublane(own.shape) == SUB - 1, north_row, onto)
         if turn_ref is None:
             here_in, back_in = jnp.where(last, 0.0, here), jnp.where(first, 0.0, back)
         else:
@@ -367,96 +372,62 @@
     out_ref[...] = found.T[: out_ref.shape[0]]
 
 
-def coefficient_rows_kernel(
-    flag_ref, mask_ref, east_ref, north_ref, flow_ref, vertical_ref, first_ref, second_ref, out_ref
+def coefficients_kernel(
+    flag_ref, mask_ref, east_ref, north_ref, flow_ref, vertical_ref, lon_first_ref, lon_second_ref,
+    field_ref, side_ref, row_ref,
 ):
     rows_n, cols_n = mask_ref.shape
-    east, west = side_columns(flag_ref, first_ref, second_ref)
-    top, last = slice(0, 1), slice(rows_n - 1, rows_n)
-    found = []
-    for at in (top, last):
-        behind = east_ref[at, :] - 0.5 * flow_ref[at, :]
-        found.append(mask_ref[at, :].astype(jnp.float32))
-        found.append(east_ref[at, :] + 0.5 * flow_ref[at, :])
-        found.append(shifted(behind, 1, 1, west[at, 6:7]))
-        found.append(north_ref[at, :])
-        if at is last:
-            found.append(north_ref[rows_n - 2 : rows_n - 1, :])
-        found.append(vertical_ref[at, :])
-    found += [east[top], east[last], west[top], west[last]]
-    for place, row in enumerate(found):
-        out_ref[place : place + 1, :] = row
-    out_ref[len(found) :, :] = jnp.zeros((out_ref.shape[0] - len(found), cols_n), jnp.float32)
-
-
-def coefficients_kernel(
-    flag_ref, mask_ref, east_ref, north_ref, flow_ref, vertical_ref,
-    lon_first_ref, lon_second_ref, lat_first_ref, lat_second_ref,
-    field_ref, side_ref, edge_ref,
-):
-    rows_n, cols_n = mask_ref.shape
-    fold = flag_ref[2] == 1
     east, west = side_columns(flag_ref, lon_first_ref, lon_second_ref)
-    up, down = lat_neighbours(flag_ref, lat_first_ref[...], lat_second_ref[...])
-    mirrored = reversed_lanes(up)
     ocean = mask_ref[...].astype(jnp.float32)
     here = east_ref[...] + 0.5 * flow_ref[...]
     behind = east_ref[...] - 0.5 * flow_ref[...]
-    north = north_ref[...]
+    north, vertical = north_ref[...], vertical_ref[...]
     back = shifted(behind, 1, 1, west[:, 6:7])
-    south = shifted(north, 1, 0, down[8:9])
-    top = sublane((rows_n, cols_n)) == rows_n - 1
-    onto = jnp.where(jnp.logical_and(top, fold), mirrored[8:9], north)
-    parts = (ocean, here + back + north + south, here, back, onto, south, vertical_ref[...])
+    south = shifted(north, 1, 0, 0.0)
+    parts = (ocean, here + back + north + south, here, back, north, south, vertical)
     for place, part in enumerate(parts):
         field_ref[place] = part
 
-    def side(ocean, here, back, north, vertical, below, fold_top):
-        south = shifted(north, 1, 0, below)
-        top = sublane(north.shape) == rows_n - 1
-        onto = jnp.where(jnp.logical_and(top, fold), fold_top, north)
-        return ocean, here + back + north + south, here, back, onto, south, vertical
+    def side(ocean, here, back, north, vertical):
+        south = shifted(north, 1, 0, 0.0)
+        return ocean, here + back + north + south, here, back, north, south, vertical
 
     def spread(columns, place):
         return jnp.broadcast_to(columns[:, place : place + 1], (columns.shape[0], cols_n))
 
     eastern = side(
-        spread(east, 0), spread(east, 1), spread(behind, cols_n - 1), spread(east, 2), spread(east, 3),
-        spread(down[12:13], 2), spread(up[14:15], 8),
+        spread(east, 0), spread(east, 1), spread(behind, cols_n - 1), spread(east, 2), spread(east, 3)
     )
     western = side(
-        spread(west, 4), spread(west, 5), spread(west, 7), spread(west, 8), spread(west, 9),
-        spread(down[14:15], 8), spread(up[12:13], 2),
+        spread(west, 4), spread(west, 5), spread(west, 7), spread(west, 8), spread(west, 9)
     )
     found = jnp.zeros((rows_n, cols_n), jnp.float32)
     for place, part in enumerate(eastern + western):
         found = jnp.where(lane(found.shape) == place, part, found)
     side_ref[...] = found
 
-    into = north[rows_n - 1 :, :]
-    plain = (up[0:1], up[1:2] + up[2:3] + up[3:4] + into, up[1:2], up[2:3], into, up[3:4], up[4:5])
-    turned = mirrored
-    folded = (
-        turned[5:6], turned[6:7] + turned[7:8] + turned[8:9] + turned[9:10],
-        turned[7:8], turned[6:7], into, turned[9:10], turned[10:11],
-    )
-    low = (
-        down[5:6], down[6:7] + down[7:8] + down[8:9] + down[9:10],
-        down[6:7], down[7:8], down[8:9], down[9:10], down[10:11],
-    )
-    for place in range(len(plain)):
-        edge_ref[place : place + 1, :] = jnp.where(fold, folded[place], plain[place])
-        edge_ref[SUB + place : SUB + place + 1, :] = low[place]
-    for place in (len(plain), SUB + len(plain)):
-        edge_ref[place : place + 1, :] = jnp.zeros((1, cols_n), jnp.float32)
-
-
-def edge_message_kernel(flag_ref, edges_ref, lon_first_ref, lon_second_ref, first_ref, second_ref):
+    top, last = slice(0, 1), slice(rows_n - 1, rows_n)
+    rows = []
+    for at in (top, last):
+        rows += [ocean[at], here[at], back[at], north[at]]
+        if at is last:
+            rows.append(north[rows_n - 2 : rows_n - 1])
+        rows.append(vertical[at])
+    rows += [east[top], east[last], west[top], west[last]]
+    for place, row in enumerate(rows):
+        row_ref[place : place + 1, :] = row
+    row_ref[len(rows) :, :] = jnp.zeros((row_ref.shape[0] - len(rows), cols_n), jnp.float32)
+
+
+def edge_message_kernel(
+    flag_ref, edges_ref, lon_first_ref, lon_second_ref, row_ref, first_ref, second_ref
+):
     places, levels, cols_n = edges_ref.shape
     last = lon_first_ref.shape[0] - 1
     even = flag_ref[1] == 1
-    first_ref[2 * levels :, :] = jnp.zeros((SUB, cols_n), jnp.float32)
-    second_ref[2 * levels :, :] = jnp.zeros((SUB, cols_n), jnp.float32)
+    for ref in (first_ref, second_ref):
+        ref[2 * levels : 2 * levels + SUB, :] = jnp.zeros((SUB, cols_n), jnp.float32)
+        ref[2 * levels + SUB :, :] = row_ref[...]
     for place, (north, south) in enumerate(((places - 1, 0), (places - 2, 1))):
         at = slice(place * levels, (place + 1) * levels)
         northern, southern = edges_ref[north], edges_ref[south]
@@ -471,10 +442,10 @@
 
 
 def steps_kernel(
-    flag_ref, inner_ref, field_ref, side_ref, edge_ref,
+    flag_ref, inner_ref, field_ref, side_in_ref,
     columns_ref, edges_ref, lon_first_ref, lon_second_ref, lat_first_ref, lat_second_ref,
     out_ref,
-    masked_ref, half_ref, turn_ref, sems,
+    masked_ref, half_ref, turn_ref, side_ref, edge_ref, sems,
 ):
     levels_n, rows_n, cols_n = inner_ref.shape
     levels = edges_ref.shape[1]
@@ -487,6 +458,44 @@
     east_up = jnp.where(fold, pltpu.roll(up[ends + 1 : ends + 2], 1, 1), up[ends : ends + 1])
     west_up = jnp.where(fold, pltpu.roll(up[ends : ends + 1], cols_n - 1, 1), up[ends + 1 : ends + 2])
     east_down, west_down = down[ends : ends + 1], down[ends + 1 : ends + 2]
+
+    up_rows, down_rows = up[ends + SUB :], down[ends + SUB :]
+    turned = reversed_lanes(up_rows)
+    into = field_ref[4, rows_n - 1 : rows_n, :]
+    south_row = down_rows[8:9]
+    north_row = jnp.where(fold, turned[8:9], into)
+    plain = (
+        up_rows[0:1], up_rows[1:2] + up_rows[2:3] + up_rows[3:4] + into,
+        up_rows[1:2], up_rows[2:3], into, up_rows[3:4], up_rows[4:5],
+    )
+    folded = (
+        turned[5:6], turned[6:7] + turned[7:8] + turned[8:9] + turned[9:10],
+        turned[7:8], turned[6:7], into, turned[9:10], turned[10:11],
+    )
+    low = (
+        down_rows[5:6], down_rows[6:7] + down_rows[7:8] + down_rows[8:9] + down_rows[9:10],
+        down_rows[6:7], down_rows[7:8], down_rows[8:9], down_rows[9:10], down_rows[10:11],
+    )
+    for place in range(len(plain)):
+        edge_ref[place : place + 1, :] = jnp.where(fold, folded[place], plain[place])
+        edge_ref[SUB + place : SUB + place + 1, :] = low[place]
+    lanes = lane((1, cols_n))
+
+    def moved(row, source, target):
+        return jnp.where(lanes == target, pltpu.roll(row, (target - source) % cols_n, 1), 0.0)
+
+    added = (
+        moved(down_rows[12:13], 2, 1) + moved(down_rows[12:13], 2, 5)
+        + moved(down_rows[14:15], 8, 8) + moved(down_rows[14:15], 8, 12)
+    )
+    side_ref[...] = side_in_ref[...]
+    side_ref[0:1, :] = side_in_ref[0:1, :] + added
+    folding = jnp.logical_and(fold, jnp.logical_or(lanes == 4, lanes == 11))
+    side_ref[rows_n - 1 : rows_n, :] = jnp.where(
+        folding,
+        moved(up_rows[14:15], 8, 4) + moved(up_rows[12:13], 2, 11),
+        side_in_ref[rows_n - 1 : rows_n, :],
+    )
 
     level_at = jnp.right_shift(lane((rows_n, cols_n)), 2)
 
@@ -569,10 +578,10 @@
             beyond = pltpu.roll(turned, (2 * cols_n - 2 - 4 * level) % cols_n, 1)
             found = inner_ref[level, at, :] + side * beyond
             if top == 0:
-                below_row = field_ref[5, 0:1, :] * below[level : level + 1, :]
+                below_row = south_row * (below - edges_ref[0])[level : level + 1, :]
                 found = found + jnp.where(place == 0, below_row, 0.0)
             if top == rows_n - SUB:
-                above_row = field_ref[4, rows_n - 1 : rows_n, :] * above[level : level + 1, :]
+                above_row = north_row * above[level : level + 1, :]
                 found = found + jnp.where(place == SUB - 1, above_row, 0.0)
             half_ref[level, at, :] = found
             masked_ref[level, inner, :] = ocean * found
@@ -589,7 +598,7 @@
             copy.start()
             copies.append(copy)
 
-    advance(half_ref, masked_ref, field_ref, turn_ref.at[1], store)
+    advance(half_ref, masked_ref, field_ref, turn_ref.at[1], store, south_row, north_row)
     for copy in copies:
         copy.wait()
 
@@ -685,37 +694,35 @@
         ],
         [pltpu.HBM] * 3,
     )(slot_cell, slot_weight, state)
+    levels = padded_levels(levels_n)
+    partial_vals, raw = lax.optimization_barrier((partial_vals, raw))
+    arrived = exchanged(partial_vals, devices)
     columns = kernel_call(8, coefficient_columns_kernel, f32(2 * SUB, rows_n))(*raw)
-    partial_vals, columns = lax.optimization_barrier((partial_vals, columns))
-    arrived = exchanged(partial_vals, devices)
     arrived, side_coefs = lax.optimization_barrier((arrived, lon_swaps(columns)))
-    row_coefs = kernel_call(8, coefficient_rows_kernel, f32(2 * SUB, cols_n), (), flagged(8))(
-        flags, *raw, *side_coefs
-    )
+
     misfit, outgoing = kernel_call(
         32,
         observe_kernel,
         (f32(levels_n, obs_n), f32(devices * half, LANES)),
         [pltpu.VMEM((obs_n, slots), bf16)],
     )(arrived, arrive_obs, obs_value, obs_invvar)
-    outgoing, row_coefs, adjoint_in, land_mask = lax.optimization_barrier(
-        (outgoing, row_coefs, adjoint_in, land_mask)
+    outgoing, raw, side_coefs, adjoint_early = lax.optimization_barrier(
+        (outgoing, raw, side_coefs, adjoint_in)
     )
     returned = exchanged(outgoing, devices)
-    levels = padded_levels(levels_n)
-    fields, sides, edges = kernel_call(
-        8,
-        coefficients_kernel,
-        (f32(7, rows_n, cols_n), f32(rows_n, cols_n), f32(2 * SUB, cols_n)),
-        (), flagged(10),
-    )(flags, *raw, *side_coefs, *lat_swaps(row_coefs, row_coefs))
     strips = kernel_call(
         8,
         seed_strips_kernel,
         (f32(rows_n, cols_n), f32(rows_n, cols_n), f32(4, levels, cols_n)),
-    )(adjoint_in, land_mask)
-    returned, fields, sides, edges, strips = lax.optimization_barrier(
-        (returned, fields, sides, edges, strips)
+    )(adjoint_early, raw[0])
+    fields, sides, row_coefs = kernel_call(
+        8,
+        coefficients_kernel,
+        (f32(7, rows_n, cols_n), f32(rows_n, cols_n), f32(2 * SUB, cols_n)),
+        (), flagged(8),
+    )(flags, *raw, *side_coefs)
+    returned, strips, fields, sides, row_coefs = lax.optimization_barrier(
+        (returned, strips, fields, sides, row_coefs)
     )
     tile = min(slots, SLOT_TILE)
     own_columns, own_edges = kernel_call(
@@ -733,9 +740,9 @@
         [pltpu.VMEM((levels_n * GROUP, 3 * tile), bf16), pltpu.VMEM((width, 3 * tile), bf16)],
     )(returned, slot_cell, slot_weight, adjoint_in)
     seed, columns_beside = lax.optimization_barrier((seed, columns_beside))
-    message = f32(2 * levels + SUB, cols_n)
-    messages = kernel_call(8, edge_message_kernel, (message, message), (), flagged(4))(
-        flags, own_edges, *columns_beside
+    message = f32(2 * levels + 3 * SUB, cols_n)
+    messages = kernel_call(8, edge_message_kernel, (message, message), (), flagged(5))(
+        flags, own_edges, *columns_beside, row_coefs
     )
     rows_beside = lat_swaps(*messages)
     seed, messages = lax.optimization_barrier((seed, messages))
@@ -754,10 +761,12 @@
             pltpu.VMEM(extended, jnp.float32),
             pltpu.VMEM((levels_n, rows_n, cols_n), jnp.float32),
             pltpu.VMEM((STEPS, rows_n, cols_n), jnp.float32),
+            pltpu.VMEM((rows_n, cols_n), jnp.float32),
+            pltpu.VMEM((2 * SUB, cols_n), jnp.float32),
             pltpu.SemaphoreType.DMA((4,)),
         ],
-        flagged(11), pltpu.HBM,
-    )(flags, inner, fields, sides, edges, own_columns, own_edges, *columns_beside, *rows_beside)
+        flagged(10), pltpu.HBM,
+    )(flags, inner, fields, sides, own_columns, own_edges, *columns_beside, *rows_beside)
     return (adjoint_state, misfit)
 
 

time: 62.2 us -> 60.6 us (0.974)
  starting transfers between devices: 28.9 us -> 23.5 us
  waiting for transfers between devices: 5.09 us -> 9.51 us
    ppermute x4 -> x2, starting transfers between devices: 9.96 us -> 5.39 us  [lat_swaps(): found.append(lax.ppermute(values[parity], BOTH, pairs))]
    all_to_all x2, waiting for transfers between devices: 2.06 us -> 5.92 us  [exchanged(): lax.all_to_all(rows, BOTH, split_axis=0, concat_axis=0, tiled=True)]
    ppermute x2, starting transfers between devices: 6.06 us -> 4.35 us  [lon_swaps(): lax.ppermute(value, 'lon', first)]
    pallas_call x2 -> x1, Pallas kernels: 1.22 us -> 0.56 us  [on_device(): kernel_call(8, edge_message_kernel, (message, message), (), flagged(5))]
    ppermute x4 -> x2, waiting for transfers between devices: 1.77 us -> 2.25 us  [lat_swaps(): found.append(lax.ppermute(values[parity], BOTH, pairs))]
  transfers between devices with their start and end apart: 10 -> 8, of which waited for: 3 -> 4; matrix products, arithmetic and copies ran while one was open for 0% -> 0% of each run, Pallas kernels for 16% -> 17%
where the time goes in v6:
time: 60.6 us; the launch traced here: 60.3 us
  Pallas kernels  26.1 us (43%)
  starting transfers between devices  23.5 us (39%)
  waiting for transfers between devices  9.51 us (16%)
  between operations  1.04 us (2%)
    all_to_all x2, starting transfers between devices, exchanged(): lax.all_to_all(rows, BOTH, split_axis=0, concat_axis=0, tiled=True)  11.2 us
    pallas_call x1, Pallas kernels, on_device(): kernel_call(60, gather_kernel, f32(devices * half, LANES), [pltpu.VMEM((1...  8.56 us
    all_to_all x2, waiting for transfers between devices, exchanged(): lax.all_to_all(rows, BOTH, split_axis=0, concat_axis=0, tiled=True)  5.92 us
    ppermute x2, starting transfers between devices, lat_swaps(): found.append(lax.ppermute(values[parity], BOTH, pairs))  5.39 us
    pallas_call x1, Pallas kernels, on_device(): kernel_call(40, scatter_kernel, f32(levels_n, rows_n, cols_n), [pltpu.VME...  5.28 us
    ppermute x2, starting transfers between devices, lon_swaps(): lax.ppermute(value, 'lon', first)  4.35 us
    pallas_call x1, Pallas kernels, on_device(): kernel_call(16, steps_kernel, f32(levels_n, rows_n, cols_n), [pltpu.VMEM(...  3.73 us
    ppermute x2, starting transfers between devices, lon_swaps(): lax.ppermute(value, 'lon', second)  2.49 us
  transfers between devices with their start and end apart: 8, of which 4 were waited for; matrix products, arithmetic and copies ran while one was open for 0% of the time, Pallas kernels for 17%

profile of v6, /device:TPU:7, one launch (start us, length us, event | category | flops | bytes accessed | tf_op | source)
XLA Modules:
  0.0 60.3 jit_solution(15005401825154046862)
XLA Ops:
  0.6 0.0 copy-start.1
  0.6 0.0 copy-start.5
  0.7 0.0 copy-start.4
  0.7 0.0 copy-start.3
  0.7 0.0 copy-start.2
  0.7 0.0 copy-start.9
  0.7 0.0 copy-start.8
  0.7 0.0 copy-start.10
  0.7 0.0 copy-start
  0.7 8.6 %shard_map.131 = f32[416,128]{1,0:T(8,128)} custom-call(s32[1,2048]{1,0:T(1,128)} %cell_ref.3, f32[1,2048]{1,0:T(1,128)} %weight_ref.3, f32[25,128,128]{2,1,0:T(8,128)} %state_in.1), custom_call_target="tpu_custom_call" | custom-call | tf_op jit(solution)/shard_map/pallas_call | solution.py:684
  9.3 6.4 %all-to-all-start = ((f32[32,1,1664]{2,1,0:T(1,128)}), f32[32,1,1664]{2,1,0:T(1,128)S(1)}, u32[]{:S(2)}, u32[]{:S(2)}) async-start(f32[32,1,1664]{2,1,0:T(1,128)} %bitcast.10), calls=%async_computation | async-start | bytes 425984 | tf_op jit(solution)/shard_map/all_to_all | solution.py:627
  15.7 0.0 copy-done.1
  15.7 0.0 copy-done.5
  15.7 0.0 copy-done.4
  15.7 0.0 copy-done.3
  15.7 0.0 copy-done.2
  15.7 0.0 copy-start.6
  15.8 0.0 copy-start.7
  15.8 0.3 shard_map.132
  16.0 1.2 %collective-permute-start.1 = (f32[16,128]{1,0:T(8,128)S(1)}, f32[16,128]{1,0:T(8,128)S(1)}, u32[]{:S(2)}, u32[]{:S(2)}) collective-permute-start(f32[16,128]{1,0:T(8,128)S(1)} %shard_map.132), channel_id=1, source_target_pairs={{0,28},{4,8},{8,4},{12,16},{16,12},{20,24},{24,20},{28,0},{1,29},{... | collective-permute-start | bytes 24584 | tf_op jit(solution)/shard_map/ppermute | solution.py:639
  17.2 3.1 %collective-permute-start = (f32[16,128]{1,0:T(8,128)S(1)}, f32[16,128]{1,0:T(8,128)S(1)}, u32[]{:S(2)}, u32[]{:S(2)}) collective-permute-start(f32[16,128]{1,0:T(8,128)S(1)} %shard_map.132), channel_id=1, source_target_pairs={{0,4},{4,0},{8,12},{12,8},{16,20},{20,16},{24,28},{28,24},{1,5},{5... | collective-permute-start | bytes 24584 | tf_op jit(solution)/shard_map/ppermute | solution.py:639
  20.3 0.0 collective-permute-done.1.lon_second_ref
  20.3 1.3 %collective-permute-done.lon_first_ref = f32[16,128]{1,0:T(8,128)S(1)} collective-permute-done((f32[16,128]{1,0:T(8,128)S(1)}, f32[16,128]{1,0:T(8,128)S(1)}, u32[]{:S(2)}, u32[]{:S(2)}) %collective-permute-start) | collective-permute-done | bytes 8224 | tf_op jit(solution)/shard_map/ppermute | solution.py:639
  21.7 1.8 %all-to-all-done = f32[32,1,1664]{2,1,0:T(1,128)S(1)} async-done(((f32[32,1,1664]{2,1,0:T(1,128)}), f32[32,1,1664]{2,1,0:T(1,128)S(1)}, u32[]{:S(2)}, u32[]{:S(2)}) %all-to-all-start) | async-done | bytes 213024 | tf_op jit(solution)/shard_map/all_to_all | solution.py:627
  23.4 0.0 copy-done.9
  23.4 0.0 copy-done.8
  23.4 0.0 copy-done.10
  23.4 2.1 %shard_map.133 = (f32[25,512]{1,0:T(8,128)}, f32[416,128]{1,0:T(8,128)}) custom-call(f32[416,128]{1,0:T(8,128)S(1)} %bitcast.9, s32[1,2048]{1,0:T(1,128)S(1)} %copy-done.10, f32[25,512]{1,0:T(8,128)S(1)} %copy-done.8, f32[25,512]{1,0:T(8,128)S(1)} %copy-done.9), custom_call_target="tpu_custom_call" | custom-call | tf_op jit(solution)/shard_map/pallas_call | solution.py:703
  25.5 4.8 %all-to-all-start.1 = ((f32[32,1,1664]{2,1,0:T(1,128)}), f32[32,1,1664]{2,1,0:T(1,128)S(1)}, u32[]{:S(2)}, u32[]{:S(2)}) async-start(f32[32,1,1664]{2,1,0:T(1,128)} %bitcast.5), calls=%async_computation.1 | async-start | bytes 425984 | tf_op jit(solution)/shard_map/all_to_all | solution.py:627
  30.4 0.1 pad_add_fusion.flag_ref
  30.4 0.0 copy-done
  30.4 2.5 %shard_map.134 = (f32[128,128]{1,0:T(8,128)S(1)}, f32[128,128]{1,0:T(8,128)S(1)}, f32[4,32,128]{2,1,0:T(8,128)S(1)}) custom-call(f32[25,128,128]{2,1,0:T(8,128)S(1)} %copy-done, s32[128,128]{1,0:T(8,128)S(1)} %copy-done.1), custom_call_target="tpu_custom_call" | custom-call | tf_op jit(solution)/shard_map/pallas_call | solution.py:713
  32.9 0.9 %shard_map.135 = (f32[7,128,128]{2,1,0:T(8,128)S(1)}, f32[128,128]{1,0:T(8,128)S(1)}, f32[16,128]{1,0:T(8,128)S(1)}) custom-call(s32[3]{0:T(128)S(1)} %pad_add_fusion.flag_ref, s32[128,128]{1,0:T(8,128)S(1)} %copy-done.1, f32[128,128]{1,0:T(8,128)S(1)} %copy-done.2, f32[128,128]{1,0:T(8,128)S(1)} %copy-done.3, f32[128,128]{1,0:T(8,128)S(1)} %copy-done.4, ...), custom_call_target="tpu_custom_call" | custom-call | tf_op jit(solution)/shard_map/pallas_call | solution.py:718
  33.8 4.2 %all-to-all-done.1 = f32[32,1,1664]{2,1,0:T(1,128)S(1)} async-done(((f32[32,1,1664]{2,1,0:T(1,128)}), f32[32,1,1664]{2,1,0:T(1,128)S(1)}, u32[]{:S(2)}, u32[]{:S(2)}) %all-to-all-start.1) | async-done | bytes 213024 | tf_op jit(solution)/shard_map/all_to_all | solution.py:627
  38.0 0.0 copy-done.6
  38.0 1.2 %shard_map.137 = (f32[128,128]{1,0:T(8,128)S(1)}, f32[4,32,128]{2,1,0:T(8,128)S(1)}) custom-call(f32[416,128]{1,0:T(8,128)S(1)} %bitcast.7, s32[1,2048]{1,0:T(1,128)S(1)} %copy-done.6, f32[1,2048]{1,0:T(1,128)S(1)} %copy-done.7, s32[128,128]{1,0:T(8,128)S(1)} %copy-done.1, f32[128,128]{1,0:T(8,128)S(1)} %get-tuple-element.72.seed_columns_ref, ...), custom_call_target="tpu_custom_call" | custom-call | tf_op jit(solution)/shard_map/pallas_call | solution.py:728
  39.2 1.3 %collective-permute-start.3 = (f32[128,128]{1,0:T(8,128)S(1)}, f32[128,128]{1,0:T(8,128)S(1)}, u32[]{:S(2)}, u32[]{:S(2)}) collective-permute-start(f32[128,128]{1,0:T(8,128)S(1)} %get-tuple-element.75.columns_ref), channel_id=1, source_target_pairs={{0,28},{4,8},{8,4},{12,16},{16,12},{20,24},{24,20},{28,0},{1,29},{... | collective-permute-start | bytes 196616 | tf_op jit(solution)/shard_map/ppermute | solution.py:639
  40.5 1.3 %collective-permute-start.2 = (f32[128,128]{1,0:T(8,128)S(1)}, f32[128,128]{1,0:T(8,128)S(1)}, u32[]{:S(2)}, u32[]{:S(2)}) collective-permute-start(f32[128,128]{1,0:T(8,128)S(1)} %get-tuple-element.75.columns_ref), channel_id=1, source_target_pairs={{0,4},{4,0},{8,12},{12,8},{16,20},{20,16},{24,28},{28,24},{1,5},{5... | collective-permute-start | bytes 196616 | tf_op jit(solution)/shard_map/ppermute | solution.py:639
  41.8 5.3 %shard_map.136.seed_ref = f32[25,128,128]{2,1,0:T(8,128)S(1)} custom-call(f32[416,128]{1,0:T(8,128)S(1)} %bitcast.8, s32[1,2048]{1,0:T(1,128)S(1)} %copy-done.6, f32[1,2048]{1,0:T(1,128)S(1)} %copy-done.7, f32[25,128,128]{2,1,0:T(8,128)S(1)} %copy-done), custom_call_target="tpu_custom_call" | custom-call | tf_op jit(solution)/shard_map/pallas_call | solution.py:736
  47.1 0.0 collective-permute-done.3.lon_second_ref
  47.1 0.0 collective-permute-done.2.lon_first_ref
  47.1 0.6 shard_map.138
  47.6 1.3 %collective-permute-start.4 = (f32[88,128]{1,0:T(8,128)S(1)}, f32[88,128]{1,0:T(8,128)S(1)}, u32[]{:S(2)}, u32[]{:S(2)}) collective-permute-start(f32[88,128]{1,0:T(8,128)S(1)} %get-tuple-element.81), channel_id=1, source_target_pairs={{0,1},{1,0},{2,3},{3,2},{4,5},{5,4},{6,7},{7,6},{8,9},{9,8},{10,11... | collective-permute-start | bytes 135176 | tf_op jit(solution)/shard_map/ppermute | solution.py:654
  48.9 4.1 %collective-permute-start.5 = (f32[88,128]{1,0:T(8,128)S(1)}, f32[88,128]{1,0:T(8,128)S(1)}, u32[]{:S(2)}, u32[]{:S(2)}) collective-permute-start(f32[88,128]{1,0:T(8,128)S(1)} %get-tuple-element.82), channel_id=1, source_target_pairs={{1,2},{2,1},{3,31},{5,6},{6,5},{7,27},{9,10},{10,9},{11,23},{13,14... | collective-permute-start | bytes 135176 | tf_op jit(solution)/shard_map/ppermute | solution.py:654
  53.0 1.1 %shard_map.139.inner_ref = f32[25,128,128]{2,1,0:T(8,128)S(1)} custom-call(f32[25,128,128]{2,1,0:T(8,128)S(1)} %shard_map.136.seed_ref, f32[7,128,128]{2,1,0:T(8,128)S(1)} %get-tuple-element.84.field_ref), custom_call_target="tpu_custom_call" | custom-call | tf_op jit(solution)/shard_map/pallas_call | solution.py:749
  54.1 0.0 collective-permute-done.4.lat_first_ref
  54.1 2.3 %collective-permute-done.5.lat_second_ref = f32[88,128]{1,0:T(8,128)S(1)} collective-permute-done((f32[88,128]{1,0:T(8,128)S(1)}, f32[88,128]{1,0:T(8,128)S(1)}, u32[]{:S(2)}, u32[]{:S(2)}) %collective-permute-start.5) | collective-permute-done | bytes 45088 | tf_op jit(solution)/shard_map/ppermute | solution.py:654
  56.4 3.7 %shard_map.140 = f32[25,128,128]{2,1,0:T(8,128)} custom-call(s32[3]{0:T(128)S(1)} %pad_add_fusion.flag_ref, f32[25,128,128]{2,1,0:T(8,128)S(1)} %shard_map.139.inner_ref, f32[7,128,128]{2,1,0:T(8,128)S(1)} %get-tuple-element.84.field_ref, f32[128,128]{1,0:T(8,128)S(1)} %get-tuple-element.86.side_in_ref, f32[128,128]{1,0:T(8,128)S(1)} %get-tuple-element.75.columns_ref, ...), custom_call_target="tpu_custom_call" | custom-call | tf_op jit(solution)/shard_map/pallas_call | solution.py:756
  (1 shorter events, 0.0 us)
Async XLA Ops:
  0.6 15.1 %copy-start.1 = (s32[128,128]{1,0:T(8,128)S(1)}, s32[128,128]{1,0:T(8,128)}, u32[]{:S(2)}) copy-start(s32[128,128]{1,0:T(8,128)} %mask_ref.4) | copy-start | bytes 196612
  0.6 15.1 %copy-start.5 = (f32[128,128]{1,0:T(8,128)S(1)}, f32[128,128]{1,0:T(8,128)}, u32[]{:S(2)}) copy-start(f32[128,128]{1,0:T(8,128)} %vertical_ref.1) | copy-start | bytes 196612
  0.7 15.1 %copy-start.4 = (f32[128,128]{1,0:T(8,128)S(1)}, f32[128,128]{1,0:T(8,128)}, u32[]{:S(2)}) copy-start(f32[128,128]{1,0:T(8,128)} %flow_ref.1) | copy-start | bytes 196612
  0.7 15.1 %copy-start.3 = (f32[128,128]{1,0:T(8,128)S(1)}, f32[128,128]{1,0:T(8,128)}, u32[]{:S(2)}) copy-start(f32[128,128]{1,0:T(8,128)} %north_ref.1) | copy-start | bytes 196612
  0.7 15.1 %copy-start.2 = (f32[128,128]{1,0:T(8,128)S(1)}, f32[128,128]{1,0:T(8,128)}, u32[]{:S(2)}) copy-start(f32[128,128]{1,0:T(8,128)} %east_ref.1) | copy-start | bytes 196612
  0.7 22.7 %copy-start.9 = (f32[25,512]{1,0:T(8,128)S(1)}, f32[25,512]{1,0:T(8,128)}, u32[]{:S(2)}) copy-start(f32[25,512]{1,0:T(8,128)} %invvar_ref.1) | copy-start | bytes 153604
  0.7 22.7 %copy-start.8 = (f32[25,512]{1,0:T(8,128)S(1)}, f32[25,512]{1,0:T(8,128)}, u32[]{:S(2)}) copy-start(f32[25,512]{1,0:T(8,128)} %value_ref.1) | copy-start | bytes 153604
  0.7 22.7 %copy-start.10 = (s32[1,2048]{1,0:T(1,128)S(1)}, s32[1,2048]{1,0:T(1,128)}, u32[]{:S(2)}) copy-start(s32[1,2048]{1,0:T(1,128)} %target_ref.1) | copy-start | bytes 24580
  0.7 29.7 %copy-start = (f32[25,128,128]{2,1,0:T(8,128)S(1)}, f32[25,128,128]{2,1,0:T(8,128)}, u32[]{:S(2)}) copy-start(f32[25,128,128]{2,1,0:T(8,128)} %adjoint_ref.2) | copy-start | bytes 4915204
  9.3 14.1 %all-to-all-start = ((f32[32,1,1664]{2,1,0:T(1,128)}), f32[32,1,1664]{2,1,0:T(1,128)S(1)}, u32[]{:S(2)}, u32[]{:S(2)}) async-start(f32[32,1,1664]{2,1,0:T(1,128)} %bitcast.10), calls=%async_computation | async-start | bytes 425984 | tf_op jit(solution)/shard_map/all_to_all | solution.py:627
  15.7 22.2 %copy-start.6 = (s32[1,2048]{1,0:T(1,128)S(1)}, s32[1,2048]{1,0:T(1,128)}, u32[]{:S(2)}) copy-start(s32[1,2048]{1,0:T(1,128)} %cell_ref.3) | copy-start | bytes 24580
  15.8 22.2 %copy-start.7 = (f32[1,2048]{1,0:T(1,128)S(1)}, f32[1,2048]{1,0:T(1,128)}, u32[]{:S(2)}) copy-start(f32[1,2048]{1,0:T(1,128)} %weight_ref.3) | copy-start | bytes 24580
  16.0 4.3 %collective-permute-start.1 = (f32[16,128]{1,0:T(8,128)S(1)}, f32[16,128]{1,0:T(8,128)S(1)}, u32[]{:S(2)}, u32[]{:S(2)}) collective-permute-start(f32[16,128]{1,0:T(8,128)S(1)} %shard_map.132), channel_id=1, source_target_pairs={{0,28},{4,8},{8,4},{12,16},{16,12},{20,24},{24,20},{28,0},{1,29},{... | collective-permute-start | bytes 24584 | tf_op jit(solution)/shard_map/ppermute | solution.py:639
  17.2 4.4 %collective-permute-start = (f32[16,128]{1,0:T(8,128)S(1)}, f32[16,128]{1,0:T(8,128)S(1)}, u32[]{:S(2)}, u32[]{:S(2)}) collective-permute-start(f32[16,128]{1,0:T(8,128)S(1)} %shard_map.132), channel_id=1, source_target_pairs={{0,4},{4,0},{8,12},{12,8},{16,20},{20,16},{24,28},{28,24},{1,5},{5... | collective-permute-start | bytes 24584 | tf_op jit(solution)/shard_map/ppermute | solution.py:639
  25.5 12.5 %all-to-all-start.1 = ((f32[32,1,1664]{2,1,0:T(1,128)}), f32[32,1,1664]{2,1,0:T(1,128)S(1)}, u32[]{:S(2)}, u32[]{:S(2)}) async-start(f32[32,1,1664]{2,1,0:T(1,128)} %bitcast.5), calls=%async_computation.1 | async-start | bytes 425984 | tf_op jit(solution)/shard_map/all_to_all | solution.py:627
  39.2 7.8 %collective-permute-start.3 = (f32[128,128]{1,0:T(8,128)S(1)}, f32[128,128]{1,0:T(8,128)S(1)}, u32[]{:S(2)}, u32[]{:S(2)}) collective-permute-start(f32[128,128]{1,0:T(8,128)S(1)} %get-tuple-element.75.columns_ref), channel_id=1, source_target_pairs={{0,28},{4,8},{8,4},{12,16},{16,12},{20,24},{24,20},{28,0},{1,29},{... | collective-permute-start | bytes 196616 | tf_op jit(solution)/shard_map/ppermute | solution.py:639
  40.5 6.6 %collective-permute-start.2 = (f32[128,128]{1,0:T(8,128)S(1)}, f32[128,128]{1,0:T(8,128)S(1)}, u32[]{:S(2)}, u32[]{:S(2)}) collective-permute-start(f32[128,128]{1,0:T(8,128)S(1)} %get-tuple-element.75.columns_ref), channel_id=1, source_target_pairs={{0,4},{4,0},{8,12},{12,8},{16,20},{20,16},{24,28},{28,24},{1,5},{5... | collective-permute-start | bytes 196616 | tf_op jit(solution)/shard_map/ppermute | solution.py:639
  47.6 6.5 %collective-permute-start.4 = (f32[88,128]{1,0:T(8,128)S(1)}, f32[88,128]{1,0:T(8,128)S(1)}, u32[]{:S(2)}, u32[]{:S(2)}) collective-permute-start(f32[88,128]{1,0:T(8,128)S(1)} %get-tuple-element.81), channel_id=1, source_target_pairs={{0,1},{1,0},{2,3},{3,2},{4,5},{5,4},{6,7},{7,6},{8,9},{9,8},{10,11... | collective-permute-start | bytes 135176 | tf_op jit(solution)/shard_map/ppermute | solution.py:654
  48.9 7.5 %collective-permute-start.5 = (f32[88,128]{1,0:T(8,128)S(1)}, f32[88,128]{1,0:T(8,128)S(1)}, u32[]{:S(2)}, u32[]{:S(2)}) collective-permute-start(f32[88,128]{1,0:T(8,128)S(1)} %get-tuple-element.82), channel_id=1, source_target_pairs={{1,2},{2,1},{3,31},{5,6},{6,5},{7,27},{9,10},{10,9},{11,23},{13,14... | collective-permute-start | bytes 135176 | tf_op jit(solution)/shard_map/ppermute | solution.py:654

commit v7 on v6

--- a/solution.py
+++ b/solution.py
@@ -7,7 +7,6 @@
 from jax.experimental.pallas import tpu as pltpu
 from jax.sharding import PartitionSpec as P
 
-STEPS = 2
 LANES = 128
 GROUP = 32
 SUB = 8
@@ -124,7 +123,7 @@
     levels_n, obs_n = value_ref.shape
     half = (levels_n + 1) // 2
     levels = padded_levels(levels_n)
-    slots = target_ref.shape[1]
+    slots = hot_ref.shape[1]
     tile = min(slots, SLOT_TILE)
     sums = None
     for start in range(0, slots, tile):
@@ -156,7 +155,7 @@
     values = unpack(
         returned_ref, (levels_n + 1) // 2, start // LANES, tile // LANES, padded_levels(levels_n)
     )
-    return pieces(values * weight)
+    return pieces(values * weight)[:2]
 
 
 def across(left, right):
@@ -189,131 +188,174 @@
 
 
 def strips_kernel(
-    levels_n, returned_ref, cell_ref, weight_ref, mask_ref, seed_columns_ref, ocean_ref, seed_edges_ref,
-    columns_ref, edges_ref,
-    left_ref, right_ref,
+    levels_n, flag_ref, returned_ref, cell_ref, weight_ref, mask_ref, seed_columns_ref, ocean_ref, seed_edges_ref,
+    columns_ref, first_ref, second_ref, edges_ref,
 ):
     rows_n, cols_n = mask_ref.shape
     places, levels, _ = edges_ref.shape
     slots = cell_ref.shape[1]
-    tile = left_ref.shape[1] // 3
+    tile = min(slots, SLOT_TILE)
     column_sum = jnp.zeros((rows_n, LANES), jnp.float32)
     edge_sum = jnp.zeros((places * levels, cols_n), jnp.float32)
     for start in range(0, slots, tile):
-        cell = jnp.maximum(cell_ref[:, start : start + tile], 0)
+        at = slice(start, start + tile)
+        cell = jnp.maximum(cell_ref[:, at], 0)
         row, column = jnp.right_shift(cell, log2(cols_n)), jnp.bitwise_and(cell, cols_n - 1)
         values = returned_values(returned_ref, cell_ref, weight_ref, levels_n, start, tile)
 
-        def chosen(index, wanted):
-            for place, number in enumerate(wanted):
-                here = jnp.where(index == number, 1.0, 0.0).astype(jnp.bfloat16)
-                for part in range(3):
-                    right_ref[place * levels : (place + 1) * levels, part * tile : (part + 1) * tile] = (
-                        values[part] * here
-                    )
-
-        def repeated(hot):
-            for part in range(3):
-                left_ref[:, part * tile : (part + 1) * tile] = hot
-
-        repeated(one_hot(row, rows_n))
-        chosen(column, (cols_n - 2, cols_n - 1, 0, 1))
-        column_sum += across(left_ref[...], right_ref[...])
-        repeated(one_hot(column, cols_n))
-        chosen(row, (0, 1, rows_n - 2, rows_n - 1))
-        edge_sum += across(right_ref[...], left_ref[...])
+        def chosen(piece, index, wanted):
+            found = [
+                piece * jnp.where(index == number, 1.0, 0.0).astype(jnp.bfloat16)
+                for number in wanted
+            ]
+            return jnp.concatenate(found, axis=0)
+
+        row_hot, column_hot = one_hot(row, rows_n), one_hot(column, cols_n)
+        for piece in values:
+            beside = chosen(piece, column, (cols_n - 2, cols_n - 1, 0, 1))
+            column_sum += across(row_hot, beside)
+            beyond = chosen(piece, row, (0, 1, rows_n - 2, rows_n - 1))
+            edge_sum += across(beyond, column_hot)
     source, target = sublane((LANES, LANES)), lane((LANES, LANES))
     turn = jnp.bitwise_and(target, 3) * levels + jnp.right_shift(target, 2)
     turn = jnp.where(source == turn, 1.0, 0.0).astype(jnp.bfloat16)
     column_sum = sum(
         jnp.dot(piece, turn, preferred_element_type=jnp.float32) for piece in pieces(column_sum)
     )
-    columns_ref[...] = (seed_columns_ref[...] + column_sum) * ocean_ref[...]
+    columns = (seed_columns_ref[...] + column_sum) * ocean_ref[...]
+    columns_ref[...] = columns
+    first_ref[...], second_ref[...] = lon_messages(flag_ref, columns)
     for place, row in enumerate((0, 1, rows_n - 2, rows_n - 1)):
         ocean = mask_ref[row : row + 1, :].astype(jnp.float32)
         forcing = edge_sum[place * levels : (place + 1) * levels]
         edges_ref[place] = (seed_edges_ref[place] + forcing) * ocean
 
 
-def scatter_kernel(returned_ref, cell_ref, weight_ref, adjoint_ref, out_ref, rows_ref, hot_ref):
+def scatter_kernel(
+    returned_ref, cell_ref, weight_ref, adjoint_ref, out_ref, rows_ref
+):
     levels_n, rows_n, cols_n = out_ref.shape
     groups = rows_n // GROUP
-    width = groups * cols_n
-    tile = hot_ref.shape[1] // 3
-    total = None
+    tile = rows_ref.shape[1]
+    total = jnp.zeros((levels_n * GROUP, groups * cols_n), jnp.float32)
     for start in range(0, cell_ref.shape[1], tile):
-        place, row = cell_parts(cell_ref[:, start : start + tile], rows_n, cols_n)
+        at = slice(start, start + tile)
         values = returned_values(returned_ref, cell_ref, weight_ref, levels_n, start, tile)
-        hot = one_hot(place, width)
-        mine = one_hot(row, GROUP)
-        for part in range(3):
-            hot_ref[:, part * tile : (part + 1) * tile] = hot
+        place, member = cell_parts(cell_ref[:, at], rows_n, cols_n)
+        hot, member = one_hot(place, groups * cols_n), one_hot(member, GROUP)
+        for part, piece in enumerate(values):
             for level in range(levels_n):
-                rows_ref[level * GROUP : (level + 1) * GROUP, part * tile : (part + 1) * tile] = (
-                    mine * values[part][level : level + 1, :]
-                )
-        found = across(rows_ref[...], hot_ref[...])
-        total = found if total is None else total + found
+                begin = (part * levels_n + level) * GROUP
+                rows_ref[begin : begin + GROUP, :] = member * piece[level : level + 1, :]
+        for part in range(len(values)):
+            begin = part * levels_n * GROUP
+            total += across(rows_ref[begin : begin + levels_n * GROUP, :], hot)
     for group in range(groups):
         at = slice(group * GROUP, (group + 1) * GROUP)
         forcing = total[:, group * cols_n : (group + 1) * cols_n].reshape(levels_n, GROUP, cols_n)
         out_ref[:, at, :] = adjoint_ref[:, at, :] + forcing
 
 
-def inner_step_kernel(seed_ref, field_ref, out_ref, masked_ref):
-    levels_n, rows_n, cols_n = out_ref.shape
-    zero = jnp.zeros((1, cols_n), jnp.float32)
-    for level in range(levels_n):
-        masked_ref[level, SUB - 1 : SUB, :] = zero
-        masked_ref[level, SUB + rows_n : SUB + rows_n + 1, :] = zero
+def beside_kernel(
+    flag_ref, seed_ref, field_ref, side_ref, columns_ref, first_ref, second_ref,
+    half_ref, masked_ref, turn_ref,
+    from_ref,
+):
+    levels_n, rows_n, cols_n = seed_ref.shape
+    east, west = lon_columns(flag_ref, first_ref[...], second_ref[...])
+    own = columns_ref[...]
+    level_at = jnp.right_shift(lane((rows_n, cols_n)), 2)
+
+    def side_step(block, eastern, western, base):
+        def coefficient(place):
+            return side_ref[:, base + place : base + place + 1]
+
+        higher = jnp.where(level_at > 0, pltpu.roll(block, 4, 1) - block, 0.0)
+        lower = jnp.where(level_at < levels_n - 1, pltpu.roll(block, cols_n - 4, 1) - block, 0.0)
+        change = (
+            coefficient(2) * eastern
+            + coefficient(3) * western
+            + coefficient(4) * shifted(block, -1, 0, 0.0)
+            + coefficient(5) * shifted(block, 1, 0, 0.0)
+            - coefficient(1) * block
+            + coefficient(6) * (higher + lower)
+        )
+        return block + coefficient(0) * change
+
+    east_next = side_step(east, pltpu.roll(east, cols_n - 1, 1), pltpu.roll(own, 1, 1), 0)
+    west_next = side_step(west, pltpu.roll(own, cols_n - 1, 1), pltpu.roll(west, 1, 1), 7)
+    turn_ref[...] = turned_columns(east_next, west_next)
     for top in range(0, rows_n, SUB):
-        ocean = field_ref[0, top : top + SUB, :]
+        at = slice(top, top + SUB)
         for level in range(levels_n):
-            masked_ref[level, SUB + top : 2 * SUB + top, :] = ocean * seed_ref[level, top : top + SUB, :]
-
-    def store(level, top, ocean, found):
-        out_ref[level, top : top + SUB, :] = found
-
-    advance(seed_ref, masked_ref, field_ref, None, store)
-
-
-def advance(source_ref, from_ref, field_ref, turn_ref, store, south_row=None, north_row=None):
+            from_ref[level, at, :] = field_ref[0, at, :] * seed_ref[level, at, :]
+    none = [jnp.zeros((1, cols_n), jnp.float32)] * levels_n
+
+    def store(level, top, found):
+        at = slice(top, top + SUB)
+        half_ref[level, at, :] = found
+        masked_ref[level, at, :] = field_ref[0, at, :] * found
+
+    advance(seed_ref, from_ref, field_ref, turned_columns(east, west), none, none, store)
+
+
+def turned_columns(eastern, western):
+    slot = jnp.bitwise_and(lane(eastern.shape), 3)
+    cols_n = eastern.shape[1]
+    return jnp.where(slot == 1, pltpu.roll(eastern, cols_n - 1, 1), pltpu.roll(western, 1, 1))
+
+
+def advance(source_ref, from_ref, field_ref, turn, below, above, store, patch=None):
     levels_n, rows_n, cols_n = source_ref.shape
+    place = sublane((SUB, cols_n))
     first = lane((SUB, cols_n)) == 0
     last = lane((SUB, cols_n)) == cols_n - 1
     for top in range(0, rows_n, SUB):
-        at, inner = slice(top, top + SUB), slice(top + SUB, top + 2 * SUB)
+        at = slice(top, top + SUB)
+        bottom, ceiling = top == 0, top == rows_n - SUB
         ocean, own, here, back, onto, south_at, mixing = (
-            field_ref[place, at, :] for place in range(7)
+            field_ref[part, at, :] for part in range(7)
         )
-        if south_row is not None and top == 0:
-            south_at = jnp.where(sublane(own.shape) == 0, south_row, south_at)
-            own = jnp.where(sublane(own.shape) == 0, own + south_row, own)
-        if north_row is not None and top == rows_n - SUB:
-            onto = jnp.where(sublane(own.shape) == SUB - 1, north_row, onto)
-        if turn_ref is None:
-            here_in, back_in = jnp.where(last, 0.0, here), jnp.where(first, 0.0, back)
-        else:
-            turned = turn_ref[at, :]
-        higher = block = from_ref[0, inner, :]
+        extra = None
+        if patch is not None and (bottom or ceiling):
+            south_row, north_row, added_below, added_above = patch
+            if bottom:
+                south_at = jnp.where(place == 0, south_row, south_at)
+                own = jnp.where(place == 0, own + south_row, own)
+                extra = [jnp.where(place == 0, row, 0.0) for row in added_below]
+            else:
+                onto = jnp.where(place == SUB - 1, north_row, onto)
+                extra = [jnp.where(place == SUB - 1, row, 0.0) for row in added_above]
+
+        def block_of(level):
+            block = from_ref[level, at, :]
+            return block if extra is None else block + ocean * extra[level]
+
+        higher = block = block_of(0)
         for level in range(levels_n):
-            lower = from_ref[level + 1, inner, :] if level + 1 < levels_n else block
+            lower = block_of(level + 1) if level + 1 < levels_n else block
             eastern, western = pltpu.roll(block, cols_n - 1, 1), pltpu.roll(block, 1, 1)
-            if turn_ref is None:
-                sides = here_in * eastern + back_in * western
+            beyond = pltpu.roll(turn[at], (2 * cols_n - 2 - 4 * level) % cols_n, 1)
+            sides = here * jnp.where(last, beyond, eastern) + back * jnp.where(first, beyond, western)
+            if ceiling:
+                north = shifted(block, -1, 0, above[level])
             else:
-                beyond = pltpu.roll(turned, (2 * cols_n - 2 - 4 * level) % cols_n, 1)
-                sides = here * jnp.where(last, beyond, eastern) + back * jnp.where(first, beyond, western)
-            north = from_ref[level, top + SUB + 1 : top + 2 * SUB + 1, :]
-            south = from_ref[level, top + SUB - 1 : top + 2 * SUB - 1, :]
+                north = from_ref[level, top + 1 : top + SUB + 1, :]
+            if bottom:
+                south = shifted(block, 1, 0, below[level])
+            else:
+                south = from_ref[level, top - 1 : top + SUB - 1, :]
+            source = source_ref[level, at, :]
+            if extra is not None:
+                source = source + extra[level]
             vertical = (higher - block) + (lower - block)
             found = (
-                (source_ref[level, at, :] - own * block)
+                (source - own * block)
                 + sides
                 + (onto * north + south_at * south)
                 + mixing * vertical
             )
-            store(level, top, ocean, found)
+            store(level, top, found)
             higher, block = block, lower
 
 
@@ -337,14 +379,32 @@
     return jnp.take_along_axis(block, at, axis=1, mode="promise_in_bounds")
 
 
+def by_flag(flag_ref, place, chosen, other):
+    flag = jnp.broadcast_to(flag_ref[place : place + 1, : chosen.shape[1]], chosen.shape)
+    return jnp.where(flag == 1, chosen, other)
+
+
 def lon_neighbours(flag_ref, first, second):
-    even = flag_ref[0] == 1
-    return jnp.where(even, first, second), jnp.where(even, second, first)
+    return by_flag(flag_ref, 0, first, second), by_flag(flag_ref, 0, second, first)
+
+
+def lon_columns(flag_ref, first, second):
+    east, west = lon_neighbours(flag_ref, first, second)
+    east = jnp.concatenate([pltpu.roll(east, 2, 1), east], axis=0)
+    west = jnp.concatenate([west, pltpu.roll(west, LANES - 2, 1)], axis=0)
+    return east, west
+
+
+def lon_messages(flag_ref, columns):
+    low, high = columns[: columns.shape[0] // 2], columns[columns.shape[0] // 2 :]
+    left = jnp.bitwise_and(lane(low.shape), 3) < 2
+    eastward = jnp.where(left, low, pltpu.roll(high, 2, 1))
+    westward = jnp.where(left, pltpu.roll(low, LANES - 2, 1), high)
+    return lon_neighbours(flag_ref, eastward, westward)
 
 
 def lat_neighbours(flag_ref, first, second):
-    even = flag_ref[1] == 1
-    return jnp.where(even, first, second), jnp.where(even, second, first)
+    return by_flag(flag_ref, 1, first, second), by_flag(flag_ref, 1, second, first)
 
 
 def side_columns(flag_ref, first_ref, second_ref):
@@ -423,47 +483,43 @@
     flag_ref, edges_ref, lon_first_ref, lon_second_ref, row_ref, first_ref, second_ref
 ):
     places, levels, cols_n = edges_ref.shape
-    last = lon_first_ref.shape[0] - 1
-    even = flag_ref[1] == 1
     for ref in (first_ref, second_ref):
         ref[2 * levels : 2 * levels + SUB, :] = jnp.zeros((SUB, cols_n), jnp.float32)
         ref[2 * levels + SUB :, :] = row_ref[...]
     for place, (north, south) in enumerate(((places - 1, 0), (places - 2, 1))):
         at = slice(place * levels, (place + 1) * levels)
         northern, southern = edges_ref[north], edges_ref[south]
-        first_ref[at, :] = jnp.where(even, northern, southern)
-        second_ref[at, :] = jnp.where(even, southern, northern)
-    northern = lon_neighbours(flag_ref, lon_first_ref[last:, :], lon_second_ref[last:, :])
-    southern = lon_neighbours(flag_ref, lon_first_ref[0:1, :], lon_second_ref[0:1, :])
+        first_ref[at, :] = by_flag(flag_ref, 1, northern, southern)
+        second_ref[at, :] = by_flag(flag_ref, 1, southern, northern)
+    east, west = lon_columns(flag_ref, lon_first_ref[...], lon_second_ref[...])
+    northern = east[-1:], west[-1:]
+    southern = east[:1], west[:1]
     for place in range(2):
         at = slice(2 * levels + place, 2 * levels + place + 1)
-        first_ref[at, :] = jnp.where(even, northern[place], southern[place])
-        second_ref[at, :] = jnp.where(even, southern[place], northern[place])
+        first_ref[at, :] = by_flag(flag_ref, 1, northern[place], southern[place])
+        second_ref[at, :] = by_flag(flag_ref, 1, southern[place], northern[place])
 
 
 def steps_kernel(
-    flag_ref, inner_ref, field_ref, side_in_ref,
-    columns_ref, edges_ref, lon_first_ref, lon_second_ref, lat_first_ref, lat_second_ref,
+    flag_ref, half_ref, masked_ref, turn_in_ref, field_ref, side_ref,
+    edges_ref, lon_first_ref, lon_second_ref, lat_first_ref, lat_second_ref,
     out_ref,
-    masked_ref, half_ref, turn_ref, side_ref, edge_ref, sems,
+    done_ref, turn_ref, edge_ref, sems,
 ):
-    levels_n, rows_n, cols_n = inner_ref.shape
+    levels_n, rows_n, cols_n = half_ref.shape
     levels = edges_ref.shape[1]
-    fold = flag_ref[2] == 1
-    east, west = lon_neighbours(flag_ref, lon_first_ref[...], lon_second_ref[...])
     up, down = lat_neighbours(flag_ref, lat_first_ref[...], lat_second_ref[...])
-    own = columns_ref[...]
 
     ends = 2 * levels
-    east_up = jnp.where(fold, pltpu.roll(up[ends + 1 : ends + 2], 1, 1), up[ends : ends + 1])
-    west_up = jnp.where(fold, pltpu.roll(up[ends : ends + 1], cols_n - 1, 1), up[ends + 1 : ends + 2])
+    east_up = by_flag(flag_ref, 2, pltpu.roll(up[ends + 1 : ends + 2], 1, 1), up[ends : ends + 1])
+    west_up = by_flag(flag_ref, 2, pltpu.roll(up[ends : ends + 1], cols_n - 1, 1), up[ends + 1 : ends + 2])
     east_down, west_down = down[ends : ends + 1], down[ends + 1 : ends + 2]
 
     up_rows, down_rows = up[ends + SUB :], down[ends + SUB :]
     turned = reversed_lanes(up_rows)
     into = field_ref[4, rows_n - 1 : rows_n, :]
     south_row = down_rows[8:9]
-    north_row = jnp.where(fold, turned[8:9], into)
+    north_row = by_flag(flag_ref, 2, turned[8:9], into)
     plain = (
         up_rows[0:1], up_rows[1:2] + up_rows[2:3] + up_rows[3:4] + into,
         up_rows[1:2], up_rows[2:3], into, up_rows[3:4], up_rows[4:5],
@@ -477,55 +533,21 @@
         down_rows[6:7], down_rows[7:8], down_rows[8:9], down_rows[9:10], down_rows[10:11],
     )
     for place in range(len(plain)):
-        edge_ref[place : place + 1, :] = jnp.where(fold, folded[place], plain[place])
+        edge_ref[place : place + 1, :] = by_flag(flag_ref, 2, folded[place], plain[place])
         edge_ref[SUB + place : SUB + place + 1, :] = low[place]
-    lanes = lane((1, cols_n))
-
-    def moved(row, source, target):
-        return jnp.where(lanes == target, pltpu.roll(row, (target - source) % cols_n, 1), 0.0)
-
-    added = (
-        moved(down_rows[12:13], 2, 1) + moved(down_rows[12:13], 2, 5)
-        + moved(down_rows[14:15], 8, 8) + moved(down_rows[14:15], 8, 12)
-    )
-    side_ref[...] = side_in_ref[...]
-    side_ref[0:1, :] = side_in_ref[0:1, :] + added
-    folding = jnp.logical_and(fold, jnp.logical_or(lanes == 4, lanes == 11))
-    side_ref[rows_n - 1 : rows_n, :] = jnp.where(
-        folding,
-        moved(up_rows[14:15], 8, 4) + moved(up_rows[12:13], 2, 11),
-        side_in_ref[rows_n - 1 : rows_n, :],
-    )
-
-    level_at = jnp.right_shift(lane((rows_n, cols_n)), 2)
-
-    def side_step(block, eastern, western, above, below, base):
-        def coefficient(place):
-            return side_ref[:, base + place : base + place + 1]
-
-        higher = jnp.where(level_at > 0, pltpu.roll(block, 4, 1) - block, 0.0)
-        lower = jnp.where(level_at < levels_n - 1, pltpu.roll(block, cols_n - 4, 1) - block, 0.0)
-        change = (
-            coefficient(2) * eastern
-            + coefficient(3) * western
-            + coefficient(4) * shifted(block, -1, 0, above)
-            + coefficient(5) * shifted(block, 1, 0, below)
-            - coefficient(1) * block
-            + coefficient(6) * (higher + lower)
-        )
-        return block + coefficient(0) * change
-
-    east_next = side_step(
-        east, pltpu.roll(east, cols_n - 1, 1), pltpu.roll(own, 1, 1), east_up, east_down, 0
-    )
-    west_next = side_step(
-        west, pltpu.roll(own, cols_n - 1, 1), pltpu.roll(west, 1, 1), west_up, west_down, 7
-    )
-    slot = jnp.bitwise_and(lane((rows_n, cols_n)), 3)
-    for step, (eastern, western) in enumerate(((east, west), (east_next, west_next))):
-        turn_ref[step] = jnp.where(
-            slot == 1, pltpu.roll(eastern, cols_n - 1, 1), pltpu.roll(western, 1, 1)
-        )
+
+    east, west = lon_columns(flag_ref, lon_first_ref[0:1, :], lon_second_ref[0:1, :])
+    east, west = east[:1], west[:1]
+    east_low = side_ref[0:1, 0:1] * down_rows[12:13, 2:3] * (east_down - east)
+    west_low = side_ref[0:1, 7:8] * down_rows[14:15, 8:9] * (west_down - west)
+    at = slice(rows_n - 1, rows_n)
+    east_onto = by_flag(flag_ref, 2, up_rows[14:15, 8:9], side_ref[at, 4:5])
+    west_onto = by_flag(flag_ref, 2, up_rows[12:13, 2:3], side_ref[at, 11:12])
+    east_high = side_ref[at, 0:1] * east_onto * east_up
+    west_high = side_ref[at, 7:8] * west_onto * west_up
+    turn_ref[...] = turn_in_ref[...]
+    turn_ref[0:1, :] = turn_in_ref[0:1, :] + turned_columns(east_low, west_low)
+    turn_ref[at, :] = turn_in_ref[at, :] + turned_columns(east_high, west_high)
 
     plane = (levels, cols_n)
     corner_at = 4 * sublane(plane)
@@ -554,8 +576,8 @@
         )
         return block + coefficient(0) * change
 
-    above = jnp.where(fold, reversed_lanes(edge(up, 0)), edge(up, 0))
-    above_outer = jnp.where(fold, reversed_lanes(edge(up, 1)), edge(up, 1))
+    above = by_flag(flag_ref, 2, reversed_lanes(edge(up, 0)), edge(up, 0))
+    above_outer = by_flag(flag_ref, 2, reversed_lanes(edge(up, 1)), edge(up, 1))
     below, below_outer = edge(down, 0), edge(down, 1)
     above_next = edge_step(
         above, above_outer, edges_ref[3], corner(east_up, 2), corner(west_up, 1), 0
@@ -563,42 +585,27 @@
     below_next = edge_step(
         below, below_outer, edges_ref[0], corner(east_down, 2), corner(west_down, 1), SUB
     )
-    for level in range(levels_n):
-        masked_ref[level, SUB + rows_n : SUB + rows_n + 1, :] = above_next[level : level + 1, :]
-        masked_ref[level, SUB - 1 : SUB, :] = below_next[level : level + 1, :]
-    first = lane((SUB, cols_n)) == 0
-    last = lane((SUB, cols_n)) == cols_n - 1
-    for top in range(0, rows_n, SUB):
-        at, inner = slice(top, top + SUB), slice(top + SUB, top + 2 * SUB)
-        ocean = field_ref[0, at, :]
-        side = jnp.where(last, field_ref[2, at, :], jnp.where(first, field_ref[3, at, :], 0.0))
-        turned = turn_ref[0, at, :]
-        place = sublane((SUB, cols_n))
-        for level in range(levels_n):
-            beyond = pltpu.roll(turned, (2 * cols_n - 2 - 4 * level) % cols_n, 1)
-            found = inner_ref[level, at, :] + side * beyond
-            if top == 0:
-                below_row = south_row * (below - edges_ref[0])[level : level + 1, :]
-                found = found + jnp.where(place == 0, below_row, 0.0)
-            if top == rows_n - SUB:
-                above_row = north_row * above[level : level + 1, :]
-                found = found + jnp.where(place == SUB - 1, above_row, 0.0)
-            half_ref[level, at, :] = found
-            masked_ref[level, inner, :] = ocean * found
-
+    def rows_of(block):
+        return [block[level : level + 1] for level in range(levels_n)]
+
+    patch = (
+        south_row, north_row, rows_of(south_row * (below - edges_ref[0])), rows_of(north_row * above)
+    )
     copies = []
 
-    def store(level, top, ocean, found):
-        half_ref[level, top : top + SUB, :] = found
+    def store(level, top, found):
+        done_ref[level, top : top + SUB, :] = found
         if level == levels_n - 1 and (top + SUB) % (rows_n // sems.shape[0]) == 0:
             rows = slice(top + SUB - rows_n // sems.shape[0], top + SUB)
             copy = pltpu.make_async_copy(
-                half_ref.at[:, rows, :], out_ref.at[:, rows, :], sems.at[len(copies)]
+                done_ref.at[:, rows, :], out_ref.at[:, rows, :], sems.at[len(copies)]
             )
             copy.start()
             copies.append(copy)
 
-    advance(half_ref, masked_ref, field_ref, turn_ref.at[1], store, south_row, north_row)
+    advance(
+        half_ref, masked_ref, field_ref, turn_ref, rows_of(below_next), rows_of(above_next), store, patch
+    )
     for copy in copies:
         copy.wait()
 
@@ -618,10 +625,6 @@
     )
 
 
-def flagged(inputs):
-    return [pltpu.SMEM] + [pltpu.VMEM] * (inputs - 1)
-
-
 def exchanged(value, devices):
     rows = value.reshape(devices, 1, value.size // devices)
     return lax.all_to_all(rows, BOTH, split_axis=0, concat_axis=0, tiled=True).reshape(value.shape)
@@ -631,12 +634,12 @@
     return jax.ShapeDtypeStruct(shape, jnp.float32)
 
 
-def lon_swaps(value):
+def lon_swaps(first_value, second_value):
     count = lax.axis_size("lon")
     assert count % 2 == 0
     first = [(i, i ^ 1) for i in range(count)]
     second = [(i, (i + 1 if i % 2 else i - 1) % count) for i in range(count)]
-    return lax.ppermute(value, "lon", first), lax.ppermute(value, "lon", second)
+    return lax.ppermute(first_value, "lon", first), lax.ppermute(second_value, "lon", second)
 
 
 def lat_swaps(*values):
@@ -676,10 +679,13 @@
     assert 2 * (slots // devices) == LANES and cols_n == LANES and 4 * levels_n <= LANES
     half = (levels_n + 1) // 2
     width = rows_n // GROUP * cols_n
+    tile = min(slots, SLOT_TILE)
+    tiles = slots // tile
     bf16 = jnp.bfloat16
     raw = (land_mask, east_coef, north_coef, zonal_flow, vertical_coef)
     lon, lat = lax.axis_index("lon"), lax.axis_index("lat")
     flags = jnp.stack([1 - lon % 2, 1 - lat % 2, lat == lax.axis_size("lat") - 1]).astype(jnp.int32)
+    flags = jnp.broadcast_to(flags[:, None], (3, LANES))
 
     partial_vals = kernel_call(
         60,
@@ -697,11 +703,11 @@
     levels = padded_levels(levels_n)
     partial_vals, raw = lax.optimization_barrier((partial_vals, raw))
     arrived = exchanged(partial_vals, devices)
-    columns = kernel_call(8, coefficient_columns_kernel, f32(2 * SUB, rows_n))(*raw)
-    arrived, side_coefs = lax.optimization_barrier((arrived, lon_swaps(columns)))
+    columns = kernel_call(4, coefficient_columns_kernel, f32(2 * SUB, rows_n))(*raw)
+    arrived, side_coefs = lax.optimization_barrier((arrived, lon_swaps(columns, columns)))
 
     misfit, outgoing = kernel_call(
-        32,
+        8 + 4 * tiles,
         observe_kernel,
         (f32(levels_n, obs_n), f32(devices * half, LANES)),
         [pltpu.VMEM((obs_n, slots), bf16)],
@@ -711,62 +717,64 @@
     )
     returned = exchanged(outgoing, devices)
     strips = kernel_call(
-        8,
+        5,
         seed_strips_kernel,
         (f32(rows_n, cols_n), f32(rows_n, cols_n), f32(4, levels, cols_n)),
     )(adjoint_early, raw[0])
     fields, sides, row_coefs = kernel_call(
-        8,
+        5,
         coefficients_kernel,
         (f32(7, rows_n, cols_n), f32(rows_n, cols_n), f32(2 * SUB, cols_n)),
-        (), flagged(8),
+        (),
     )(flags, *raw, *side_coefs)
     returned, strips, fields, sides, row_coefs = lax.optimization_barrier(
         (returned, strips, fields, sides, row_coefs)
     )
-    tile = min(slots, SLOT_TILE)
-    own_columns, own_edges = kernel_call(
-        32,
+    own_columns, for_first, for_second, own_edges = kernel_call(
+        7 + 3 * tiles,
         functools.partial(strips_kernel, levels_n),
-        (f32(rows_n, cols_n), f32(4, levels, cols_n)),
-        [pltpu.VMEM((rows_n, 3 * tile), bf16), pltpu.VMEM((4 * levels, 3 * tile), bf16)],
-    )(returned, slot_cell, slot_weight, land_mask, *strips)
-    columns_beside = lon_swaps(own_columns)
-    extended = (levels_n, rows_n + 2 * SUB, cols_n)
+        (
+            f32(rows_n, cols_n),
+            f32(rows_n // 2, cols_n),
+            f32(rows_n // 2, cols_n),
+            f32(4, levels, cols_n),
+        ),
+        (),
+    )(flags, returned, slot_cell, slot_weight, land_mask, *strips)
+    columns_beside = lon_swaps(for_first, for_second)
+    whole = (levels_n, rows_n, cols_n)
     seed = kernel_call(
-        40,
+        22 + 3 * tiles,
         scatter_kernel,
         f32(levels_n, rows_n, cols_n),
-        [pltpu.VMEM((levels_n * GROUP, 3 * tile), bf16), pltpu.VMEM((width, 3 * tile), bf16)],
+        [pltpu.VMEM((2 * levels_n * GROUP, tile), bf16)],
     )(returned, slot_cell, slot_weight, adjoint_in)
     seed, columns_beside = lax.optimization_barrier((seed, columns_beside))
     message = f32(2 * levels + 3 * SUB, cols_n)
-    messages = kernel_call(8, edge_message_kernel, (message, message), (), flagged(5))(
+    messages = kernel_call(2, edge_message_kernel, (message, message), ())(
         flags, own_edges, *columns_beside, row_coefs
     )
     rows_beside = lat_swaps(*messages)
     seed, messages = lax.optimization_barrier((seed, messages))
-    inner = kernel_call(
-        16,
-        inner_step_kernel,
-        f32(levels_n, rows_n, cols_n),
-        [pltpu.VMEM(extended, jnp.float32)],
-    )(seed, fields)
-    inner, rows_beside = lax.optimization_barrier((inner, rows_beside))
+    beside = kernel_call(
+        8,
+        beside_kernel,
+        (f32(*whole), f32(*whole), f32(rows_n, cols_n)),
+        [pltpu.VMEM(whole, jnp.float32)],
+    )(flags, seed, fields, sides, own_columns, *columns_beside)
+    beside, rows_beside = lax.optimization_barrier((beside, rows_beside))
     adjoint_state = kernel_call(
-        16,
+        10,
         steps_kernel,
-        f32(levels_n, rows_n, cols_n),
+        f32(*whole),
         [
-            pltpu.VMEM(extended, jnp.float32),
-            pltpu.VMEM((levels_n, rows_n, cols_n), jnp.float32),
-            pltpu.VMEM((STEPS, rows_n, cols_n), jnp.float32),
+            pltpu.VMEM(whole, jnp.float32),
             pltpu.VMEM((rows_n, cols_n), jnp.float32),
             pltpu.VMEM((2 * SUB, cols_n), jnp.float32),
             pltpu.SemaphoreType.DMA((4,)),
         ],
-        flagged(10), pltpu.HBM,
-    )(flags, inner, fields, sides, own_columns, own_edges, *columns_beside, *rows_beside)
+        [pltpu.VMEM] * 11, pltpu.HBM,
+    )(flags, *beside, fields, sides, own_edges, *columns_beside, *rows_beside)
     return (adjoint_state, misfit)
 
 

time: 60.6 us -> 58.4 us (0.964)
  the two profiles are of different devices: /device:TPU:7 before, /device:TPU:5 now
where the time goes in v7:
time: 58.4 us; the launch traced here: 58.1 us
  Pallas kernels  22.7 us (39%)
  starting transfers between devices  21.9 us (38%)
  waiting for transfers between devices  12.3 us (21%)
  between operations  1.03 us (2%)
    all_to_all x2, starting transfers between devices, exchanged(): lax.all_to_all(rows, BOTH, split_axis=0, concat_axis=0, tiled=True)  10.1 us
    pallas_call x1, Pallas kernels, on_device(): kernel_call(60, gather_kernel, f32(devices * half, LANES), [pltpu.VMEM((1...  8.56 us
    all_to_all x2, waiting for transfers between devices, exchanged(): lax.all_to_all(rows, BOTH, split_axis=0, concat_axis=0, tiled=True)  6.24 us
    ppermute x2, starting transfers between devices, lon_swaps(): lax.ppermute(second_value, 'lon', second)  5.86 us
    ppermute x2, starting transfers between devices, lat_swaps(): found.append(lax.ppermute(values[parity], BOTH, pairs))  5.57 us
    ppermute x2, waiting for transfers between devices, lon_swaps(): lax.ppermute(second_value, 'lon', second)  3.81 us
    pallas_call x1, Pallas kernels, on_device(): kernel_call(22 + 3 * tiles, scatter_kernel, f32(levels_n, rows_n, cols_n)...  3.59 us
    pallas_call x1, Pallas kernels, on_device(): kernel_call(5, seed_strips_kernel, (f32(rows_n, cols_n), f32(rows_n, cols...  2.46 us
  transfers between devices with their start and end apart: 8, of which 4 were waited for; matrix products, arithmetic and copies ran while one was open for 0% of the time, Pallas kernels for 15%

profile of v7, /device:TPU:5, one launch (start us, length us, event | category | flops | bytes accessed | tf_op | source)
XLA Modules:
  0.0 58.1 jit_solution(18409706136097635241)
XLA Ops:
  0.6 0.0 copy-start.1
  0.6 0.0 copy-start.5
  0.7 0.0 copy-start.4
  0.7 0.0 copy-start.3
  0.7 0.0 copy-start.2
  0.7 0.0 copy-start.9
  0.7 0.0 copy-start.8
  0.7 0.0 copy-start.10
  0.7 0.0 copy-start
  0.7 8.6 %shard_map.131 = f32[416,128]{1,0:T(8,128)} custom-call(s32[1,2048]{1,0:T(1,128)} %cell_ref.3, f32[1,2048]{1,0:T(1,128)} %weight_ref.3, f32[25,128,128]{2,1,0:T(8,128)} %state_in.1), custom_call_target="tpu_custom_call" | custom-call | tf_op jit(solution)/shard_map/pallas_call | solution.py:690
  9.3 6.4 %all-to-all-start = ((f32[32,1,1664]{2,1,0:T(1,128)}), f32[32,1,1664]{2,1,0:T(1,128)S(1)}, u32[]{:S(2)}, u32[]{:S(2)}) async-start(f32[32,1,1664]{2,1,0:T(1,128)} %bitcast.10), calls=%async_computation | async-start | bytes 425984 | tf_op jit(solution)/shard_map/all_to_all | solution.py:630
  15.7 0.0 copy-done.1
  15.7 0.0 copy-done.5
  15.7 0.0 copy-done.4
  15.7 0.0 copy-done.3
  15.8 0.0 copy-done.2
  15.8 0.0 copy-start.6
  15.8 0.0 copy-start.7
  15.8 0.3 shard_map.132
  16.0 4.0 %collective-permute-start.1 = (f32[16,128]{1,0:T(8,128)S(1)}, f32[16,128]{1,0:T(8,128)S(1)}, u32[]{:S(2)}, u32[]{:S(2)}) collective-permute-start(f32[16,128]{1,0:T(8,128)S(1)} %shard_map.132), channel_id=1, source_target_pairs={{0,28},{4,8},{8,4},{12,16},{16,12},{20,24},{24,20},{28,0},{1,29},{... | collective-permute-start | bytes 24584 | tf_op jit(solution)/shard_map/ppermute | solution.py:642
  20.1 0.0 collective-permute-start
  20.1 3.8 %collective-permute-done.1.lon_second_ref = f32[16,128]{1,0:T(8,128)S(1)} collective-permute-done((f32[16,128]{1,0:T(8,128)S(1)}, f32[16,128]{1,0:T(8,128)S(1)}, u32[]{:S(2)}, u32[]{:S(2)}) %collective-permute-start.1) | collective-permute-done | bytes 8224 | tf_op jit(solution)/shard_map/ppermute | solution.py:642
  23.9 0.0 collective-permute-done.lon_first_ref
  23.9 0.8 %all-to-all-done = f32[32,1,1664]{2,1,0:T(1,128)S(1)} async-done(((f32[32,1,1664]{2,1,0:T(1,128)}), f32[32,1,1664]{2,1,0:T(1,128)S(1)}, u32[]{:S(2)}, u32[]{:S(2)}) %all-to-all-start) | async-done | bytes 213024 | tf_op jit(solution)/shard_map/all_to_all | solution.py:630
  24.6 0.0 copy-done.9
  24.6 0.0 copy-done.8
  24.6 0.0 copy-done.10
  24.6 2.1 %shard_map.133 = (f32[25,512]{1,0:T(8,128)}, f32[416,128]{1,0:T(8,128)}) custom-call(f32[416,128]{1,0:T(8,128)S(1)} %bitcast.9, s32[1,2048]{1,0:T(1,128)S(1)} %copy-done.10, f32[25,512]{1,0:T(8,128)S(1)} %copy-done.8, f32[25,512]{1,0:T(8,128)S(1)} %copy-done.9), custom_call_target="tpu_custom_call" | custom-call | tf_op jit(solution)/shard_map/pallas_call | solution.py:709
  26.7 3.7 %all-to-all-start.1 = ((f32[32,1,1664]{2,1,0:T(1,128)}), f32[32,1,1664]{2,1,0:T(1,128)S(1)}, u32[]{:S(2)}, u32[]{:S(2)}) async-start(f32[32,1,1664]{2,1,0:T(1,128)} %bitcast.5), calls=%async_computation.1 | async-start | bytes 425984 | tf_op jit(solution)/shard_map/all_to_all | solution.py:630
  30.4 0.1 pad_add_fusion
  30.5 2.5 %shard_map.134 = (f32[128,128]{1,0:T(8,128)S(1)}, f32[128,128]{1,0:T(8,128)S(1)}, f32[4,32,128]{2,1,0:T(8,128)S(1)}) custom-call(f32[25,128,128]{2,1,0:T(8,128)S(1)} %copy-done, s32[128,128]{1,0:T(8,128)S(1)} %copy-done.1), custom_call_target="tpu_custom_call" | custom-call | tf_op jit(solution)/shard_map/pallas_call | solution.py:719
  32.9 0.1 broadcast_in_dim.2.flag_ref
  33.0 0.4 shard_map.135
  33.4 5.5 %all-to-all-done.1 = f32[32,1,1664]{2,1,0:T(1,128)S(1)} async-done(((f32[32,1,1664]{2,1,0:T(1,128)}), f32[32,1,1664]{2,1,0:T(1,128)S(1)}, u32[]{:S(2)}, u32[]{:S(2)}) %all-to-all-start.1) | async-done | bytes 213024 | tf_op jit(solution)/shard_map/all_to_all | solution.py:630
  38.8 0.0 copy-done.6
  38.9 1.1 %shard_map.137 = (f32[128,128]{1,0:T(8,128)S(1)}, f32[64,128]{1,0:T(8,128)S(1)}, f32[64,128]{1,0:T(8,128)S(1)}, f32[4,32,128]{2,1,0:T(8,128)S(1)}) custom-call(s32[3,128]{1,0:T(4,128)S(1)} %broadcast_in_dim.2.flag_ref, f32[416,128]{1,0:T(8,128)S(1)} %bitcast.7, s32[1,2048]{1,0:T(1,128)S(1)} %copy-done.6, f32[1,2048]{1,0:T(1,128)S(1)} %copy-done.7, ...), custom_call_target="tpu_custom_call" | custom-call | tf_op jit(solution)/shard_map/pallas_call | solution.py:733
  39.9 0.4 collective-permute-start.2
  40.3 1.8 %collective-permute-start.3 = (f32[64,128]{1,0:T(8,128)S(1)}, f32[64,128]{1,0:T(8,128)S(1)}, u32[]{:S(2)}, u32[]{:S(2)}) collective-permute-start(f32[64,128]{1,0:T(8,128)S(1)} %get-tuple-element.83), channel_id=1, source_target_pairs={{0,28},{4,8},{8,4},{12,16},{16,12},{20,24},{24,20},{28,0},{1,29},{... | collective-permute-start | bytes 98312 | tf_op jit(solution)/shard_map/ppermute | solution.py:642
  42.2 3.6 %shard_map.136.seed_ref = f32[25,128,128]{2,1,0:T(8,128)S(1)} custom-call(f32[416,128]{1,0:T(8,128)S(1)} %bitcast.8, s32[1,2048]{1,0:T(1,128)S(1)} %copy-done.6, f32[1,2048]{1,0:T(1,128)S(1)} %copy-done.7, f32[25,128,128]{2,1,0:T(8,128)S(1)} %copy-done), custom_call_target="tpu_custom_call" | custom-call | tf_op jit(solution)/shard_map/pallas_call | solution.py:746
  45.8 0.0 collective-permute-done.2.lon_first_ref.first_ref
  45.8 0.0 collective-permute-done.3.lon_second_ref.second_ref
  45.8 0.1 shard_map.138
  45.9 2.2 %collective-permute-start.4 = (f32[88,128]{1,0:T(8,128)S(1)}, f32[88,128]{1,0:T(8,128)S(1)}, u32[]{:S(2)}, u32[]{:S(2)}) collective-permute-start(f32[88,128]{1,0:T(8,128)S(1)} %get-tuple-element.89), channel_id=1, source_target_pairs={{0,1},{1,0},{2,3},{3,2},{4,5},{5,4},{6,7},{7,6},{8,9},{9,8},{10,11... | collective-permute-start | bytes 135176 | tf_op jit(solution)/shard_map/ppermute | solution.py:657
  48.1 3.4 %collective-permute-start.5 = (f32[88,128]{1,0:T(8,128)S(1)}, f32[88,128]{1,0:T(8,128)S(1)}, u32[]{:S(2)}, u32[]{:S(2)}) collective-permute-start(f32[88,128]{1,0:T(8,128)S(1)} %get-tuple-element.90), channel_id=1, source_target_pairs={{1,2},{2,1},{3,31},{5,6},{6,5},{7,27},{9,10},{10,9},{11,23},{13,14... | collective-permute-start | bytes 135176 | tf_op jit(solution)/shard_map/ppermute | solution.py:657
  51.4 1.9 %shard_map.139 = (f32[25,128,128]{2,1,0:T(8,128)S(1)}, f32[25,128,128]{2,1,0:T(8,128)S(1)}, f32[128,128]{1,0:T(8,128)S(1)}) custom-call(s32[3,128]{1,0:T(4,128)S(1)} %broadcast_in_dim.2.flag_ref, f32[25,128,128]{2,1,0:T(8,128)S(1)} %shard_map.136.seed_ref, f32[7,128,128]{2,1,0:T(8,128)S(1)} %get-tuple-element.92.field_ref, ...), custom_call_target="tpu_custom_call" | custom-call | tf_op jit(solution)/shard_map/pallas_call | solution.py:759
  53.3 0.0 collective-permute-done.4.lat_first_ref
  53.3 2.2 %collective-permute-done.5.lat_second_ref = f32[88,128]{1,0:T(8,128)S(1)} collective-permute-done((f32[88,128]{1,0:T(8,128)S(1)}, f32[88,128]{1,0:T(8,128)S(1)}, u32[]{:S(2)}, u32[]{:S(2)}) %collective-permute-start.5) | collective-permute-done | bytes 45088 | tf_op jit(solution)/shard_map/ppermute | solution.py:657
  55.6 2.4 %shard_map.140 = f32[25,128,128]{2,1,0:T(8,128)} custom-call(s32[3,128]{1,0:T(4,128)S(1)} %broadcast_in_dim.2.flag_ref, f32[25,128,128]{2,1,0:T(8,128)S(1)} %get-tuple-element.98.half_ref, f32[25,128,128]{2,1,0:T(8,128)S(1)} %get-tuple-element.99.masked_ref, f32[128,128]{1,0:T(8,128)S(1)} %get-tuple-element.100.turn_in_ref, ...), custom_call_target="tpu_custom_call" | custom-call | tf_op jit(solution)/shard_map/pallas_call | solution.py:766
  (2 shorter events, 0.0 us)
Async XLA Ops:
  0.6 15.1 %copy-start.1 = (s32[128,128]{1,0:T(8,128)S(1)}, s32[128,128]{1,0:T(8,128)}, u32[]{:S(2)}) copy-start(s32[128,128]{1,0:T(8,128)} %mask_ref.4) | copy-start | bytes 196612
  0.6 15.1 %copy-start.5 = (f32[128,128]{1,0:T(8,128)S(1)}, f32[128,128]{1,0:T(8,128)}, u32[]{:S(2)}) copy-start(f32[128,128]{1,0:T(8,128)} %vertical_ref.1) | copy-start | bytes 196612
  0.7 15.1 %copy-start.4 = (f32[128,128]{1,0:T(8,128)S(1)}, f32[128,128]{1,0:T(8,128)}, u32[]{:S(2)}) copy-start(f32[128,128]{1,0:T(8,128)} %flow_ref.1) | copy-start | bytes 196612
  0.7 15.1 %copy-start.3 = (f32[128,128]{1,0:T(8,128)S(1)}, f32[128,128]{1,0:T(8,128)}, u32[]{:S(2)}) copy-start(f32[128,128]{1,0:T(8,128)} %north_ref.1) | copy-start | bytes 196612
  0.7 15.1 %copy-start.2 = (f32[128,128]{1,0:T(8,128)S(1)}, f32[128,128]{1,0:T(8,128)}, u32[]{:S(2)}) copy-start(f32[128,128]{1,0:T(8,128)} %east_ref.1) | copy-start | bytes 196612
  0.7 24.0 %copy-start.9 = (f32[25,512]{1,0:T(8,128)S(1)}, f32[25,512]{1,0:T(8,128)}, u32[]{:S(2)}) copy-start(f32[25,512]{1,0:T(8,128)} %invvar_ref.1) | copy-start | bytes 153604
  0.7 23.9 %copy-start.8 = (f32[25,512]{1,0:T(8,128)S(1)}, f32[25,512]{1,0:T(8,128)}, u32[]{:S(2)}) copy-start(f32[25,512]{1,0:T(8,128)} %value_ref.1) | copy-start | bytes 153604
  0.7 23.9 %copy-start.10 = (s32[1,2048]{1,0:T(1,128)S(1)}, s32[1,2048]{1,0:T(1,128)}, u32[]{:S(2)}) copy-start(s32[1,2048]{1,0:T(1,128)} %target_ref.1) | copy-start | bytes 24580
  0.7 29.8 %copy-start = (f32[25,128,128]{2,1,0:T(8,128)S(1)}, f32[25,128,128]{2,1,0:T(8,128)}, u32[]{:S(2)}) copy-start(f32[25,128,128]{2,1,0:T(8,128)} %adjoint_ref.2) | copy-start | bytes 4915204
  9.3 15.3 %all-to-all-start = ((f32[32,1,1664]{2,1,0:T(1,128)}), f32[32,1,1664]{2,1,0:T(1,128)S(1)}, u32[]{:S(2)}, u32[]{:S(2)}) async-start(f32[32,1,1664]{2,1,0:T(1,128)} %bitcast.10), calls=%async_computation | async-start | bytes 425984 | tf_op jit(solution)/shard_map/all_to_all | solution.py:630
  15.8 23.1 %copy-start.6 = (s32[1,2048]{1,0:T(1,128)S(1)}, s32[1,2048]{1,0:T(1,128)}, u32[]{:S(2)}) copy-start(s32[1,2048]{1,0:T(1,128)} %cell_ref.3) | copy-start | bytes 24580
  15.8 23.1 %copy-start.7 = (f32[1,2048]{1,0:T(1,128)S(1)}, f32[1,2048]{1,0:T(1,128)}, u32[]{:S(2)}) copy-start(f32[1,2048]{1,0:T(1,128)} %weight_ref.3) | copy-start | bytes 24580
  16.0 7.8 %collective-permute-start.1 = (f32[16,128]{1,0:T(8,128)S(1)}, f32[16,128]{1,0:T(8,128)S(1)}, u32[]{:S(2)}, u32[]{:S(2)}) collective-permute-start(f32[16,128]{1,0:T(8,128)S(1)} %shard_map.132), channel_id=1, source_target_pairs={{0,28},{4,8},{8,4},{12,16},{16,12},{20,24},{24,20},{28,0},{1,29},{... | collective-permute-start | bytes 24584 | tf_op jit(solution)/shard_map/ppermute | solution.py:642
  20.1 3.8 %collective-permute-start = (f32[16,128]{1,0:T(8,128)S(1)}, f32[16,128]{1,0:T(8,128)S(1)}, u32[]{:S(2)}, u32[]{:S(2)}) collective-permute-start(f32[16,128]{1,0:T(8,128)S(1)} %shard_map.132), channel_id=1, source_target_pairs={{0,4},{4,0},{8,12},{12,8},{16,20},{20,16},{24,28},{28,24},{1,5},{5... | collective-permute-start | bytes 24584 | tf_op jit(solution)/shard_map/ppermute | solution.py:642
  26.7 12.1 %all-to-all-start.1 = ((f32[32,1,1664]{2,1,0:T(1,128)}), f32[32,1,1664]{2,1,0:T(1,128)S(1)}, u32[]{:S(2)}, u32[]{:S(2)}) async-start(f32[32,1,1664]{2,1,0:T(1,128)} %bitcast.5), calls=%async_computation.1 | async-start | bytes 425984 | tf_op jit(solution)/shard_map/all_to_all | solution.py:630
  39.9 5.8 %collective-permute-start.2 = (f32[64,128]{1,0:T(8,128)S(1)}, f32[64,128]{1,0:T(8,128)S(1)}, u32[]{:S(2)}, u32[]{:S(2)}) collective-permute-start(f32[64,128]{1,0:T(8,128)S(1)} %get-tuple-element.82), channel_id=1, source_target_pairs={{0,4},{4,0},{8,12},{12,8},{16,20},{20,16},{24,28},{28,24},{1,5},{5... | collective-permute-start | bytes 98312 | tf_op jit(solution)/shard_map/ppermute | solution.py:642
  40.3 5.5 %collective-permute-start.3 = (f32[64,128]{1,0:T(8,128)S(1)}, f32[64,128]{1,0:T(8,128)S(1)}, u32[]{:S(2)}, u32[]{:S(2)}) collective-permute-start(f32[64,128]{1,0:T(8,128)S(1)} %get-tuple-element.83), channel_id=1, source_target_pairs={{0,28},{4,8},{8,4},{12,16},{16,12},{20,24},{24,20},{28,0},{1,29},{... | collective-permute-start | bytes 98312 | tf_op jit(solution)/shard_map/ppermute | solution.py:642
  45.9 7.5 %collective-permute-start.4 = (f32[88,128]{1,0:T(8,128)S(1)}, f32[88,128]{1,0:T(8,128)S(1)}, u32[]{:S(2)}, u32[]{:S(2)}) collective-permute-start(f32[88,128]{1,0:T(8,128)S(1)} %get-tuple-element.89), channel_id=1, source_target_pairs={{0,1},{1,0},{2,3},{3,2},{4,5},{5,4},{6,7},{7,6},{8,9},{9,8},{10,11... | collective-permute-start | bytes 135176 | tf_op jit(solution)/shard_map/ppermute | solution.py:657
  48.1 7.5 %collective-permute-start.5 = (f32[88,128]{1,0:T(8,128)S(1)}, f32[88,128]{1,0:T(8,128)S(1)}, u32[]{:S(2)}, u32[]{:S(2)}) collective-permute-start(f32[88,128]{1,0:T(8,128)S(1)} %get-tuple-element.90), channel_id=1, source_target_pairs={{1,2},{2,1},{3,31},{5,6},{6,5},{7,27},{9,10},{10,9},{11,23},{13,14... | collective-permute-start | bytes 135176 | tf_op jit(solution)/shard_map/ppermute | solution.py:657

commit v8 on v7

--- a/solution.py
+++ b/solution.py
@@ -79,7 +79,7 @@
     width = groups * cols_n
     slots = cell_ref.shape[1]
     tile = min(slots, SLOT_TILE)
-    chunk = max(n for n in range(1, 9) if levels_n % n == 0)
+    chunk = levels_n
     copies = [
         pltpu.make_async_copy(cell_in, cell_ref, sems.at[0]),
         pltpu.make_async_copy(weight_in, weight_ref, sems.at[1]),
@@ -189,7 +189,7 @@
 
 def strips_kernel(
     levels_n, flag_ref, returned_ref, cell_ref, weight_ref, mask_ref, seed_columns_ref, ocean_ref, seed_edges_ref,
-    columns_ref, first_ref, second_ref, edges_ref,
+    columns_ref, second_ref, first_ref, edges_ref,
 ):
     rows_n, cols_n = mask_ref.shape
     places, levels, _ = edges_ref.shape
@@ -480,7 +480,7 @@
 
 
 def edge_message_kernel(
-    flag_ref, edges_ref, lon_first_ref, lon_second_ref, row_ref, first_ref, second_ref
+    flag_ref, edges_ref, lon_first_ref, lon_second_ref, row_ref, second_ref, first_ref
 ):
     places, levels, cols_n = edges_ref.shape
     for ref in (first_ref, second_ref):
@@ -730,7 +730,7 @@
     returned, strips, fields, sides, row_coefs = lax.optimization_barrier(
         (returned, strips, fields, sides, row_coefs)
     )
-    own_columns, for_first, for_second, own_edges = kernel_call(
+    own_columns, for_second, for_first, own_edges = kernel_call(
         7 + 3 * tiles,
         functools.partial(strips_kernel, levels_n),
         (
@@ -754,7 +754,7 @@
     messages = kernel_call(2, edge_message_kernel, (message, message), ())(
         flags, own_edges, *columns_beside, row_coefs
     )
-    rows_beside = lat_swaps(*messages)
+    rows_beside = lat_swaps(messages[1], messages[0])
     seed, messages = lax.optimization_barrier((seed, messages))
     beside = kernel_call(
         8,

time: 58.4 us -> 56.8 us (0.973)
  the two profiles are of different devices: /device:TPU:5 before, /device:TPU:0 now
where the time goes in v8:
time: 56.8 us; the launch traced here: 56.5 us
  Pallas kernels  22.1 us (39%)
  starting transfers between devices  21.5 us (38%)
  waiting for transfers between devices  11.7 us (21%)
  between operations  1.04 us (2%)
    all_to_all x2, starting transfers between devices, exchanged(): lax.all_to_all(rows, BOTH, split_axis=0, concat_axis=0, tiled=True)  10.5 us
    pallas_call x1, Pallas kernels, on_device(): kernel_call(60, gather_kernel, f32(devices * half, LANES), [pltpu.VMEM((1...  8.01 us
    ppermute x2, starting transfers between devices, lon_swaps(): lax.ppermute(second_value, 'lon', second)  6.76 us
    all_to_all x2, waiting for transfers between devices, exchanged(): lax.all_to_all(rows, BOTH, split_axis=0, concat_axis=0, tiled=True)  6.52 us
    ppermute x2, waiting for transfers between devices, lon_swaps(): lax.ppermute(second_value, 'lon', second)  5.13 us
    pallas_call x1, Pallas kernels, on_device(): kernel_call(22 + 3 * tiles, scatter_kernel, f32(levels_n, rows_n, cols_n)...  3.59 us
    ppermute x2, starting transfers between devices, lat_swaps(): found.append(lax.ppermute(values[parity], BOTH, pairs))  3.27 us
    pallas_call x1, Pallas kernels, on_device(): kernel_call(5, seed_strips_kernel, (f32(rows_n, cols_n), f32(rows_n, cols...  2.46 us
  transfers between devices with their start and end apart: 8, of which 4 were waited for; matrix products, arithmetic and copies ran while one was open for 0% of the time, Pallas kernels for 15%

profile of v8, /device:TPU:0, one launch (start us, length us, event | category | flops | bytes accessed | tf_op | source)
XLA Modules:
  0.0 56.5 jit_solution(15632465943813194327)
XLA Ops:
  0.6 0.0 copy-start.1
  0.6 0.0 copy-start.5
  0.7 0.0 copy-start.4
  0.7 0.0 copy-start.3
  0.7 0.0 copy-start.2
  0.7 0.0 copy-start.9
  0.7 0.0 copy-start.8
  0.7 0.0 copy-start.10
  0.7 0.0 copy-start
  0.7 8.0 %shard_map.131 = f32[416,128]{1,0:T(8,128)} custom-call(s32[1,2048]{1,0:T(1,128)} %cell_ref.3, f32[1,2048]{1,0:T(1,128)} %weight_ref.3, f32[25,128,128]{2,1,0:T(8,128)} %state_in.1), custom_call_target="tpu_custom_call" | custom-call | tf_op jit(solution)/shard_map/pallas_call | solution.py:690
  8.7 7.3 %all-to-all-start = ((f32[32,1,1664]{2,1,0:T(1,128)}), f32[32,1,1664]{2,1,0:T(1,128)S(1)}, u32[]{:S(2)}, u32[]{:S(2)}) async-start(f32[32,1,1664]{2,1,0:T(1,128)} %bitcast.10), calls=%async_computation | async-start | bytes 425984 | tf_op jit(solution)/shard_map/all_to_all | solution.py:630
  16.0 0.0 copy-done.1
  16.1 0.0 copy-done.5
  16.1 0.0 copy-done.4
  16.1 0.0 copy-done.3
  16.1 0.0 copy-done.2
  16.1 0.0 copy-start.6
  16.1 0.0 copy-start.7
  16.1 0.3 shard_map.132
  16.4 4.6 %collective-permute-start.1 = (f32[16,128]{1,0:T(8,128)S(1)}, f32[16,128]{1,0:T(8,128)S(1)}, u32[]{:S(2)}, u32[]{:S(2)}) collective-permute-start(f32[16,128]{1,0:T(8,128)S(1)} %shard_map.132), channel_id=1, source_target_pairs={{0,28},{4,8},{8,4},{12,16},{16,12},{20,24},{24,20},{28,0},{1,29},{... | collective-permute-start | bytes 24584 | tf_op jit(solution)/shard_map/ppermute | solution.py:642
  21.0 0.0 collective-permute-start
  21.0 4.3 %collective-permute-done.1.lon_second_ref = f32[16,128]{1,0:T(8,128)S(1)} collective-permute-done((f32[16,128]{1,0:T(8,128)S(1)}, f32[16,128]{1,0:T(8,128)S(1)}, u32[]{:S(2)}, u32[]{:S(2)}) %collective-permute-start.1) | collective-permute-done | bytes 8224 | tf_op jit(solution)/shard_map/ppermute | solution.py:642
  25.3 0.0 collective-permute-done.lon_first_ref
  25.3 0.1 all-to-all-done
  25.4 0.0 copy-done.9
  25.4 0.0 copy-done.8
  25.4 0.0 copy-done.10
  25.4 2.1 %shard_map.133 = (f32[25,512]{1,0:T(8,128)}, f32[416,128]{1,0:T(8,128)}) custom-call(f32[416,128]{1,0:T(8,128)S(1)} %bitcast.9, s32[1,2048]{1,0:T(1,128)S(1)} %copy-done.10, f32[25,512]{1,0:T(8,128)S(1)} %copy-done.8, f32[25,512]{1,0:T(8,128)S(1)} %copy-done.9), custom_call_target="tpu_custom_call" | custom-call | tf_op jit(solution)/shard_map/pallas_call | solution.py:709
  27.5 3.2 %all-to-all-start.1 = ((f32[32,1,1664]{2,1,0:T(1,128)}), f32[32,1,1664]{2,1,0:T(1,128)S(1)}, u32[]{:S(2)}, u32[]{:S(2)}) async-start(f32[32,1,1664]{2,1,0:T(1,128)} %bitcast.5), calls=%async_computation.1 | async-start | bytes 425984 | tf_op jit(solution)/shard_map/all_to_all | solution.py:630
  30.7 0.1 pad_add_fusion
  30.8 2.5 %shard_map.134 = (f32[128,128]{1,0:T(8,128)S(1)}, f32[128,128]{1,0:T(8,128)S(1)}, f32[4,32,128]{2,1,0:T(8,128)S(1)}) custom-call(f32[25,128,128]{2,1,0:T(8,128)S(1)} %copy-done, s32[128,128]{1,0:T(8,128)S(1)} %copy-done.1), custom_call_target="tpu_custom_call" | custom-call | tf_op jit(solution)/shard_map/pallas_call | solution.py:719
  33.3 0.1 broadcast_in_dim.2.flag_ref
  33.3 0.4 shard_map.135
  33.7 6.4 %all-to-all-done.1 = f32[32,1,1664]{2,1,0:T(1,128)S(1)} async-done(((f32[32,1,1664]{2,1,0:T(1,128)}), f32[32,1,1664]{2,1,0:T(1,128)S(1)}, u32[]{:S(2)}, u32[]{:S(2)}) %all-to-all-start.1) | async-done | bytes 213024 | tf_op jit(solution)/shard_map/all_to_all | solution.py:630
  40.1 0.0 copy-done.6
  40.1 1.1 %shard_map.137 = (f32[128,128]{1,0:T(8,128)S(1)}, f32[64,128]{1,0:T(8,128)S(1)}, f32[64,128]{1,0:T(8,128)S(1)}, f32[4,32,128]{2,1,0:T(8,128)S(1)}) custom-call(s32[3,128]{1,0:T(4,128)S(1)} %broadcast_in_dim.2.flag_ref, f32[416,128]{1,0:T(8,128)S(1)} %bitcast.7, s32[1,2048]{1,0:T(1,128)S(1)} %copy-done.6, f32[1,2048]{1,0:T(1,128)S(1)} %copy-done.7, ...), custom_call_target="tpu_custom_call" | custom-call | tf_op jit(solution)/shard_map/pallas_call | solution.py:733
  41.1 1.0 %collective-permute-start.2 = (f32[64,128]{1,0:T(8,128)S(1)}, f32[64,128]{1,0:T(8,128)S(1)}, u32[]{:S(2)}, u32[]{:S(2)}) collective-permute-start(f32[64,128]{1,0:T(8,128)S(1)} %get-tuple-element.82), channel_id=1, source_target_pairs={{0,4},{4,0},{8,12},{12,8},{16,20},{20,16},{24,28},{28,24},{1,5},{5... | collective-permute-start | bytes 98312 | tf_op jit(solution)/shard_map/ppermute | solution.py:642
  42.1 2.2 %collective-permute-start.3 = (f32[64,128]{1,0:T(8,128)S(1)}, f32[64,128]{1,0:T(8,128)S(1)}, u32[]{:S(2)}, u32[]{:S(2)}) collective-permute-start(f32[64,128]{1,0:T(8,128)S(1)} %get-tuple-element.83), channel_id=1, source_target_pairs={{0,28},{4,8},{8,4},{12,16},{16,12},{20,24},{24,20},{28,0},{1,29},{... | collective-permute-start | bytes 98312 | tf_op jit(solution)/shard_map/ppermute | solution.py:642
  44.3 3.6 %shard_map.136.seed_ref = f32[25,128,128]{2,1,0:T(8,128)S(1)} custom-call(f32[416,128]{1,0:T(8,128)S(1)} %bitcast.8, s32[1,2048]{1,0:T(1,128)S(1)} %copy-done.6, f32[1,2048]{1,0:T(1,128)S(1)} %copy-done.7, f32[25,128,128]{2,1,0:T(8,128)S(1)} %copy-done), custom_call_target="tpu_custom_call" | custom-call | tf_op jit(solution)/shard_map/pallas_call | solution.py:746
  47.9 0.0 collective-permute-done.2.lon_first_ref.first_ref
  47.9 0.8 %collective-permute-done.3.lon_second_ref.second_ref = f32[64,128]{1,0:T(8,128)S(1)} collective-permute-done((f32[64,128]{1,0:T(8,128)S(1)}, f32[64,128]{1,0:T(8,128)S(1)}, u32[]{:S(2)}, u32[]{:S(2)}) %collective-permute-start.3) | collective-permute-done | bytes 32800 | tf_op jit(solution)/shard_map/ppermute | solution.py:642
  48.7 0.1 shard_map.138
  48.8 0.8 %collective-permute-start.5 = (f32[88,128]{1,0:T(8,128)S(1)}, f32[88,128]{1,0:T(8,128)S(1)}, u32[]{:S(2)}, u32[]{:S(2)}) collective-permute-start(f32[88,128]{1,0:T(8,128)S(1)} %get-tuple-element.89), channel_id=1, source_target_pairs={{1,2},{2,1},{3,31},{5,6},{6,5},{7,27},{9,10},{10,9},{11,23},{13,14... | collective-permute-start | bytes 135176 | tf_op jit(solution)/shard_map/ppermute | solution.py:657
  49.6 2.4 %collective-permute-start.4 = (f32[88,128]{1,0:T(8,128)S(1)}, f32[88,128]{1,0:T(8,128)S(1)}, u32[]{:S(2)}, u32[]{:S(2)}) collective-permute-start(f32[88,128]{1,0:T(8,128)S(1)} %get-tuple-element.90), channel_id=1, source_target_pairs={{0,1},{1,0},{2,3},{3,2},{4,5},{5,4},{6,7},{7,6},{8,9},{9,8},{10,11... | collective-permute-start | bytes 135176 | tf_op jit(solution)/shard_map/ppermute | solution.py:657
  52.1 1.9 %shard_map.139 = (f32[25,128,128]{2,1,0:T(8,128)S(1)}, f32[25,128,128]{2,1,0:T(8,128)S(1)}, f32[128,128]{1,0:T(8,128)S(1)}) custom-call(s32[3,128]{1,0:T(4,128)S(1)} %broadcast_in_dim.2.flag_ref, f32[25,128,128]{2,1,0:T(8,128)S(1)} %shard_map.136.seed_ref, f32[7,128,128]{2,1,0:T(8,128)S(1)} %get-tuple-element.92.field_ref, ...), custom_call_target="tpu_custom_call" | custom-call | tf_op jit(solution)/shard_map/pallas_call | solution.py:759
  54.0 0.0 collective-permute-done.5.lat_second_ref
  54.0 0.0 collective-permute-done.4.lat_first_ref
  54.0 2.4 %shard_map.140 = f32[25,128,128]{2,1,0:T(8,128)} custom-call(s32[3,128]{1,0:T(4,128)S(1)} %broadcast_in_dim.2.flag_ref, f32[25,128,128]{2,1,0:T(8,128)S(1)} %get-tuple-element.98.half_ref, f32[25,128,128]{2,1,0:T(8,128)S(1)} %get-tuple-element.99.masked_ref, f32[128,128]{1,0:T(8,128)S(1)} %get-tuple-element.100.turn_in_ref, ...), custom_call_target="tpu_custom_call" | custom-call | tf_op jit(solution)/shard_map/pallas_call | solution.py:766
  (2 shorter events, 0.0 us)
Async XLA Ops:
  0.6 15.4 %copy-start.1 = (s32[128,128]{1,0:T(8,128)S(1)}, s32[128,128]{1,0:T(8,128)}, u32[]{:S(2)}) copy-start(s32[128,128]{1,0:T(8,128)} %mask_ref.4) | copy-start | bytes 196612
  0.6 15.4 %copy-start.5 = (f32[128,128]{1,0:T(8,128)S(1)}, f32[128,128]{1,0:T(8,128)}, u32[]{:S(2)}) copy-start(f32[128,128]{1,0:T(8,128)} %vertical_ref.1) | copy-start | bytes 196612
  0.7 15.4 %copy-start.4 = (f32[128,128]{1,0:T(8,128)S(1)}, f32[128,128]{1,0:T(8,128)}, u32[]{:S(2)}) copy-start(f32[128,128]{1,0:T(8,128)} %flow_ref.1) | copy-start | bytes 196612
  0.7 15.4 %copy-start.3 = (f32[128,128]{1,0:T(8,128)S(1)}, f32[128,128]{1,0:T(8,128)}, u32[]{:S(2)}) copy-start(f32[128,128]{1,0:T(8,128)} %north_ref.1) | copy-start | bytes 196612
  0.7 15.4 %copy-start.2 = (f32[128,128]{1,0:T(8,128)S(1)}, f32[128,128]{1,0:T(8,128)}, u32[]{:S(2)}) copy-start(f32[128,128]{1,0:T(8,128)} %east_ref.1) | copy-start | bytes 196612
  0.7 24.7 %copy-start.9 = (f32[25,512]{1,0:T(8,128)S(1)}, f32[25,512]{1,0:T(8,128)}, u32[]{:S(2)}) copy-start(f32[25,512]{1,0:T(8,128)} %invvar_ref.1) | copy-start | bytes 153604
  0.7 24.7 %copy-start.8 = (f32[25,512]{1,0:T(8,128)S(1)}, f32[25,512]{1,0:T(8,128)}, u32[]{:S(2)}) copy-start(f32[25,512]{1,0:T(8,128)} %value_ref.1) | copy-start | bytes 153604
  0.7 24.7 %copy-start.10 = (s32[1,2048]{1,0:T(1,128)S(1)}, s32[1,2048]{1,0:T(1,128)}, u32[]{:S(2)}) copy-start(s32[1,2048]{1,0:T(1,128)} %target_ref.1) | copy-start | bytes 24580
  0.7 30.1 %copy-start = (f32[25,128,128]{2,1,0:T(8,128)S(1)}, f32[25,128,128]{2,1,0:T(8,128)}, u32[]{:S(2)}) copy-start(f32[25,128,128]{2,1,0:T(8,128)} %adjoint_ref.2) | copy-start | bytes 4915204
  8.7 16.7 %all-to-all-start = ((f32[32,1,1664]{2,1,0:T(1,128)}), f32[32,1,1664]{2,1,0:T(1,128)S(1)}, u32[]{:S(2)}, u32[]{:S(2)}) async-start(f32[32,1,1664]{2,1,0:T(1,128)} %bitcast.10), calls=%async_computation | async-start | bytes 425984 | tf_op jit(solution)/shard_map/all_to_all | solution.py:630
  16.1 24.0 %copy-start.6 = (s32[1,2048]{1,0:T(1,128)S(1)}, s32[1,2048]{1,0:T(1,128)}, u32[]{:S(2)}) copy-start(s32[1,2048]{1,0:T(1,128)} %cell_ref.3) | copy-start | bytes 24580
  16.1 24.0 %copy-start.7 = (f32[1,2048]{1,0:T(1,128)S(1)}, f32[1,2048]{1,0:T(1,128)}, u32[]{:S(2)}) copy-start(f32[1,2048]{1,0:T(1,128)} %weight_ref.3) | copy-start | bytes 24580
  16.4 8.9 %collective-permute-start.1 = (f32[16,128]{1,0:T(8,128)S(1)}, f32[16,128]{1,0:T(8,128)S(1)}, u32[]{:S(2)}, u32[]{:S(2)}) collective-permute-start(f32[16,128]{1,0:T(8,128)S(1)} %shard_map.132), channel_id=1, source_target_pairs={{0,28},{4,8},{8,4},{12,16},{16,12},{20,24},{24,20},{28,0},{1,29},{... | collective-permute-start | bytes 24584 | tf_op jit(solution)/shard_map/ppermute | solution.py:642
  21.0 4.3 %collective-permute-start = (f32[16,128]{1,0:T(8,128)S(1)}, f32[16,128]{1,0:T(8,128)S(1)}, u32[]{:S(2)}, u32[]{:S(2)}) collective-permute-start(f32[16,128]{1,0:T(8,128)S(1)} %shard_map.132), channel_id=1, source_target_pairs={{0,4},{4,0},{8,12},{12,8},{16,20},{20,16},{24,28},{28,24},{1,5},{5... | collective-permute-start | bytes 24584 | tf_op jit(solution)/shard_map/ppermute | solution.py:642
  27.5 12.6 %all-to-all-start.1 = ((f32[32,1,1664]{2,1,0:T(1,128)}), f32[32,1,1664]{2,1,0:T(1,128)S(1)}, u32[]{:S(2)}, u32[]{:S(2)}) async-start(f32[32,1,1664]{2,1,0:T(1,128)} %bitcast.5), calls=%async_computation.1 | async-start | bytes 425984 | tf_op jit(solution)/shard_map/all_to_all | solution.py:630
  41.1 6.8 %collective-permute-start.2 = (f32[64,128]{1,0:T(8,128)S(1)}, f32[64,128]{1,0:T(8,128)S(1)}, u32[]{:S(2)}, u32[]{:S(2)}) collective-permute-start(f32[64,128]{1,0:T(8,128)S(1)} %get-tuple-element.82), channel_id=1, source_target_pairs={{0,4},{4,0},{8,12},{12,8},{16,20},{20,16},{24,28},{28,24},{1,5},{5... | collective-permute-start | bytes 98312 | tf_op jit(solution)/shard_map/ppermute | solution.py:642
  42.1 6.6 %collective-permute-start.3 = (f32[64,128]{1,0:T(8,128)S(1)}, f32[64,128]{1,0:T(8,128)S(1)}, u32[]{:S(2)}, u32[]{:S(2)}) collective-permute-start(f32[64,128]{1,0:T(8,128)S(1)} %get-tuple-element.83), channel_id=1, source_target_pairs={{0,28},{4,8},{8,4},{12,16},{16,12},{20,24},{24,20},{28,0},{1,29},{... | collective-permute-start | bytes 98312 | tf_op jit(solution)/shard_map/ppermute | solution.py:642
  48.8 5.2 %collective-permute-start.5 = (f32[88,128]{1,0:T(8,128)S(1)}, f32[88,128]{1,0:T(8,128)S(1)}, u32[]{:S(2)}, u32[]{:S(2)}) collective-permute-start(f32[88,128]{1,0:T(8,128)S(1)} %get-tuple-element.89), channel_id=1, source_target_pairs={{1,2},{2,1},{3,31},{5,6},{6,5},{7,27},{9,10},{10,9},{11,23},{13,14... | collective-permute-start | bytes 135176 | tf_op jit(solution)/shard_map/ppermute | solution.py:657
  49.6 4.3 %collective-permute-start.4 = (f32[88,128]{1,0:T(8,128)S(1)}, f32[88,128]{1,0:T(8,128)S(1)}, u32[]{:S(2)}, u32[]{:S(2)}) collective-permute-start(f32[88,128]{1,0:T(8,128)S(1)} %get-tuple-element.90), channel_id=1, source_target_pairs={{0,1},{1,0},{2,3},{3,2},{4,5},{5,4},{6,7},{7,6},{8,9},{9,8},{10,11... | collective-permute-start | bytes 135176 | tf_op jit(solution)/shard_map/ppermute | solution.py:657

commit v9 on v8

--- a/solution.py
+++ b/solution.py
@@ -119,7 +119,9 @@
         pack(jnp.concatenate(values, axis=0) * weight, out_ref, start // LANES)
 
 
-def observe_kernel(arrived_ref, target_ref, value_ref, invvar_ref, misfit_ref, out_ref, hot_ref):
+def observe_kernel(
+    arrived_ref, target_ref, value_ref, invvar_ref, misfit_out, out_ref, hot_ref, misfit_ref, part_ref, sems
+):
     levels_n, obs_n = value_ref.shape
     half = (levels_n + 1) // 2
     levels = padded_levels(levels_n)
@@ -135,14 +137,24 @@
     interp = sums[:levels] + sums[levels : 2 * levels] + sums[2 * levels :]
     misfit = invvar_ref[...] * (interp[:levels_n] - value_ref[...])
     misfit_ref[...] = misfit
+    copies = [pltpu.make_async_copy(misfit_ref, misfit_out, sems.at[0])]
+    copies[0].start()
     filler = jnp.zeros((levels - levels_n, obs_n), jnp.float32)
     back = jnp.concatenate(pieces(jnp.concatenate([misfit, filler], axis=0)), axis=0)
-    for start in range(0, slots, tile):
+    part = slots // (sems.shape[0] - 1)
+    rows_n = part_ref.shape[0] * part // slots
+    for index in range(slots // part):
+        start = index * part
         found = jnp.dot(
-            back, hot_ref[:, start : start + tile], preferred_element_type=jnp.float32
+            back, hot_ref[:, start : start + part], preferred_element_type=jnp.float32
         )
         values = found[:levels] + found[levels : 2 * levels] + found[2 * levels :]
-        pack(values[: 2 * half], out_ref, start // LANES)
+        pack(values[: 2 * half], part_ref, start // LANES)
+        rows = slice(index * rows_n, (index + 1) * rows_n)
+        copies.append(pltpu.make_async_copy(part_ref.at[rows], out_ref.at[rows], sems.at[index + 1]))
+        copies[-1].start()
+    for copy in copies:
+        copy.wait()
 
 
 def padded_levels(levels_n):
@@ -189,7 +201,7 @@
 
 def strips_kernel(
     levels_n, flag_ref, returned_ref, cell_ref, weight_ref, mask_ref, seed_columns_ref, ocean_ref, seed_edges_ref,
-    columns_ref, second_ref, first_ref, edges_ref,
+    second_ref, first_ref, columns_ref, edges_ref,
 ):
     rows_n, cols_n = mask_ref.shape
     places, levels, _ = edges_ref.shape
@@ -257,7 +269,7 @@
 
 
 def beside_kernel(
-    flag_ref, seed_ref, field_ref, side_ref, columns_ref, first_ref, second_ref,
+    flag_ref, seed_ref, field_ref, side_ref, columns_ref, second_ref, first_ref,
     half_ref, masked_ref, turn_ref,
     from_ref,
 ):
@@ -480,29 +492,30 @@
 
 
 def edge_message_kernel(
-    flag_ref, edges_ref, lon_first_ref, lon_second_ref, row_ref, second_ref, first_ref
+    levels_n, flag_ref, edges_ref, lon_second_ref, lon_first_ref, row_ref, second_ref, first_ref
 ):
     places, levels, cols_n = edges_ref.shape
+    begin = row_ref.shape[0] + 2
     for ref in (first_ref, second_ref):
-        ref[2 * levels : 2 * levels + SUB, :] = jnp.zeros((SUB, cols_n), jnp.float32)
-        ref[2 * levels + SUB :, :] = row_ref[...]
+        ref[: row_ref.shape[0], :] = row_ref[...]
+        ref[begin + 2 * levels_n :, :] = jnp.zeros((ref.shape[0] - begin - 2 * levels_n, cols_n), jnp.float32)
     for place, (north, south) in enumerate(((places - 1, 0), (places - 2, 1))):
-        at = slice(place * levels, (place + 1) * levels)
-        northern, southern = edges_ref[north], edges_ref[south]
+        at = slice(begin + place * levels_n, begin + (place + 1) * levels_n)
+        northern, southern = edges_ref[north][:levels_n], edges_ref[south][:levels_n]
         first_ref[at, :] = by_flag(flag_ref, 1, northern, southern)
         second_ref[at, :] = by_flag(flag_ref, 1, southern, northern)
     east, west = lon_columns(flag_ref, lon_first_ref[...], lon_second_ref[...])
     northern = east[-1:], west[-1:]
     southern = east[:1], west[:1]
     for place in range(2):
-        at = slice(2 * levels + place, 2 * levels + place + 1)
+        at = slice(begin - 2 + place, begin - 1 + place)
         first_ref[at, :] = by_flag(flag_ref, 1, northern[place], southern[place])
         second_ref[at, :] = by_flag(flag_ref, 1, southern[place], northern[place])
 
 
 def steps_kernel(
     flag_ref, half_ref, masked_ref, turn_in_ref, field_ref, side_ref,
-    edges_ref, lon_first_ref, lon_second_ref, lat_first_ref, lat_second_ref,
+    edges_ref, lon_second_ref, lon_first_ref, lat_first_ref, lat_second_ref,
     out_ref,
     done_ref, turn_ref, edge_ref, sems,
 ):
@@ -510,12 +523,12 @@
     levels = edges_ref.shape[1]
     up, down = lat_neighbours(flag_ref, lat_first_ref[...], lat_second_ref[...])
 
-    ends = 2 * levels
+    ends = 2 * SUB
     east_up = by_flag(flag_ref, 2, pltpu.roll(up[ends + 1 : ends + 2], 1, 1), up[ends : ends + 1])
     west_up = by_flag(flag_ref, 2, pltpu.roll(up[ends : ends + 1], cols_n - 1, 1), up[ends + 1 : ends + 2])
     east_down, west_down = down[ends : ends + 1], down[ends + 1 : ends + 2]
 
-    up_rows, down_rows = up[ends + SUB :], down[ends + SUB :]
+    up_rows, down_rows = up[:ends], down[:ends]
     turned = reversed_lanes(up_rows)
     into = field_ref[4, rows_n - 1 : rows_n, :]
     south_row = down_rows[8:9]
@@ -557,7 +570,9 @@
         return jnp.sum(found, axis=1, keepdims=True)
 
     def edge(block, place):
-        return block[place * levels : (place + 1) * levels]
+        begin = ends + 2 + place * levels_n
+        filler = jnp.zeros((levels - levels_n, cols_n), jnp.float32)
+        return jnp.concatenate([block[begin : begin + levels_n], filler], axis=0)
 
     def edge_step(block, outer, inner, eastern, western, base):
         def coefficient(place):
@@ -615,7 +630,8 @@
     if ins is not None:
         memory["in_specs"] = [pl.BlockSpec(memory_space=space) for space in ins]
     if outs is not None:
-        memory["out_specs"] = pl.BlockSpec(memory_space=outs)
+        spec = pl.BlockSpec(memory_space=outs)
+        memory["out_specs"] = (spec,) * len(out_shape) if isinstance(out_shape, tuple) else spec
     return pl.pallas_call(
         body,
         out_shape=out_shape,
@@ -639,7 +655,8 @@
     assert count % 2 == 0
     first = [(i, i ^ 1) for i in range(count)]
     second = [(i, (i + 1 if i % 2 else i - 1) % count) for i in range(count)]
-    return lax.ppermute(first_value, "lon", first), lax.ppermute(second_value, "lon", second)
+    second_found = lax.ppermute(second_value, "lon", second)
+    return lax.ppermute(first_value, "lon", first), second_found
 
 
 def lat_swaps(*values):
@@ -710,7 +727,13 @@
         8 + 4 * tiles,
         observe_kernel,
         (f32(levels_n, obs_n), f32(devices * half, LANES)),
-        [pltpu.VMEM((obs_n, slots), bf16)],
+        [
+            pltpu.VMEM((obs_n, slots), bf16),
+            pltpu.VMEM((levels_n, obs_n), jnp.float32),
+            pltpu.VMEM((devices * half, LANES), jnp.float32),
+            pltpu.SemaphoreType.DMA((5,)),
+        ],
+        [pltpu.VMEM] * 4, pltpu.HBM,
     )(arrived, arrive_obs, obs_value, obs_invvar)
     outgoing, raw, side_coefs, adjoint_early = lax.optimization_barrier(
         (outgoing, raw, side_coefs, adjoint_in)
@@ -730,18 +753,18 @@
     returned, strips, fields, sides, row_coefs = lax.optimization_barrier(
         (returned, strips, fields, sides, row_coefs)
     )
-    own_columns, for_second, for_first, own_edges = kernel_call(
+    for_second, for_first, own_columns, own_edges = kernel_call(
         7 + 3 * tiles,
         functools.partial(strips_kernel, levels_n),
         (
-            f32(rows_n, cols_n),
             f32(rows_n // 2, cols_n),
             f32(rows_n // 2, cols_n),
+            f32(rows_n, cols_n),
             f32(4, levels, cols_n),
         ),
         (),
     )(flags, returned, slot_cell, slot_weight, land_mask, *strips)
-    columns_beside = lon_swaps(for_first, for_second)
+    columns_beside = lon_swaps(for_first, for_second)[::-1]
     whole = (levels_n, rows_n, cols_n)
     seed = kernel_call(
         22 + 3 * tiles,
@@ -750,8 +773,9 @@
         [pltpu.VMEM((2 * levels_n * GROUP, tile), bf16)],
     )(returned, slot_cell, slot_weight, adjoint_in)
     seed, columns_beside = lax.optimization_barrier((seed, columns_beside))
-    message = f32(2 * levels + 3 * SUB, cols_n)
-    messages = kernel_call(2, edge_message_kernel, (message, message), ())(
+    message = f32((2 * levels_n + 2 * SUB + 2 + SUB - 1) // SUB * SUB, cols_n)
+    message_kernel = functools.partial(edge_message_kernel, levels_n)
+    messages = kernel_call(2, message_kernel, (message, message), ())(
         flags, own_edges, *columns_beside, row_coefs
     )
     rows_beside = lat_swaps(messages[1], messages[0])
@@ -771,7 +795,7 @@
             pltpu.VMEM(whole, jnp.float32),
             pltpu.VMEM((rows_n, cols_n), jnp.float32),
             pltpu.VMEM((2 * SUB, cols_n), jnp.float32),
-            pltpu.SemaphoreType.DMA((4,)),
+            pltpu.SemaphoreType.DMA((8,)),
         ],
         [pltpu.VMEM] * 11, pltpu.HBM,
     )(flags, *beside, fields, sides, own_edges, *columns_beside, *rows_beside)

time: 56.8 us -> 55.7 us (0.981)
  the two profiles are of different devices: /device:TPU:0 before, /device:TPU:7 now
where the time goes in v9:
time: 55.7 us; the launch traced here: 54.6 us
  starting transfers between devices  23 us (41%)
  Pallas kernels  22.1 us (40%)
  waiting for transfers between devices  8.26 us (15%)
  between operations  1.05 us (2%)
    all_to_all x2, starting transfers between devices, exchanged(): lax.all_to_all(rows, BOTH, split_axis=0, concat_axis=0, tiled=True)  11.2 us
    pallas_call x1, Pallas kernels, on_device(): kernel_call(60, gather_kernel, f32(devices * half, LANES), [pltpu.VMEM((1...  8.01 us
    all_to_all x2, waiting for transfers between devices, exchanged(): lax.all_to_all(rows, BOTH, split_axis=0, concat_axis=0, tiled=True)  6.4 us
    ppermute x2, starting transfers between devices, lat_swaps(): found.append(lax.ppermute(values[parity], BOTH, pairs))  4.97 us
    ppermute x2, starting transfers between devices, lon_swaps(): return (lax.ppermute(first_value, 'lon', first), second_found)  4.35 us
    pallas_call x1, Pallas kernels, on_device(): kernel_call(22 + 3 * tiles, scatter_kernel, f32(levels_n, rows_n, cols_n)...  3.59 us
    ppermute x2, starting transfers between devices, lon_swaps(): second_found = lax.ppermute(second_value, 'lon', second)  2.49 us
    pallas_call x1, Pallas kernels, on_device(): kernel_call(5, seed_strips_kernel, (f32(rows_n, cols_n), f32(rows_n, cols...  2.46 us
  transfers between devices with their start and end apart: 8, of which 4 were waited for; matrix products, arithmetic and copies ran while one was open for 0% of the time, Pallas kernels for 16%

profile of v9, /device:TPU:7, one launch (start us, length us, event | category | flops | bytes accessed | tf_op | source)
XLA Modules:
  0.0 54.6 jit_solution(8871652264570158403)
XLA Ops:
  0.6 0.0 copy-start.1
  0.6 0.0 copy-start.5
  0.7 0.0 copy-start.4
  0.7 0.0 copy-start.3
  0.7 0.0 copy-start.2
  0.7 0.0 copy-start.9
  0.7 0.0 copy-start.8
  0.7 0.0 copy-start.10
  0.7 0.0 copy-start
  0.7 8.0 %shard_map.131 = f32[416,128]{1,0:T(8,128)} custom-call(s32[1,2048]{1,0:T(1,128)} %cell_ref.3, f32[1,2048]{1,0:T(1,128)} %weight_ref.3, f32[25,128,128]{2,1,0:T(8,128)} %state_in.1), custom_call_target="tpu_custom_call" | custom-call | tf_op jit(solution)/shard_map/pallas_call | solution.py:707
  8.7 6.4 %all-to-all-start = ((f32[32,1,1664]{2,1,0:T(1,128)}), f32[32,1,1664]{2,1,0:T(1,128)S(1)}, u32[]{:S(2)}, u32[]{:S(2)}) async-start(f32[32,1,1664]{2,1,0:T(1,128)} %bitcast.10), calls=%async_computation | async-start | bytes 425984 | tf_op jit(solution)/shard_map/all_to_all | solution.py:646
  15.1 0.0 copy-done.1
  15.1 0.0 copy-done.5
  15.2 0.0 copy-done.4
  15.2 0.0 copy-done.3
  15.2 0.0 copy-done.2
  15.2 0.0 copy-start.6
  15.2 0.0 copy-start.7
  15.2 0.3 shard_map.132
  15.5 1.2 %collective-permute-start.1 = (f32[16,128]{1,0:T(8,128)S(1)}, f32[16,128]{1,0:T(8,128)S(1)}, u32[]{:S(2)}, u32[]{:S(2)}) collective-permute-start(f32[16,128]{1,0:T(8,128)S(1)} %shard_map.132), channel_id=1, source_target_pairs={{0,28},{4,8},{8,4},{12,16},{16,12},{20,24},{24,20},{28,0},{1,29},{... | collective-permute-start | bytes 24584 | tf_op jit(solution)/shard_map/ppermute | solution.py:658
  16.7 3.1 %collective-permute-start = (f32[16,128]{1,0:T(8,128)S(1)}, f32[16,128]{1,0:T(8,128)S(1)}, u32[]{:S(2)}, u32[]{:S(2)}) collective-permute-start(f32[16,128]{1,0:T(8,128)S(1)} %shard_map.132), channel_id=1, source_target_pairs={{0,4},{4,0},{8,12},{12,8},{16,20},{20,16},{24,28},{28,24},{1,5},{5... | collective-permute-start | bytes 24584 | tf_op jit(solution)/shard_map/ppermute | solution.py:659
  19.8 0.0 collective-permute-done.1.lon_second_ref
  19.8 1.3 %collective-permute-done.lon_first_ref = f32[16,128]{1,0:T(8,128)S(1)} collective-permute-done((f32[16,128]{1,0:T(8,128)S(1)}, f32[16,128]{1,0:T(8,128)S(1)}, u32[]{:S(2)}, u32[]{:S(2)}) %collective-permute-start) | collective-permute-done | bytes 8224 | tf_op jit(solution)/shard_map/ppermute | solution.py:659
  21.1 1.8 %all-to-all-done = f32[32,1,1664]{2,1,0:T(1,128)S(1)} async-done(((f32[32,1,1664]{2,1,0:T(1,128)}), f32[32,1,1664]{2,1,0:T(1,128)S(1)}, u32[]{:S(2)}, u32[]{:S(2)}) %all-to-all-start) | async-done | bytes 213024 | tf_op jit(solution)/shard_map/all_to_all | solution.py:646
  22.9 0.0 copy-done.9
  22.9 0.0 copy-done.8
  22.9 0.0 copy-done.10
  22.9 2.0 %shard_map.133 = (f32[25,512]{1,0:T(8,128)}, f32[416,128]{1,0:T(8,128)}) custom-call(f32[416,128]{1,0:T(8,128)S(1)} %bitcast.9, s32[1,2048]{1,0:T(1,128)S(1)} %copy-done.10, f32[25,512]{1,0:T(8,128)S(1)} %copy-done.8, f32[25,512]{1,0:T(8,128)S(1)} %copy-done.9), custom_call_target="tpu_custom_call" | custom-call | tf_op jit(solution)/shard_map/pallas_call | solution.py:726
  24.9 4.8 %all-to-all-start.1 = ((f32[32,1,1664]{2,1,0:T(1,128)}), f32[32,1,1664]{2,1,0:T(1,128)S(1)}, u32[]{:S(2)}, u32[]{:S(2)}) async-start(f32[32,1,1664]{2,1,0:T(1,128)} %bitcast.5), calls=%async_computation.1 | async-start | bytes 425984 | tf_op jit(solution)/shard_map/all_to_all | solution.py:646
  29.8 0.1 pad_add_fusion
  29.9 0.0 copy-done
  29.9 2.5 %shard_map.134 = (f32[128,128]{1,0:T(8,128)S(1)}, f32[128,128]{1,0:T(8,128)S(1)}, f32[4,32,128]{2,1,0:T(8,128)S(1)}) custom-call(f32[25,128,128]{2,1,0:T(8,128)S(1)} %copy-done, s32[128,128]{1,0:T(8,128)S(1)} %copy-done.1), custom_call_target="tpu_custom_call" | custom-call | tf_op jit(solution)/shard_map/pallas_call | solution.py:742
  32.3 0.1 broadcast_in_dim.2.flag_ref
  32.4 0.4 shard_map.135
  32.8 4.6 %all-to-all-done.1 = f32[32,1,1664]{2,1,0:T(1,128)S(1)} async-done(((f32[32,1,1664]{2,1,0:T(1,128)}), f32[32,1,1664]{2,1,0:T(1,128)S(1)}, u32[]{:S(2)}, u32[]{:S(2)}) %all-to-all-start.1) | async-done | bytes 213024 | tf_op jit(solution)/shard_map/all_to_all | solution.py:646
  37.4 1.1 %shard_map.137 = (f32[64,128]{1,0:T(8,128)S(1)}, f32[64,128]{1,0:T(8,128)S(1)}, f32[128,128]{1,0:T(8,128)S(1)}, f32[4,32,128]{2,1,0:T(8,128)S(1)}) custom-call(s32[3,128]{1,0:T(4,128)S(1)} %broadcast_in_dim.2.flag_ref, f32[416,128]{1,0:T(8,128)S(1)} %bitcast.7, s32[1,2048]{1,0:T(1,128)S(1)} %copy-done.6, f32[1,2048]{1,0:T(1,128)S(1)} %copy-done.7, ...), custom_call_target="tpu_custom_call" | custom-call | tf_op jit(solution)/shard_map/pallas_call | solution.py:756
  38.5 1.3 %collective-permute-start.2 = (f32[64,128]{1,0:T(8,128)S(1)}, f32[64,128]{1,0:T(8,128)S(1)}, u32[]{:S(2)}, u32[]{:S(2)}) collective-permute-start(f32[64,128]{1,0:T(8,128)S(1)} %get-tuple-element.82), channel_id=1, source_target_pairs={{0,28},{4,8},{8,4},{12,16},{16,12},{20,24},{24,20},{28,0},{1,29},{... | collective-permute-start | bytes 98312 | tf_op jit(solution)/shard_map/ppermute | solution.py:658
  39.8 1.3 %collective-permute-start.3 = (f32[64,128]{1,0:T(8,128)S(1)}, f32[64,128]{1,0:T(8,128)S(1)}, u32[]{:S(2)}, u32[]{:S(2)}) collective-permute-start(f32[64,128]{1,0:T(8,128)S(1)} %get-tuple-element.83), channel_id=1, source_target_pairs={{0,4},{4,0},{8,12},{12,8},{16,20},{20,16},{24,28},{28,24},{1,5},{5... | collective-permute-start | bytes 98312 | tf_op jit(solution)/shard_map/ppermute | solution.py:659
  41.0 3.6 %shard_map.136.seed_ref = f32[25,128,128]{2,1,0:T(8,128)S(1)} custom-call(f32[416,128]{1,0:T(8,128)S(1)} %bitcast.8, s32[1,2048]{1,0:T(1,128)S(1)} %copy-done.6, f32[1,2048]{1,0:T(1,128)S(1)} %copy-done.7, f32[25,128,128]{2,1,0:T(8,128)S(1)} %copy-done), custom_call_target="tpu_custom_call" | custom-call | tf_op jit(solution)/shard_map/pallas_call | solution.py:769
  44.6 0.0 collective-permute-done.2.lon_second_ref.second_ref
  44.6 0.0 collective-permute-done.3.lon_first_ref.first_ref
  44.7 0.1 shard_map.138
  44.7 4.9 %collective-permute-start.5 = (f32[72,128]{1,0:T(8,128)S(1)}, f32[72,128]{1,0:T(8,128)S(1)}, u32[]{:S(2)}, u32[]{:S(2)}) collective-permute-start(f32[72,128]{1,0:T(8,128)S(1)} %get-tuple-element.89), channel_id=1, source_target_pairs={{1,2},{2,1},{3,31},{5,6},{6,5},{7,27},{9,10},{10,9},{11,23},{13,14... | collective-permute-start | bytes 110600 | tf_op jit(solution)/shard_map/ppermute | solution.py:674
  49.6 0.1 collective-permute-start.4
  49.7 1.9 %shard_map.139 = (f32[25,128,128]{2,1,0:T(8,128)S(1)}, f32[25,128,128]{2,1,0:T(8,128)S(1)}, f32[128,128]{1,0:T(8,128)S(1)}) custom-call(s32[3,128]{1,0:T(4,128)S(1)} %broadcast_in_dim.2.flag_ref, f32[25,128,128]{2,1,0:T(8,128)S(1)} %shard_map.136.seed_ref, f32[7,128,128]{2,1,0:T(8,128)S(1)} %get-tuple-element.92.field_ref, ...), custom_call_target="tpu_custom_call" | custom-call | tf_op jit(solution)/shard_map/pallas_call | solution.py:783
  51.6 0.5 collective-permute-done.5.lat_second_ref
  52.1 0.0 collective-permute-done.4.lat_first_ref
  52.1 2.3 %shard_map.140 = f32[25,128,128]{2,1,0:T(8,128)} custom-call(s32[3,128]{1,0:T(4,128)S(1)} %broadcast_in_dim.2.flag_ref, f32[25,128,128]{2,1,0:T(8,128)S(1)} %get-tuple-element.98.half_ref, f32[25,128,128]{2,1,0:T(8,128)S(1)} %get-tuple-element.99.masked_ref, f32[128,128]{1,0:T(8,128)S(1)} %get-tuple-element.100.turn_in_ref, ...), custom_call_target="tpu_custom_call" | custom-call | tf_op jit(solution)/shard_map/pallas_call | solution.py:790
  (2 shorter events, 0.0 us)
Async XLA Ops:
  0.6 14.5 %copy-start.1 = (s32[128,128]{1,0:T(8,128)S(1)}, s32[128,128]{1,0:T(8,128)}, u32[]{:S(2)}) copy-start(s32[128,128]{1,0:T(8,128)} %mask_ref.4) | copy-start | bytes 196612
  0.6 14.5 %copy-start.5 = (f32[128,128]{1,0:T(8,128)S(1)}, f32[128,128]{1,0:T(8,128)}, u32[]{:S(2)}) copy-start(f32[128,128]{1,0:T(8,128)} %vertical_ref.1) | copy-start | bytes 196612
  0.7 14.5 %copy-start.4 = (f32[128,128]{1,0:T(8,128)S(1)}, f32[128,128]{1,0:T(8,128)}, u32[]{:S(2)}) copy-start(f32[128,128]{1,0:T(8,128)} %flow_ref.1) | copy-start | bytes 196612
  0.7 14.5 %copy-start.3 = (f32[128,128]{1,0:T(8,128)S(1)}, f32[128,128]{1,0:T(8,128)}, u32[]{:S(2)}) copy-start(f32[128,128]{1,0:T(8,128)} %north_ref.1) | copy-start | bytes 196612
  0.7 14.5 %copy-start.2 = (f32[128,128]{1,0:T(8,128)S(1)}, f32[128,128]{1,0:T(8,128)}, u32[]{:S(2)}) copy-start(f32[128,128]{1,0:T(8,128)} %east_ref.1) | copy-start | bytes 196612
  0.7 22.2 %copy-start.9 = (f32[25,512]{1,0:T(8,128)S(1)}, f32[25,512]{1,0:T(8,128)}, u32[]{:S(2)}) copy-start(f32[25,512]{1,0:T(8,128)} %invvar_ref.1) | copy-start | bytes 153604
  0.7 22.2 %copy-start.8 = (f32[25,512]{1,0:T(8,128)S(1)}, f32[25,512]{1,0:T(8,128)}, u32[]{:S(2)}) copy-start(f32[25,512]{1,0:T(8,128)} %value_ref.1) | copy-start | bytes 153604
  0.7 22.2 %copy-start.10 = (s32[1,2048]{1,0:T(1,128)S(1)}, s32[1,2048]{1,0:T(1,128)}, u32[]{:S(2)}) copy-start(s32[1,2048]{1,0:T(1,128)} %target_ref.1) | copy-start | bytes 24580
  0.7 29.2 %copy-start = (f32[25,128,128]{2,1,0:T(8,128)S(1)}, f32[25,128,128]{2,1,0:T(8,128)}, u32[]{:S(2)}) copy-start(f32[25,128,128]{2,1,0:T(8,128)} %adjoint_ref.2) | copy-start | bytes 4915204
  8.7 14.1 %all-to-all-start = ((f32[32,1,1664]{2,1,0:T(1,128)}), f32[32,1,1664]{2,1,0:T(1,128)S(1)}, u32[]{:S(2)}, u32[]{:S(2)}) async-start(f32[32,1,1664]{2,1,0:T(1,128)} %bitcast.10), calls=%async_computation | async-start | bytes 425984 | tf_op jit(solution)/shard_map/all_to_all | solution.py:646
  15.2 22.2 %copy-start.6 = (s32[1,2048]{1,0:T(1,128)S(1)}, s32[1,2048]{1,0:T(1,128)}, u32[]{:S(2)}) copy-start(s32[1,2048]{1,0:T(1,128)} %cell_ref.3) | copy-start | bytes 24580
  15.2 22.2 %copy-start.7 = (f32[1,2048]{1,0:T(1,128)S(1)}, f32[1,2048]{1,0:T(1,128)}, u32[]{:S(2)}) copy-start(f32[1,2048]{1,0:T(1,128)} %weight_ref.3) | copy-start | bytes 24580
  15.5 4.3 %collective-permute-start.1 = (f32[16,128]{1,0:T(8,128)S(1)}, f32[16,128]{1,0:T(8,128)S(1)}, u32[]{:S(2)}, u32[]{:S(2)}) collective-permute-start(f32[16,128]{1,0:T(8,128)S(1)} %shard_map.132), channel_id=1, source_target_pairs={{0,28},{4,8},{8,4},{12,16},{16,12},{20,24},{24,20},{28,0},{1,29},{... | collective-permute-start | bytes 24584 | tf_op jit(solution)/shard_map/ppermute | solution.py:658
  16.7 4.4 %collective-permute-start = (f32[16,128]{1,0:T(8,128)S(1)}, f32[16,128]{1,0:T(8,128)S(1)}, u32[]{:S(2)}, u32[]{:S(2)}) collective-permute-start(f32[16,128]{1,0:T(8,128)S(1)} %shard_map.132), channel_id=1, source_target_pairs={{0,4},{4,0},{8,12},{12,8},{16,20},{20,16},{24,28},{28,24},{1,5},{5... | collective-permute-start | bytes 24584 | tf_op jit(solution)/shard_map/ppermute | solution.py:659
  24.9 12.5 %all-to-all-start.1 = ((f32[32,1,1664]{2,1,0:T(1,128)}), f32[32,1,1664]{2,1,0:T(1,128)S(1)}, u32[]{:S(2)}, u32[]{:S(2)}) async-start(f32[32,1,1664]{2,1,0:T(1,128)} %bitcast.5), calls=%async_computation.1 | async-start | bytes 425984 | tf_op jit(solution)/shard_map/all_to_all | solution.py:646
  38.5 6.1 %collective-permute-start.2 = (f32[64,128]{1,0:T(8,128)S(1)}, f32[64,128]{1,0:T(8,128)S(1)}, u32[]{:S(2)}, u32[]{:S(2)}) collective-permute-start(f32[64,128]{1,0:T(8,128)S(1)} %get-tuple-element.82), channel_id=1, source_target_pairs={{0,28},{4,8},{8,4},{12,16},{16,12},{20,24},{24,20},{28,0},{1,29},{... | collective-permute-start | bytes 98312 | tf_op jit(solution)/shard_map/ppermute | solution.py:658
  39.8 4.9 %collective-permute-start.3 = (f32[64,128]{1,0:T(8,128)S(1)}, f32[64,128]{1,0:T(8,128)S(1)}, u32[]{:S(2)}, u32[]{:S(2)}) collective-permute-start(f32[64,128]{1,0:T(8,128)S(1)} %get-tuple-element.83), channel_id=1, source_target_pairs={{0,4},{4,0},{8,12},{12,8},{16,20},{20,16},{24,28},{28,24},{1,5},{5... | collective-permute-start | bytes 98312 | tf_op jit(solution)/shard_map/ppermute | solution.py:659
  44.7 7.4 %collective-permute-start.5 = (f32[72,128]{1,0:T(8,128)S(1)}, f32[72,128]{1,0:T(8,128)S(1)}, u32[]{:S(2)}, u32[]{:S(2)}) collective-permute-start(f32[72,128]{1,0:T(8,128)S(1)} %get-tuple-element.89), channel_id=1, source_target_pairs={{1,2},{2,1},{3,31},{5,6},{6,5},{7,27},{9,10},{10,9},{11,23},{13,14... | collective-permute-start | bytes 110600 | tf_op jit(solution)/shard_map/ppermute | solution.py:674
  49.6 2.5 %collective-permute-start.4 = (f32[72,128]{1,0:T(8,128)S(1)}, f32[72,128]{1,0:T(8,128)S(1)}, u32[]{:S(2)}, u32[]{:S(2)}) collective-permute-start(f32[72,128]{1,0:T(8,128)S(1)} %get-tuple-element.90), channel_id=1, source_target_pairs={{0,1},{1,0},{2,3},{3,2},{4,5},{5,4},{6,7},{7,6},{8,9},{9,8},{10,11... | collective-permute-start | bytes 110600 | tf_op jit(solution)/shard_map/ppermute | solution.py:674

commit v10 on v9

--- a/solution.py
+++ b/solution.py
@@ -176,7 +176,7 @@
     )
 
 
-def seed_strips_kernel(adjoint_ref, mask_ref, columns_ref, ocean_ref, edges_ref):
+def seed_columns_kernel(adjoint_ref, mask_ref, columns_ref, ocean_ref):
     levels_n, rows_n, cols_n = adjoint_ref.shape
     level_at = jnp.right_shift(lane((SUB, cols_n)), 2)
     for top in range(0, rows_n, SUB):
@@ -192,59 +192,38 @@
             spread = spread + pltpu.roll(spread, shift, 1)
             shift *= 2
         ocean_ref[at, :] = spread
-    places, levels, _ = edges_ref.shape
-    for place, row in enumerate((0, 1, rows_n - 2, rows_n - 1)):
-        for level in range(levels_n):
-            edges_ref[place, level : level + 1, :] = adjoint_ref[level, row : row + 1, :]
-        edges_ref[place, levels_n:, :] = jnp.zeros((levels - levels_n, cols_n), jnp.float32)
-
-
-def strips_kernel(
-    levels_n, flag_ref, returned_ref, cell_ref, weight_ref, mask_ref, seed_columns_ref, ocean_ref, seed_edges_ref,
-    second_ref, first_ref, columns_ref, edges_ref,
+
+
+def columns_kernel(
+    levels_n, flag_ref, returned_ref, cell_ref, weight_ref, seed_ref, ocean_ref,
+    second_ref, first_ref, columns_ref,
 ):
-    rows_n, cols_n = mask_ref.shape
-    places, levels, _ = edges_ref.shape
+    rows_n, cols_n = seed_ref.shape
+    levels = padded_levels(levels_n)
     slots = cell_ref.shape[1]
     tile = min(slots, SLOT_TILE)
-    column_sum = jnp.zeros((rows_n, LANES), jnp.float32)
-    edge_sum = jnp.zeros((places * levels, cols_n), jnp.float32)
+    total = jnp.zeros((rows_n, LANES), jnp.float32)
     for start in range(0, slots, tile):
-        at = slice(start, start + tile)
-        cell = jnp.maximum(cell_ref[:, at], 0)
+        cell = jnp.maximum(cell_ref[:, start : start + tile], 0)
         row, column = jnp.right_shift(cell, log2(cols_n)), jnp.bitwise_and(cell, cols_n - 1)
-        values = returned_values(returned_ref, cell_ref, weight_ref, levels_n, start, tile)
-
-        def chosen(piece, index, wanted):
-            found = [
-                piece * jnp.where(index == number, 1.0, 0.0).astype(jnp.bfloat16)
-                for number in wanted
+        hot = one_hot(row, rows_n)
+        for piece in returned_values(returned_ref, cell_ref, weight_ref, levels_n, start, tile):
+            chosen = [
+                piece * jnp.where(column == wanted, 1.0, 0.0).astype(jnp.bfloat16)
+                for wanted in (cols_n - 2, cols_n - 1, 0, 1)
             ]
-            return jnp.concatenate(found, axis=0)
-
-        row_hot, column_hot = one_hot(row, rows_n), one_hot(column, cols_n)
-        for piece in values:
-            beside = chosen(piece, column, (cols_n - 2, cols_n - 1, 0, 1))
-            column_sum += across(row_hot, beside)
-            beyond = chosen(piece, row, (0, 1, rows_n - 2, rows_n - 1))
-            edge_sum += across(beyond, column_hot)
+            total += across(hot, jnp.concatenate(chosen, axis=0))
     source, target = sublane((LANES, LANES)), lane((LANES, LANES))
     turn = jnp.bitwise_and(target, 3) * levels + jnp.right_shift(target, 2)
     turn = jnp.where(source == turn, 1.0, 0.0).astype(jnp.bfloat16)
-    column_sum = sum(
-        jnp.dot(piece, turn, preferred_element_type=jnp.float32) for piece in pieces(column_sum)
-    )
-    columns = (seed_columns_ref[...] + column_sum) * ocean_ref[...]
+    total = sum(jnp.dot(piece, turn, preferred_element_type=jnp.float32) for piece in pieces(total))
+    columns = (seed_ref[...] + total) * ocean_ref[...]
     columns_ref[...] = columns
     first_ref[...], second_ref[...] = lon_messages(flag_ref, columns)
-    for place, row in enumerate((0, 1, rows_n - 2, rows_n - 1)):
-        ocean = mask_ref[row : row + 1, :].astype(jnp.float32)
-        forcing = edge_sum[place * levels : (place + 1) * levels]
-        edges_ref[place] = (seed_edges_ref[place] + forcing) * ocean
 
 
 def scatter_kernel(
-    returned_ref, cell_ref, weight_ref, adjoint_ref, out_ref, rows_ref
+    returned_ref, cell_ref, weight_ref, adjoint_ref, mask_ref, out_ref, edges_ref, rows_ref
 ):
     levels_n, rows_n, cols_n = out_ref.shape
     groups = rows_n // GROUP
@@ -266,6 +245,12 @@
         at = slice(group * GROUP, (group + 1) * GROUP)
         forcing = total[:, group * cols_n : (group + 1) * cols_n].reshape(levels_n, GROUP, cols_n)
         out_ref[:, at, :] = adjoint_ref[:, at, :] + forcing
+    places, levels, _ = edges_ref.shape
+    for place, row in enumerate((0, 1, rows_n - 2, rows_n - 1)):
+        ocean = mask_ref[row : row + 1, :].astype(jnp.float32)
+        for level in range(levels_n):
+            edges_ref[place, level : level + 1, :] = out_ref[level, row : row + 1, :] * ocean
+        edges_ref[place, levels_n:, :] = jnp.zeros((levels - levels_n, cols_n), jnp.float32)
 
 
 def beside_kernel(
@@ -741,8 +726,8 @@
     returned = exchanged(outgoing, devices)
     strips = kernel_call(
         5,
-        seed_strips_kernel,
-        (f32(rows_n, cols_n), f32(rows_n, cols_n), f32(4, levels, cols_n)),
+        seed_columns_kernel,
+        (f32(rows_n, cols_n), f32(rows_n, cols_n)),
     )(adjoint_early, raw[0])
     fields, sides, row_coefs = kernel_call(
         5,
@@ -753,25 +738,19 @@
     returned, strips, fields, sides, row_coefs = lax.optimization_barrier(
         (returned, strips, fields, sides, row_coefs)
     )
-    for_second, for_first, own_columns, own_edges = kernel_call(
-        7 + 3 * tiles,
-        functools.partial(strips_kernel, levels_n),
-        (
-            f32(rows_n // 2, cols_n),
-            f32(rows_n // 2, cols_n),
-            f32(rows_n, cols_n),
-            f32(4, levels, cols_n),
-        ),
-        (),
-    )(flags, returned, slot_cell, slot_weight, land_mask, *strips)
+    for_second, for_first, own_columns = kernel_call(
+        6 + 3 * tiles,
+        functools.partial(columns_kernel, levels_n),
+        (f32(rows_n // 2, cols_n), f32(rows_n // 2, cols_n), f32(rows_n, cols_n)),
+    )(flags, returned, slot_cell, slot_weight, *strips)
     columns_beside = lon_swaps(for_first, for_second)[::-1]
     whole = (levels_n, rows_n, cols_n)
-    seed = kernel_call(
+    seed, own_edges = kernel_call(
         22 + 3 * tiles,
         scatter_kernel,
-        f32(levels_n, rows_n, cols_n),
+        (f32(*whole), f32(4, levels, cols_n)),
         [pltpu.VMEM((2 * levels_n * GROUP, tile), bf16)],
-    )(returned, slot_cell, slot_weight, adjoint_in)
+    )(returned, slot_cell, slot_weight, adjoint_in, land_mask)
     seed, columns_beside = lax.optimization_barrier((seed, columns_beside))
     message = f32((2 * levels_n + 2 * SUB + 2 + SUB - 1) // SUB * SUB, cols_n)
     message_kernel = functools.partial(edge_message_kernel, levels_n)

time: 55.7 us -> 55.4 us (level)
  no operation moved by 1% of the time
where the time goes in v10:
time: 55.4 us; the launch traced here: 54.4 us
  starting transfers between devices  23 us (42%)
  Pallas kernels  21.9 us (40%)
  waiting for transfers between devices  8.28 us (15%)
  between operations  1.04 us (2%)
    all_to_all x2, starting transfers between devices, exchanged(): lax.all_to_all(rows, BOTH, split_axis=0, concat_axis=0, tiled=True)  11.2 us
    pallas_call x1, Pallas kernels, on_device(): kernel_call(60, gather_kernel, f32(devices * half, LANES), [pltpu.VMEM((1...  8.01 us
    all_to_all x2, waiting for transfers between devices, exchanged(): lax.all_to_all(rows, BOTH, split_axis=0, concat_axis=0, tiled=True)  6.4 us
    ppermute x2, starting transfers between devices, lat_swaps(): found.append(lax.ppermute(values[parity], BOTH, pairs))  4.96 us
    ppermute x2, starting transfers between devices, lon_swaps(): return (lax.ppermute(first_value, 'lon', first), second_found)  4.36 us
    pallas_call x1, Pallas kernels, on_device(): kernel_call(22 + 3 * tiles, scatter_kernel, (f32(*whole), f32(4, levels,...  3.67 us
    ppermute x2, starting transfers between devices, lon_swaps(): second_found = lax.ppermute(second_value, 'lon', second)  2.48 us
    pallas_call x1, Pallas kernels, on_device(): kernel_call(5, seed_columns_kernel, (f32(rows_n, cols_n), f32(rows_n, col...  2.46 us
  transfers between devices with their start and end apart: 8, of which 4 were waited for; matrix products, arithmetic and copies ran while one was open for 0% of the time, Pallas kernels for 16%

profile of v10, /device:TPU:7, one launch (start us, length us, event | category | flops | bytes accessed | tf_op | source)
XLA Modules:
  0.0 54.4 jit_solution(17744346766668979788)
XLA Ops:
  0.6 0.0 copy-start.1
  0.6 0.0 copy-start.5
  0.7 0.0 copy-start.4
  0.7 0.0 copy-start.3
  0.7 0.0 copy-start.2
  0.7 0.0 copy-start.9
  0.7 0.0 copy-start.8
  0.7 0.0 copy-start.10
  0.7 0.0 copy-start
  0.7 8.0 %shard_map.131 = f32[416,128]{1,0:T(8,128)} custom-call(s32[1,2048]{1,0:T(1,128)} %cell_ref.3, f32[1,2048]{1,0:T(1,128)} %weight_ref.3, f32[25,128,128]{2,1,0:T(8,128)} %state_in.1), custom_call_target="tpu_custom_call" | custom-call | tf_op jit(solution)/shard_map/pallas_call | solution.py:692
  8.7 6.4 %all-to-all-start = ((f32[32,1,1664]{2,1,0:T(1,128)}), f32[32,1,1664]{2,1,0:T(1,128)S(1)}, u32[]{:S(2)}, u32[]{:S(2)}) async-start(f32[32,1,1664]{2,1,0:T(1,128)} %bitcast.10), calls=%async_computation | async-start | bytes 425984 | tf_op jit(solution)/shard_map/all_to_all | solution.py:631
  15.1 0.0 copy-done.1
  15.1 0.0 copy-done.5
  15.2 0.0 copy-done.4
  15.2 0.0 copy-done.3
  15.2 0.0 copy-done.2
  15.2 0.0 copy-start.6
  15.2 0.0 copy-start.7
  15.2 0.3 shard_map.132
  15.5 1.2 %collective-permute-start.1 = (f32[16,128]{1,0:T(8,128)S(1)}, f32[16,128]{1,0:T(8,128)S(1)}, u32[]{:S(2)}, u32[]{:S(2)}) collective-permute-start(f32[16,128]{1,0:T(8,128)S(1)} %shard_map.132), channel_id=1, source_target_pairs={{0,28},{4,8},{8,4},{12,16},{16,12},{20,24},{24,20},{28,0},{1,29},{... | collective-permute-start | bytes 24584 | tf_op jit(solution)/shard_map/ppermute | solution.py:643
  16.7 3.1 %collective-permute-start = (f32[16,128]{1,0:T(8,128)S(1)}, f32[16,128]{1,0:T(8,128)S(1)}, u32[]{:S(2)}, u32[]{:S(2)}) collective-permute-start(f32[16,128]{1,0:T(8,128)S(1)} %shard_map.132), channel_id=1, source_target_pairs={{0,4},{4,0},{8,12},{12,8},{16,20},{20,16},{24,28},{28,24},{1,5},{5... | collective-permute-start | bytes 24584 | tf_op jit(solution)/shard_map/ppermute | solution.py:644
  19.8 0.0 collective-permute-done.1.lon_second_ref
  19.8 1.3 %collective-permute-done.lon_first_ref = f32[16,128]{1,0:T(8,128)S(1)} collective-permute-done((f32[16,128]{1,0:T(8,128)S(1)}, f32[16,128]{1,0:T(8,128)S(1)}, u32[]{:S(2)}, u32[]{:S(2)}) %collective-permute-start) | collective-permute-done | bytes 8224 | tf_op jit(solution)/shard_map/ppermute | solution.py:644
  21.1 1.8 %all-to-all-done = f32[32,1,1664]{2,1,0:T(1,128)S(1)} async-done(((f32[32,1,1664]{2,1,0:T(1,128)}), f32[32,1,1664]{2,1,0:T(1,128)S(1)}, u32[]{:S(2)}, u32[]{:S(2)}) %all-to-all-start) | async-done | bytes 213024 | tf_op jit(solution)/shard_map/all_to_all | solution.py:631
  22.9 0.0 copy-done.9
  22.9 0.0 copy-done.8
  22.9 0.0 copy-done.10
  22.9 2.0 %shard_map.133 = (f32[25,512]{1,0:T(8,128)}, f32[416,128]{1,0:T(8,128)}) custom-call(f32[416,128]{1,0:T(8,128)S(1)} %bitcast.9, s32[1,2048]{1,0:T(1,128)S(1)} %copy-done.10, f32[25,512]{1,0:T(8,128)S(1)} %copy-done.8, f32[25,512]{1,0:T(8,128)S(1)} %copy-done.9), custom_call_target="tpu_custom_call" | custom-call | tf_op jit(solution)/shard_map/pallas_call | solution.py:711
  24.9 4.8 %all-to-all-start.1 = ((f32[32,1,1664]{2,1,0:T(1,128)}), f32[32,1,1664]{2,1,0:T(1,128)S(1)}, u32[]{:S(2)}, u32[]{:S(2)}) async-start(f32[32,1,1664]{2,1,0:T(1,128)} %bitcast.5), calls=%async_computation.1 | async-start | bytes 425984 | tf_op jit(solution)/shard_map/all_to_all | solution.py:631
  29.8 0.1 pad_add_fusion
  29.9 0.0 copy-done
  29.9 2.5 %shard_map.134 = (f32[128,128]{1,0:T(8,128)S(1)}, f32[128,128]{1,0:T(8,128)S(1)}) custom-call(f32[25,128,128]{2,1,0:T(8,128)S(1)} %copy-done, s32[128,128]{1,0:T(8,128)S(1)} %copy-done.1), custom_call_target="tpu_custom_call" | custom-call | tf_op jit(solution)/shard_map/pallas_call | solution.py:727
  32.3 0.1 broadcast_in_dim.2.flag_ref
  32.4 0.4 shard_map.135
  32.8 4.6 %all-to-all-done.1 = f32[32,1,1664]{2,1,0:T(1,128)S(1)} async-done(((f32[32,1,1664]{2,1,0:T(1,128)}), f32[32,1,1664]{2,1,0:T(1,128)S(1)}, u32[]{:S(2)}, u32[]{:S(2)}) %all-to-all-start.1) | async-done | bytes 213024 | tf_op jit(solution)/shard_map/all_to_all | solution.py:631
  37.4 0.8 %shard_map.137 = (f32[64,128]{1,0:T(8,128)S(1)}, f32[64,128]{1,0:T(8,128)S(1)}, f32[128,128]{1,0:T(8,128)S(1)}) custom-call(s32[3,128]{1,0:T(4,128)S(1)} %broadcast_in_dim.2.flag_ref, f32[416,128]{1,0:T(8,128)S(1)} %bitcast.7, s32[1,2048]{1,0:T(1,128)S(1)} %copy-done.6, f32[1,2048]{1,0:T(1,128)S(1)} %copy-done.7, f32[128,128]{1,0:T(8,128)S(1)} %get-tuple-element.78.seed_ref, ...), custom_call_target="tpu_custom_call" | custom-call | tf_op jit(solution)/shard_map/pallas_call | solution.py:741
  38.2 1.3 %collective-permute-start.2 = (f32[64,128]{1,0:T(8,128)S(1)}, f32[64,128]{1,0:T(8,128)S(1)}, u32[]{:S(2)}, u32[]{:S(2)}) collective-permute-start(f32[64,128]{1,0:T(8,128)S(1)} %get-tuple-element.80), channel_id=1, source_target_pairs={{0,28},{4,8},{8,4},{12,16},{16,12},{20,24},{24,20},{28,0},{1,29},{... | collective-permute-start | bytes 98312 | tf_op jit(solution)/shard_map/ppermute | solution.py:643
  39.5 1.3 %collective-permute-start.3 = (f32[64,128]{1,0:T(8,128)S(1)}, f32[64,128]{1,0:T(8,128)S(1)}, u32[]{:S(2)}, u32[]{:S(2)}) collective-permute-start(f32[64,128]{1,0:T(8,128)S(1)} %get-tuple-element.81), channel_id=1, source_target_pairs={{0,4},{4,0},{8,12},{12,8},{16,20},{20,16},{24,28},{28,24},{1,5},{5... | collective-permute-start | bytes 98312 | tf_op jit(solution)/shard_map/ppermute | solution.py:644
  40.8 3.7 %shard_map.136 = (f32[25,128,128]{2,1,0:T(8,128)S(1)}, f32[4,32,128]{2,1,0:T(8,128)S(1)}) custom-call(f32[416,128]{1,0:T(8,128)S(1)} %bitcast.8, s32[1,2048]{1,0:T(1,128)S(1)} %copy-done.6, f32[1,2048]{1,0:T(1,128)S(1)} %copy-done.7, f32[25,128,128]{2,1,0:T(8,128)S(1)} %copy-done, s32[128,128]{1,0:T(8,128)S(1)} %copy-done.1), custom_call_target="tpu_custom_call" | custom-call | tf_op jit(solution)/shard_map/pallas_call | solution.py:748
  44.4 0.0 collective-permute-done.2.lon_second_ref.second_ref
  44.4 0.0 collective-permute-done.3.lon_first_ref.first_ref
  44.5 0.1 shard_map.138
  44.5 4.9 %collective-permute-start.5 = (f32[72,128]{1,0:T(8,128)S(1)}, f32[72,128]{1,0:T(8,128)S(1)}, u32[]{:S(2)}, u32[]{:S(2)}) collective-permute-start(f32[72,128]{1,0:T(8,128)S(1)} %get-tuple-element.87), channel_id=1, source_target_pairs={{1,2},{2,1},{3,31},{5,6},{6,5},{7,27},{9,10},{10,9},{11,23},{13,14... | collective-permute-start | bytes 110600 | tf_op jit(solution)/shard_map/ppermute | solution.py:659
  49.4 0.1 collective-permute-start.4
  49.5 1.9 %shard_map.139 = (f32[25,128,128]{2,1,0:T(8,128)S(1)}, f32[25,128,128]{2,1,0:T(8,128)S(1)}, f32[128,128]{1,0:T(8,128)S(1)}) custom-call(s32[3,128]{1,0:T(4,128)S(1)} %broadcast_in_dim.2.flag_ref, f32[25,128,128]{2,1,0:T(8,128)S(1)} %get-tuple-element.89.seed_ref, f32[7,128,128]{2,1,0:T(8,128)S(1)} %get-tuple-element.90.field_ref, ...), custom_call_target="tpu_custom_call" | custom-call | tf_op jit(solution)/shard_map/pallas_call | solution.py:762
  51.4 0.5 collective-permute-done.5.lat_second_ref
  51.9 0.0 collective-permute-done.4.lat_first_ref
  51.9 2.3 %shard_map.140 = f32[25,128,128]{2,1,0:T(8,128)} custom-call(s32[3,128]{1,0:T(4,128)S(1)} %broadcast_in_dim.2.flag_ref, f32[25,128,128]{2,1,0:T(8,128)S(1)} %get-tuple-element.96.half_ref, f32[25,128,128]{2,1,0:T(8,128)S(1)} %get-tuple-element.97.masked_ref, f32[128,128]{1,0:T(8,128)S(1)} %get-tuple-element.98.turn_in_ref, ...), custom_call_target="tpu_custom_call" | custom-call | tf_op jit(solution)/shard_map/pallas_call | solution.py:769
  (2 shorter events, 0.0 us)
Async XLA Ops:
  0.6 14.5 %copy-start.1 = (s32[128,128]{1,0:T(8,128)S(1)}, s32[128,128]{1,0:T(8,128)}, u32[]{:S(2)}) copy-start(s32[128,128]{1,0:T(8,128)} %mask_ref.4) | copy-start | bytes 196612
  0.6 14.5 %copy-start.5 = (f32[128,128]{1,0:T(8,128)S(1)}, f32[128,128]{1,0:T(8,128)}, u32[]{:S(2)}) copy-start(f32[128,128]{1,0:T(8,128)} %vertical_ref.1) | copy-start | bytes 196612
  0.7 14.5 %copy-start.4 = (f32[128,128]{1,0:T(8,128)S(1)}, f32[128,128]{1,0:T(8,128)}, u32[]{:S(2)}) copy-start(f32[128,128]{1,0:T(8,128)} %flow_ref.1) | copy-start | bytes 196612
  0.7 14.5 %copy-start.3 = (f32[128,128]{1,0:T(8,128)S(1)}, f32[128,128]{1,0:T(8,128)}, u32[]{:S(2)}) copy-start(f32[128,128]{1,0:T(8,128)} %north_ref.1) | copy-start | bytes 196612
  0.7 14.5 %copy-start.2 = (f32[128,128]{1,0:T(8,128)S(1)}, f32[128,128]{1,0:T(8,128)}, u32[]{:S(2)}) copy-start(f32[128,128]{1,0:T(8,128)} %east_ref.1) | copy-start | bytes 196612
  0.7 22.2 %copy-start.9 = (f32[25,512]{1,0:T(8,128)S(1)}, f32[25,512]{1,0:T(8,128)}, u32[]{:S(2)}) copy-start(f32[25,512]{1,0:T(8,128)} %invvar_ref.1) | copy-start | bytes 153604
  0.7 22.2 %copy-start.8 = (f32[25,512]{1,0:T(8,128)S(1)}, f32[25,512]{1,0:T(8,128)}, u32[]{:S(2)}) copy-start(f32[25,512]{1,0:T(8,128)} %value_ref.1) | copy-start | bytes 153604
  0.7 22.2 %copy-start.10 = (s32[1,2048]{1,0:T(1,128)S(1)}, s32[1,2048]{1,0:T(1,128)}, u32[]{:S(2)}) copy-start(s32[1,2048]{1,0:T(1,128)} %target_ref.1) | copy-start | bytes 24580
  0.7 29.2 %copy-start = (f32[25,128,128]{2,1,0:T(8,128)S(1)}, f32[25,128,128]{2,1,0:T(8,128)}, u32[]{:S(2)}) copy-start(f32[25,128,128]{2,1,0:T(8,128)} %adjoint_ref.2) | copy-start | bytes 4915204
  8.7 14.1 %all-to-all-start = ((f32[32,1,1664]{2,1,0:T(1,128)}), f32[32,1,1664]{2,1,0:T(1,128)S(1)}, u32[]{:S(2)}, u32[]{:S(2)}) async-start(f32[32,1,1664]{2,1,0:T(1,128)} %bitcast.10), calls=%async_computation | async-start | bytes 425984 | tf_op jit(solution)/shard_map/all_to_all | solution.py:631
  15.2 22.2 %copy-start.6 = (s32[1,2048]{1,0:T(1,128)S(1)}, s32[1,2048]{1,0:T(1,128)}, u32[]{:S(2)}) copy-start(s32[1,2048]{1,0:T(1,128)} %cell_ref.3) | copy-start | bytes 24580
  15.2 22.2 %copy-start.7 = (f32[1,2048]{1,0:T(1,128)S(1)}, f32[1,2048]{1,0:T(1,128)}, u32[]{:S(2)}) copy-start(f32[1,2048]{1,0:T(1,128)} %weight_ref.3) | copy-start | bytes 24580
  15.5 4.3 %collective-permute-start.1 = (f32[16,128]{1,0:T(8,128)S(1)}, f32[16,128]{1,0:T(8,128)S(1)}, u32[]{:S(2)}, u32[]{:S(2)}) collective-permute-start(f32[16,128]{1,0:T(8,128)S(1)} %shard_map.132), channel_id=1, source_target_pairs={{0,28},{4,8},{8,4},{12,16},{16,12},{20,24},{24,20},{28,0},{1,29},{... | collective-permute-start | bytes 24584 | tf_op jit(solution)/shard_map/ppermute | solution.py:643
  16.7 4.4 %collective-permute-start = (f32[16,128]{1,0:T(8,128)S(1)}, f32[16,128]{1,0:T(8,128)S(1)}, u32[]{:S(2)}, u32[]{:S(2)}) collective-permute-start(f32[16,128]{1,0:T(8,128)S(1)} %shard_map.132), channel_id=1, source_target_pairs={{0,4},{4,0},{8,12},{12,8},{16,20},{20,16},{24,28},{28,24},{1,5},{5... | collective-permute-start | bytes 24584 | tf_op jit(solution)/shard_map/ppermute | solution.py:644
  24.9 12.5 %all-to-all-start.1 = ((f32[32,1,1664]{2,1,0:T(1,128)}), f32[32,1,1664]{2,1,0:T(1,128)S(1)}, u32[]{:S(2)}, u32[]{:S(2)}) async-start(f32[32,1,1664]{2,1,0:T(1,128)} %bitcast.5), calls=%async_computation.1 | async-start | bytes 425984 | tf_op jit(solution)/shard_map/all_to_all | solution.py:631
  38.2 6.2 %collective-permute-start.2 = (f32[64,128]{1,0:T(8,128)S(1)}, f32[64,128]{1,0:T(8,128)S(1)}, u32[]{:S(2)}, u32[]{:S(2)}) collective-permute-start(f32[64,128]{1,0:T(8,128)S(1)} %get-tuple-element.80), channel_id=1, source_target_pairs={{0,28},{4,8},{8,4},{12,16},{16,12},{20,24},{24,20},{28,0},{1,29},{... | collective-permute-start | bytes 98312 | tf_op jit(solution)/shard_map/ppermute | solution.py:643
  39.5 5.0 %collective-permute-start.3 = (f32[64,128]{1,0:T(8,128)S(1)}, f32[64,128]{1,0:T(8,128)S(1)}, u32[]{:S(2)}, u32[]{:S(2)}) collective-permute-start(f32[64,128]{1,0:T(8,128)S(1)} %get-tuple-element.81), channel_id=1, source_target_pairs={{0,4},{4,0},{8,12},{12,8},{16,20},{20,16},{24,28},{28,24},{1,5},{5... | collective-permute-start | bytes 98312 | tf_op jit(solution)/shard_map/ppermute | solution.py:644
  44.5 7.4 %collective-permute-start.5 = (f32[72,128]{1,0:T(8,128)S(1)}, f32[72,128]{1,0:T(8,128)S(1)}, u32[]{:S(2)}, u32[]{:S(2)}) collective-permute-start(f32[72,128]{1,0:T(8,128)S(1)} %get-tuple-element.87), channel_id=1, source_target_pairs={{1,2},{2,1},{3,31},{5,6},{6,5},{7,27},{9,10},{10,9},{11,23},{13,14... | collective-permute-start | bytes 110600 | tf_op jit(solution)/shard_map/ppermute | solution.py:659
  49.4 2.5 %collective-permute-start.4 = (f32[72,128]{1,0:T(8,128)S(1)}, f32[72,128]{1,0:T(8,128)S(1)}, u32[]{:S(2)}, u32[]{:S(2)}) collective-permute-start(f32[72,128]{1,0:T(8,128)S(1)} %get-tuple-element.88), channel_id=1, source_target_pairs={{0,1},{1,0},{2,3},{3,2},{4,5},{5,4},{6,7},{7,6},{8,9},{9,8},{10,11... | collective-permute-start | bytes 110600 | tf_op jit(solution)/shard_map/ppermute | solution.py:659

commit v11 on v10

--- a/solution.py
+++ b/solution.py
@@ -263,25 +263,22 @@
     own = columns_ref[...]
     level_at = jnp.right_shift(lane((rows_n, cols_n)), 2)
 
-    def side_step(block, eastern, western, base):
-        def coefficient(place):
-            return side_ref[:, base + place : base + place + 1]
-
-        higher = jnp.where(level_at > 0, pltpu.roll(block, 4, 1) - block, 0.0)
-        lower = jnp.where(level_at < levels_n - 1, pltpu.roll(block, cols_n - 4, 1) - block, 0.0)
-        change = (
-            coefficient(2) * eastern
-            + coefficient(3) * western
-            + coefficient(4) * shifted(block, -1, 0, 0.0)
-            + coefficient(5) * shifted(block, 1, 0, 0.0)
-            - coefficient(1) * block
-            + coefficient(6) * (higher + lower)
-        )
-        return block + coefficient(0) * change
-
-    east_next = side_step(east, pltpu.roll(east, cols_n - 1, 1), pltpu.roll(own, 1, 1), 0)
-    west_next = side_step(west, pltpu.roll(own, cols_n - 1, 1), pltpu.roll(west, 1, 1), 7)
-    turn_ref[...] = turned_columns(east_next, west_next)
+    slot = jnp.bitwise_and(lane((rows_n, cols_n)), 3)
+    block = jnp.where(slot < 2, west, east)
+    eastern = pltpu.roll(jnp.where(slot == 3, east, own), cols_n - 1, 1)
+    western = pltpu.roll(jnp.where(slot == 0, west, own), 1, 1)
+    higher = jnp.where(level_at > 0, pltpu.roll(block, 4, 1) - block, 0.0)
+    lower = jnp.where(level_at < levels_n - 1, pltpu.roll(block, cols_n - 4, 1) - block, 0.0)
+    change = (
+        side_ref[2] * eastern
+        + side_ref[3] * western
+        + side_ref[4] * shifted(block, -1, 0, 0.0)
+        + side_ref[5] * shifted(block, 1, 0, 0.0)
+        - side_ref[1] * block
+        + side_ref[6] * (higher + lower)
+    )
+    changed = block + side_ref[0] * change
+    turn_ref[...] = turned_columns(changed, changed)
     for top in range(0, rows_n, SUB):
         at = slice(top, top + SUB)
         for level in range(levels_n):
@@ -458,10 +455,9 @@
     western = side(
         spread(west, 4), spread(west, 5), spread(west, 7), spread(west, 8), spread(west, 9)
     )
-    found = jnp.zeros((rows_n, cols_n), jnp.float32)
-    for place, part in enumerate(eastern + western):
-        found = jnp.where(lane(found.shape) == place, part, found)
-    side_ref[...] = found
+    slot = jnp.bitwise_and(lane((rows_n, cols_n)), 3)
+    for place in range(len(eastern)):
+        side_ref[place] = jnp.where(slot < 2, western[place], eastern[place])
 
     top, last = slice(0, 1), slice(rows_n - 1, rows_n)
     rows = []
@@ -536,13 +532,13 @@
 
     east, west = lon_columns(flag_ref, lon_first_ref[0:1, :], lon_second_ref[0:1, :])
     east, west = east[:1], west[:1]
-    east_low = side_ref[0:1, 0:1] * down_rows[12:13, 2:3] * (east_down - east)
-    west_low = side_ref[0:1, 7:8] * down_rows[14:15, 8:9] * (west_down - west)
+    east_low = side_ref[0, 0:1, 2:3] * down_rows[12:13, 2:3] * (east_down - east)
+    west_low = side_ref[0, 0:1, 1:2] * down_rows[14:15, 8:9] * (west_down - west)
     at = slice(rows_n - 1, rows_n)
-    east_onto = by_flag(flag_ref, 2, up_rows[14:15, 8:9], side_ref[at, 4:5])
-    west_onto = by_flag(flag_ref, 2, up_rows[12:13, 2:3], side_ref[at, 11:12])
-    east_high = side_ref[at, 0:1] * east_onto * east_up
-    west_high = side_ref[at, 7:8] * west_onto * west_up
+    east_onto = by_flag(flag_ref, 2, up_rows[14:15, 8:9], side_ref[4, at, 2:3])
+    west_onto = by_flag(flag_ref, 2, up_rows[12:13, 2:3], side_ref[4, at, 1:2])
+    east_high = side_ref[0, at, 2:3] * east_onto * east_up
+    west_high = side_ref[0, at, 1:2] * west_onto * west_up
     turn_ref[...] = turn_in_ref[...]
     turn_ref[0:1, :] = turn_in_ref[0:1, :] + turned_columns(east_low, west_low)
     turn_ref[at, :] = turn_in_ref[at, :] + turned_columns(east_high, west_high)
@@ -732,7 +728,7 @@
     fields, sides, row_coefs = kernel_call(
         5,
         coefficients_kernel,
-        (f32(7, rows_n, cols_n), f32(rows_n, cols_n), f32(2 * SUB, cols_n)),
+        (f32(7, rows_n, cols_n), f32(7, rows_n, cols_n), f32(2 * SUB, cols_n)),
         (),
     )(flags, *raw, *side_coefs)
     returned, strips, fields, sides, row_coefs = lax.optimization_barrier(

time: 55.4 us -> 55.1 us (level)
  transfers between devices with their start and end apart: 8 -> 8, of which waited for: 4 -> 4; matrix products, arithmetic and copies ran while one was open for 0% -> 0% of each run, Pallas kernels for 16% -> 15%
where the time goes in v11:
time: 55.1 us; the launch traced here: 54.4 us
  starting transfers between devices  23 us (42%)
  Pallas kernels  21.6 us (39%)
  waiting for transfers between devices  8.56 us (16%)
  between operations  1.04 us (2%)
    all_to_all x2, starting transfers between devices, exchanged(): lax.all_to_all(rows, BOTH, split_axis=0, concat_axis=0, tiled=True)  11.2 us
    pallas_call x1, Pallas kernels, on_device(): kernel_call(60, gather_kernel, f32(devices * half, LANES), [pltpu.VMEM((1...  8.01 us
    all_to_all x2, waiting for transfers between devices, exchanged(): lax.all_to_all(rows, BOTH, split_axis=0, concat_axis=0, tiled=True)  6.4 us
    ppermute x2, starting transfers between devices, lat_swaps(): found.append(lax.ppermute(values[parity], BOTH, pairs))  4.96 us
    ppermute x2, starting transfers between devices, lon_swaps(): return (lax.ppermute(first_value, 'lon', first), second_found)  4.36 us
    pallas_call x1, Pallas kernels, on_device(): kernel_call(22 + 3 * tiles, scatter_kernel, (f32(*whole), f32(4, levels,...  3.67 us
    ppermute x2, starting transfers between devices, lon_swaps(): second_found = lax.ppermute(second_value, 'lon', second)  2.48 us
    pallas_call x1, Pallas kernels, on_device(): kernel_call(5, seed_columns_kernel, (f32(rows_n, cols_n), f32(rows_n, col...  2.46 us
  transfers between devices with their start and end apart: 8, of which 4 were waited for; matrix products, arithmetic and copies ran while one was open for 0% of the time, Pallas kernels for 15%

profile of v11, /device:TPU:7, one launch (start us, length us, event | category | flops | bytes accessed | tf_op | source)
XLA Modules:
  0.0 54.4 jit_solution(10051164475439302745)
XLA Ops:
  0.6 0.0 copy-start.1
  0.6 0.0 copy-start.5
  0.7 0.0 copy-start.4
  0.7 0.0 copy-start.3
  0.7 0.0 copy-start.2
  0.7 0.0 copy-start.9
  0.7 0.0 copy-start.8
  0.7 0.0 copy-start.10
  0.7 0.0 copy-start
  0.7 8.0 %shard_map.131 = f32[416,128]{1,0:T(8,128)} custom-call(s32[1,2048]{1,0:T(1,128)} %cell_ref.3, f32[1,2048]{1,0:T(1,128)} %weight_ref.3, f32[25,128,128]{2,1,0:T(8,128)} %state_in.1), custom_call_target="tpu_custom_call" | custom-call | tf_op jit(solution)/shard_map/pallas_call | solution.py:688
  8.7 6.4 %all-to-all-start = ((f32[32,1,1664]{2,1,0:T(1,128)}), f32[32,1,1664]{2,1,0:T(1,128)S(1)}, u32[]{:S(2)}, u32[]{:S(2)}) async-start(f32[32,1,1664]{2,1,0:T(1,128)} %bitcast.10), calls=%async_computation | async-start | bytes 425984 | tf_op jit(solution)/shard_map/all_to_all | solution.py:627
  15.1 0.0 copy-done.1
  15.1 0.0 copy-done.5
  15.2 0.0 copy-done.4
  15.2 0.0 copy-done.3
  15.2 0.0 copy-done.2
  15.2 0.0 copy-start.6
  15.2 0.0 copy-start.7
  15.2 0.3 shard_map.132
  15.5 1.2 %collective-permute-start.1 = (f32[16,128]{1,0:T(8,128)S(1)}, f32[16,128]{1,0:T(8,128)S(1)}, u32[]{:S(2)}, u32[]{:S(2)}) collective-permute-start(f32[16,128]{1,0:T(8,128)S(1)} %shard_map.132), channel_id=1, source_target_pairs={{0,28},{4,8},{8,4},{12,16},{16,12},{20,24},{24,20},{28,0},{1,29},{... | collective-permute-start | bytes 24584 | tf_op jit(solution)/shard_map/ppermute | solution.py:639
  16.7 3.1 %collective-permute-start = (f32[16,128]{1,0:T(8,128)S(1)}, f32[16,128]{1,0:T(8,128)S(1)}, u32[]{:S(2)}, u32[]{:S(2)}) collective-permute-start(f32[16,128]{1,0:T(8,128)S(1)} %shard_map.132), channel_id=1, source_target_pairs={{0,4},{4,0},{8,12},{12,8},{16,20},{20,16},{24,28},{28,24},{1,5},{5... | collective-permute-start | bytes 24584 | tf_op jit(solution)/shard_map/ppermute | solution.py:640
  19.8 0.0 collective-permute-done.1.lon_second_ref
  19.8 1.3 %collective-permute-done.lon_first_ref = f32[16,128]{1,0:T(8,128)S(1)} collective-permute-done((f32[16,128]{1,0:T(8,128)S(1)}, f32[16,128]{1,0:T(8,128)S(1)}, u32[]{:S(2)}, u32[]{:S(2)}) %collective-permute-start) | collective-permute-done | bytes 8224 | tf_op jit(solution)/shard_map/ppermute | solution.py:640
  21.1 1.8 %all-to-all-done = f32[32,1,1664]{2,1,0:T(1,128)S(1)} async-done(((f32[32,1,1664]{2,1,0:T(1,128)}), f32[32,1,1664]{2,1,0:T(1,128)S(1)}, u32[]{:S(2)}, u32[]{:S(2)}) %all-to-all-start) | async-done | bytes 213024 | tf_op jit(solution)/shard_map/all_to_all | solution.py:627
  22.9 0.0 copy-done.9
  22.9 0.0 copy-done.8
  22.9 0.0 copy-done.10
  22.9 2.0 %shard_map.133 = (f32[25,512]{1,0:T(8,128)}, f32[416,128]{1,0:T(8,128)}) custom-call(f32[416,128]{1,0:T(8,128)S(1)} %bitcast.9, s32[1,2048]{1,0:T(1,128)S(1)} %copy-done.10, f32[25,512]{1,0:T(8,128)S(1)} %copy-done.8, f32[25,512]{1,0:T(8,128)S(1)} %copy-done.9), custom_call_target="tpu_custom_call" | custom-call | tf_op jit(solution)/shard_map/pallas_call | solution.py:707
  24.9 4.8 %all-to-all-start.1 = ((f32[32,1,1664]{2,1,0:T(1,128)}), f32[32,1,1664]{2,1,0:T(1,128)S(1)}, u32[]{:S(2)}, u32[]{:S(2)}) async-start(f32[32,1,1664]{2,1,0:T(1,128)} %bitcast.5), calls=%async_computation.1 | async-start | bytes 425984 | tf_op jit(solution)/shard_map/all_to_all | solution.py:627
  29.8 0.1 pad_add_fusion
  29.9 0.0 copy-done
  29.9 2.5 %shard_map.134 = (f32[128,128]{1,0:T(8,128)S(1)}, f32[128,128]{1,0:T(8,128)S(1)}) custom-call(f32[25,128,128]{2,1,0:T(8,128)S(1)} %copy-done, s32[128,128]{1,0:T(8,128)S(1)} %copy-done.1), custom_call_target="tpu_custom_call" | custom-call | tf_op jit(solution)/shard_map/pallas_call | solution.py:723
  32.3 0.1 broadcast_in_dim.2.flag_ref
  32.4 0.4 shard_map.135
  32.8 4.6 %all-to-all-done.1 = f32[32,1,1664]{2,1,0:T(1,128)S(1)} async-done(((f32[32,1,1664]{2,1,0:T(1,128)}), f32[32,1,1664]{2,1,0:T(1,128)S(1)}, u32[]{:S(2)}, u32[]{:S(2)}) %all-to-all-start.1) | async-done | bytes 213024 | tf_op jit(solution)/shard_map/all_to_all | solution.py:627
  37.4 0.8 %shard_map.137 = (f32[64,128]{1,0:T(8,128)S(1)}, f32[64,128]{1,0:T(8,128)S(1)}, f32[128,128]{1,0:T(8,128)S(1)}) custom-call(s32[3,128]{1,0:T(4,128)S(1)} %broadcast_in_dim.2.flag_ref, f32[416,128]{1,0:T(8,128)S(1)} %bitcast.7, s32[1,2048]{1,0:T(1,128)S(1)} %copy-done.6, f32[1,2048]{1,0:T(1,128)S(1)} %copy-done.7, f32[128,128]{1,0:T(8,128)S(1)} %get-tuple-element.78.seed_ref, ...), custom_call_target="tpu_custom_call" | custom-call | tf_op jit(solution)/shard_map/pallas_call | solution.py:737
  38.2 1.3 %collective-permute-start.2 = (f32[64,128]{1,0:T(8,128)S(1)}, f32[64,128]{1,0:T(8,128)S(1)}, u32[]{:S(2)}, u32[]{:S(2)}) collective-permute-start(f32[64,128]{1,0:T(8,128)S(1)} %get-tuple-element.80), channel_id=1, source_target_pairs={{0,28},{4,8},{8,4},{12,16},{16,12},{20,24},{24,20},{28,0},{1,29},{... | collective-permute-start | bytes 98312 | tf_op jit(solution)/shard_map/ppermute | solution.py:639
  39.5 1.3 %collective-permute-start.3 = (f32[64,128]{1,0:T(8,128)S(1)}, f32[64,128]{1,0:T(8,128)S(1)}, u32[]{:S(2)}, u32[]{:S(2)}) collective-permute-start(f32[64,128]{1,0:T(8,128)S(1)} %get-tuple-element.81), channel_id=1, source_target_pairs={{0,4},{4,0},{8,12},{12,8},{16,20},{20,16},{24,28},{28,24},{1,5},{5... | collective-permute-start | bytes 98312 | tf_op jit(solution)/shard_map/ppermute | solution.py:640
  40.8 3.7 %shard_map.136 = (f32[25,128,128]{2,1,0:T(8,128)S(1)}, f32[4,32,128]{2,1,0:T(8,128)S(1)}) custom-call(f32[416,128]{1,0:T(8,128)S(1)} %bitcast.8, s32[1,2048]{1,0:T(1,128)S(1)} %copy-done.6, f32[1,2048]{1,0:T(1,128)S(1)} %copy-done.7, f32[25,128,128]{2,1,0:T(8,128)S(1)} %copy-done, s32[128,128]{1,0:T(8,128)S(1)} %copy-done.1), custom_call_target="tpu_custom_call" | custom-call | tf_op jit(solution)/shard_map/pallas_call | solution.py:744
  44.4 0.0 collective-permute-done.2.lon_second_ref.second_ref
  44.4 0.0 collective-permute-done.3.lon_first_ref.first_ref
  44.5 0.1 shard_map.138
  44.5 4.9 %collective-permute-start.5 = (f32[72,128]{1,0:T(8,128)S(1)}, f32[72,128]{1,0:T(8,128)S(1)}, u32[]{:S(2)}, u32[]{:S(2)}) collective-permute-start(f32[72,128]{1,0:T(8,128)S(1)} %get-tuple-element.87), channel_id=1, source_target_pairs={{1,2},{2,1},{3,31},{5,6},{6,5},{7,27},{9,10},{10,9},{11,23},{13,14... | collective-permute-start | bytes 110600 | tf_op jit(solution)/shard_map/ppermute | solution.py:655
  49.4 0.1 collective-permute-start.4
  49.5 1.6 %shard_map.139 = (f32[25,128,128]{2,1,0:T(8,128)S(1)}, f32[25,128,128]{2,1,0:T(8,128)S(1)}, f32[128,128]{1,0:T(8,128)S(1)}) custom-call(s32[3,128]{1,0:T(4,128)S(1)} %broadcast_in_dim.2.flag_ref, f32[25,128,128]{2,1,0:T(8,128)S(1)} %get-tuple-element.89.seed_ref, f32[7,128,128]{2,1,0:T(8,128)S(1)} %get-tuple-element.90.field_ref, ...), custom_call_target="tpu_custom_call" | custom-call | tf_op jit(solution)/shard_map/pallas_call | solution.py:758
  51.1 0.8 %collective-permute-done.5.lat_second_ref = f32[72,128]{1,0:T(8,128)S(1)} collective-permute-done((f32[72,128]{1,0:T(8,128)S(1)}, f32[72,128]{1,0:T(8,128)S(1)}, u32[]{:S(2)}, u32[]{:S(2)}) %collective-permute-start.5) | collective-permute-done | bytes 36896 | tf_op jit(solution)/shard_map/ppermute | solution.py:655
  51.9 0.0 collective-permute-done.4.lat_first_ref
  51.9 2.3 %shard_map.140 = f32[25,128,128]{2,1,0:T(8,128)} custom-call(s32[3,128]{1,0:T(4,128)S(1)} %broadcast_in_dim.2.flag_ref, f32[25,128,128]{2,1,0:T(8,128)S(1)} %get-tuple-element.96.half_ref, f32[25,128,128]{2,1,0:T(8,128)S(1)} %get-tuple-element.97.masked_ref, f32[128,128]{1,0:T(8,128)S(1)} %get-tuple-element.98.turn_in_ref, ...), custom_call_target="tpu_custom_call" | custom-call | tf_op jit(solution)/shard_map/pallas_call | solution.py:765
  (2 shorter events, 0.0 us)
Async XLA Ops:
  0.6 14.5 %copy-start.1 = (s32[128,128]{1,0:T(8,128)S(1)}, s32[128,128]{1,0:T(8,128)}, u32[]{:S(2)}) copy-start(s32[128,128]{1,0:T(8,128)} %mask_ref.4) | copy-start | bytes 196612
  0.6 14.5 %copy-start.5 = (f32[128,128]{1,0:T(8,128)S(1)}, f32[128,128]{1,0:T(8,128)}, u32[]{:S(2)}) copy-start(f32[128,128]{1,0:T(8,128)} %vertical_ref.1) | copy-start | bytes 196612
  0.7 14.5 %copy-start.4 = (f32[128,128]{1,0:T(8,128)S(1)}, f32[128,128]{1,0:T(8,128)}, u32[]{:S(2)}) copy-start(f32[128,128]{1,0:T(8,128)} %flow_ref.1) | copy-start | bytes 196612
  0.7 14.5 %copy-start.3 = (f32[128,128]{1,0:T(8,128)S(1)}, f32[128,128]{1,0:T(8,128)}, u32[]{:S(2)}) copy-start(f32[128,128]{1,0:T(8,128)} %north_ref.1) | copy-start | bytes 196612
  0.7 14.5 %copy-start.2 = (f32[128,128]{1,0:T(8,128)S(1)}, f32[128,128]{1,0:T(8,128)}, u32[]{:S(2)}) copy-start(f32[128,128]{1,0:T(8,128)} %east_ref.1) | copy-start | bytes 196612
  0.7 22.2 %copy-start.9 = (f32[25,512]{1,0:T(8,128)S(1)}, f32[25,512]{1,0:T(8,128)}, u32[]{:S(2)}) copy-start(f32[25,512]{1,0:T(8,128)} %invvar_ref.1) | copy-start | bytes 153604
  0.7 22.2 %copy-start.8 = (f32[25,512]{1,0:T(8,128)S(1)}, f32[25,512]{1,0:T(8,128)}, u32[]{:S(2)}) copy-start(f32[25,512]{1,0:T(8,128)} %value_ref.1) | copy-start | bytes 153604
  0.7 22.2 %copy-start.10 = (s32[1,2048]{1,0:T(1,128)S(1)}, s32[1,2048]{1,0:T(1,128)}, u32[]{:S(2)}) copy-start(s32[1,2048]{1,0:T(1,128)} %target_ref.1) | copy-start | bytes 24580
  0.7 29.2 %copy-start = (f32[25,128,128]{2,1,0:T(8,128)S(1)}, f32[25,128,128]{2,1,0:T(8,128)}, u32[]{:S(2)}) copy-start(f32[25,128,128]{2,1,0:T(8,128)} %adjoint_ref.2) | copy-start | bytes 4915204
  8.7 14.1 %all-to-all-start = ((f32[32,1,1664]{2,1,0:T(1,128)}), f32[32,1,1664]{2,1,0:T(1,128)S(1)}, u32[]{:S(2)}, u32[]{:S(2)}) async-start(f32[32,1,1664]{2,1,0:T(1,128)} %bitcast.10), calls=%async_computation | async-start | bytes 425984 | tf_op jit(solution)/shard_map/all_to_all | solution.py:627
  15.2 22.2 %copy-start.6 = (s32[1,2048]{1,0:T(1,128)S(1)}, s32[1,2048]{1,0:T(1,128)}, u32[]{:S(2)}) copy-start(s32[1,2048]{1,0:T(1,128)} %cell_ref.3) | copy-start | bytes 24580
  15.2 22.2 %copy-start.7 = (f32[1,2048]{1,0:T(1,128)S(1)}, f32[1,2048]{1,0:T(1,128)}, u32[]{:S(2)}) copy-start(f32[1,2048]{1,0:T(1,128)} %weight_ref.3) | copy-start | bytes 24580
  15.5 4.3 %collective-permute-start.1 = (f32[16,128]{1,0:T(8,128)S(1)}, f32[16,128]{1,0:T(8,128)S(1)}, u32[]{:S(2)}, u32[]{:S(2)}) collective-permute-start(f32[16,128]{1,0:T(8,128)S(1)} %shard_map.132), channel_id=1, source_target_pairs={{0,28},{4,8},{8,4},{12,16},{16,12},{20,24},{24,20},{28,0},{1,29},{... | collective-permute-start | bytes 24584 | tf_op jit(solution)/shard_map/ppermute | solution.py:639
  16.7 4.4 %collective-permute-start = (f32[16,128]{1,0:T(8,128)S(1)}, f32[16,128]{1,0:T(8,128)S(1)}, u32[]{:S(2)}, u32[]{:S(2)}) collective-permute-start(f32[16,128]{1,0:T(8,128)S(1)} %shard_map.132), channel_id=1, source_target_pairs={{0,4},{4,0},{8,12},{12,8},{16,20},{20,16},{24,28},{28,24},{1,5},{5... | collective-permute-start | bytes 24584 | tf_op jit(solution)/shard_map/ppermute | solution.py:640
  24.9 12.5 %all-to-all-start.1 = ((f32[32,1,1664]{2,1,0:T(1,128)}), f32[32,1,1664]{2,1,0:T(1,128)S(1)}, u32[]{:S(2)}, u32[]{:S(2)}) async-start(f32[32,1,1664]{2,1,0:T(1,128)} %bitcast.5), calls=%async_computation.1 | async-start | bytes 425984 | tf_op jit(solution)/shard_map/all_to_all | solution.py:627
  38.2 6.2 %collective-permute-start.2 = (f32[64,128]{1,0:T(8,128)S(1)}, f32[64,128]{1,0:T(8,128)S(1)}, u32[]{:S(2)}, u32[]{:S(2)}) collective-permute-start(f32[64,128]{1,0:T(8,128)S(1)} %get-tuple-element.80), channel_id=1, source_target_pairs={{0,28},{4,8},{8,4},{12,16},{16,12},{20,24},{24,20},{28,0},{1,29},{... | collective-permute-start | bytes 98312 | tf_op jit(solution)/shard_map/ppermute | solution.py:639
  39.5 5.0 %collective-permute-start.3 = (f32[64,128]{1,0:T(8,128)S(1)}, f32[64,128]{1,0:T(8,128)S(1)}, u32[]{:S(2)}, u32[]{:S(2)}) collective-permute-start(f32[64,128]{1,0:T(8,128)S(1)} %get-tuple-element.81), channel_id=1, source_target_pairs={{0,4},{4,0},{8,12},{12,8},{16,20},{20,16},{24,28},{28,24},{1,5},{5... | collective-permute-start | bytes 98312 | tf_op jit(solution)/shard_map/ppermute | solution.py:640
  44.5 7.4 %collective-permute-start.5 = (f32[72,128]{1,0:T(8,128)S(1)}, f32[72,128]{1,0:T(8,128)S(1)}, u32[]{:S(2)}, u32[]{:S(2)}) collective-permute-start(f32[72,128]{1,0:T(8,128)S(1)} %get-tuple-element.87), channel_id=1, source_target_pairs={{1,2},{2,1},{3,31},{5,6},{6,5},{7,27},{9,10},{10,9},{11,23},{13,14... | collective-permute-start | bytes 110600 | tf_op jit(solution)/shard_map/ppermute | solution.py:655
  49.4 2.5 %collective-permute-start.4 = (f32[72,128]{1,0:T(8,128)S(1)}, f32[72,128]{1,0:T(8,128)S(1)}, u32[]{:S(2)}, u32[]{:S(2)}) collective-permute-start(f32[72,128]{1,0:T(8,128)S(1)} %get-tuple-element.88), channel_id=1, source_target_pairs={{0,1},{1,0},{2,3},{3,2},{4,5},{5,4},{6,7},{7,6},{8,9},{9,8},{10,11... | collective-permute-start | bytes 110600 | tf_op jit(solution)/shard_map/ppermute | solution.py:655

commit v12 on v11

--- a/solution.py
+++ b/solution.py
@@ -207,16 +207,23 @@
         cell = jnp.maximum(cell_ref[:, start : start + tile], 0)
         row, column = jnp.right_shift(cell, log2(cols_n)), jnp.bitwise_and(cell, cols_n - 1)
         hot = one_hot(row, rows_n)
-        for piece in returned_values(returned_ref, cell_ref, weight_ref, levels_n, start, tile):
-            chosen = [
-                piece * jnp.where(column == wanted, 1.0, 0.0).astype(jnp.bfloat16)
-                for wanted in (cols_n - 2, cols_n - 1, 0, 1)
-            ]
-            total += across(hot, jnp.concatenate(chosen, axis=0))
+        values = returned_values(returned_ref, cell_ref, weight_ref, levels_n, start, tile)
+        values = jnp.concatenate(values, axis=1)
+        column = jnp.concatenate([column, column], axis=1)
+        chosen = [
+            values * jnp.where(column == wanted, 1.0, 0.0).astype(jnp.bfloat16)
+            for wanted in (cols_n - 2, cols_n - 1, 0, 1)
+        ]
+        hot = jnp.concatenate([hot, hot], axis=1)
+        total += across(hot, jnp.concatenate(chosen, axis=0))
     source, target = sublane((LANES, LANES)), lane((LANES, LANES))
     turn = jnp.bitwise_and(target, 3) * levels + jnp.right_shift(target, 2)
     turn = jnp.where(source == turn, 1.0, 0.0).astype(jnp.bfloat16)
-    total = sum(jnp.dot(piece, turn, preferred_element_type=jnp.float32) for piece in pieces(total))
+    total = jnp.dot(
+        jnp.concatenate(pieces(total), axis=1),
+        jnp.concatenate([turn, turn, turn], axis=0),
+        preferred_element_type=jnp.float32,
+    )
     columns = (seed_ref[...] + total) * ocean_ref[...]
     columns_ref[...] = columns
     first_ref[...], second_ref[...] = lon_messages(flag_ref, columns)

time: 55.1 us -> 55 us (level)
  no operation moved by 1% of the time
where the time goes in v12:
time: 55 us; the launch traced here: 54.4 us
  starting transfers between devices  23 us (42%)
  Pallas kernels  21.5 us (39%)
  waiting for transfers between devices  8.55 us (16%)
  between operations  1.04 us (2%)
    all_to_all x2, starting transfers between devices, exchanged(): lax.all_to_all(rows, BOTH, split_axis=0, concat_axis=0, tiled=True)  11.2 us
    pallas_call x1, Pallas kernels, on_device(): kernel_call(60, gather_kernel, f32(devices * half, LANES), [pltpu.VMEM((1...  8.01 us
    all_to_all x2, waiting for transfers between devices, exchanged(): lax.all_to_all(rows, BOTH, split_axis=0, concat_axis=0, tiled=True)  6.4 us
    ppermute x2, starting transfers between devices, lat_swaps(): found.append(lax.ppermute(values[parity], BOTH, pairs))  4.97 us
    ppermute x2, starting transfers between devices, lon_swaps(): return (lax.ppermute(first_value, 'lon', first), second_found)  4.35 us
    pallas_call x1, Pallas kernels, on_device(): kernel_call(22 + 3 * tiles, scatter_kernel, (f32(*whole), f32(4, levels,...  3.66 us
    ppermute x2, starting transfers between devices, lon_swaps(): second_found = lax.ppermute(second_value, 'lon', second)  2.48 us
    pallas_call x1, Pallas kernels, on_device(): kernel_call(5, seed_columns_kernel, (f32(rows_n, cols_n), f32(rows_n, col...  2.46 us
  transfers between devices with their start and end apart: 8, of which 4 were waited for; matrix products, arithmetic and copies ran while one was open for 0% of the time, Pallas kernels for 15%

profile of v12, /device:TPU:7, one launch (start us, length us, event | category | flops | bytes accessed | tf_op | source)
XLA Modules:
  0.0 54.4 jit_solution(11836944959739422247)
XLA Ops:
  0.6 0.0 copy-start.1
  0.6 0.0 copy-start.5
  0.7 0.0 copy-start.4
  0.7 0.0 copy-start.3
  0.7 0.0 copy-start.2
  0.7 0.0 copy-start.9
  0.7 0.0 copy-start.8
  0.7 0.0 copy-start.10
  0.7 0.0 copy-start
  0.7 8.0 %shard_map.131 = f32[416,128]{1,0:T(8,128)} custom-call(s32[1,2048]{1,0:T(1,128)} %cell_ref.3, f32[1,2048]{1,0:T(1,128)} %weight_ref.3, f32[25,128,128]{2,1,0:T(8,128)} %state_in.1), custom_call_target="tpu_custom_call" | custom-call | tf_op jit(solution)/shard_map/pallas_call | solution.py:695
  8.7 6.4 %all-to-all-start = ((f32[32,1,1664]{2,1,0:T(1,128)}), f32[32,1,1664]{2,1,0:T(1,128)S(1)}, u32[]{:S(2)}, u32[]{:S(2)}) async-start(f32[32,1,1664]{2,1,0:T(1,128)} %bitcast.10), calls=%async_computation | async-start | bytes 425984 | tf_op jit(solution)/shard_map/all_to_all | solution.py:634
  15.1 0.0 copy-done.1
  15.1 0.0 copy-done.5
  15.2 0.0 copy-done.4
  15.2 0.0 copy-done.3
  15.2 0.0 copy-done.2
  15.2 0.0 copy-start.6
  15.2 0.0 copy-start.7
  15.2 0.3 shard_map.132
  15.5 1.2 %collective-permute-start.1 = (f32[16,128]{1,0:T(8,128)S(1)}, f32[16,128]{1,0:T(8,128)S(1)}, u32[]{:S(2)}, u32[]{:S(2)}) collective-permute-start(f32[16,128]{1,0:T(8,128)S(1)} %shard_map.132), channel_id=1, source_target_pairs={{0,28},{4,8},{8,4},{12,16},{16,12},{20,24},{24,20},{28,0},{1,29},{... | collective-permute-start | bytes 24584 | tf_op jit(solution)/shard_map/ppermute | solution.py:646
  16.7 3.1 %collective-permute-start = (f32[16,128]{1,0:T(8,128)S(1)}, f32[16,128]{1,0:T(8,128)S(1)}, u32[]{:S(2)}, u32[]{:S(2)}) collective-permute-start(f32[16,128]{1,0:T(8,128)S(1)} %shard_map.132), channel_id=1, source_target_pairs={{0,4},{4,0},{8,12},{12,8},{16,20},{20,16},{24,28},{28,24},{1,5},{5... | collective-permute-start | bytes 24584 | tf_op jit(solution)/shard_map/ppermute | solution.py:647
  19.8 0.0 collective-permute-done.1.lon_second_ref
  19.8 1.3 %collective-permute-done.lon_first_ref = f32[16,128]{1,0:T(8,128)S(1)} collective-permute-done((f32[16,128]{1,0:T(8,128)S(1)}, f32[16,128]{1,0:T(8,128)S(1)}, u32[]{:S(2)}, u32[]{:S(2)}) %collective-permute-start) | collective-permute-done | bytes 8224 | tf_op jit(solution)/shard_map/ppermute | solution.py:647
  21.1 1.8 %all-to-all-done = f32[32,1,1664]{2,1,0:T(1,128)S(1)} async-done(((f32[32,1,1664]{2,1,0:T(1,128)}), f32[32,1,1664]{2,1,0:T(1,128)S(1)}, u32[]{:S(2)}, u32[]{:S(2)}) %all-to-all-start) | async-done | bytes 213024 | tf_op jit(solution)/shard_map/all_to_all | solution.py:634
  22.9 0.0 copy-done.9
  22.9 0.0 copy-done.8
  22.9 0.0 copy-done.10
  22.9 2.0 %shard_map.133 = (f32[25,512]{1,0:T(8,128)}, f32[416,128]{1,0:T(8,128)}) custom-call(f32[416,128]{1,0:T(8,128)S(1)} %bitcast.9, s32[1,2048]{1,0:T(1,128)S(1)} %copy-done.10, f32[25,512]{1,0:T(8,128)S(1)} %copy-done.8, f32[25,512]{1,0:T(8,128)S(1)} %copy-done.9), custom_call_target="tpu_custom_call" | custom-call | tf_op jit(solution)/shard_map/pallas_call | solution.py:714
  24.9 4.8 %all-to-all-start.1 = ((f32[32,1,1664]{2,1,0:T(1,128)}), f32[32,1,1664]{2,1,0:T(1,128)S(1)}, u32[]{:S(2)}, u32[]{:S(2)}) async-start(f32[32,1,1664]{2,1,0:T(1,128)} %bitcast.5), calls=%async_computation.1 | async-start | bytes 425984 | tf_op jit(solution)/shard_map/all_to_all | solution.py:634
  29.8 0.1 pad_add_fusion
  29.9 0.0 copy-done
  29.9 2.5 %shard_map.134 = (f32[128,128]{1,0:T(8,128)S(1)}, f32[128,128]{1,0:T(8,128)S(1)}) custom-call(f32[25,128,128]{2,1,0:T(8,128)S(1)} %copy-done, s32[128,128]{1,0:T(8,128)S(1)} %copy-done.1), custom_call_target="tpu_custom_call" | custom-call | tf_op jit(solution)/shard_map/pallas_call | solution.py:730
  32.3 0.1 broadcast_in_dim.2.flag_ref
  32.4 0.4 shard_map.135
  32.8 4.6 %all-to-all-done.1 = f32[32,1,1664]{2,1,0:T(1,128)S(1)} async-done(((f32[32,1,1664]{2,1,0:T(1,128)}), f32[32,1,1664]{2,1,0:T(1,128)S(1)}, u32[]{:S(2)}, u32[]{:S(2)}) %all-to-all-start.1) | async-done | bytes 213024 | tf_op jit(solution)/shard_map/all_to_all | solution.py:634
  37.4 0.8 %shard_map.137 = (f32[64,128]{1,0:T(8,128)S(1)}, f32[64,128]{1,0:T(8,128)S(1)}, f32[128,128]{1,0:T(8,128)S(1)}) custom-call(s32[3,128]{1,0:T(4,128)S(1)} %broadcast_in_dim.2.flag_ref, f32[416,128]{1,0:T(8,128)S(1)} %bitcast.7, s32[1,2048]{1,0:T(1,128)S(1)} %copy-done.6, f32[1,2048]{1,0:T(1,128)S(1)} %copy-done.7, f32[128,128]{1,0:T(8,128)S(1)} %get-tuple-element.78.seed_ref, ...), custom_call_target="tpu_custom_call" | custom-call | tf_op jit(solution)/shard_map/pallas_call | solution.py:744
  38.2 1.3 %collective-permute-start.2 = (f32[64,128]{1,0:T(8,128)S(1)}, f32[64,128]{1,0:T(8,128)S(1)}, u32[]{:S(2)}, u32[]{:S(2)}) collective-permute-start(f32[64,128]{1,0:T(8,128)S(1)} %get-tuple-element.80), channel_id=1, source_target_pairs={{0,28},{4,8},{8,4},{12,16},{16,12},{20,24},{24,20},{28,0},{1,29},{... | collective-permute-start | bytes 98312 | tf_op jit(solution)/shard_map/ppermute | solution.py:646
  39.5 1.3 %collective-permute-start.3 = (f32[64,128]{1,0:T(8,128)S(1)}, f32[64,128]{1,0:T(8,128)S(1)}, u32[]{:S(2)}, u32[]{:S(2)}) collective-permute-start(f32[64,128]{1,0:T(8,128)S(1)} %get-tuple-element.81), channel_id=1, source_target_pairs={{0,4},{4,0},{8,12},{12,8},{16,20},{20,16},{24,28},{28,24},{1,5},{5... | collective-permute-start | bytes 98312 | tf_op jit(solution)/shard_map/ppermute | solution.py:647
  40.7 3.7 %shard_map.136 = (f32[25,128,128]{2,1,0:T(8,128)S(1)}, f32[4,32,128]{2,1,0:T(8,128)S(1)}) custom-call(f32[416,128]{1,0:T(8,128)S(1)} %bitcast.8, s32[1,2048]{1,0:T(1,128)S(1)} %copy-done.6, f32[1,2048]{1,0:T(1,128)S(1)} %copy-done.7, f32[25,128,128]{2,1,0:T(8,128)S(1)} %copy-done, s32[128,128]{1,0:T(8,128)S(1)} %copy-done.1), custom_call_target="tpu_custom_call" | custom-call | tf_op jit(solution)/shard_map/pallas_call | solution.py:751
  44.4 0.0 collective-permute-done.2.lon_second_ref.second_ref
  44.4 0.0 collective-permute-done.3.lon_first_ref.first_ref
  44.4 0.1 shard_map.138
  44.5 4.9 %collective-permute-start.5 = (f32[72,128]{1,0:T(8,128)S(1)}, f32[72,128]{1,0:T(8,128)S(1)}, u32[]{:S(2)}, u32[]{:S(2)}) collective-permute-start(f32[72,128]{1,0:T(8,128)S(1)} %get-tuple-element.87), channel_id=1, source_target_pairs={{1,2},{2,1},{3,31},{5,6},{6,5},{7,27},{9,10},{10,9},{11,23},{13,14... | collective-permute-start | bytes 110600 | tf_op jit(solution)/shard_map/ppermute | solution.py:662
  49.4 0.1 collective-permute-start.4
  49.5 1.6 %shard_map.139 = (f32[25,128,128]{2,1,0:T(8,128)S(1)}, f32[25,128,128]{2,1,0:T(8,128)S(1)}, f32[128,128]{1,0:T(8,128)S(1)}) custom-call(s32[3,128]{1,0:T(4,128)S(1)} %broadcast_in_dim.2.flag_ref, f32[25,128,128]{2,1,0:T(8,128)S(1)} %get-tuple-element.89.seed_ref, f32[7,128,128]{2,1,0:T(8,128)S(1)} %get-tuple-element.90.field_ref, ...), custom_call_target="tpu_custom_call" | custom-call | tf_op jit(solution)/shard_map/pallas_call | solution.py:765
  51.1 0.8 %collective-permute-done.5.lat_second_ref = f32[72,128]{1,0:T(8,128)S(1)} collective-permute-done((f32[72,128]{1,0:T(8,128)S(1)}, f32[72,128]{1,0:T(8,128)S(1)}, u32[]{:S(2)}, u32[]{:S(2)}) %collective-permute-start.5) | collective-permute-done | bytes 36896 | tf_op jit(solution)/shard_map/ppermute | solution.py:662
  51.9 0.0 collective-permute-done.4.lat_first_ref
  51.9 2.3 %shard_map.140 = f32[25,128,128]{2,1,0:T(8,128)} custom-call(s32[3,128]{1,0:T(4,128)S(1)} %broadcast_in_dim.2.flag_ref, f32[25,128,128]{2,1,0:T(8,128)S(1)} %get-tuple-element.96.half_ref, f32[25,128,128]{2,1,0:T(8,128)S(1)} %get-tuple-element.97.masked_ref, f32[128,128]{1,0:T(8,128)S(1)} %get-tuple-element.98.turn_in_ref, ...), custom_call_target="tpu_custom_call" | custom-call | tf_op jit(solution)/shard_map/pallas_call | solution.py:772
  (2 shorter events, 0.0 us)
Async XLA Ops:
  0.6 14.5 %copy-start.1 = (s32[128,128]{1,0:T(8,128)S(1)}, s32[128,128]{1,0:T(8,128)}, u32[]{:S(2)}) copy-start(s32[128,128]{1,0:T(8,128)} %mask_ref.4) | copy-start | bytes 196612
  0.6 14.5 %copy-start.5 = (f32[128,128]{1,0:T(8,128)S(1)}, f32[128,128]{1,0:T(8,128)}, u32[]{:S(2)}) copy-start(f32[128,128]{1,0:T(8,128)} %vertical_ref.1) | copy-start | bytes 196612
  0.7 14.5 %copy-start.4 = (f32[128,128]{1,0:T(8,128)S(1)}, f32[128,128]{1,0:T(8,128)}, u32[]{:S(2)}) copy-start(f32[128,128]{1,0:T(8,128)} %flow_ref.1) | copy-start | bytes 196612
  0.7 14.5 %copy-start.3 = (f32[128,128]{1,0:T(8,128)S(1)}, f32[128,128]{1,0:T(8,128)}, u32[]{:S(2)}) copy-start(f32[128,128]{1,0:T(8,128)} %north_ref.1) | copy-start | bytes 196612
  0.7 14.5 %copy-start.2 = (f32[128,128]{1,0:T(8,128)S(1)}, f32[128,128]{1,0:T(8,128)}, u32[]{:S(2)}) copy-start(f32[128,128]{1,0:T(8,128)} %east_ref.1) | copy-start | bytes 196612
  0.7 22.2 %copy-start.9 = (f32[25,512]{1,0:T(8,128)S(1)}, f32[25,512]{1,0:T(8,128)}, u32[]{:S(2)}) copy-start(f32[25,512]{1,0:T(8,128)} %invvar_ref.1) | copy-start | bytes 153604
  0.7 22.2 %copy-start.8 = (f32[25,512]{1,0:T(8,128)S(1)}, f32[25,512]{1,0:T(8,128)}, u32[]{:S(2)}) copy-start(f32[25,512]{1,0:T(8,128)} %value_ref.1) | copy-start | bytes 153604
  0.7 22.2 %copy-start.10 = (s32[1,2048]{1,0:T(1,128)S(1)}, s32[1,2048]{1,0:T(1,128)}, u32[]{:S(2)}) copy-start(s32[1,2048]{1,0:T(1,128)} %target_ref.1) | copy-start | bytes 24580
  0.7 29.2 %copy-start = (f32[25,128,128]{2,1,0:T(8,128)S(1)}, f32[25,128,128]{2,1,0:T(8,128)}, u32[]{:S(2)}) copy-start(f32[25,128,128]{2,1,0:T(8,128)} %adjoint_ref.2) | copy-start | bytes 4915204
  8.7 14.1 %all-to-all-start = ((f32[32,1,1664]{2,1,0:T(1,128)}), f32[32,1,1664]{2,1,0:T(1,128)S(1)}, u32[]{:S(2)}, u32[]{:S(2)}) async-start(f32[32,1,1664]{2,1,0:T(1,128)} %bitcast.10), calls=%async_computation | async-start | bytes 425984 | tf_op jit(solution)/shard_map/all_to_all | solution.py:634
  15.2 22.2 %copy-start.6 = (s32[1,2048]{1,0:T(1,128)S(1)}, s32[1,2048]{1,0:T(1,128)}, u32[]{:S(2)}) copy-start(s32[1,2048]{1,0:T(1,128)} %cell_ref.3) | copy-start | bytes 24580
  15.2 22.2 %copy-start.7 = (f32[1,2048]{1,0:T(1,128)S(1)}, f32[1,2048]{1,0:T(1,128)}, u32[]{:S(2)}) copy-start(f32[1,2048]{1,0:T(1,128)} %weight_ref.3) | copy-start | bytes 24580
  15.5 4.3 %collective-permute-start.1 = (f32[16,128]{1,0:T(8,128)S(1)}, f32[16,128]{1,0:T(8,128)S(1)}, u32[]{:S(2)}, u32[]{:S(2)}) collective-permute-start(f32[16,128]{1,0:T(8,128)S(1)} %shard_map.132), channel_id=1, source_target_pairs={{0,28},{4,8},{8,4},{12,16},{16,12},{20,24},{24,20},{28,0},{1,29},{... | collective-permute-start | bytes 24584 | tf_op jit(solution)/shard_map/ppermute | solution.py:646
  16.7 4.4 %collective-permute-start = (f32[16,128]{1,0:T(8,128)S(1)}, f32[16,128]{1,0:T(8,128)S(1)}, u32[]{:S(2)}, u32[]{:S(2)}) collective-permute-start(f32[16,128]{1,0:T(8,128)S(1)} %shard_map.132), channel_id=1, source_target_pairs={{0,4},{4,0},{8,12},{12,8},{16,20},{20,16},{24,28},{28,24},{1,5},{5... | collective-permute-start | bytes 24584 | tf_op jit(solution)/shard_map/ppermute | solution.py:647
  24.9 12.5 %all-to-all-start.1 = ((f32[32,1,1664]{2,1,0:T(1,128)}), f32[32,1,1664]{2,1,0:T(1,128)S(1)}, u32[]{:S(2)}, u32[]{:S(2)}) async-start(f32[32,1,1664]{2,1,0:T(1,128)} %bitcast.5), calls=%async_computation.1 | async-start | bytes 425984 | tf_op jit(solution)/shard_map/all_to_all | solution.py:634
  38.2 6.2 %collective-permute-start.2 = (f32[64,128]{1,0:T(8,128)S(1)}, f32[64,128]{1,0:T(8,128)S(1)}, u32[]{:S(2)}, u32[]{:S(2)}) collective-permute-start(f32[64,128]{1,0:T(8,128)S(1)} %get-tuple-element.80), channel_id=1, source_target_pairs={{0,28},{4,8},{8,4},{12,16},{16,12},{20,24},{24,20},{28,0},{1,29},{... | collective-permute-start | bytes 98312 | tf_op jit(solution)/shard_map/ppermute | solution.py:646
  39.5 4.9 %collective-permute-start.3 = (f32[64,128]{1,0:T(8,128)S(1)}, f32[64,128]{1,0:T(8,128)S(1)}, u32[]{:S(2)}, u32[]{:S(2)}) collective-permute-start(f32[64,128]{1,0:T(8,128)S(1)} %get-tuple-element.81), channel_id=1, source_target_pairs={{0,4},{4,0},{8,12},{12,8},{16,20},{20,16},{24,28},{28,24},{1,5},{5... | collective-permute-start | bytes 98312 | tf_op jit(solution)/shard_map/ppermute | solution.py:647
  44.5 7.4 %collective-permute-start.5 = (f32[72,128]{1,0:T(8,128)S(1)}, f32[72,128]{1,0:T(8,128)S(1)}, u32[]{:S(2)}, u32[]{:S(2)}) collective-permute-start(f32[72,128]{1,0:T(8,128)S(1)} %get-tuple-element.87), channel_id=1, source_target_pairs={{1,2},{2,1},{3,31},{5,6},{6,5},{7,27},{9,10},{10,9},{11,23},{13,14... | collective-permute-start | bytes 110600 | tf_op jit(solution)/shard_map/ppermute | solution.py:662
  49.4 2.5 %collective-permute-start.4 = (f32[72,128]{1,0:T(8,128)S(1)}, f32[72,128]{1,0:T(8,128)S(1)}, u32[]{:S(2)}, u32[]{:S(2)}) collective-permute-start(f32[72,128]{1,0:T(8,128)S(1)} %get-tuple-element.88), channel_id=1, source_target_pairs={{0,1},{1,0},{2,3},{3,2},{4,5},{5,4},{6,7},{7,6},{8,9},{9,8},{10,11... | collective-permute-start | bytes 110600 | tf_op jit(solution)/shard_map/ppermute | solution.py:662

commit v13 on v11

--- a/solution.py
+++ b/solution.py
@@ -84,8 +84,9 @@
         pltpu.make_async_copy(cell_in, cell_ref, sems.at[0]),
         pltpu.make_async_copy(weight_in, weight_ref, sems.at[1]),
     ]
-    for place, level in enumerate(range(0, levels_n, chunk)):
-        at = slice(level, level + chunk)
+    step = max(n for n in range(1, 9) if levels_n % n == 0)
+    for place, level in enumerate(range(0, levels_n, step)):
+        at = slice(level, level + step)
         copies.append(pltpu.make_async_copy(state_in.at[at], state_ref.at[at], sems.at[2 + place]))
     for copy in copies:
         copy.start()
@@ -97,10 +98,11 @@
         hot = jnp.concatenate([hot, hot, hot], axis=0)
         mine = sublane((GROUP, tile)) == row
         values = []
-        for index, level in enumerate(range(0, levels_n, chunk)):
+        for level in range(0, levels_n, chunk):
             at = slice(level * GROUP, (level + chunk) * GROUP)
             if start == 0:
-                copies[2 + index].wait()
+                for copy in copies[2:]:
+                    copy.wait()
                 for group in range(groups):
                     block = state_ref[
                         level : level + chunk, group * GROUP : (group + 1) * GROUP, :

time: 55.1 us -> 55 us (level)
  no operation moved by 1% of the time
where the time goes in v13:
time: 55 us; the launch traced here: 54.3 us
  starting transfers between devices  23.1 us (42%)
  Pallas kernels  21.5 us (39%)
  waiting for transfers between devices  8.55 us (16%)
  between operations  1.04 us (2%)
    all_to_all x2, starting transfers between devices, exchanged(): lax.all_to_all(rows, BOTH, split_axis=0, concat_axis=0, tiled=True)  11.3 us
    pallas_call x1, Pallas kernels, on_device(): kernel_call(60, gather_kernel, f32(devices * half, LANES), [pltpu.VMEM((1...  7.92 us
    all_to_all x2, waiting for transfers between devices, exchanged(): lax.all_to_all(rows, BOTH, split_axis=0, concat_axis=0, tiled=True)  6.4 us
    ppermute x2, starting transfers between devices, lat_swaps(): found.append(lax.ppermute(values[parity], BOTH, pairs))  4.97 us
    ppermute x2, starting transfers between devices, lon_swaps(): return (lax.ppermute(first_value, 'lon', first), second_found)  4.35 us
    pallas_call x1, Pallas kernels, on_device(): kernel_call(22 + 3 * tiles, scatter_kernel, (f32(*whole), f32(4, levels,...  3.66 us
    ppermute x2, starting transfers between devices, lon_swaps(): second_found = lax.ppermute(second_value, 'lon', second)  2.49 us
    pallas_call x1, Pallas kernels, on_device(): kernel_call(5, seed_columns_kernel, (f32(rows_n, cols_n), f32(rows_n, col...  2.46 us
  transfers between devices with their start and end apart: 8, of which 4 were waited for; matrix products, arithmetic and copies ran while one was open for 0% of the time, Pallas kernels for 15%

profile of v13, /device:TPU:7, one launch (start us, length us, event | category | flops | bytes accessed | tf_op | source)
XLA Modules:
  0.0 54.3 jit_solution(9644469280386816688)
XLA Ops:
  0.6 0.0 copy-start.1
  0.6 0.0 copy-start.5
  0.7 0.0 copy-start.4
  0.7 0.0 copy-start.3
  0.7 0.0 copy-start.2
  0.7 0.0 copy-start.9
  0.7 0.0 copy-start.8
  0.7 0.0 copy-start.10
  0.7 0.0 copy-start
  0.7 7.9 %shard_map.131 = f32[416,128]{1,0:T(8,128)} custom-call(s32[1,2048]{1,0:T(1,128)} %cell_ref.3, f32[1,2048]{1,0:T(1,128)} %weight_ref.3, f32[25,128,128]{2,1,0:T(8,128)} %state_in.1), custom_call_target="tpu_custom_call" | custom-call | tf_op jit(solution)/shard_map/pallas_call | solution.py:690
  8.7 6.4 %all-to-all-start = ((f32[32,1,1664]{2,1,0:T(1,128)}), f32[32,1,1664]{2,1,0:T(1,128)S(1)}, u32[]{:S(2)}, u32[]{:S(2)}) async-start(f32[32,1,1664]{2,1,0:T(1,128)} %bitcast.10), calls=%async_computation | async-start | bytes 425984 | tf_op jit(solution)/shard_map/all_to_all | solution.py:629
  15.1 0.0 copy-done.1
  15.1 0.0 copy-done.5
  15.1 0.0 copy-done.4
  15.1 0.0 copy-done.3
  15.1 0.0 copy-done.2
  15.1 0.0 copy-start.6
  15.1 0.0 copy-start.7
  15.1 0.3 shard_map.132
  15.4 1.2 %collective-permute-start.1 = (f32[16,128]{1,0:T(8,128)S(1)}, f32[16,128]{1,0:T(8,128)S(1)}, u32[]{:S(2)}, u32[]{:S(2)}) collective-permute-start(f32[16,128]{1,0:T(8,128)S(1)} %shard_map.132), channel_id=1, source_target_pairs={{0,28},{4,8},{8,4},{12,16},{16,12},{20,24},{24,20},{28,0},{1,29},{... | collective-permute-start | bytes 24584 | tf_op jit(solution)/shard_map/ppermute | solution.py:641
  16.6 3.1 %collective-permute-start = (f32[16,128]{1,0:T(8,128)S(1)}, f32[16,128]{1,0:T(8,128)S(1)}, u32[]{:S(2)}, u32[]{:S(2)}) collective-permute-start(f32[16,128]{1,0:T(8,128)S(1)} %shard_map.132), channel_id=1, source_target_pairs={{0,4},{4,0},{8,12},{12,8},{16,20},{20,16},{24,28},{28,24},{1,5},{5... | collective-permute-start | bytes 24584 | tf_op jit(solution)/shard_map/ppermute | solution.py:642
  19.7 0.0 collective-permute-done.1.lon_second_ref
  19.7 1.3 %collective-permute-done.lon_first_ref = f32[16,128]{1,0:T(8,128)S(1)} collective-permute-done((f32[16,128]{1,0:T(8,128)S(1)}, f32[16,128]{1,0:T(8,128)S(1)}, u32[]{:S(2)}, u32[]{:S(2)}) %collective-permute-start) | collective-permute-done | bytes 8224 | tf_op jit(solution)/shard_map/ppermute | solution.py:642
  21.0 1.8 %all-to-all-done = f32[32,1,1664]{2,1,0:T(1,128)S(1)} async-done(((f32[32,1,1664]{2,1,0:T(1,128)}), f32[32,1,1664]{2,1,0:T(1,128)S(1)}, u32[]{:S(2)}, u32[]{:S(2)}) %all-to-all-start) | async-done | bytes 213024 | tf_op jit(solution)/shard_map/all_to_all | solution.py:629
  22.8 0.0 copy-done.9
  22.8 0.0 copy-done.10
  22.8 2.0 %shard_map.133 = (f32[25,512]{1,0:T(8,128)}, f32[416,128]{1,0:T(8,128)}) custom-call(f32[416,128]{1,0:T(8,128)S(1)} %bitcast.9, s32[1,2048]{1,0:T(1,128)S(1)} %copy-done.10, f32[25,512]{1,0:T(8,128)S(1)} %copy-done.8, f32[25,512]{1,0:T(8,128)S(1)} %copy-done.9), custom_call_target="tpu_custom_call" | custom-call | tf_op jit(solution)/shard_map/pallas_call | solution.py:709
  24.9 4.8 %all-to-all-start.1 = ((f32[32,1,1664]{2,1,0:T(1,128)}), f32[32,1,1664]{2,1,0:T(1,128)S(1)}, u32[]{:S(2)}, u32[]{:S(2)}) async-start(f32[32,1,1664]{2,1,0:T(1,128)} %bitcast.5), calls=%async_computation.1 | async-start | bytes 425984 | tf_op jit(solution)/shard_map/all_to_all | solution.py:629
  29.7 0.1 pad_add_fusion
  29.8 0.0 copy-done
  29.8 2.5 %shard_map.134 = (f32[128,128]{1,0:T(8,128)S(1)}, f32[128,128]{1,0:T(8,128)S(1)}) custom-call(f32[25,128,128]{2,1,0:T(8,128)S(1)} %copy-done, s32[128,128]{1,0:T(8,128)S(1)} %copy-done.1), custom_call_target="tpu_custom_call" | custom-call | tf_op jit(solution)/shard_map/pallas_call | solution.py:725
  32.3 0.1 broadcast_in_dim.2.flag_ref
  32.3 0.4 shard_map.135
  32.7 4.6 %all-to-all-done.1 = f32[32,1,1664]{2,1,0:T(1,128)S(1)} async-done(((f32[32,1,1664]{2,1,0:T(1,128)}), f32[32,1,1664]{2,1,0:T(1,128)S(1)}, u32[]{:S(2)}, u32[]{:S(2)}) %all-to-all-start.1) | async-done | bytes 213024 | tf_op jit(solution)/shard_map/all_to_all | solution.py:629
  37.4 0.0 copy-done.6
  37.4 0.8 %shard_map.137 = (f32[64,128]{1,0:T(8,128)S(1)}, f32[64,128]{1,0:T(8,128)S(1)}, f32[128,128]{1,0:T(8,128)S(1)}) custom-call(s32[3,128]{1,0:T(4,128)S(1)} %broadcast_in_dim.2.flag_ref, f32[416,128]{1,0:T(8,128)S(1)} %bitcast.7, s32[1,2048]{1,0:T(1,128)S(1)} %copy-done.6, f32[1,2048]{1,0:T(1,128)S(1)} %copy-done.7, f32[128,128]{1,0:T(8,128)S(1)} %get-tuple-element.78.seed_ref, ...), custom_call_target="tpu_custom_call" | custom-call | tf_op jit(solution)/shard_map/pallas_call | solution.py:739
  38.2 1.3 %collective-permute-start.2 = (f32[64,128]{1,0:T(8,128)S(1)}, f32[64,128]{1,0:T(8,128)S(1)}, u32[]{:S(2)}, u32[]{:S(2)}) collective-permute-start(f32[64,128]{1,0:T(8,128)S(1)} %get-tuple-element.80), channel_id=1, source_target_pairs={{0,28},{4,8},{8,4},{12,16},{16,12},{20,24},{24,20},{28,0},{1,29},{... | collective-permute-start | bytes 98312 | tf_op jit(solution)/shard_map/ppermute | solution.py:641
  39.4 1.3 %collective-permute-start.3 = (f32[64,128]{1,0:T(8,128)S(1)}, f32[64,128]{1,0:T(8,128)S(1)}, u32[]{:S(2)}, u32[]{:S(2)}) collective-permute-start(f32[64,128]{1,0:T(8,128)S(1)} %get-tuple-element.81), channel_id=1, source_target_pairs={{0,4},{4,0},{8,12},{12,8},{16,20},{20,16},{24,28},{28,24},{1,5},{5... | collective-permute-start | bytes 98312 | tf_op jit(solution)/shard_map/ppermute | solution.py:642
  40.7 3.7 %shard_map.136 = (f32[25,128,128]{2,1,0:T(8,128)S(1)}, f32[4,32,128]{2,1,0:T(8,128)S(1)}) custom-call(f32[416,128]{1,0:T(8,128)S(1)} %bitcast.8, s32[1,2048]{1,0:T(1,128)S(1)} %copy-done.6, f32[1,2048]{1,0:T(1,128)S(1)} %copy-done.7, f32[25,128,128]{2,1,0:T(8,128)S(1)} %copy-done, s32[128,128]{1,0:T(8,128)S(1)} %copy-done.1), custom_call_target="tpu_custom_call" | custom-call | tf_op jit(solution)/shard_map/pallas_call | solution.py:746
  44.4 0.0 collective-permute-done.2.lon_second_ref.second_ref
  44.4 0.0 collective-permute-done.3.lon_first_ref.first_ref
  44.4 0.1 shard_map.138
  44.5 4.9 %collective-permute-start.5 = (f32[72,128]{1,0:T(8,128)S(1)}, f32[72,128]{1,0:T(8,128)S(1)}, u32[]{:S(2)}, u32[]{:S(2)}) collective-permute-start(f32[72,128]{1,0:T(8,128)S(1)} %get-tuple-element.87), channel_id=1, source_target_pairs={{1,2},{2,1},{3,31},{5,6},{6,5},{7,27},{9,10},{10,9},{11,23},{13,14... | collective-permute-start | bytes 110600 | tf_op jit(solution)/shard_map/ppermute | solution.py:657
  49.4 0.1 collective-permute-start.4
  49.4 1.6 %shard_map.139 = (f32[25,128,128]{2,1,0:T(8,128)S(1)}, f32[25,128,128]{2,1,0:T(8,128)S(1)}, f32[128,128]{1,0:T(8,128)S(1)}) custom-call(s32[3,128]{1,0:T(4,128)S(1)} %broadcast_in_dim.2.flag_ref, f32[25,128,128]{2,1,0:T(8,128)S(1)} %get-tuple-element.89.seed_ref, f32[7,128,128]{2,1,0:T(8,128)S(1)} %get-tuple-element.90.field_ref, ...), custom_call_target="tpu_custom_call" | custom-call | tf_op jit(solution)/shard_map/pallas_call | solution.py:760
  51.0 0.8 %collective-permute-done.5.lat_second_ref = f32[72,128]{1,0:T(8,128)S(1)} collective-permute-done((f32[72,128]{1,0:T(8,128)S(1)}, f32[72,128]{1,0:T(8,128)S(1)}, u32[]{:S(2)}, u32[]{:S(2)}) %collective-permute-start.5) | collective-permute-done | bytes 36896 | tf_op jit(solution)/shard_map/ppermute | solution.py:657
  51.8 0.0 collective-permute-done.4.lat_first_ref
  51.8 2.3 %shard_map.140 = f32[25,128,128]{2,1,0:T(8,128)} custom-call(s32[3,128]{1,0:T(4,128)S(1)} %broadcast_in_dim.2.flag_ref, f32[25,128,128]{2,1,0:T(8,128)S(1)} %get-tuple-element.96.half_ref, f32[25,128,128]{2,1,0:T(8,128)S(1)} %get-tuple-element.97.masked_ref, f32[128,128]{1,0:T(8,128)S(1)} %get-tuple-element.98.turn_in_ref, ...), custom_call_target="tpu_custom_call" | custom-call | tf_op jit(solution)/shard_map/pallas_call | solution.py:767
  (2 shorter events, 0.0 us)
Async XLA Ops:
  0.6 14.4 %copy-start.1 = (s32[128,128]{1,0:T(8,128)S(1)}, s32[128,128]{1,0:T(8,128)}, u32[]{:S(2)}) copy-start(s32[128,128]{1,0:T(8,128)} %mask_ref.4) | copy-start | bytes 196612
  0.6 14.4 %copy-start.5 = (f32[128,128]{1,0:T(8,128)S(1)}, f32[128,128]{1,0:T(8,128)}, u32[]{:S(2)}) copy-start(f32[128,128]{1,0:T(8,128)} %vertical_ref.1) | copy-start | bytes 196612
  0.7 14.4 %copy-start.4 = (f32[128,128]{1,0:T(8,128)S(1)}, f32[128,128]{1,0:T(8,128)}, u32[]{:S(2)}) copy-start(f32[128,128]{1,0:T(8,128)} %flow_ref.1) | copy-start | bytes 196612
  0.7 14.4 %copy-start.3 = (f32[128,128]{1,0:T(8,128)S(1)}, f32[128,128]{1,0:T(8,128)}, u32[]{:S(2)}) copy-start(f32[128,128]{1,0:T(8,128)} %north_ref.1) | copy-start | bytes 196612
  0.7 14.4 %copy-start.2 = (f32[128,128]{1,0:T(8,128)S(1)}, f32[128,128]{1,0:T(8,128)}, u32[]{:S(2)}) copy-start(f32[128,128]{1,0:T(8,128)} %east_ref.1) | copy-start | bytes 196612
  0.7 22.1 %copy-start.9 = (f32[25,512]{1,0:T(8,128)S(1)}, f32[25,512]{1,0:T(8,128)}, u32[]{:S(2)}) copy-start(f32[25,512]{1,0:T(8,128)} %invvar_ref.1) | copy-start | bytes 153604
  0.7 22.1 %copy-start.8 = (f32[25,512]{1,0:T(8,128)S(1)}, f32[25,512]{1,0:T(8,128)}, u32[]{:S(2)}) copy-start(f32[25,512]{1,0:T(8,128)} %value_ref.1) | copy-start | bytes 153604
  0.7 22.1 %copy-start.10 = (s32[1,2048]{1,0:T(1,128)S(1)}, s32[1,2048]{1,0:T(1,128)}, u32[]{:S(2)}) copy-start(s32[1,2048]{1,0:T(1,128)} %target_ref.1) | copy-start | bytes 24580
  0.7 29.1 %copy-start = (f32[25,128,128]{2,1,0:T(8,128)S(1)}, f32[25,128,128]{2,1,0:T(8,128)}, u32[]{:S(2)}) copy-start(f32[25,128,128]{2,1,0:T(8,128)} %adjoint_ref.2) | copy-start | bytes 4915204
  8.7 14.1 %all-to-all-start = ((f32[32,1,1664]{2,1,0:T(1,128)}), f32[32,1,1664]{2,1,0:T(1,128)S(1)}, u32[]{:S(2)}, u32[]{:S(2)}) async-start(f32[32,1,1664]{2,1,0:T(1,128)} %bitcast.10), calls=%async_computation | async-start | bytes 425984 | tf_op jit(solution)/shard_map/all_to_all | solution.py:629
  15.1 22.2 %copy-start.6 = (s32[1,2048]{1,0:T(1,128)S(1)}, s32[1,2048]{1,0:T(1,128)}, u32[]{:S(2)}) copy-start(s32[1,2048]{1,0:T(1,128)} %cell_ref.3) | copy-start | bytes 24580
  15.1 22.2 %copy-start.7 = (f32[1,2048]{1,0:T(1,128)S(1)}, f32[1,2048]{1,0:T(1,128)}, u32[]{:S(2)}) copy-start(f32[1,2048]{1,0:T(1,128)} %weight_ref.3) | copy-start | bytes 24580
  15.4 4.3 %collective-permute-start.1 = (f32[16,128]{1,0:T(8,128)S(1)}, f32[16,128]{1,0:T(8,128)S(1)}, u32[]{:S(2)}, u32[]{:S(2)}) collective-permute-start(f32[16,128]{1,0:T(8,128)S(1)} %shard_map.132), channel_id=1, source_target_pairs={{0,28},{4,8},{8,4},{12,16},{16,12},{20,24},{24,20},{28,0},{1,29},{... | collective-permute-start | bytes 24584 | tf_op jit(solution)/shard_map/ppermute | solution.py:641
  16.6 4.4 %collective-permute-start = (f32[16,128]{1,0:T(8,128)S(1)}, f32[16,128]{1,0:T(8,128)S(1)}, u32[]{:S(2)}, u32[]{:S(2)}) collective-permute-start(f32[16,128]{1,0:T(8,128)S(1)} %shard_map.132), channel_id=1, source_target_pairs={{0,4},{4,0},{8,12},{12,8},{16,20},{20,16},{24,28},{28,24},{1,5},{5... | collective-permute-start | bytes 24584 | tf_op jit(solution)/shard_map/ppermute | solution.py:642
  24.9 12.5 %all-to-all-start.1 = ((f32[32,1,1664]{2,1,0:T(1,128)}), f32[32,1,1664]{2,1,0:T(1,128)S(1)}, u32[]{:S(2)}, u32[]{:S(2)}) async-start(f32[32,1,1664]{2,1,0:T(1,128)} %bitcast.5), calls=%async_computation.1 | async-start | bytes 425984 | tf_op jit(solution)/shard_map/all_to_all | solution.py:629
  38.2 6.2 %collective-permute-start.2 = (f32[64,128]{1,0:T(8,128)S(1)}, f32[64,128]{1,0:T(8,128)S(1)}, u32[]{:S(2)}, u32[]{:S(2)}) collective-permute-start(f32[64,128]{1,0:T(8,128)S(1)} %get-tuple-element.80), channel_id=1, source_target_pairs={{0,28},{4,8},{8,4},{12,16},{16,12},{20,24},{24,20},{28,0},{1,29},{... | collective-permute-start | bytes 98312 | tf_op jit(solution)/shard_map/ppermute | solution.py:641
  39.4 4.9 %collective-permute-start.3 = (f32[64,128]{1,0:T(8,128)S(1)}, f32[64,128]{1,0:T(8,128)S(1)}, u32[]{:S(2)}, u32[]{:S(2)}) collective-permute-start(f32[64,128]{1,0:T(8,128)S(1)} %get-tuple-element.81), channel_id=1, source_target_pairs={{0,4},{4,0},{8,12},{12,8},{16,20},{20,16},{24,28},{28,24},{1,5},{5... | collective-permute-start | bytes 98312 | tf_op jit(solution)/shard_map/ppermute | solution.py:642
  44.5 7.4 %collective-permute-start.5 = (f32[72,128]{1,0:T(8,128)S(1)}, f32[72,128]{1,0:T(8,128)S(1)}, u32[]{:S(2)}, u32[]{:S(2)}) collective-permute-start(f32[72,128]{1,0:T(8,128)S(1)} %get-tuple-element.87), channel_id=1, source_target_pairs={{1,2},{2,1},{3,31},{5,6},{6,5},{7,27},{9,10},{10,9},{11,23},{13,14... | collective-permute-start | bytes 110600 | tf_op jit(solution)/shard_map/ppermute | solution.py:657
  49.4 2.5 %collective-permute-start.4 = (f32[72,128]{1,0:T(8,128)S(1)}, f32[72,128]{1,0:T(8,128)S(1)}, u32[]{:S(2)}, u32[]{:S(2)}) collective-permute-start(f32[72,128]{1,0:T(8,128)S(1)} %get-tuple-element.88), channel_id=1, source_target_pairs={{0,1},{1,0},{2,3},{3,2},{4,5},{5,4},{6,7},{7,6},{8,9},{9,8},{10,11... | collective-permute-start | bytes 110600 | tf_op jit(solution)/shard_map/ppermute | solution.py:657
